TPU v7x, 512 devices: a whole 4x8x8 slice. The times are simulated.
512 devices in a mesh: lat: 32 (over z_lo, y), lon: 16 (over x, z_hi, core).
Axes of the slice: x: 4, y: 8, z: 8 (z_hi: 2, z_lo: 4; z = z_hi * 4 + z_lo), core: 2. Of those that a mesh axis runs over, the one named last changes fastest.
Arguments:
- saved: bfloat16 [384, 1440, 128], P('lat', 'lon'), may hold values from -6 to 6
- cotangent: bfloat16 [384, 1440, 128], P('lat', 'lon'), may hold values from -6 to 6
- w_in: bfloat16 [128, 512], replicated, may hold values from -0.5 to 0.5
- b_in: float32 [512], replicated, may hold values from -4 to 4
- w_mid: bfloat16 [512, 512], replicated, may hold values from -0.25 to 0.25
- b_mid: float32 [512], replicated, may hold values from -4 to 4
- w_out: bfloat16 [512, 128], replicated, may hold values from -0.25 to 0.25
- spectral_gain: float32 [384, 128], replicated, may hold values from 0.2 to 2
- basis_in: bfloat16 [384, 368, 384], P(None, 'lon', 'lat'), may hold values from -0.3125 to 0.3125
- basis_out: bfloat16 [384, 368, 384], P('lat', 'lon'), may hold values from -0.3125 to 0.3125
Outputs:
- state_grad: float32 [384, 1440, 128], P('lat', 'lon')
All inputs are finite; a program needn't handle non-finite values.
Results may differ from a plain program's by a relative error of at most 0.0065.
Values may be sent and summed in bfloat16 or wider, within the bound.
No kernel may reach another device: no remote copies, remote signals or barrier semaphores. Data moves between devices by JAX's collectives and lax.ppermute only.
A program may use at most 64 MiB of HBM per device.

v0:
```python
import math

import jax
import jax.numpy as jnp
from jax import lax
from jax.sharding import PartitionSpec as P

full_turn = 2.0 * math.pi
highest = lax.Precision.HIGHEST


def silu_slope(value):
    sigm = jax.nn.sigmoid(value)
    return sigm * (1.0 + value * (1.0 - sigm))


def on_device(
    saved, cotangent, w_in, b_in, w_mid, b_mid, w_out, spectral_gain, basis_in, basis_out
):
    first = jnp.einsum("xyc,cu->xyu", saved, w_in, preferred_element_type=jnp.float32) + b_in
    act_one = jax.nn.silu(first).astype(jnp.bfloat16)
    second = jnp.einsum("xyu,uv->xyv", act_one, w_mid, preferred_element_type=jnp.float32) + b_mid
    upward = jnp.einsum("xyc,uc->xyu", cotangent, w_out, preferred_element_type=jnp.float32)
    back_two = (upward * silu_slope(second)).astype(jnp.bfloat16)
    inward = jnp.einsum("xyv,uv->xyu", back_two, w_mid, preferred_element_type=jnp.float32)
    back_one = (inward * silu_slope(first)).astype(jnp.bfloat16)
    grad_grid = cotangent.astype(jnp.float32) + jnp.einsum(
        "xyu,cu->xyc", back_one, w_in, preferred_element_type=jnp.float32
    )
    lon_total = saved.shape[1] * lax.axis_size("lon")
    mode_block = basis_out.shape[1]
    mode_total = mode_block * lax.axis_size("lon")
    wave_total = basis_out.shape[2]
    wave_share = basis_in.shape[2]
    lon_index = jnp.arange(lon_total, dtype=jnp.int32)
    mode_index = jnp.arange(mode_total, dtype=jnp.int32)
    turns = lon_index[:, None] * mode_index[None, :] % lon_total
    angles = turns.astype(jnp.float32) * (full_turn / lon_total)
    cos_table = jnp.cos(angles)
    sin_table = jnp.sin(angles)
    weights = jnp.where(mode_index == 0, 1.0, 2.0).astype(jnp.float32) / lon_total
    circles = lax.all_to_all(grad_grid, "lon", split_axis=2, concat_axis=1, tiled=True)
    real_part = jnp.einsum("xyc,ym->xmc", circles, cos_table, precision=highest)
    imag_part = -jnp.einsum("xyc,ym->xmc", circles, sin_table, precision=highest)
    fourier = lax.all_to_all(
        jnp.stack([real_part, imag_part], 0).astype(jnp.bfloat16),
        "lon",
        split_axis=2,
        concat_axis=3,
        tiled=True,
    )
    global_modes = lax.axis_index("lon") * mode_block + jnp.arange(mode_block, dtype=jnp.int32)
    share_waves = lax.axis_index("lat") * wave_share + jnp.arange(wave_share, dtype=jnp.int32)
    keep_in = share_waves[None, None, :] >= global_modes[None, :, None]
    used_in = jnp.where(keep_in, basis_in, jnp.zeros_like(basis_in))
    all_waves = jnp.arange(wave_total, dtype=jnp.int32)
    keep_out = all_waves[None, None, :] >= global_modes[None, :, None]
    used_out = jnp.where(keep_out, basis_out, jnp.zeros_like(basis_out))
    block_basis = used_in
    spectra = jnp.einsum(
        "xml,rxmc->rlmc",
        block_basis,
        lax.all_gather(fourier, "lat", axis=1, tiled=True),
        preferred_element_type=jnp.float32,
    )
    gain_rows = lax.dynamic_slice_in_dim(
        spectral_gain, lax.axis_index("lat") * wave_share, wave_share, 0
    )
    filtered = (spectra * gain_rows[None, :, None, :]).astype(jnp.bfloat16)
    block_basis = used_out
    latitude_fourier = jnp.einsum(
        "xml,rlmc->rxmc",
        block_basis,
        lax.all_gather(filtered, "lat", axis=1, tiled=True),
        preferred_element_type=jnp.float32,
    )
    circles_two = lax.all_to_all(latitude_fourier, "lon", split_axis=3, concat_axis=2, tiled=True)
    real_part = circles_two[0] * weights[None, :, None]
    imag_part = circles_two[1] * weights[None, :, None]
    result = jnp.einsum("xmc,ym->xyc", real_part, cos_table, precision=highest)
    return lax.all_to_all(
        result - jnp.einsum("xmc,ym->xyc", imag_part, sin_table, precision=highest),
        "lon",
        split_axis=1,
        concat_axis=2,
        tiled=True,
    )


def solution(mesh):
    placed = (
        P("lat", "lon", None),
        P("lat", "lon", None),
        P(),
        P(),
        P(),
        P(),
        P(),
        P(),
        P(None, "lon", "lat"),
        P("lat", "lon", None),
    )
    return jax.shard_map(
        on_device, mesh=mesh, in_specs=placed, out_specs=P("lat", "lon", None), check_vma=False
    )
```

profile of v0, /device:TPU:1, one launch (start us, length us, event | category | flops | bytes accessed | tf_op | source)
XLA Modules:
  0.0 523.7 jit_solution(9579479593294856628)
XLA Ops:
  6.5 1.5 fusion.75
  8.1 0.8 fusion.36
  8.9 0.1 copy-done.3
  9.1 2.0 multiply_convert_fusion.1
  11.1 2.9 fusion.24
  14.0 0.5 copy.54
  14.5 33.6 %all_to_all.69 = f32[12,90,128]{1,0,2:T(8,128)S(1)} all-to-all(f32[12,90,128]{1,0,2:T(8,128)S(1)} %copy.54), channel_id=1, replica_groups=mesh['lat'=32,'lon'=16] {'lon'}, dimensions={2} | all-to-all | bytes 1105920 | tf_op jit(solution)/shard_map/all_to_all | solution.py:42
  48.1 0.5 copy.89
  48.6 0.4 reshape.83
  49.0 10.4 %fusion.52 = bf16[1,12,368,8]{2,1,3,0:T(8,128)(2,1)S(1)} fusion(f32[12,1440,8]{1,0,2:T(8,128)S(1)} %reshape.83), kind=kOutput, calls=%fused_computation.40 | convolution fusion | flops 615307776 | bytes 623616 | tf_op jit(solution)/shard_map/xyc,ym->xmc/dot_general | solution.py:44
  59.3 10.8 %fusion.49 = bf16[1,12,368,8]{2,1,3,0:T(8,128)(2,1)S(1)} fusion(f32[12,1440,8]{1,0,2:T(8,128)S(1)} %reshape.83), kind=kOutput, calls=%fused_computation.39 | convolution fusion | flops 615272448 | bytes 623616 | tf_op jit(solution)/shard_map/xyc,ym->xmc/dot_general | solution.py:43
  70.2 1.4 copy.59
  71.6 1.7 reshape.84
  73.4 22.8 %all_to_all.70 = bf16[16,2,2208]{2,1,0:T(2,128)(2,1)S(1)} all-to-all(bf16[16,2,2208]{2,1,0:T(2,128)(2,1)S(1)} %reshape.84), channel_id=1, replica_groups=mesh['lat'=32,'lon'=16] {'lon'}, dimensions={0} | all-to-all | bytes 282624 | tf_op jit(solution)/shard_map/all_to_all | solution.py:45
  96.2 1.7 reshape.85
  97.9 2.5 copy.61
  100.5 1.0 copy.62
  101.6 0.7 constant_dynamic-slice_fusion
  102.3 0.1 broadcast_compare_fusion
  102.4 0.1 select_bitcast_fusion.1
  102.5 139.4 %all-gather.3.cloned.1.call-done = bf16[2,384,23,128]{3,0,2,1:T(2,128)(2,1)} async-done(((bf16[2,12,23,128]{3,0,2,1:T(2,128)(2,1)}), bf16[2,384,23,128]{3,0,2,1:T(2,128)(2,1)}) %all-gather.3.cloned.1.call-update) | async-done | bytes 4522000 | tf_op jit(solution)/shard_map/all_gather | solution.py:63
  241.9 3.0 fusion.37
  244.9 0.8 copy.65
  245.7 0.1 iota_compare_fusion
  245.8 155.4 %all-gather.5.cloned.1.call-done = bf16[2,384,23,128]{3,0,2,1:T(2,128)(2,1)} async-done(((bf16[2,12,23,128]{3,0,2,1:T(2,128)(2,1)}), bf16[2,384,23,128]{3,0,2,1:T(2,128)(2,1)}) %all-gather.5.cloned.1.call-update) | async-done | bytes 4522000 | tf_op jit(solution)/shard_map/all_gather | solution.py:74
  401.2 3.0 fusion.28
  404.2 1.6 copy.68
  405.8 3.2 reshape.86
  409.1 27.1 %all-to-all-start.2 = ((f32[16,1,4416]{2,1,0:T(1,128)}), f32[16,1,4416]{2,1,0:T(1,128)S(1)}, u32[]{:S(2)}, u32[]{:S(2)}) async-start(f32[16,1,4416]{2,1,0:T(1,128)} %reshape.86), calls=%async_computation.2 | async-start | bytes 573440 | tf_op jit(solution)/shard_map/all_to_all | solution.py:77
  436.2 11.0 %all-to-all-done.2 = f32[16,1,4416]{2,1,0:T(1,128)S(1)} async-done(((f32[16,1,4416]{2,1,0:T(1,128)}), f32[16,1,4416]{2,1,0:T(1,128)S(1)}, u32[]{:S(2)}, u32[]{:S(2)}) %all-to-all-start.2) | async-done | bytes 282656 | tf_op jit(solution)/shard_map/all_to_all | solution.py:77
  447.2 0.5 broadcast.79
  447.7 1.3 reduce
  449.1 2.5 reshape.87
  451.6 0.3 copy.112
  451.9 0.1 fusion.92
  452.1 0.1 copy.72
  452.2 0.4 squeeze.7
  452.6 0.1 copy.70
  452.7 0.4 squeeze.6
  453.1 11.2 %fusion.10 = f32[1440,12,8]{0,1,2:T(8,128)S(1)} fusion(f32[12,368,8]{1,2,0:T(8,128)S(1)} %get-tuple-element.8), kind=kOutput, calls=%fused_computation.16 | convolution fusion | flops 615237120 | bytes 694272 | tf_op jit(solution)/shard_map/xmc,ym->xyc/dot_general | solution.py:80
  464.3 11.0 %fusion.4 = f32[12,1440,8]{1,0,2:T(8,128)S(1)} fusion(f32[1440,12,8]{0,1,2:T(8,128)S(1)} %fusion.10, f32[12,368,8]{1,2,0:T(8,128)S(1)} %get-tuple-element.7), kind=kOutput, calls=%fused_computation.6 | convolution fusion | flops 615375360 | bytes 1247232 | tf_op jit(solution)/shard_map/xmc,ym->xyc/dot_general | solution.py:82
  475.3 3.9 copy.74
  479.3 6.1 %reshape.88 = f32[16,1,8640]{2,1,0:T(1,128)S(1)} reshape(f32[1440,8,12]{2,1,0:T(8,128)} %bitcast.97) | data formatting | bytes 1105920
  485.4 18.5 %all_to_all.71 = f32[16,1,8640]{2,1,0:T(1,128)S(1)} all-to-all(f32[16,1,8640]{2,1,0:T(1,128)S(1)} %reshape.88), channel_id=1, replica_groups=mesh['lat'=32,'lon'=16] {'lon'}, dimensions={0} | all-to-all | bytes 1105920 | tf_op jit(solution)/shard_map/all_to_all | solution.py:81
  503.9 2.0 reduce.1
  505.9 5.0 reshape.89
  510.9 4.7 copy.76
  515.6 1.1 copy.77
  (23 shorter events, 0.3 us)
Async XLA Ops:
  6.5 1.5 copy-start
  6.5 1.5 copy-start.6
  6.5 235.4 %all-gather.3.cloned.1.call-start = ((), (), s32[]{:S(2)}) async-start(), calls=%async_computation.4 | async-start | bytes 4663296 | tf_op jit(solution)/shard_map/all_gather | solution.py:63
  8.1 1.0 copy-start.3
  8.1 1.0 copy-start.4
  8.1 1.0 copy-start.5
  96.2 6.2 %copy-start.1 = (bf16[384,23,12]{0,1,2:T(8,128)(2,1)S(1)}, bf16[384,23,12]{0,1,2:T(8,128)(2,1)}, u32[]{:S(2)}) copy-start(bf16[384,23,12]{0,1,2:T(8,128)(2,1)} %param.18) | copy-start | bytes 635908
  101.5 299.7 %all-gather.5.cloned.1.call-start = ((), (), s32[]{:S(2)}) async-start(), calls=%async_computation.5 | async-start | bytes 4663296 | tf_op jit(solution)/shard_map/all_gather | solution.py:74
  102.5 143.3 %copy-start.2 = (bf16[12,23,384]{2,1,0:T(8,128)(2,1)S(1)}, bf16[12,23,384]{2,1,0:T(8,128)(2,1)}, u32[]{:S(2)}) copy-start(bf16[12,23,384]{2,1,0:T(8,128)(2,1)} %param.19) | copy-start | bytes 635908
  409.1 38.2 %all-to-all-start.2 = ((f32[16,1,4416]{2,1,0:T(1,128)}), f32[16,1,4416]{2,1,0:T(1,128)S(1)}, u32[]{:S(2)}, u32[]{:S(2)}) async-start(f32[16,1,4416]{2,1,0:T(1,128)} %reshape.86), calls=%async_computation.2 | async-start | bytes 573440 | tf_op jit(solution)/shard_map/all_to_all | solution.py:77
Sparse Core Ops, SparseCore 0:
  101.6 140.2 all-gather.2
  245.8 155.3 all-gather.4
where the time goes:
time: 528 us; the launch traced here: 524 us
  waiting for transfers between devices  306 us (58%)
  blocking collectives  74.9 us (14%)
  matrix products  56.6 us (11%)
  local copies, waits for them, and re-layouts  41.6 us (8%)
  starting transfers between devices  27.2 us (5%)
  between operations  13.9 us (3%)
    all_gather x1, waiting for transfers between devices, on_device(): lax.all_gather(filtered, 'lat', axis=1, tiled=True)  155 us
    all_gather x1, waiting for transfers between devices, on_device(): lax.all_gather(fourier, 'lat', axis=1, tiled=True)  139 us
    all_to_all x1, blocking collectives, on_device(): lax.all_to_all(grad_grid, 'lon', split_axis=2, concat_axis=1, tiled=True)  33.6 us
    all_to_all x1, starting transfers between devices, on_device(): lax.all_to_all(latitude_fourier, 'lon', split_axis=3, concat_axis=2, tile...  27.1 us
    all_to_all x1, blocking collectives, on_device(): lax.all_to_all(jnp.stack([real_part, imag_part], 0).astype(jnp.bfloat16),...  22.8 us
    unnamed x20, local copies, waits for them, and re-layouts  20.6 us
    all_to_all x1, blocking collectives, on_device(): lax.all_to_all(result - jnp.einsum('xmc,ym->xyc', imag_part, sin_table, p...  18.5 us
    dot_general x1, matrix products, on_device(): result = jnp.einsum('xmc,ym->xyc', real_part, cos_table, precision=highest)  11.2 us
  transfers between devices with their start and end apart: 3, of which 3 were waited for; matrix products, arithmetic and copies ran while one was open for 0% of the time, Pallas kernels for 0%

commit v1 on v0

v1 whole, which is shorter than its diff:
```python
import numpy as np
import jax
import jax.numpy as jnp
from jax import lax
from jax.experimental import pallas as pl
from jax.experimental.pallas import tpu as pltpu
from jax.sharding import PartitionSpec as P

bf16 = jnp.bfloat16
f32 = jnp.float32

LAT_DEV, LON_DEV = 32, 16
X_DEV, Y_DEV = 12, 90
Y_PAD = 96
NLAT, NLON, NM, NL, CHAN = 384, 1440, 368, 384, 128
M_DEV = 23
X_SUB, C_SUB = 3, 32
CG = CHAN // C_SUB
XG = X_DEV // X_SUB
DEVS = LAT_DEV * LON_DEV
ROWS = 2 * NM
VMEM = 40 * 1024 * 1024


def zonal_tables():
    order = (M_DEV * np.arange(LON_DEV)[None, :] + np.arange(M_DEV)[:, None]).reshape(-1)
    turns = (order[:, None] * np.arange(NLON)[None, :]) % NLON
    angles = turns.astype(np.float64) * (2.0 * np.pi / NLON)
    table = np.stack([np.cos(angles), -np.sin(angles)], 1).reshape(ROWS, NLON)
    weight = np.where(order == 0, 1.0, 2.0) / NLON
    back = (table * np.repeat(weight, 2)[:, None]).T

    def pad_y(t, axis):
        shape = list(t.shape)
        shape[axis : axis + 1] = [LON_DEV, Y_DEV]
        widths = [(0, 0)] * len(shape)
        widths[axis + 1] = (0, Y_PAD - Y_DEV)
        t = np.pad(t.reshape(shape), widths)
        shape = list(t.shape)
        shape[axis : axis + 2] = [LON_DEV * Y_PAD]
        return t.reshape(shape)

    return (
        np.asarray(pad_y(table, 1), dtype=jnp.bfloat16),
        np.asarray(pad_y(back, 0), dtype=jnp.bfloat16),
    )


def order_tables():
    index = np.arange(NL)
    pick_in = np.zeros((NL, LAT_DEV * 24), np.float32)
    pick_in[index, 24 * (index // 12) + index % 12] = 1
    xx, i, xg = np.meshgrid(np.arange(X_SUB), np.arange(LAT_DEV), np.arange(XG), indexing="ij")
    xx, i, xg = xx.reshape(-1), i.reshape(-1), xg.reshape(-1)
    pick_out = np.zeros((NLAT, LAT_DEV * 24), np.float32)
    pick_out[index, 24 * i + 12 + X_SUB * xg + xx] = 1
    natural = np.zeros((NLAT, NLAT), np.float32)
    natural[12 * i + X_SUB * xg + xx, index] = 1
    return (
        np.asarray(pick_in, dtype=jnp.bfloat16),
        np.asarray(pick_out, dtype=jnp.bfloat16),
        np.asarray(natural, dtype=jnp.bfloat16),
    )


def dot(a, b):
    return lax.dot_general(a, b, (((1,), (0,)), ((), ())), preferred_element_type=f32)


def dot_t(a, b):
    return lax.dot_general(a, b, (((1,), (1,)), ((), ())), preferred_element_type=f32)


def sigmoid(v):
    return 0.5 * jnp.tanh(0.5 * v) + 0.5


def network_kernel(saved, cotan, w_in, b_in, w_mid, b_mid, w_out, out, rows_s, rows_c):
    rows_s[...] = jnp.zeros_like(rows_s)
    rows_c[...] = jnp.zeros_like(rows_c)
    for x in range(X_DEV):
        rows_s[x, 0:Y_DEV, :] = saved[x]
        rows_c[x, 0:Y_DEV, :] = cotan[x]
    for xg in range(XG):
        s = rows_s[X_SUB * xg : X_SUB * (xg + 1)].reshape(X_SUB * Y_PAD, CHAN)
        c = rows_c[X_SUB * xg : X_SUB * (xg + 1)].reshape(X_SUB * Y_PAD, CHAN)
        first = dot(s, w_in[...]) + b_in[...]
        sig = sigmoid(first)
        act = first * sig
        slope_one = sig + act * (1.0 - sig)
        second = dot(act.astype(bf16), w_mid[...]) + b_mid[...]
        sig = sigmoid(second)
        slope_two = sig * (1.0 + second * (1.0 - sig))
        back_two = (dot_t(c, w_out[...]) * slope_two).astype(bf16)
        back_one = (dot_t(back_two, w_mid[...]) * slope_one).astype(bf16)
        grad = c.astype(f32) + dot_t(back_one, w_in[...])
        grad = grad.reshape(X_SUB, Y_PAD, CHAN)
        for cg in range(CG):
            parts = [grad[xx][:, C_SUB * cg : C_SUB * (cg + 1)] for xx in range(X_SUB)]
            parts.append(jnp.zeros((Y_PAD, C_SUB), f32))
            out[CG * xg + cg] = jnp.concatenate(parts, axis=1).astype(bf16)


def zonal_kernel(circles, table, out):
    g = circles[...].reshape(LON_DEV * Y_PAD, 128)
    out[0:ROWS, :] = dot(table[...], g).astype(bf16)
    out[ROWS:, :] = jnp.zeros((2 * DEVS - ROWS, 128), bf16)


def legendre_kernel(mode, coeffs, bases, gain, pick_in, pick_out, natural, out, rows):
    m = mode[0]
    rows[...] = coeffs[...].astype(f32)
    packs = [rows[pl.ds(s, 128, stride=8), :] for s in range(2 * CG)]
    stack = []
    for xx in range(X_SUB):
        parts = [
            packs[2 * cg + r][:, C_SUB * xx : C_SUB * (xx + 1)] for r in range(2) for cg in range(CG)
        ]
        stack.append(jnp.concatenate(parts, axis=1))
    fourier = jnp.concatenate(stack, axis=0).astype(bf16)
    fourier = dot(natural[...], fourier).astype(bf16)
    table = dot(pick_in[...], bases[...])
    waves = lax.broadcasted_iota(jnp.int32, (NL, NLAT), 0)
    table = jnp.where(waves >= m, table, 0.0).astype(bf16)
    gains = jnp.concatenate([gain[...], gain[...]], axis=1)
    filtered = (dot(table, fourier) * gains).astype(bf16)
    table = dot(pick_out[...], bases[...])
    waves = lax.broadcasted_iota(jnp.int32, (NLAT, NL), 1)
    table = jnp.where(waves >= m, table, 0.0).astype(bf16)
    result = dot(table, filtered)
    for cg in range(CG):
        for r in range(2):
            first = CHAN * r + C_SUB * cg
            parts = [result[128 * xx : 128 * (xx + 1), first : first + C_SUB] for xx in range(X_SUB)]
            parts.append(jnp.zeros((128, C_SUB), f32))
            rows[pl.ds(2 * cg + r, 128, stride=8), :] = jnp.concatenate(parts, axis=1)
    out[...] = rows[...].astype(bf16)


def inverse_kernel(coeffs, table, out):
    z = coeffs[0:ROWS, :]
    out[...] = dot(table[...], z).astype(bf16).reshape(LON_DEV, Y_PAD, 128)


def grid_kernel(pieces, out):
    for xg in range(XG):
        blocks = [pieces[CG * xg + cg].astype(f32) for cg in range(CG)]
        for xx in range(X_SUB):
            parts = [b[:, C_SUB * xx : C_SUB * (xx + 1)] for b in blocks]
            out[X_SUB * xg + xx] = jnp.concatenate(parts, axis=1)[0:Y_DEV]


def call(kernel, shape, dtype, scratch=(), smem=0, flops=0, moved=0):
    def run(*args):
        specs = [
            pl.BlockSpec(memory_space=pltpu.SMEM if k < smem else pltpu.VMEM) for k in range(len(args))
        ]
        return pl.pallas_call(
            kernel,
            out_shape=jax.ShapeDtypeStruct(shape, dtype),
            in_specs=specs,
            out_specs=pl.BlockSpec(memory_space=pltpu.VMEM),
            scratch_shapes=list(scratch),
            compiler_params=pltpu.CompilerParams(vmem_limit_bytes=VMEM),
            cost_estimate=pl.CostEstimate(flops=flops, bytes_accessed=moved, transcendentals=0),
        )(*args)

    return run


def on_device(
    saved, cotangent, w_in, b_in, w_mid, b_mid, w_out, spectral_gain, basis_in, basis_out
):
    forward, back = zonal_tables()
    pick_in, pick_out, natural = order_tables()
    bases = jnp.concatenate(
        [jnp.transpose(basis_in, (1, 2, 0)), jnp.transpose(basis_out, (1, 0, 2))], axis=1
    )
    bases = jnp.pad(bases, ((0, LAT_DEV - M_DEV), (0, 0), (0, 0)))
    bases = lax.all_to_all(bases, "lat", 0, 0, tiled=True).reshape(LAT_DEV * 24, NL)

    pad = pltpu.VMEM((X_DEV, Y_PAD, CHAN), bf16)
    pieces = call(network_kernel, (LON_DEV, Y_PAD, 128), bf16, (pad, pad), flops=1_700_000_000)(
        saved, cotangent, w_in, b_in.reshape(1, -1), w_mid, b_mid.reshape(1, -1), w_out
    )
    pieces = lax.all_to_all(pieces, "lon", 0, 0, tiled=True)
    coeffs = call(zonal_kernel, (2 * DEVS, 128), bf16, flops=300_000_000)(pieces, jnp.asarray(forward))
    coeffs = lax.all_to_all(coeffs.reshape(DEVS, 2, 128), ("lat", "lon"), 0, 0, tiled=True)
    mode = (M_DEV * lax.axis_index("lon") + lax.axis_index("lat")).astype(jnp.int32).reshape(1)
    coeffs = call(
        legendre_kernel,
        (2 * DEVS, 128),
        bf16,
        (pltpu.VMEM((2 * DEVS, 128), f32),),
        smem=1,
        flops=800_000_000,
    )(
        mode,
        coeffs.reshape(2 * DEVS, 128),
        bases,
        spectral_gain,
        jnp.asarray(pick_in),
        jnp.asarray(pick_out),
        jnp.asarray(natural),
    )
    coeffs = lax.all_to_all(coeffs.reshape(DEVS, 2, 128), ("lat", "lon"), 0, 0, tiled=True)
    pieces = call(inverse_kernel, (LON_DEV, Y_PAD, 128), bf16, flops=300_000_000)(
        coeffs.reshape(2 * DEVS, 128), jnp.asarray(back)
    )
    pieces = lax.all_to_all(pieces, "lon", 0, 0, tiled=True)
    return call(grid_kernel, (X_DEV, Y_DEV, CHAN), f32)(pieces)


def solution(mesh):
    placed = (
        P("lat", "lon", None),
        P("lat", "lon", None),
        P(),
        P(),
        P(),
        P(),
        P(),
        P(),
        P(None, "lon", "lat"),
        P("lat", "lon", None),
    )
    return jax.shard_map(
        on_device, mesh=mesh, in_specs=placed, out_specs=P("lat", "lon", None), check_vma=False
    )
```

time: 528 us -> 149 us (0.28)
  waiting for transfers between devices: 306 us -> 43.6 us
  matrix products: 56.6 us -> 0 us
  local copies, waits for them, and re-layouts: 41.6 us -> 9.32 us
  blocking collectives: 74.9 us -> 43 us
  between operations: 13.9 us -> 0.1 us
  starting transfers between devices: 27.2 us -> 39.5 us
  Pallas kernels: 0 us -> 9.87 us
    all_gather x2 -> x0, waiting for transfers between devices: 295 us -> none  [the longest x1 155 us: on_device(): lax.all_gather(filtered, 'lat', axis=1, tiled=True)]
    dot_general x10 -> x0, matrix products: 56.6 us -> none  [the longest x1 11.2 us: on_device(): result = jnp.einsum('xmc,ym->xyc', real_part, cos_table, precision=highest)]
    all_to_all x1 -> x3, waiting for transfers between devices: 11 us -> 43.6 us  [the longest x1 17.5 us: on_device(): lax.all_to_all(coeffs.reshape(DEVS, 2, 128), ('lat', 'lon'), 0, 0, tiled=...]
    all_to_all x3 -> x2, blocking collectives: 74.9 us -> 43 us  [the longest x1 26.7 us: on_device(): lax.all_to_all(coeffs.reshape(DEVS, 2, 128), ('lat', 'lon'), 0, 0, tiled=...]
    all_to_all x1 -> x3, starting transfers between devices: 27.1 us -> 39.5 us  [the longest x1 14.4 us: on_device(): pieces = lax.all_to_all(pieces, 'lon', 0, 0, tiled=True)]
    unnamed x20 -> x32, local copies, waits for them, and re-layouts: 20.6 us -> 9.32 us
    all_to_all x8 -> x0, local copies, waits for them, and re-layouts: 11 us -> none  [the longest x2 5.76 us: on_device(): lax.all_to_all(result - jnp.einsum('xmc,ym->xyc', imag_part, sin_table, p...]
    pallas_call x0 -> x5, Pallas kernels: none -> 9.87 us  [run(): pl.pallas_call(kernel, out_shape=jax.ShapeDtypeStruct(shape, dtype), in_s...]
  transfers between devices with their start and end apart: 3 -> 3, of which waited for: 3 -> 3; matrix products, arithmetic and copies ran while one was open for 0% -> 1% of each run, Pallas kernels for 0% -> 1%
where the time goes in v1:
time: 149 us; the launch traced here: 146 us
  waiting for transfers between devices  43.6 us (29%)
  blocking collectives  43 us (29%)
  starting transfers between devices  39.5 us (27%)
  Pallas kernels  9.87 us (7%)
  local copies, waits for them, and re-layouts  9.32 us (6%)
    all_to_all x1, blocking collectives, on_device(): lax.all_to_all(coeffs.reshape(DEVS, 2, 128), ('lat', 'lon'), 0, 0, tiled=...  26.7 us
    all_to_all x1, waiting for transfers between devices, on_device(): lax.all_to_all(coeffs.reshape(DEVS, 2, 128), ('lat', 'lon'), 0, 0, tiled=...  17.5 us
    all_to_all x1, blocking collectives, on_device(): pieces = lax.all_to_all(pieces, 'lon', 0, 0, tiled=True)  16.3 us
    all_to_all x1, waiting for transfers between devices, on_device(): lax.all_to_all(bases, 'lat', 0, 0, tiled=True).reshape(LAT_DEV * 24, NL)  14.7 us
    all_to_all x1, starting transfers between devices, on_device(): pieces = lax.all_to_all(pieces, 'lon', 0, 0, tiled=True)  14.4 us
    all_to_all x1, starting transfers between devices, on_device(): lax.all_to_all(bases, 'lat', 0, 0, tiled=True).reshape(LAT_DEV * 24, NL)  13.8 us
    all_to_all x1, waiting for transfers between devices, on_device(): pieces = lax.all_to_all(pieces, 'lon', 0, 0, tiled=True)  11.4 us
    all_to_all x1, starting transfers between devices, on_device(): lax.all_to_all(coeffs.reshape(DEVS, 2, 128), ('lat', 'lon'), 0, 0, tiled=...  11.3 us
  transfers between devices with their start and end apart: 3, of which 3 were waited for; matrix products, arithmetic and copies ran while one was open for 1% of the time, Pallas kernels for 1%

profile of v1, /device:TPU:1, one launch (start us, length us, event | category | flops | bytes accessed | tf_op | source)
XLA Modules:
  0.0 146.3 jit_solution(2480772297746165311)
XLA Ops:
  0.0 0.0 copy-start.2
  0.0 1.0 copy-done.2
  1.0 0.0 copy-start.3
  1.0 1.0 copy-done.3
  2.0 0.0 copy-start.4
  2.0 1.0 copy-done.4
  3.0 0.0 copy-start.6
  3.0 0.9 copy-done.6
  3.9 0.0 copy-start.7
  3.9 0.9 copy-done.7
  4.8 0.0 copy-start.8
  4.8 0.7 copy-done.8
  5.5 0.0 copy-start.9
  5.5 0.7 copy-done.9
  6.1 0.0 copy-start.13
  6.1 4.7 %shard_map.145 = bf16[16,96,128]{2,1,0:T(8,128)(2,1)} custom-call(bf16[12,90,128]{2,1,0:T(8,128)(2,1)S(1)} %copy-done.3, bf16[12,90,128]{2,1,0:T(8,128)(2,1)S(1)} %copy-done.4, bf16[128,512]{1,0:T(8,128)(2,1)S(1)} %copy-done.6, f32[1,512]{1,0:T(1,128)S(1)} %bitcast.18, bf16[512,512]{1,0:T(8,128)(2,1)S(1)} %copy-done.2, f32[1,512]{1,0:T(1,128)S(1)} %bitcast.19, ...), custom_call_target="tpu_custom_call" | custom-call | flops 1700000000 | tf_op jit(solution)/shard_map/pallas_call | solution.py:158
  10.9 0.0 copy-start.14
  10.9 14.4 %all-to-all-start = ((bf16[16,96,128]{2,1,0:T(8,128)(2,1)}), bf16[16,96,128]{2,1,0:T(8,128)(2,1)S(1)}, u32[]{:S(2)}, u32[]{:S(2)}) async-start(bf16[16,96,128]{2,1,0:T(8,128)(2,1)} %shard_map.145), calls=%async_computation | async-start | bytes 786432 | tf_op jit(solution)/shard_map/all_to_all | solution.py:186
  25.3 0.0 copy-done.13
  25.3 0.0 copy-done.14
  25.4 0.0 copy-start.1
  25.4 0.9 fusion.2
  26.3 11.4 %all-to-all-done.circles = bf16[16,96,128]{2,1,0:T(8,128)(2,1)S(1)} async-done(((bf16[16,96,128]{2,1,0:T(8,128)(2,1)}), bf16[16,96,128]{2,1,0:T(8,128)(2,1)S(1)}, u32[]{:S(2)}, u32[]{:S(2)}) %all-to-all-start) | async-done | bytes 393248 | tf_op jit(solution)/shard_map/all_to_all | solution.py:186
  37.7 13.8 %all-to-all-start.2 = ((bf16[32,24,384]{2,1,0:T(8,128)(2,1)}), bf16[32,24,384]{2,1,0:T(8,128)(2,1)S(1)}, u32[]{:S(2)}, u32[]{:S(2)}) async-start(bf16[32,24,384]{2,1,0:T(8,128)(2,1)} %fusion.2), calls=%async_computation.2 | async-start | bytes 1179648 | tf_op jit(solution)/shard_map/all_to_all | solution.py:180
  51.5 0.0 copy-done.1
  51.6 0.0 copy-start.5
  51.6 1.4 shard_map.146
  53.0 14.7 %all-to-all-done.2 = bf16[32,24,384]{2,1,0:T(8,128)(2,1)S(1)} async-done(((bf16[32,24,384]{2,1,0:T(8,128)(2,1)}), bf16[32,24,384]{2,1,0:T(8,128)(2,1)S(1)}, u32[]{:S(2)}, u32[]{:S(2)}) %all-to-all-start.2) | async-done | bytes 589856 | tf_op jit(solution)/shard_map/all_to_all | solution.py:180
  67.7 11.3 %all-to-all-start.1 = ((bf16[512,2,128]{2,1,0:T(2,128)(2,1)}), bf16[512,2,128]{2,1,0:T(2,128)(2,1)S(1)}, u32[]{:S(2)}, u32[]{:S(2)}) async-start(bf16[512,2,128]{2,1,0:T(2,128)(2,1)} %bitcast.3), calls=%async_computation.1 | async-start | bytes 524288 | tf_op jit(solution)/shard_map/all_to_all | solution.py:188
  79.1 17.5 %all-to-all-done.1 = bf16[512,2,128]{2,1,0:T(2,128)(2,1)S(1)} async-done(((bf16[512,2,128]{2,1,0:T(2,128)(2,1)}), bf16[512,2,128]{2,1,0:T(2,128)(2,1)S(1)}, u32[]{:S(2)}, u32[]{:S(2)}) %all-to-all-start.1) | async-done | bytes 262176 | tf_op jit(solution)/shard_map/all_to_all | solution.py:188
  96.6 0.0 copy-done.5
  96.6 0.0 copy-start.10
  96.6 1.1 copy-done.10
  97.6 0.0 copy-start.11
  97.6 1.1 copy-done.11
  98.7 0.0 copy-start.12
  98.7 1.0 copy-done.12
  99.7 0.0 copy-start
  99.7 1.8 %shard_map.147 = bf16[1024,128]{1,0:T(8,128)(2,1)S(1)} custom-call(s32[1]{0:T(128)} %bitcast.mode, bf16[1024,128]{1,0:T(8,128)(2,1)S(1)} %bitcast.16, bf16[768,384]{1,0:T(8,128)(2,1)S(1)} %bitcast.15, f32[384,128]{1,0:T(8,128)S(1)} %copy-done.5, bf16[384,768]{1,0:T(8,128)(2,1)S(1)} %copy-done.11, bf16[384,768]{1,0:T(8,128)(2,1)S(1)} %copy-done.10, ...), custom_call_target="tpu_custom_call" | custom-call | flops 800000000 | tf_op jit(solution)/shard_map/pallas_call | solution.py:158
  101.4 26.7 %all_to_all.25 = bf16[512,2,128]{2,1,0:T(2,128)(2,1)S(1)} all-to-all(bf16[512,2,128]{2,1,0:T(2,128)(2,1)S(1)} %bitcast.17), channel_id=1, replica_groups=mesh['lat'=32,'lon'=16] {'lat','lon'}, dimensions={0} | all-to-all | bytes 524288 | tf_op jit(solution)/shard_map/all_to_all | solution.py:206
  128.1 0.0 copy-done
  128.1 0.8 shard_map.148
  128.9 16.3 %all_to_all.26.pieces = bf16[16,96,128]{2,1,0:T(8,128)(2,1)S(1)} all-to-all(bf16[16,96,128]{2,1,0:T(8,128)(2,1)S(1)} %shard_map.148), channel_id=1, replica_groups=mesh['lat'=32,'lon'=16] {'lon'}, dimensions={0} | all-to-all | bytes 786432 | tf_op jit(solution)/shard_map/all_to_all | solution.py:210
  145.2 1.1 shard_map.149
  (2 shorter events, 0.1 us)
Async XLA Ops:
  0.0 1.0 copy-start.2
  1.0 1.0 copy-start.3
  2.0 1.0 copy-start.4
  3.0 0.9 copy-start.6
  3.9 0.9 copy-start.7
  4.8 0.7 copy-start.8
  5.5 0.7 copy-start.9
  6.1 19.1 %copy-start.13 = (bf16[384,23,12]{0,1,2:T(8,128)(2,1)S(1)}, bf16[384,23,12]{0,1,2:T(8,128)(2,1)}, u32[]{:S(2)}) copy-start(bf16[384,23,12]{0,1,2:T(8,128)(2,1)} %param.23) | copy-start | bytes 635908
  10.9 14.4 %copy-start.14 = (bf16[12,23,384]{2,1,0:T(8,128)(2,1)S(1)}, bf16[12,23,384]{2,1,0:T(8,128)(2,1)}, u32[]{:S(2)}) copy-start(bf16[12,23,384]{2,1,0:T(8,128)(2,1)} %param.24) | copy-start | bytes 635908
  10.9 26.8 %all-to-all-start = ((bf16[16,96,128]{2,1,0:T(8,128)(2,1)}), bf16[16,96,128]{2,1,0:T(8,128)(2,1)S(1)}, u32[]{:S(2)}, u32[]{:S(2)}) async-start(bf16[16,96,128]{2,1,0:T(8,128)(2,1)} %shard_map.145), calls=%async_computation | async-start | bytes 786432 | tf_op jit(solution)/shard_map/all_to_all | solution.py:186
  25.4 26.2 %copy-start.1 = (bf16[736,1536]{1,0:T(8,128)(2,1)S(1)}, bf16[736,1536]{1,0:T(8,128)(2,1)}, u32[]{:S(2)}) copy-start(bf16[736,1536]{1,0:T(8,128)(2,1)} %constant.24.clone.table) | copy-start | bytes 6782980
  37.7 30.0 %all-to-all-start.2 = ((bf16[32,24,384]{2,1,0:T(8,128)(2,1)}), bf16[32,24,384]{2,1,0:T(8,128)(2,1)S(1)}, u32[]{:S(2)}, u32[]{:S(2)}) async-start(bf16[32,24,384]{2,1,0:T(8,128)(2,1)} %fusion.2), calls=%async_computation.2 | async-start | bytes 1179648 | tf_op jit(solution)/shard_map/all_to_all | solution.py:180
  51.6 45.0 %copy-start.5 = (f32[384,128]{1,0:T(8,128)S(1)}, f32[384,128]{1,0:T(8,128)}, u32[]{:S(2)}) copy-start(f32[384,128]{1,0:T(8,128)} %gain.1) | copy-start | bytes 589828
  67.7 28.8 %all-to-all-start.1 = ((bf16[512,2,128]{2,1,0:T(2,128)(2,1)}), bf16[512,2,128]{2,1,0:T(2,128)(2,1)S(1)}, u32[]{:S(2)}, u32[]{:S(2)}) async-start(bf16[512,2,128]{2,1,0:T(2,128)(2,1)} %bitcast.3), calls=%async_computation.1 | async-start | bytes 524288 | tf_op jit(solution)/shard_map/all_to_all | solution.py:188
  96.6 1.1 copy-start.10
  97.6 1.1 copy-start.11
  98.7 1.0 copy-start.12
  99.7 28.5 %copy-start = (bf16[1536,736]{1,0:T(8,128)(2,1)S(1)}, bf16[1536,736]{1,0:T(8,128)(2,1)}, u32[]{:S(2)}) copy-start(bf16[1536,736]{1,0:T(8,128)(2,1)} %constant.28.clone.table) | copy-start | bytes 6782980

commit v2 on v1

v2 whole, which is shorter than its diff:
```python
import numpy as np
import jax
import jax.numpy as jnp
from jax import lax
from jax.experimental import pallas as pl
from jax.experimental.pallas import tpu as pltpu
from jax.sharding import PartitionSpec as P

bf16 = jnp.bfloat16
f32 = jnp.float32

LAT_DEV, LON_DEV = 32, 16
X_DEV, Y_DEV = 12, 90
Y_PAD = 96
Y_MAIN, Y_EXT = 72, 24
NLAT, NLON, NM, NL, CHAN = 384, 1440, 368, 384, 128
M_DEV = 23
X_SUB, C_SUB = 3, 32
CG = CHAN // C_SUB
XG = X_DEV // X_SUB
DEVS = LAT_DEV * LON_DEV
ROWS = 2 * NM
VMEM = 40 * 1024 * 1024


def zonal_tables():
    order = (M_DEV * np.arange(LON_DEV)[None, :] + np.arange(M_DEV)[:, None]).reshape(-1)
    turns = (order[:, None] * np.arange(NLON)[None, :]) % NLON
    angles = turns.astype(np.float64) * (2.0 * np.pi / NLON)
    table = np.stack([np.cos(angles), -np.sin(angles)], 1).reshape(ROWS, NLON)
    weight = np.where(order == 0, 1.0, 2.0) / NLON
    back = table * np.repeat(weight, 2)[:, None]

    def split_y(t):
        t = np.pad(t.reshape(ROWS, LON_DEV, Y_DEV), ((0, 0), (0, 0), (0, Y_PAD - Y_DEV)))
        main = t[:, :, :Y_MAIN].reshape(ROWS, LON_DEV * Y_MAIN)
        extra = t[:, :, Y_MAIN:].reshape(ROWS, LON_DEV * Y_EXT)
        return np.concatenate([main, extra], 1)

    return (
        np.asarray(split_y(table), dtype=jnp.bfloat16),
        np.ascontiguousarray(split_y(back).T).astype(jnp.bfloat16),
    )


def dot(a, b):
    return lax.dot_general(a, b, (((1,), (0,)), ((), ())), preferred_element_type=f32)


def dot_t(a, b):
    return lax.dot_general(a, b, (((1,), (1,)), ((), ())), preferred_element_type=f32)


def sigmoid(v):
    return 0.5 * jnp.tanh(0.5 * v) + 0.5


def network_kernel(
    saved_h, cotan_h, w_in_h, b_in_h, w_mid_h, b_mid_h, w_out_h, out,
    saved, cotan, w_in, b_in, w_mid, b_mid, w_out, rows_s, rows_c, sems,
):
    pairs = (
        (saved_h, saved), (w_in_h, w_in), (b_in_h, b_in), (w_mid_h, w_mid),
        (b_mid_h, b_mid), (cotan_h, cotan), (w_out_h, w_out),
    )
    copies = [pltpu.make_async_copy(a, b, sems.at[k]) for k, (a, b) in enumerate(pairs)]
    for copy in copies:
        copy.start()
    rows_s[...] = jnp.zeros_like(rows_s)
    rows_c[...] = jnp.zeros_like(rows_c)
    for copy in copies:
        copy.wait()
    for x in range(X_DEV):
        rows_s[x, 0:Y_DEV, :] = saved[x]
        rows_c[x, 0:Y_DEV, :] = cotan[x]
    for xg in range(XG):
        s = rows_s[X_SUB * xg : X_SUB * (xg + 1)].reshape(X_SUB * Y_PAD, CHAN)
        c = rows_c[X_SUB * xg : X_SUB * (xg + 1)].reshape(X_SUB * Y_PAD, CHAN)
        first = dot(s, w_in[...]) + b_in[...]
        sig = sigmoid(first)
        act = first * sig
        slope_one = sig + act * (1.0 - sig)
        second = dot(act.astype(bf16), w_mid[...]) + b_mid[...]
        sig = sigmoid(second)
        slope_two = sig * (1.0 + second * (1.0 - sig))
        back_two = (dot_t(c, w_out[...]) * slope_two).astype(bf16)
        back_one = (dot_t(back_two, w_mid[...]) * slope_one).astype(bf16)
        grad = c.astype(f32) + dot_t(back_one, w_in[...])
        grad = grad.reshape(X_SUB, Y_PAD, CHAN)
        for cg in range(CG):
            parts = [grad[xx][:, C_SUB * cg : C_SUB * (cg + 1)] for xx in range(X_SUB)]
            parts = [p[0:Y_MAIN] for p in parts] + [
                jnp.concatenate([p[Y_MAIN:] for p in parts], axis=0)
            ]
            out[CG * xg + cg] = jnp.concatenate(parts, axis=1).astype(bf16)


def zonal_kernel(circles, table, out):
    main, extra = [], []
    for j in range(LON_DEV):
        piece = circles[j].astype(f32)
        main.append(piece)
        parts = [piece[Y_EXT * xx : Y_EXT * (xx + 1), 96:128] for xx in range(X_SUB)]
        extra.append(jnp.concatenate(parts + [jnp.zeros((Y_EXT, C_SUB), f32)], axis=1))
    g = jnp.concatenate(main + extra, axis=0).astype(bf16)
    out[0:ROWS, :] = dot(table[...], g).astype(bf16)
    out[ROWS:, :] = jnp.zeros((2 * DEVS - ROWS, 128), bf16)


def bases_kernel(mode, bases, out):
    m = mode[0]

    def index(shape, axis):
        return lax.broadcasted_iota(jnp.int32, shape, axis)

    def pick(mask):
        return jnp.where(mask, 1.0, 0.0).astype(bf16)

    wave = index((NL, 1), 0)
    tile = lax.shift_right_logical(wave * 5462, 16)
    rows = pick(index((NL, LAT_DEV * 24), 1) == wave + 12 * tile)
    table = dot(rows, bases[...])
    table = jnp.where(index((NL, NLAT), 0) >= m, table, 0.0).astype(bf16)
    place = index((1, NLAT), 1)
    x = 12 * ((place >> 2) & 31) + X_SUB * (place & 3) + (place >> 7)
    columns = pick(index((NLAT, NLAT), 0) == x)
    out[0] = dot(table, columns).astype(bf16)
    place = index((NLAT, 1), 0)
    row = 24 * ((place >> 2) & 31) + 12 + X_SUB * (place & 3) + (place >> 7)
    rows = pick(index((NLAT, LAT_DEV * 24), 1) == row)
    table = dot(rows, bases[...])
    out[1] = jnp.where(index((NLAT, NL), 1) >= m, table, 0.0).astype(bf16)


def legendre_kernel(coeffs, tables, gain, out, rows):
    rows[...] = coeffs[...].astype(f32)
    packs = [rows[pl.ds(s, 128, stride=8), :] for s in range(2 * CG)]
    stack = []
    for xx in range(X_SUB):
        parts = [
            packs[2 * cg + r][:, C_SUB * xx : C_SUB * (xx + 1)] for r in range(2) for cg in range(CG)
        ]
        stack.append(jnp.concatenate(parts, axis=1))
    fourier = jnp.concatenate(stack, axis=0).astype(bf16)
    gains = jnp.concatenate([gain[...], gain[...]], axis=1)
    filtered = (dot(tables[0], fourier) * gains).astype(bf16)
    result = dot(tables[1], filtered)
    for cg in range(CG):
        for r in range(2):
            first = CHAN * r + C_SUB * cg
            parts = [result[128 * xx : 128 * (xx + 1), first : first + C_SUB] for xx in range(X_SUB)]
            parts.append(jnp.zeros((128, C_SUB), f32))
            rows[pl.ds(2 * cg + r, 128, stride=8), :] = jnp.concatenate(parts, axis=1)
    out[...] = rows[...].astype(bf16)


def inverse_kernel(coeffs, table, out):
    g = dot(table[...], coeffs[0:ROWS, :])
    for j in range(LON_DEV):
        main = g[Y_MAIN * j : Y_MAIN * (j + 1), 0:96]
        first = LON_DEV * Y_MAIN + Y_EXT * j
        extra = g[first : first + Y_EXT]
        parts = [extra[:, C_SUB * xx : C_SUB * (xx + 1)] for xx in range(X_SUB)]
        out[j] = jnp.concatenate([main, jnp.concatenate(parts, axis=0)], axis=1).astype(bf16)


def grid_kernel(pieces, out):
    for xg in range(XG):
        blocks = [pieces[CG * xg + cg].astype(f32) for cg in range(CG)]
        for xx in range(X_SUB):
            main = [b[:, C_SUB * xx : C_SUB * (xx + 1)] for b in blocks]
            extra = [b[Y_EXT * xx : Y_EXT * (xx + 1), 96:128] for b in blocks]
            out[X_SUB * xg + xx, 0:Y_MAIN, :] = jnp.concatenate(main, axis=1)
            out[X_SUB * xg + xx, Y_MAIN:, :] = jnp.concatenate(extra, axis=1)[0 : Y_DEV - Y_MAIN]


def call(kernel, shape, dtype, scratch=(), smem=0, space=pltpu.VMEM, flops=0, moved=0):
    def run(*args):
        specs = [
            pl.BlockSpec(memory_space=pltpu.SMEM if k < smem else space) for k in range(len(args))
        ]
        return pl.pallas_call(
            kernel,
            out_shape=jax.ShapeDtypeStruct(shape, dtype),
            in_specs=specs,
            out_specs=pl.BlockSpec(memory_space=pltpu.VMEM),
            scratch_shapes=list(scratch),
            compiler_params=pltpu.CompilerParams(vmem_limit_bytes=VMEM),
            cost_estimate=pl.CostEstimate(flops=flops, bytes_accessed=moved, transcendentals=0),
        )(*args)

    return run


def on_device(
    saved, cotangent, w_in, b_in, w_mid, b_mid, w_out, spectral_gain, basis_in, basis_out
):
    forward, back = zonal_tables()
    bases = jnp.concatenate(
        [jnp.transpose(basis_in, (1, 2, 0)), jnp.transpose(basis_out, (1, 0, 2))], axis=1
    )
    bases = jnp.pad(bases, ((0, LAT_DEV - M_DEV), (0, 0), (0, 0)))
    bases, saved = lax.optimization_barrier((bases, saved))
    bases = lax.all_to_all(bases, "lat", 0, 0, tiled=True)

    weights = (w_in, b_in.reshape(1, -1), w_mid, b_mid.reshape(1, -1), w_out)
    held = [pltpu.VMEM(a.shape, a.dtype) for a in (saved, cotangent) + weights]
    pad = pltpu.VMEM((X_DEV, Y_PAD, CHAN), bf16)
    pieces = call(
        network_kernel,
        (LON_DEV, Y_MAIN, 128),
        bf16,
        held + [pad, pad, pltpu.SemaphoreType.DMA((7,))],
        space=pltpu.HBM,
        flops=1_700_000_000,
        moved=4_000_000,
    )(saved, cotangent, *weights)
    bases, pieces = lax.optimization_barrier((bases, pieces))
    pieces = lax.all_to_all(pieces, "lon", 0, 0, tiled=True)
    mode = (M_DEV * lax.axis_index("lon") + lax.axis_index("lat")).astype(jnp.int32).reshape(1)
    tables = call(bases_kernel, (2, NL, NLAT), bf16, smem=1, flops=600_000_000, moved=3_000_000)(
        mode, bases.reshape(LAT_DEV * 24, NL)
    )
    coeffs = call(zonal_kernel, (2 * DEVS, 128), bf16, flops=300_000_000)(pieces, jnp.asarray(forward))
    coeffs = lax.all_to_all(coeffs.reshape(DEVS, 2, 128), ("lat", "lon"), 0, 0, tiled=True)
    coeffs = call(
        legendre_kernel,
        (2 * DEVS, 128),
        bf16,
        (pltpu.VMEM((2 * DEVS, 128), f32),),
        flops=200_000_000,
    )(coeffs.reshape(2 * DEVS, 128), tables, spectral_gain)
    coeffs = lax.all_to_all(coeffs.reshape(DEVS, 2, 128), ("lat", "lon"), 0, 0, tiled=True)
    pieces = call(inverse_kernel, (LON_DEV, Y_MAIN, 128), bf16, flops=300_000_000)(
        coeffs.reshape(2 * DEVS, 128), jnp.asarray(back)
    )
    pieces = lax.all_to_all(pieces, "lon", 0, 0, tiled=True)
    return call(grid_kernel, (X_DEV, Y_DEV, CHAN), f32)(pieces)


def solution(mesh):
    placed = (
        P("lat", "lon", None),
        P("lat", "lon", None),
        P(),
        P(),
        P(),
        P(),
        P(),
        P(),
        P(None, "lon", "lat"),
        P("lat", "lon", None),
    )
    return jax.shard_map(
        on_device, mesh=mesh, in_specs=placed, out_specs=P("lat", "lon", None), check_vma=False
    )
```

time: 149 us -> 136 us (0.913)
  blocking collectives: 43 us -> 67.8 us
  waiting for transfers between devices: 43.6 us -> 23.3 us
  starting transfers between devices: 39.5 us -> 23.9 us
  local copies, waits for them, and re-layouts: 9.32 us -> 7.66 us
    all_to_all x1 -> x2, blocking collectives: 16.3 us -> 41.1 us  [on_device(): pieces = lax.all_to_all(pieces, 'lon', 0, 0, tiled=True)]
    all_to_all x2 -> x1, waiting for transfers between devices: 26.1 us -> 7.84 us  [on_device(): bases = lax.all_to_all(bases, 'lat', 0, 0, tiled=True)]
    all_to_all x2 -> x1, starting transfers between devices: 28.2 us -> 13.5 us  [on_device(): bases = lax.all_to_all(bases, 'lat', 0, 0, tiled=True)]
    all_to_all x1, waiting for transfers between devices: 17.5 us -> 15.5 us  [on_device(): lax.all_to_all(coeffs.reshape(DEVS, 2, 128), ('lat', 'lon'), 0, 0, tiled=...]
    unnamed x32 -> x26, local copies, waits for them, and re-layouts: 9.32 us -> 7.66 us
    pallas_call x5 -> x6, Pallas kernels: 9.87 us -> 10.7 us  [run(): pl.pallas_call(kernel, out_shape=jax.ShapeDtypeStruct(shape, dtype), in_s...]
  transfers between devices with their start and end apart: 3 -> 2, of which waited for: 3 -> 2; matrix products, arithmetic and copies ran while one was open for 1% -> 0% of each run, Pallas kernels for 1% -> 4%
where the time goes in v2:
time: 136 us; the launch traced here: 134 us
  blocking collectives  67.8 us (50%)
  starting transfers between devices  23.9 us (18%)
  waiting for transfers between devices  23.3 us (17%)
  Pallas kernels  10.7 us (8%)
  local copies, waits for them, and re-layouts  7.66 us (6%)
    all_to_all x2, blocking collectives, on_device(): pieces = lax.all_to_all(pieces, 'lon', 0, 0, tiled=True)  41.1 us
    all_to_all x1, blocking collectives, on_device(): lax.all_to_all(coeffs.reshape(DEVS, 2, 128), ('lat', 'lon'), 0, 0, tiled=...  26.7 us
    all_to_all x1, waiting for transfers between devices, on_device(): lax.all_to_all(coeffs.reshape(DEVS, 2, 128), ('lat', 'lon'), 0, 0, tiled=...  15.5 us
    all_to_all x1, starting transfers between devices, on_device(): bases = lax.all_to_all(bases, 'lat', 0, 0, tiled=True)  13.5 us
    pallas_call x6, Pallas kernels, run(): pl.pallas_call(kernel, out_shape=jax.ShapeDtypeStruct(shape, dtype), in_s...  10.7 us
    all_to_all x1, starting transfers between devices, on_device(): lax.all_to_all(coeffs.reshape(DEVS, 2, 128), ('lat', 'lon'), 0, 0, tiled=...  10.4 us
    all_to_all x1, waiting for transfers between devices, on_device(): bases = lax.all_to_all(bases, 'lat', 0, 0, tiled=True)  7.84 us
    unnamed x26, local copies, waits for them, and re-layouts  7.66 us
  transfers between devices with their start and end apart: 2, of which 2 were waited for; matrix products, arithmetic and copies ran while one was open for 0% of the time, Pallas kernels for 4%

profile of v2, /device:TPU:1, one launch (start us, length us, event | category | flops | bytes accessed | tf_op | source)
XLA Modules:
  0.0 134.5 jit_solution(6292162243778097625)
XLA Ops:
  0.0 1.0 copy.18
  1.0 1.0 copy.19
  2.0 0.0 copy-start.6
  2.0 0.0 copy-start.10
  2.0 0.0 copy-start.11
  2.0 0.9 fusion.2
  2.9 13.5 %all-to-all-start = ((bf16[32,24,384]{2,1,0:T(8,128)(2,1)}), bf16[32,24,384]{2,1,0:T(8,128)(2,1)S(1)}, u32[]{:S(2)}, u32[]{:S(2)}) async-start(bf16[32,24,384]{2,1,0:T(8,128)(2,1)} %fusion.2), calls=%async_computation | async-start | bytes 1179648 | tf_op jit(solution)/shard_map/all_to_all | solution.py:204
  16.4 0.0 copy-done.6
  16.4 0.0 copy-done.10
  16.4 0.0 copy-done.11
  16.4 0.0 copy-start.5
  16.4 1.0 copy-done.5
  17.5 0.0 copy-start.7
  17.5 1.0 copy-done.7
  18.4 0.0 copy-start.8
  18.4 0.9 copy-done.8
  19.3 0.0 copy-start.9
  19.3 0.9 copy-done.9
  20.2 0.0 copy-start.1
  20.2 4.5 %shard_map.118 = bf16[16,72,128]{2,1,0:T(8,128)(2,1)S(1)} custom-call(bf16[12,90,128]{2,1,0:T(8,128)(2,1)S(1)} %copy-done.6, bf16[12,90,128]{2,1,0:T(8,128)(2,1)S(1)} %copy-done.7, bf16[128,512]{1,0:T(8,128)(2,1)S(1)} %copy-done.8, f32[1,512]{1,0:T(1,128)S(1)} %bitcast.18, bf16[512,512]{1,0:T(8,128)(2,1)S(1)} %copy-done.5, f32[1,512]{1,0:T(1,128)S(1)} %bitcast.19, ...), custom_call_target="tpu_custom_call" | custom-call | flops 1700000000 | bytes 4000000 | tf_op jit(solution)/shard_map/pallas_call | solution.py:182
  24.7 7.8 %all-to-all-done = bf16[32,24,384]{2,1,0:T(8,128)(2,1)S(1)} async-done(((bf16[32,24,384]{2,1,0:T(8,128)(2,1)}), bf16[32,24,384]{2,1,0:T(8,128)(2,1)S(1)}, u32[]{:S(2)}, u32[]{:S(2)}) %all-to-all-start) | async-done | bytes 589856 | tf_op jit(solution)/shard_map/all_to_all | solution.py:204
  32.6 25.9 %all_to_all.25.circles = bf16[16,72,128]{2,1,0:T(8,128)(2,1)S(1)} all-to-all(bf16[16,72,128]{2,1,0:T(8,128)(2,1)S(1)} %shard_map.118), channel_id=1, replica_groups=mesh['lat'=32,'lon'=16] {'lon'}, dimensions={0} | all-to-all | bytes 589824 | tf_op jit(solution)/shard_map/all_to_all | solution.py:219
  58.5 0.0 copy-done.1
  58.5 1.4 %shard_map.119 = bf16[1024,128]{1,0:T(8,128)(2,1)} custom-call(bf16[16,72,128]{2,1,0:T(8,128)(2,1)S(1)} %all_to_all.25.circles, bf16[736,1536]{1,0:T(8,128)(2,1)S(1)} %copy-done.1), custom_call_target="tpu_custom_call" | custom-call | flops 300000000 | tf_op jit(solution)/shard_map/pallas_call | solution.py:182
  59.9 0.0 copy-start.4
  59.9 10.4 %all-to-all-start.2 = ((bf16[512,2,128]{2,1,0:T(2,128)(2,1)}), bf16[512,2,128]{2,1,0:T(2,128)(2,1)S(1)}, u32[]{:S(2)}, u32[]{:S(2)}) async-start(bf16[512,2,128]{2,1,0:T(2,128)(2,1)} %bitcast.4), calls=%async_computation.2 | async-start | bytes 524288 | tf_op jit(solution)/shard_map/all_to_all | solution.py:225
  70.3 0.0 copy-start
  70.3 1.0 shard_map.120.tables
  71.3 0.0 copy-start.2
  71.4 0.8 copy-done.2
  72.2 15.5 %all-to-all-done.2 = bf16[512,2,128]{2,1,0:T(2,128)(2,1)S(1)} async-done(((bf16[512,2,128]{2,1,0:T(2,128)(2,1)}), bf16[512,2,128]{2,1,0:T(2,128)(2,1)S(1)}, u32[]{:S(2)}, u32[]{:S(2)}) %all-to-all-start.2) | async-done | bytes 262176 | tf_op jit(solution)/shard_map/all_to_all | solution.py:225
  87.7 0.0 copy-done.4
  87.7 0.0 copy-start.3
  87.7 1.1 copy-done.3
  88.7 1.1 shard_map.121
  89.9 26.7 %all_to_all.26 = bf16[512,2,128]{2,1,0:T(2,128)(2,1)S(1)} all-to-all(bf16[512,2,128]{2,1,0:T(2,128)(2,1)S(1)} %bitcast.15), channel_id=1, replica_groups=mesh['lat'=32,'lon'=16] {'lat','lon'}, dimensions={0} | all-to-all | bytes 524288 | tf_op jit(solution)/shard_map/all_to_all | solution.py:233
  116.6 0.0 copy-done
  116.6 1.6 %shard_map.122 = bf16[16,72,128]{2,1,0:T(8,128)(2,1)S(1)} custom-call(bf16[1024,128]{1,0:T(8,128)(2,1)S(1)} %bitcast.16, bf16[1536,736]{1,0:T(8,128)(2,1)S(1)} %copy-done), custom_call_target="tpu_custom_call" | custom-call | flops 300000000 | tf_op jit(solution)/shard_map/pallas_call | solution.py:182
  118.1 15.2 %all_to_all.27.pieces = bf16[16,72,128]{2,1,0:T(8,128)(2,1)S(1)} all-to-all(bf16[16,72,128]{2,1,0:T(8,128)(2,1)S(1)} %shard_map.122), channel_id=1, replica_groups=mesh['lat'=32,'lon'=16] {'lon'}, dimensions={0} | all-to-all | bytes 589824 | tf_op jit(solution)/shard_map/all_to_all | solution.py:237
  133.4 1.1 shard_map.123
Async XLA Ops:
  2.0 14.5 %copy-start.6 = (bf16[12,90,128]{2,1,0:T(8,128)(2,1)S(1)}, bf16[12,90,128]{2,1,0:T(8,128)(2,1)}, u32[]{:S(2)}) copy-start(bf16[12,90,128]{2,1,0:T(8,128)(2,1)} %saved_h) | copy-start | bytes 829444
  2.0 14.4 %copy-start.10 = (f32[512]{0:T(512)S(1)}, f32[512]{0:T(512)}, u32[]{:S(2)}) copy-start(f32[512]{0:T(512)} %param.15) | copy-start | bytes 6148
  2.0 14.4 %copy-start.11 = (f32[512]{0:T(512)S(1)}, f32[512]{0:T(512)}, u32[]{:S(2)}) copy-start(f32[512]{0:T(512)} %param.17) | copy-start | bytes 6148
  2.9 29.6 %all-to-all-start = ((bf16[32,24,384]{2,1,0:T(8,128)(2,1)}), bf16[32,24,384]{2,1,0:T(8,128)(2,1)S(1)}, u32[]{:S(2)}, u32[]{:S(2)}) async-start(bf16[32,24,384]{2,1,0:T(8,128)(2,1)} %fusion.2), calls=%async_computation | async-start | bytes 1179648 | tf_op jit(solution)/shard_map/all_to_all | solution.py:204
  16.4 1.0 copy-start.5
  17.5 1.0 copy-start.7
  18.4 0.9 copy-start.8
  19.3 0.9 copy-start.9
  20.2 38.2 %copy-start.1 = (bf16[736,1536]{1,0:T(8,128)(2,1)S(1)}, bf16[736,1536]{1,0:T(8,128)(2,1)}, u32[]{:S(2)}) copy-start(bf16[736,1536]{1,0:T(8,128)(2,1)} %constant.18.clone.table) | copy-start | bytes 6782980
  59.9 27.8 %copy-start.4 = (f32[384,128]{1,0:T(8,128)S(1)}, f32[384,128]{1,0:T(8,128)}, u32[]{:S(2)}) copy-start(f32[384,128]{1,0:T(8,128)} %gain.1) | copy-start | bytes 589828
  59.9 27.7 %all-to-all-start.2 = ((bf16[512,2,128]{2,1,0:T(2,128)(2,1)}), bf16[512,2,128]{2,1,0:T(2,128)(2,1)S(1)}, u32[]{:S(2)}, u32[]{:S(2)}) async-start(bf16[512,2,128]{2,1,0:T(2,128)(2,1)} %bitcast.4), calls=%async_computation.2 | async-start | bytes 524288 | tf_op jit(solution)/shard_map/all_to_all | solution.py:225
  70.3 46.2 %copy-start = (bf16[1536,736]{1,0:T(8,128)(2,1)S(1)}, bf16[1536,736]{1,0:T(8,128)(2,1)}, u32[]{:S(2)}) copy-start(bf16[1536,736]{1,0:T(8,128)(2,1)} %constant.19.clone.table) | copy-start | bytes 6782980
  71.3 0.8 copy-start.2
  87.7 1.1 copy-start.3

commit v3 on v2

--- a/solution.py
+++ b/solution.py
@@ -21,6 +21,7 @@
 DEVS = LAT_DEV * LON_DEV
 ROWS = 2 * NM
 VMEM = 40 * 1024 * 1024
+NETWORK_VMEM = 59 * 1024 * 1024
 
 
 def zonal_tables():
@@ -95,7 +96,7 @@
             out[CG * xg + cg] = jnp.concatenate(parts, axis=1).astype(bf16)
 
 
-def zonal_kernel(circles, table, out):
+def zonal_kernel(circles, table, bases, out):
     main, extra = [], []
     for j in range(LON_DEV):
         piece = circles[j].astype(f32)
@@ -103,8 +104,32 @@
         parts = [piece[Y_EXT * xx : Y_EXT * (xx + 1), 96:128] for xx in range(X_SUB)]
         extra.append(jnp.concatenate(parts + [jnp.zeros((Y_EXT, C_SUB), f32)], axis=1))
     g = jnp.concatenate(main + extra, axis=0).astype(bf16)
-    out[0:ROWS, :] = dot(table[...], g).astype(bf16)
-    out[ROWS:, :] = jnp.zeros((2 * DEVS - ROWS, 128), bf16)
+    spectrum = dot(table[...], g)
+    for i in range(M_DEV):
+        first = 2 * LON_DEV * i
+        rest = spectrum[first + 24 : first + 32]
+        parts = [rest[:, C_SUB * xx : C_SUB * (xx + 1)] for xx in range(X_SUB)]
+        block = [spectrum[first : first + 24, 0:96], jnp.concatenate(parts, axis=0)]
+        out[i, :, 0:128] = jnp.concatenate(block, axis=1).astype(bf16)
+        out[i, :, 128:512] = bases[i]
+    out[M_DEV:] = jnp.zeros((LAT_DEV - M_DEV, 24, 512), bf16)
+
+
+def regroup_kernel(arrived, out, bases, rows):
+    for i in range(LAT_DEV):
+        block = arrived[i, :, 0:128].astype(f32)
+        parts = [block[8 * xx : 8 * (xx + 1), 96:128] for xx in range(X_SUB)]
+        rows[32 * i : 32 * i + 24, :] = block
+        rows[32 * i + 24 : 32 * (i + 1), :] = jnp.concatenate(
+            parts + [jnp.zeros((8, C_SUB), f32)], axis=1
+        )
+    for j in range(LON_DEV):
+        real = rows[pl.ds(2 * j, LAT_DEV, stride=32), :]
+        imag = rows[pl.ds(2 * j + 1, LAT_DEV, stride=32), :]
+        parts = [imag[16:32, C_SUB * xx : C_SUB * (xx + 1)] for xx in range(X_SUB)]
+        main = jnp.concatenate([real, imag[0:16]], axis=0)[:, 0:96]
+        out[j] = jnp.concatenate([main, jnp.concatenate(parts, axis=0)], axis=1).astype(bf16)
+    bases[...] = arrived[:, :, 128:512]
 
 
 def bases_kernel(mode, bases, out):
@@ -116,41 +141,54 @@
     def pick(mask):
         return jnp.where(mask, 1.0, 0.0).astype(bf16)
 
+    rows = bases[...].astype(f32).reshape(LAT_DEV * 24, NL).astype(bf16)
     wave = index((NL, 1), 0)
     tile = lax.shift_right_logical(wave * 5462, 16)
-    rows = pick(index((NL, LAT_DEV * 24), 1) == wave + 12 * tile)
-    table = dot(rows, bases[...])
+    chosen = pick(index((NL, LAT_DEV * 24), 1) == wave + 12 * tile)
+    table = dot(chosen, rows)
     table = jnp.where(index((NL, NLAT), 0) >= m, table, 0.0).astype(bf16)
     place = index((1, NLAT), 1)
-    x = 12 * ((place >> 2) & 31) + X_SUB * (place & 3) + (place >> 7)
+    x = 12 * (place & 31) + X_SUB * ((place >> 5) & 3) + (place >> 7)
     columns = pick(index((NLAT, NLAT), 0) == x)
     out[0] = dot(table, columns).astype(bf16)
     place = index((NLAT, 1), 0)
-    row = 24 * ((place >> 2) & 31) + 12 + X_SUB * (place & 3) + (place >> 7)
-    rows = pick(index((NLAT, LAT_DEV * 24), 1) == row)
-    table = dot(rows, bases[...])
+    row = 24 * (place & 31) + 12 + X_SUB * ((place >> 5) & 3) + (place >> 7)
+    chosen = pick(index((NLAT, LAT_DEV * 24), 1) == row)
+    table = dot(chosen, rows)
     out[1] = jnp.where(index((NLAT, NL), 1) >= m, table, 0.0).astype(bf16)
 
 
 def legendre_kernel(coeffs, tables, gain, out, rows):
-    rows[...] = coeffs[...].astype(f32)
-    packs = [rows[pl.ds(s, 128, stride=8), :] for s in range(2 * CG)]
+    blocks = []
+    for j in range(LON_DEV):
+        block = coeffs[j].astype(f32)
+        parts = [block[16 * xx : 16 * (xx + 1), 96:128] for xx in range(X_SUB)]
+        last = jnp.concatenate(parts + [jnp.zeros((16, C_SUB), f32)], axis=1)
+        blocks.append((block[0:32], jnp.concatenate([block[32:48], last], axis=0)))
     stack = []
     for xx in range(X_SUB):
-        parts = [
-            packs[2 * cg + r][:, C_SUB * xx : C_SUB * (xx + 1)] for r in range(2) for cg in range(CG)
-        ]
-        stack.append(jnp.concatenate(parts, axis=1))
+        for xg in range(XG):
+            parts = [
+                blocks[CG * xg + cg][r][:, C_SUB * xx : C_SUB * (xx + 1)]
+                for r in range(2)
+                for cg in range(CG)
+            ]
+            stack.append(jnp.concatenate(parts, axis=1))
     fourier = jnp.concatenate(stack, axis=0).astype(bf16)
     gains = jnp.concatenate([gain[...], gain[...]], axis=1)
     filtered = (dot(tables[0], fourier) * gains).astype(bf16)
     result = dot(tables[1], filtered)
-    for cg in range(CG):
-        for r in range(2):
-            first = CHAN * r + C_SUB * cg
-            parts = [result[128 * xx : 128 * (xx + 1), first : first + C_SUB] for xx in range(X_SUB)]
-            parts.append(jnp.zeros((128, C_SUB), f32))
-            rows[pl.ds(2 * cg + r, 128, stride=8), :] = jnp.concatenate(parts, axis=1)
+    for xg in range(XG):
+        for cg in range(CG):
+            for r in range(2):
+                first = CHAN * r + C_SUB * cg
+                parts = [
+                    result[32 * (XG * xx + xg) : 32 * (XG * xx + xg + 1), first : first + C_SUB]
+                    for xx in range(X_SUB)
+                ]
+                parts.append(jnp.zeros((LAT_DEV, C_SUB), f32))
+                place = 2 * (CG * xg + cg) + r
+                rows[pl.ds(place, LAT_DEV, stride=32), :] = jnp.concatenate(parts, axis=1)
     out[...] = rows[...].astype(bf16)
 
 
@@ -174,18 +212,24 @@
             out[X_SUB * xg + xx, Y_MAIN:, :] = jnp.concatenate(extra, axis=1)[0 : Y_DEV - Y_MAIN]
 
 
-def call(kernel, shape, dtype, scratch=(), smem=0, space=pltpu.VMEM, flops=0, moved=0):
+def call(
+    kernel, shape, dtype, scratch=(), smem=0, space=pltpu.VMEM, flops=0, moved=0, limit=VMEM
+):
+    outs = [jax.ShapeDtypeStruct(s, dtype) for s in (shape if isinstance(shape, list) else [shape])]
+    places = [pl.BlockSpec(memory_space=pltpu.VMEM) for _ in outs]
+    single = not isinstance(shape, list)
+
     def run(*args):
         specs = [
             pl.BlockSpec(memory_space=pltpu.SMEM if k < smem else space) for k in range(len(args))
         ]
         return pl.pallas_call(
             kernel,
-            out_shape=jax.ShapeDtypeStruct(shape, dtype),
+            out_shape=outs[0] if single else outs,
             in_specs=specs,
-            out_specs=pl.BlockSpec(memory_space=pltpu.VMEM),
+            out_specs=places[0] if single else places,
             scratch_shapes=list(scratch),
-            compiler_params=pltpu.CompilerParams(vmem_limit_bytes=VMEM),
+            compiler_params=pltpu.CompilerParams(vmem_limit_bytes=limit),
             cost_estimate=pl.CostEstimate(flops=flops, bytes_accessed=moved, transcendentals=0),
         )(*args)
 
@@ -196,13 +240,6 @@
     saved, cotangent, w_in, b_in, w_mid, b_mid, w_out, spectral_gain, basis_in, basis_out
 ):
     forward, back = zonal_tables()
-    bases = jnp.concatenate(
-        [jnp.transpose(basis_in, (1, 2, 0)), jnp.transpose(basis_out, (1, 0, 2))], axis=1
-    )
-    bases = jnp.pad(bases, ((0, LAT_DEV - M_DEV), (0, 0), (0, 0)))
-    bases, saved = lax.optimization_barrier((bases, saved))
-    bases = lax.all_to_all(bases, "lat", 0, 0, tiled=True)
-
     weights = (w_in, b_in.reshape(1, -1), w_mid, b_mid.reshape(1, -1), w_out)
     held = [pltpu.VMEM(a.shape, a.dtype) for a in (saved, cotangent) + weights]
     pad = pltpu.VMEM((X_DEV, Y_PAD, CHAN), bf16)
@@ -214,22 +251,34 @@
         space=pltpu.HBM,
         flops=1_700_000_000,
         moved=4_000_000,
+        limit=NETWORK_VMEM,
     )(saved, cotangent, *weights)
-    bases, pieces = lax.optimization_barrier((bases, pieces))
     pieces = lax.all_to_all(pieces, "lon", 0, 0, tiled=True)
+    bases = jnp.concatenate(
+        [jnp.transpose(basis_in, (1, 2, 0)), jnp.transpose(basis_out, (1, 0, 2))], axis=1
+    )
+    coeffs = call(zonal_kernel, (LAT_DEV, 24, 512), bf16, flops=300_000_000)(
+        pieces, jnp.asarray(forward), bases
+    )
+    coeffs = lax.all_to_all(coeffs, "lat", 0, 0, tiled=True)
+    coeffs, bases = call(
+        regroup_kernel,
+        [(LON_DEV, 48, 128), (LAT_DEV, 24, NL)],
+        bf16,
+        (pltpu.VMEM((2 * DEVS, 128), f32),),
+    )(coeffs)
+    coeffs = lax.all_to_all(coeffs, "lon", 0, 0, tiled=True)
     mode = (M_DEV * lax.axis_index("lon") + lax.axis_index("lat")).astype(jnp.int32).reshape(1)
     tables = call(bases_kernel, (2, NL, NLAT), bf16, smem=1, flops=600_000_000, moved=3_000_000)(
-        mode, bases.reshape(LAT_DEV * 24, NL)
-    )
-    coeffs = call(zonal_kernel, (2 * DEVS, 128), bf16, flops=300_000_000)(pieces, jnp.asarray(forward))
-    coeffs = lax.all_to_all(coeffs.reshape(DEVS, 2, 128), ("lat", "lon"), 0, 0, tiled=True)
+        mode, bases
+    )
     coeffs = call(
         legendre_kernel,
         (2 * DEVS, 128),
         bf16,
         (pltpu.VMEM((2 * DEVS, 128), f32),),
         flops=200_000_000,
-    )(coeffs.reshape(2 * DEVS, 128), tables, spectral_gain)
+    )(coeffs, tables, spectral_gain)
     coeffs = lax.all_to_all(coeffs.reshape(DEVS, 2, 128), ("lat", "lon"), 0, 0, tiled=True)
     pieces = call(inverse_kernel, (LON_DEV, Y_MAIN, 128), bf16, flops=300_000_000)(
         coeffs.reshape(2 * DEVS, 128), jnp.asarray(back)

time: 136 us -> 134 us (0.985)
  blocking collectives: 67.8 us -> 75 us
  local copies, waits for them, and re-layouts: 7.66 us -> 1.97 us
  waiting for transfers between devices: 23.3 us -> 19.7 us
  Pallas kernels: 10.7 us -> 13 us
  starting transfers between devices: 23.9 us -> 22.2 us
    all_to_all x0 -> x1, blocking collectives: none -> 32.8 us  [on_device(): coeffs = lax.all_to_all(coeffs, 'lat', 0, 0, tiled=True)]
    all_to_all x2 -> x1, blocking collectives: 41.1 us -> 15.2 us  [on_device(): pieces = lax.all_to_all(pieces, 'lon', 0, 0, tiled=True)]
    unnamed x26 -> x16, local copies, waits for them, and re-layouts: 7.66 us -> 1.97 us
    all_to_all x2, waiting for transfers between devices: 23.3 us -> 19.7 us  [the longest x1 11.2 us: on_device(): pieces = lax.all_to_all(pieces, 'lon', 0, 0, tiled=True)]
    pallas_call x6 -> x7, Pallas kernels: 10.7 us -> 13 us  [run(): pl.pallas_call(kernel, out_shape=outs[0] if single else outs, in_specs=sp...]
    all_to_all x2, starting transfers between devices: 23.9 us -> 22.2 us  [the longest x1 14.4 us: on_device(): pieces = lax.all_to_all(pieces, 'lon', 0, 0, tiled=True)]
  transfers between devices with their start and end apart: 2 -> 2, of which waited for: 2 -> 2; matrix products, arithmetic and copies ran while one was open for 0% -> 0% of each run, Pallas kernels for 4% -> 1%
where the time goes in v3:
time: 134 us; the launch traced here: 132 us
  blocking collectives  75 us (56%)
  starting transfers between devices  22.2 us (17%)
  waiting for transfers between devices  19.7 us (15%)
  Pallas kernels  13 us (10%)
  local copies, waits for them, and re-layouts  1.97 us (1%)
    all_to_all x1, blocking collectives, on_device(): coeffs = lax.all_to_all(coeffs, 'lat', 0, 0, tiled=True)  32.8 us
    all_to_all x1, blocking collectives, on_device(): lax.all_to_all(coeffs.reshape(DEVS, 2, 128), ('lat', 'lon'), 0, 0, tiled=...  27 us
    all_to_all x1, blocking collectives, on_device(): pieces = lax.all_to_all(pieces, 'lon', 0, 0, tiled=True)  15.2 us
    all_to_all x1, starting transfers between devices, on_device(): pieces = lax.all_to_all(pieces, 'lon', 0, 0, tiled=True)  14.4 us
    pallas_call x7, Pallas kernels, run(): pl.pallas_call(kernel, out_shape=outs[0] if single else outs, in_specs=sp...  13 us
    all_to_all x1, waiting for transfers between devices, on_device(): pieces = lax.all_to_all(pieces, 'lon', 0, 0, tiled=True)  11.2 us
    all_to_all x1, waiting for transfers between devices, on_device(): coeffs = lax.all_to_all(coeffs, 'lon', 0, 0, tiled=True)  8.55 us
    all_to_all x1, starting transfers between devices, on_device(): coeffs = lax.all_to_all(coeffs, 'lon', 0, 0, tiled=True)  7.76 us
  transfers between devices with their start and end apart: 2, of which 2 were waited for; matrix products, arithmetic and copies ran while one was open for 0% of the time, Pallas kernels for 1%

profile of v3, /device:TPU:1, one launch (start us, length us, event | category | flops | bytes accessed | tf_op | source)
XLA Modules:
  0.0 132.1 jit_solution(9390613600522837091)
XLA Ops:
  0.0 0.0 copy-start.5
  0.0 0.0 copy-start.6
  0.0 6.0 %shard_map.118 = bf16[16,72,128]{2,1,0:T(8,128)(2,1)} custom-call(bf16[12,90,128]{2,1,0:T(8,128)(2,1)} %saved_h.1, bf16[12,90,128]{2,1,0:T(8,128)(2,1)} %cotan_h.1, bf16[128,512]{1,0:T(8,128)(2,1)} %w_in_h.1, f32[1,512]{1,0:T(1,128)} %bitcast.15, bf16[512,512]{1,0:T(8,128)(2,1)} %w_mid_h.1, f32[1,512]{1,0:T(1,128)} %bitcast.16, bf16[512,128]{1,0:T(8,128)(2,1)} %w_out_h.1), custom_call_target="tpu_custom_call" | custom-call | flops 1700000000 | bytes 4000000 | tf_op jit(solution)/shard_map/pallas_call | solution.py:226
  6.0 0.0 copy-start.1
  6.0 14.4 %all-to-all-start = ((bf16[16,72,128]{2,1,0:T(8,128)(2,1)}), bf16[16,72,128]{2,1,0:T(8,128)(2,1)S(1)}, u32[]{:S(2)}, u32[]{:S(2)}) async-start(bf16[16,72,128]{2,1,0:T(8,128)(2,1)} %shard_map.118), calls=%async_computation | async-start | bytes 589824 | tf_op jit(solution)/shard_map/all_to_all | solution.py:256
  20.5 0.0 copy-done.5
  20.5 0.0 copy-done.6
  20.6 0.1 pad_maximum_fusion.bases
  20.7 11.2 %all-to-all-done.circles = bf16[16,72,128]{2,1,0:T(8,128)(2,1)S(1)} async-done(((bf16[16,72,128]{2,1,0:T(8,128)(2,1)}), bf16[16,72,128]{2,1,0:T(8,128)(2,1)S(1)}, u32[]{:S(2)}, u32[]{:S(2)}) %all-to-all-start) | async-done | bytes 294944 | tf_op jit(solution)/shard_map/all_to_all | solution.py:256
  31.8 0.0 copy-done.1
  31.8 0.9 shard_map.119
  32.7 0.0 copy-start.2
  32.7 32.8 %all_to_all.25.arrived = bf16[32,24,512]{2,1,0:T(8,128)(2,1)S(1)} all-to-all(bf16[32,24,512]{2,1,0:T(8,128)(2,1)S(1)} %shard_map.119), channel_id=1, replica_groups=mesh['lat'=32,'lon'=16] {'lat'}, dimensions={0} | all-to-all | bytes 1572864 | tf_op jit(solution)/shard_map/all_to_all | solution.py:263
  65.6 1.1 shard_map.120
  66.6 0.0 copy-start.3
  66.6 0.8 copy-done.3
  67.4 0.0 copy-start
  67.4 7.8 %all-to-all-start.2 = ((bf16[16,48,128]{2,1,0:T(8,128)(2,1)}), bf16[16,48,128]{2,1,0:T(8,128)(2,1)S(1)}, u32[]{:S(2)}, u32[]{:S(2)}) async-start(bf16[16,48,128]{2,1,0:T(8,128)(2,1)} %get-tuple-element.7), calls=%async_computation.2 | async-start | bytes 393216 | tf_op jit(solution)/shard_map/all_to_all | solution.py:270
  75.2 0.0 copy-start.4
  75.2 1.1 copy-done.4
  76.3 1.0 shard_map.121.tables
  77.3 8.6 %all-to-all-done.2.coeffs = bf16[16,48,128]{2,1,0:T(8,128)(2,1)S(1)} async-done(((bf16[16,48,128]{2,1,0:T(8,128)(2,1)}), bf16[16,48,128]{2,1,0:T(8,128)(2,1)S(1)}, u32[]{:S(2)}, u32[]{:S(2)}) %all-to-all-start.2) | async-done | bytes 196640 | tf_op jit(solution)/shard_map/all_to_all | solution.py:270
  85.8 0.0 copy-done.2
  85.8 1.4 %shard_map.122 = bf16[1024,128]{1,0:T(8,128)(2,1)S(1)} custom-call(bf16[16,48,128]{2,1,0:T(8,128)(2,1)S(1)} %all-to-all-done.2.coeffs, bf16[2,384,384]{2,1,0:T(8,128)(2,1)S(1)} %shard_map.121.tables, f32[384,128]{1,0:T(8,128)S(1)} %copy-done.2), custom_call_target="tpu_custom_call" | custom-call | flops 200000000 | tf_op jit(solution)/shard_map/pallas_call | solution.py:226
  87.2 27.0 %all_to_all.26 = bf16[512,2,128]{2,1,0:T(2,128)(2,1)S(1)} all-to-all(bf16[512,2,128]{2,1,0:T(2,128)(2,1)S(1)} %bitcast.11), channel_id=1, replica_groups=mesh['lat'=32,'lon'=16] {'lat','lon'}, dimensions={0} | all-to-all | bytes 524288 | tf_op jit(solution)/shard_map/all_to_all | solution.py:282
  114.2 0.0 copy-done
  114.2 1.6 %shard_map.123 = bf16[16,72,128]{2,1,0:T(8,128)(2,1)S(1)} custom-call(bf16[1024,128]{1,0:T(8,128)(2,1)S(1)} %bitcast.12, bf16[1536,736]{1,0:T(8,128)(2,1)S(1)} %copy-done), custom_call_target="tpu_custom_call" | custom-call | flops 300000000 | tf_op jit(solution)/shard_map/pallas_call | solution.py:226
  115.8 15.2 %all_to_all.27.pieces = bf16[16,72,128]{2,1,0:T(8,128)(2,1)S(1)} all-to-all(bf16[16,72,128]{2,1,0:T(8,128)(2,1)S(1)} %shard_map.123), channel_id=1, replica_groups=mesh['lat'=32,'lon'=16] {'lon'}, dimensions={0} | all-to-all | bytes 589824 | tf_op jit(solution)/shard_map/all_to_all | solution.py:286
  131.0 1.1 shard_map.124
  (2 shorter events, 0.1 us)
Async XLA Ops:
  0.0 20.5 %copy-start.5 = (bf16[12,23,384]{2,1,0:T(8,128)(2,1)S(1)}, bf16[12,23,384]{2,1,0:T(8,128)(2,1)}, u32[]{:S(2)}) copy-start(bf16[12,23,384]{2,1,0:T(8,128)(2,1)} %param.21) | copy-start | bytes 635908
  0.0 20.5 %copy-start.6 = (bf16[384,23,12]{0,1,2:T(8,128)(2,1)S(1)}, bf16[384,23,12]{0,1,2:T(8,128)(2,1)}, u32[]{:S(2)}) copy-start(bf16[384,23,12]{0,1,2:T(8,128)(2,1)} %param.20) | copy-start | bytes 635908
  6.0 25.8 %copy-start.1 = (bf16[736,1536]{1,0:T(8,128)(2,1)S(1)}, bf16[736,1536]{1,0:T(8,128)(2,1)}, u32[]{:S(2)}) copy-start(bf16[736,1536]{1,0:T(8,128)(2,1)} %constant.15.clone.table) | copy-start | bytes 6782980
  6.0 25.8 %all-to-all-start = ((bf16[16,72,128]{2,1,0:T(8,128)(2,1)}), bf16[16,72,128]{2,1,0:T(8,128)(2,1)S(1)}, u32[]{:S(2)}, u32[]{:S(2)}) async-start(bf16[16,72,128]{2,1,0:T(8,128)(2,1)} %shard_map.118), calls=%async_computation | async-start | bytes 589824 | tf_op jit(solution)/shard_map/all_to_all | solution.py:256
  32.7 53.1 %copy-start.2 = (f32[384,128]{1,0:T(8,128)S(1)}, f32[384,128]{1,0:T(8,128)}, u32[]{:S(2)}) copy-start(f32[384,128]{1,0:T(8,128)} %gain.1) | copy-start | bytes 589828
  66.6 0.8 copy-start.3
  67.4 46.8 %copy-start = (bf16[1536,736]{1,0:T(8,128)(2,1)S(1)}, bf16[1536,736]{1,0:T(8,128)(2,1)}, u32[]{:S(2)}) copy-start(bf16[1536,736]{1,0:T(8,128)(2,1)} %constant.16.clone.table) | copy-start | bytes 6782980
  67.4 18.4 %all-to-all-start.2 = ((bf16[16,48,128]{2,1,0:T(8,128)(2,1)}), bf16[16,48,128]{2,1,0:T(8,128)(2,1)S(1)}, u32[]{:S(2)}, u32[]{:S(2)}) async-start(bf16[16,48,128]{2,1,0:T(8,128)(2,1)} %get-tuple-element.7), calls=%async_computation.2 | async-start | bytes 393216 | tf_op jit(solution)/shard_map/all_to_all | solution.py:270
  75.2 1.1 copy-start.4

commit v4 on v3

--- a/solution.py
+++ b/solution.py
@@ -20,7 +20,7 @@
 XG = X_DEV // X_SUB
 DEVS = LAT_DEV * LON_DEV
 ROWS = 2 * NM
-VMEM = 40 * 1024 * 1024
+VMEM = 16 * 1024 * 1024
 NETWORK_VMEM = 59 * 1024 * 1024
 
 
@@ -67,23 +67,33 @@
     copies = [pltpu.make_async_copy(a, b, sems.at[k]) for k, (a, b) in enumerate(pairs)]
     for copy in copies:
         copy.start()
-    rows_s[...] = jnp.zeros_like(rows_s)
-    rows_c[...] = jnp.zeros_like(rows_c)
-    for copy in copies:
-        copy.wait()
+    got = dict(zip(("saved", "w_in", "b_in", "w_mid", "b_mid", "cotan", "w_out"), copies))
+    edge = jnp.zeros((X_DEV, 16, CHAN), bf16)
+    rows_s[:, Y_PAD - 16 :, :] = edge
+    rows_c[:, Y_PAD - 16 :, :] = edge
+    got["saved"].wait()
     for x in range(X_DEV):
         rows_s[x, 0:Y_DEV, :] = saved[x]
-        rows_c[x, 0:Y_DEV, :] = cotan[x]
+    got["w_in"].wait()
+    got["b_in"].wait()
     for xg in range(XG):
         s = rows_s[X_SUB * xg : X_SUB * (xg + 1)].reshape(X_SUB * Y_PAD, CHAN)
-        c = rows_c[X_SUB * xg : X_SUB * (xg + 1)].reshape(X_SUB * Y_PAD, CHAN)
         first = dot(s, w_in[...]) + b_in[...]
         sig = sigmoid(first)
         act = first * sig
         slope_one = sig + act * (1.0 - sig)
+        if xg == 0:
+            got["w_mid"].wait()
+            got["b_mid"].wait()
         second = dot(act.astype(bf16), w_mid[...]) + b_mid[...]
         sig = sigmoid(second)
         slope_two = sig * (1.0 + second * (1.0 - sig))
+        if xg == 0:
+            got["cotan"].wait()
+            got["w_out"].wait()
+            for x in range(X_DEV):
+                rows_c[x, 0:Y_DEV, :] = cotan[x]
+        c = rows_c[X_SUB * xg : X_SUB * (xg + 1)].reshape(X_SUB * Y_PAD, CHAN)
         back_two = (dot_t(c, w_out[...]) * slope_two).astype(bf16)
         back_one = (dot_t(back_two, w_mid[...]) * slope_one).astype(bf16)
         grad = c.astype(f32) + dot_t(back_one, w_in[...])

time: 134 us -> 134 us (level)
  no operation moved by 1% of the time
where the time goes in v4:
time: 134 us; the launch traced here: 132 us
  blocking collectives  75.1 us (56%)
  starting transfers between devices  22.1 us (16%)
  waiting for transfers between devices  19.7 us (15%)
  Pallas kernels  13 us (10%)
  local copies, waits for them, and re-layouts  1.97 us (1%)
    all_to_all x1, blocking collectives, on_device(): coeffs = lax.all_to_all(coeffs, 'lat', 0, 0, tiled=True)  32.8 us
    all_to_all x1, blocking collectives, on_device(): lax.all_to_all(coeffs.reshape(DEVS, 2, 128), ('lat', 'lon'), 0, 0, tiled=...  27 us
    all_to_all x1, blocking collectives, on_device(): pieces = lax.all_to_all(pieces, 'lon', 0, 0, tiled=True)  15.2 us
    all_to_all x1, starting transfers between devices, on_device(): pieces = lax.all_to_all(pieces, 'lon', 0, 0, tiled=True)  14.4 us
    pallas_call x7, Pallas kernels, run(): pl.pallas_call(kernel, out_shape=outs[0] if single else outs, in_specs=sp...  13 us
    all_to_all x1, waiting for transfers between devices, on_device(): pieces = lax.all_to_all(pieces, 'lon', 0, 0, tiled=True)  11.2 us
    all_to_all x1, waiting for transfers between devices, on_device(): coeffs = lax.all_to_all(coeffs, 'lon', 0, 0, tiled=True)  8.55 us
    all_to_all x1, starting transfers between devices, on_device(): coeffs = lax.all_to_all(coeffs, 'lon', 0, 0, tiled=True)  7.74 us
  transfers between devices with their start and end apart: 2, of which 2 were waited for; matrix products, arithmetic and copies ran while one was open for 0% of the time, Pallas kernels for 1%

profile of v4, /device:TPU:1, one launch (start us, length us, event | category | flops | bytes accessed | tf_op | source)
XLA Modules:
  0.0 132.1 jit_solution(232259233583374090)
XLA Ops:
  0.0 0.0 copy-start.5
  0.0 0.0 copy-start.6
  0.0 6.0 %shard_map.118 = bf16[16,72,128]{2,1,0:T(8,128)(2,1)} custom-call(bf16[12,90,128]{2,1,0:T(8,128)(2,1)} %saved_h.1, bf16[12,90,128]{2,1,0:T(8,128)(2,1)} %cotan_h.1, bf16[128,512]{1,0:T(8,128)(2,1)} %w_in_h.1, f32[1,512]{1,0:T(1,128)} %bitcast.15, bf16[512,512]{1,0:T(8,128)(2,1)} %w_mid_h.1, f32[1,512]{1,0:T(1,128)} %bitcast.16, bf16[512,128]{1,0:T(8,128)(2,1)} %w_out_h.1), custom_call_target="tpu_custom_call" | custom-call | flops 1700000000 | bytes 4000000 | tf_op jit(solution)/shard_map/pallas_call | solution.py:236
  6.0 0.0 copy-start.1
  6.0 14.4 %all-to-all-start = ((bf16[16,72,128]{2,1,0:T(8,128)(2,1)}), bf16[16,72,128]{2,1,0:T(8,128)(2,1)S(1)}, u32[]{:S(2)}, u32[]{:S(2)}) async-start(bf16[16,72,128]{2,1,0:T(8,128)(2,1)} %shard_map.118), calls=%async_computation | async-start | bytes 589824 | tf_op jit(solution)/shard_map/all_to_all | solution.py:266
  20.4 0.0 copy-done.5
  20.5 0.0 copy-done.6
  20.5 0.1 pad_maximum_fusion.bases
  20.7 11.2 %all-to-all-done.circles = bf16[16,72,128]{2,1,0:T(8,128)(2,1)S(1)} async-done(((bf16[16,72,128]{2,1,0:T(8,128)(2,1)}), bf16[16,72,128]{2,1,0:T(8,128)(2,1)S(1)}, u32[]{:S(2)}, u32[]{:S(2)}) %all-to-all-start) | async-done | bytes 294944 | tf_op jit(solution)/shard_map/all_to_all | solution.py:266
  31.8 0.0 copy-done.1
  31.8 0.9 shard_map.119
  32.7 0.0 copy-start.2
  32.7 32.8 %all_to_all.25.arrived = bf16[32,24,512]{2,1,0:T(8,128)(2,1)S(1)} all-to-all(bf16[32,24,512]{2,1,0:T(8,128)(2,1)S(1)} %shard_map.119), channel_id=1, replica_groups=mesh['lat'=32,'lon'=16] {'lat'}, dimensions={0} | all-to-all | bytes 1572864 | tf_op jit(solution)/shard_map/all_to_all | solution.py:273
  65.5 1.1 shard_map.120
  66.6 0.0 copy-start.3
  66.6 0.8 copy-done.3
  67.4 0.0 copy-start
  67.4 7.7 %all-to-all-start.2 = ((bf16[16,48,128]{2,1,0:T(8,128)(2,1)}), bf16[16,48,128]{2,1,0:T(8,128)(2,1)S(1)}, u32[]{:S(2)}, u32[]{:S(2)}) async-start(bf16[16,48,128]{2,1,0:T(8,128)(2,1)} %get-tuple-element.7), calls=%async_computation.2 | async-start | bytes 393216 | tf_op jit(solution)/shard_map/all_to_all | solution.py:280
  75.2 0.0 copy-start.4
  75.2 1.1 copy-done.4
  76.2 1.0 shard_map.121.tables
  77.2 8.6 %all-to-all-done.2.coeffs = bf16[16,48,128]{2,1,0:T(8,128)(2,1)S(1)} async-done(((bf16[16,48,128]{2,1,0:T(8,128)(2,1)}), bf16[16,48,128]{2,1,0:T(8,128)(2,1)S(1)}, u32[]{:S(2)}, u32[]{:S(2)}) %all-to-all-start.2) | async-done | bytes 196640 | tf_op jit(solution)/shard_map/all_to_all | solution.py:280
  85.8 0.0 copy-done.2
  85.8 1.4 %shard_map.122 = bf16[1024,128]{1,0:T(8,128)(2,1)S(1)} custom-call(bf16[16,48,128]{2,1,0:T(8,128)(2,1)S(1)} %all-to-all-done.2.coeffs, bf16[2,384,384]{2,1,0:T(8,128)(2,1)S(1)} %shard_map.121.tables, f32[384,128]{1,0:T(8,128)S(1)} %copy-done.2), custom_call_target="tpu_custom_call" | custom-call | flops 200000000 | tf_op jit(solution)/shard_map/pallas_call | solution.py:236
  87.2 27.0 %all_to_all.26 = bf16[512,2,128]{2,1,0:T(2,128)(2,1)S(1)} all-to-all(bf16[512,2,128]{2,1,0:T(2,128)(2,1)S(1)} %bitcast.11), channel_id=1, replica_groups=mesh['lat'=32,'lon'=16] {'lat','lon'}, dimensions={0} | all-to-all | bytes 524288 | tf_op jit(solution)/shard_map/all_to_all | solution.py:292
  114.2 0.0 copy-done
  114.2 1.6 %shard_map.123 = bf16[16,72,128]{2,1,0:T(8,128)(2,1)S(1)} custom-call(bf16[1024,128]{1,0:T(8,128)(2,1)S(1)} %bitcast.12, bf16[1536,736]{1,0:T(8,128)(2,1)S(1)} %copy-done), custom_call_target="tpu_custom_call" | custom-call | flops 300000000 | tf_op jit(solution)/shard_map/pallas_call | solution.py:236
  115.8 15.2 %all_to_all.27.pieces = bf16[16,72,128]{2,1,0:T(8,128)(2,1)S(1)} all-to-all(bf16[16,72,128]{2,1,0:T(8,128)(2,1)S(1)} %shard_map.123), channel_id=1, replica_groups=mesh['lat'=32,'lon'=16] {'lon'}, dimensions={0} | all-to-all | bytes 589824 | tf_op jit(solution)/shard_map/all_to_all | solution.py:296
  131.0 1.1 shard_map.124
  (2 shorter events, 0.1 us)
Async XLA Ops:
  0.0 20.4 %copy-start.5 = (bf16[12,23,384]{2,1,0:T(8,128)(2,1)S(1)}, bf16[12,23,384]{2,1,0:T(8,128)(2,1)}, u32[]{:S(2)}) copy-start(bf16[12,23,384]{2,1,0:T(8,128)(2,1)} %param.21) | copy-start | bytes 635908
  0.0 20.5 %copy-start.6 = (bf16[384,23,12]{0,1,2:T(8,128)(2,1)S(1)}, bf16[384,23,12]{0,1,2:T(8,128)(2,1)}, u32[]{:S(2)}) copy-start(bf16[384,23,12]{0,1,2:T(8,128)(2,1)} %param.20) | copy-start | bytes 635908
  6.0 25.8 %copy-start.1 = (bf16[736,1536]{1,0:T(8,128)(2,1)S(1)}, bf16[736,1536]{1,0:T(8,128)(2,1)}, u32[]{:S(2)}) copy-start(bf16[736,1536]{1,0:T(8,128)(2,1)} %constant.15.clone.table) | copy-start | bytes 6782980
  6.0 25.8 %all-to-all-start = ((bf16[16,72,128]{2,1,0:T(8,128)(2,1)}), bf16[16,72,128]{2,1,0:T(8,128)(2,1)S(1)}, u32[]{:S(2)}, u32[]{:S(2)}) async-start(bf16[16,72,128]{2,1,0:T(8,128)(2,1)} %shard_map.118), calls=%async_computation | async-start | bytes 589824 | tf_op jit(solution)/shard_map/all_to_all | solution.py:266
  32.7 53.1 %copy-start.2 = (f32[384,128]{1,0:T(8,128)S(1)}, f32[384,128]{1,0:T(8,128)}, u32[]{:S(2)}) copy-start(f32[384,128]{1,0:T(8,128)} %gain.1) | copy-start | bytes 589828
  66.6 0.8 copy-start.3
  67.4 46.8 %copy-start = (bf16[1536,736]{1,0:T(8,128)(2,1)S(1)}, bf16[1536,736]{1,0:T(8,128)(2,1)}, u32[]{:S(2)}) copy-start(bf16[1536,736]{1,0:T(8,128)(2,1)} %constant.16.clone.table) | copy-start | bytes 6782980
  67.4 18.4 %all-to-all-start.2 = ((bf16[16,48,128]{2,1,0:T(8,128)(2,1)}), bf16[16,48,128]{2,1,0:T(8,128)(2,1)S(1)}, u32[]{:S(2)}, u32[]{:S(2)}) async-start(bf16[16,48,128]{2,1,0:T(8,128)(2,1)} %get-tuple-element.7), calls=%async_computation.2 | async-start | bytes 393216 | tf_op jit(solution)/shard_map/all_to_all | solution.py:280
  75.2 1.1 copy-start.4

commit v5 on v4

--- a/solution.py
+++ b/solution.py
@@ -4,12 +4,13 @@
 from jax import lax
 from jax.experimental import pallas as pl
 from jax.experimental.pallas import tpu as pltpu
-from jax.sharding import PartitionSpec as P
+from jax.sharding import Mesh, PartitionSpec as P
 
 bf16 = jnp.bfloat16
 f32 = jnp.float32
 
 LAT_DEV, LON_DEV = 32, 16
+PAIRS = LON_DEV // 2
 X_DEV, Y_DEV = 12, 90
 Y_PAD = 96
 Y_MAIN, Y_EXT = 72, 24
@@ -20,6 +21,7 @@
 XG = X_DEV // X_SUB
 DEVS = LAT_DEV * LON_DEV
 ROWS = 2 * NM
+LON = ("pair", "core")
 VMEM = 16 * 1024 * 1024
 NETWORK_VMEM = 59 * 1024 * 1024
 
@@ -42,6 +44,10 @@
         np.asarray(split_y(table), dtype=jnp.bfloat16),
         np.ascontiguousarray(split_y(back).T).astype(jnp.bfloat16),
     )
+
+
+def owner(xg, cg):
+    return CG * xg + 2 * (cg % 2) + cg // 2
 
 
 def dot(a, b):
@@ -103,7 +109,7 @@
             parts = [p[0:Y_MAIN] for p in parts] + [
                 jnp.concatenate([p[Y_MAIN:] for p in parts], axis=0)
             ]
-            out[CG * xg + cg] = jnp.concatenate(parts, axis=1).astype(bf16)
+            out[owner(xg, cg)] = jnp.concatenate(parts, axis=1).astype(bf16)
 
 
 def zonal_kernel(circles, table, bases, out):
@@ -133,17 +139,16 @@
         rows[32 * i + 24 : 32 * (i + 1), :] = jnp.concatenate(
             parts + [jnp.zeros((8, C_SUB), f32)], axis=1
         )
-    for j in range(LON_DEV):
-        real = rows[pl.ds(2 * j, LAT_DEV, stride=32), :]
-        imag = rows[pl.ds(2 * j + 1, LAT_DEV, stride=32), :]
-        parts = [imag[16:32, C_SUB * xx : C_SUB * (xx + 1)] for xx in range(X_SUB)]
-        main = jnp.concatenate([real, imag[0:16]], axis=0)[:, 0:96]
-        out[j] = jnp.concatenate([main, jnp.concatenate(parts, axis=0)], axis=1).astype(bf16)
+    for k in range(PAIRS):
+        quarter = [rows[pl.ds(4 * k + n, LAT_DEV, stride=32), :] for n in range(4)]
+        parts = [quarter[3][:, C_SUB * xx : C_SUB * (xx + 1)] for xx in range(X_SUB)]
+        main = jnp.concatenate(quarter[0:3], axis=0)[:, 0:96]
+        out[k] = jnp.concatenate([main, jnp.concatenate(parts, axis=0)], axis=1).astype(bf16)
     bases[...] = arrived[:, :, 128:512]
 
 
-def bases_kernel(mode, bases, out):
-    m = mode[0]
+def bases_kernel(place, bases, out):
+    m = place[0]
 
     def index(shape, axis):
         return lax.broadcasted_iota(jnp.int32, shape, axis)
@@ -157,48 +162,59 @@
     chosen = pick(index((NL, LAT_DEV * 24), 1) == wave + 12 * tile)
     table = dot(chosen, rows)
     table = jnp.where(index((NL, NLAT), 0) >= m, table, 0.0).astype(bf16)
-    place = index((1, NLAT), 1)
-    x = 12 * (place & 31) + X_SUB * ((place >> 5) & 3) + (place >> 7)
+    spot = index((1, NLAT), 1)
+    x = 12 * (spot & 31) + X_SUB * ((spot >> 5) & 3) + (spot >> 7)
     columns = pick(index((NLAT, NLAT), 0) == x)
     out[0] = dot(table, columns).astype(bf16)
-    place = index((NLAT, 1), 0)
-    row = 24 * (place & 31) + 12 + X_SUB * ((place >> 5) & 3) + (place >> 7)
+    spot = index((NLAT, 1), 0)
+    row = 24 * (spot & 31) + 12 + X_SUB * ((spot >> 5) & 3) + (spot >> 7)
     chosen = pick(index((NLAT, LAT_DEV * 24), 1) == row)
     table = dot(chosen, rows)
     out[1] = jnp.where(index((NLAT, NL), 1) >= m, table, 0.0).astype(bf16)
 
 
-def legendre_kernel(coeffs, tables, gain, out, rows):
+def legendre_kernel(place, coeffs, tables, others, gain, out, rows):
+    core = place[1]
+
+    def swapped(pair):
+        return jnp.where(core == 0, pair[0], pair[1]), jnp.where(core == 0, pair[1], pair[0])
+
     blocks = []
-    for j in range(LON_DEV):
-        block = coeffs[j].astype(f32)
-        parts = [block[16 * xx : 16 * (xx + 1), 96:128] for xx in range(X_SUB)]
-        last = jnp.concatenate(parts + [jnp.zeros((16, C_SUB), f32)], axis=1)
-        blocks.append((block[0:32], jnp.concatenate([block[32:48], last], axis=0)))
-    stack = []
-    for xx in range(X_SUB):
-        for xg in range(XG):
-            parts = [
-                blocks[CG * xg + cg][r][:, C_SUB * xx : C_SUB * (xx + 1)]
-                for r in range(2)
-                for cg in range(CG)
-            ]
-            stack.append(jnp.concatenate(parts, axis=1))
-    fourier = jnp.concatenate(stack, axis=0).astype(bf16)
-    gains = jnp.concatenate([gain[...], gain[...]], axis=1)
-    filtered = (dot(tables[0], fourier) * gains).astype(bf16)
-    result = dot(tables[1], filtered)
-    for xg in range(XG):
-        for cg in range(CG):
+    for k in range(PAIRS):
+        block = coeffs[k].astype(f32)
+        parts = [block[32 * xx : 32 * (xx + 1), 96:128] for xx in range(X_SUB)]
+        last = jnp.concatenate(parts + [jnp.zeros((32, C_SUB), f32)], axis=1)
+        blocks.append([block[0:32], block[32:64], block[64:96], last])
+    modes = []
+    for h in range(2):
+        stack = []
+        for xx in range(X_SUB):
+            for xg in range(XG):
+                parts = [
+                    blocks[2 * xg + cq][2 * h + r][:, C_SUB * xx : C_SUB * (xx + 1)]
+                    for r in range(2)
+                    for cq in range(2)
+                ]
+                stack.append(jnp.concatenate(parts, axis=1))
+        modes.append(jnp.concatenate(stack, axis=0))
+    half = jnp.where(core == 0, gain[:, 0:64], gain[:, 64:128])
+    gains = jnp.concatenate([half, half], axis=1)
+    results = []
+    for fourier, table in zip(swapped(modes), (tables, others)):
+        filtered = (dot(table[0], fourier.astype(bf16)) * gains).astype(bf16)
+        results.append(dot(table[1], filtered))
+    results = swapped(results)
+    for k in range(PAIRS):
+        xg, cq = k // 2, k % 2
+        for h in range(2):
             for r in range(2):
-                first = CHAN * r + C_SUB * cg
+                first = 64 * r + C_SUB * cq
                 parts = [
-                    result[32 * (XG * xx + xg) : 32 * (XG * xx + xg + 1), first : first + C_SUB]
+                    results[h][32 * (XG * xx + xg) : 32 * (XG * xx + xg + 1), first : first + C_SUB]
                     for xx in range(X_SUB)
                 ]
                 parts.append(jnp.zeros((LAT_DEV, C_SUB), f32))
-                place = 2 * (CG * xg + cg) + r
-                rows[pl.ds(place, LAT_DEV, stride=32), :] = jnp.concatenate(parts, axis=1)
+                rows[pl.ds(4 * k + 2 * h + r, LAT_DEV, stride=32), :] = jnp.concatenate(parts, axis=1)
     out[...] = rows[...].astype(bf16)
 
 
@@ -214,7 +230,7 @@
 
 def grid_kernel(pieces, out):
     for xg in range(XG):
-        blocks = [pieces[CG * xg + cg].astype(f32) for cg in range(CG)]
+        blocks = [pieces[owner(xg, cg)].astype(f32) for cg in range(CG)]
         for xx in range(X_SUB):
             main = [b[:, C_SUB * xx : C_SUB * (xx + 1)] for b in blocks]
             extra = [b[Y_EXT * xx : Y_EXT * (xx + 1), 96:128] for b in blocks]
@@ -263,7 +279,7 @@
         moved=4_000_000,
         limit=NETWORK_VMEM,
     )(saved, cotangent, *weights)
-    pieces = lax.all_to_all(pieces, "lon", 0, 0, tiled=True)
+    pieces = lax.all_to_all(pieces, LON, 0, 0, tiled=True)
     bases = jnp.concatenate(
         [jnp.transpose(basis_in, (1, 2, 0)), jnp.transpose(basis_out, (1, 0, 2))], axis=1
     )
@@ -273,43 +289,35 @@
     coeffs = lax.all_to_all(coeffs, "lat", 0, 0, tiled=True)
     coeffs, bases = call(
         regroup_kernel,
-        [(LON_DEV, 48, 128), (LAT_DEV, 24, NL)],
+        [(PAIRS, 96, 128), (LAT_DEV, 24, NL)],
         bf16,
         (pltpu.VMEM((2 * DEVS, 128), f32),),
     )(coeffs)
-    coeffs = lax.all_to_all(coeffs, "lon", 0, 0, tiled=True)
-    mode = (M_DEV * lax.axis_index("lon") + lax.axis_index("lat")).astype(jnp.int32).reshape(1)
+    coeffs = lax.all_to_all(coeffs, "pair", 0, 0, tiled=True)
+    mode = M_DEV * lax.axis_index(LON) + lax.axis_index("lat")
+    place = jnp.stack([mode, lax.axis_index("core")]).astype(jnp.int32)
     tables = call(bases_kernel, (2, NL, NLAT), bf16, smem=1, flops=600_000_000, moved=3_000_000)(
-        mode, bases
-    )
+        place, bases
+    )
+    others = lax.ppermute(tables, "core", [(0, 1), (1, 0)])
     coeffs = call(
         legendre_kernel,
         (2 * DEVS, 128),
         bf16,
         (pltpu.VMEM((2 * DEVS, 128), f32),),
+        smem=1,
         flops=200_000_000,
-    )(coeffs, tables, spectral_gain)
-    coeffs = lax.all_to_all(coeffs.reshape(DEVS, 2, 128), ("lat", "lon"), 0, 0, tiled=True)
+    )(place, coeffs, tables, others, spectral_gain)
+    coeffs = lax.all_to_all(coeffs.reshape(DEVS // 2, 4, 128), ("lat", "pair"), 0, 0, tiled=True)
     pieces = call(inverse_kernel, (LON_DEV, Y_MAIN, 128), bf16, flops=300_000_000)(
         coeffs.reshape(2 * DEVS, 128), jnp.asarray(back)
     )
-    pieces = lax.all_to_all(pieces, "lon", 0, 0, tiled=True)
+    pieces = lax.all_to_all(pieces, LON, 0, 0, tiled=True)
     return call(grid_kernel, (X_DEV, Y_DEV, CHAN), f32)(pieces)
 
 
 def solution(mesh):
-    placed = (
-        P("lat", "lon", None),
-        P("lat", "lon", None),
-        P(),
-        P(),
-        P(),
-        P(),
-        P(),
-        P(),
-        P(None, "lon", "lat"),
-        P("lat", "lon", None),
-    )
-    return jax.shard_map(
-        on_device, mesh=mesh, in_specs=placed, out_specs=P("lat", "lon", None), check_vma=False
-    )
+    grid = P("lat", LON, None)
+    placed = (grid, grid, P(), P(), P(), P(), P(), P(), P(None, LON, "lat"), grid)
+    fine = Mesh(mesh.devices.reshape(LAT_DEV, PAIRS, 2), ("lat",) + LON)
+    return jax.shard_map(on_device, mesh=fine, in_specs=placed, out_specs=grid, check_vma=False)

time: 134 us -> 136 us (1.015)
  blocking collectives: 75.1 us -> 55.1 us
  waiting for transfers between devices: 19.7 us -> 31.2 us
  starting transfers between devices: 22.1 us -> 33.5 us
  local copies, waits for them, and re-layouts: 1.97 us -> 0.1 us
  Pallas kernels: 13 us -> 14.4 us
    all_to_all x3, blocking collectives: 75.1 us -> 55.1 us  [the longest x1 23.2 us: on_device(): lax.all_to_all(coeffs.reshape(DEVS // 2, 4, 128), ('lat', 'pair'), 0, 0,...]
    all_to_all x2, waiting for transfers between devices: 19.7 us -> 31.2 us  [the longest x1 20.1 us: on_device(): coeffs = lax.all_to_all(coeffs, 'lat', 0, 0, tiled=True)]
    ppermute x0 -> x1, starting transfers between devices: none -> 6.21 us  [on_device(): others = lax.ppermute(tables, 'core', [(0, 1), (1, 0)])]
    all_to_all x2, starting transfers between devices: 22.1 us -> 27.3 us  [the longest x1 14.4 us: on_device(): pieces = lax.all_to_all(pieces, LON, 0, 0, tiled=True)]
    unnamed x16 -> x12, local copies, waits for them, and re-layouts: 1.97 us -> 0.1 us
    pallas_call x7, Pallas kernels: 13 us -> 14.4 us  [run(): pl.pallas_call(kernel, out_shape=outs[0] if single else outs, in_specs=sp...]
  transfers between devices with their start and end apart: 2 -> 3, of which waited for: 2 -> 2; matrix products, arithmetic and copies ran while one was open for 0% -> 0% of each run, Pallas kernels for 1% -> 0%
where the time goes in v5:
time: 136 us; the launch traced here: 135 us
  blocking collectives  55.1 us (41%)
  starting transfers between devices  33.5 us (25%)
  waiting for transfers between devices  31.2 us (23%)
  Pallas kernels  14.4 us (11%)
    all_to_all x1, blocking collectives, on_device(): lax.all_to_all(coeffs.reshape(DEVS // 2, 4, 128), ('lat', 'pair'), 0, 0,...  23.2 us
    all_to_all x1, waiting for transfers between devices, on_device(): coeffs = lax.all_to_all(coeffs, 'lat', 0, 0, tiled=True)  20.1 us
    all_to_all x1, blocking collectives, on_device(): pieces = lax.all_to_all(pieces, LON, 0, 0, tiled=True)  18.9 us
    pallas_call x7, Pallas kernels, run(): pl.pallas_call(kernel, out_shape=outs[0] if single else outs, in_specs=sp...  14.4 us
    all_to_all x1, starting transfers between devices, on_device(): pieces = lax.all_to_all(pieces, LON, 0, 0, tiled=True)  14.4 us
    all_to_all x1, blocking collectives, on_device(): coeffs = lax.all_to_all(coeffs, 'pair', 0, 0, tiled=True)  13 us
    all_to_all x1, starting transfers between devices, on_device(): coeffs = lax.all_to_all(coeffs, 'lat', 0, 0, tiled=True)  12.9 us
    all_to_all x1, waiting for transfers between devices, on_device(): pieces = lax.all_to_all(pieces, LON, 0, 0, tiled=True)  11.2 us
  transfers between devices with their start and end apart: 3, of which 2 were waited for; matrix products, arithmetic and copies ran while one was open for 0% of the time, Pallas kernels for 0%

profile of v5, /device:TPU:1, one launch (start us, length us, event | category | flops | bytes accessed | tf_op | source)
XLA Modules:
  0.0 134.6 jit_solution(5459205987062543416)
XLA Ops:
  0.0 0.0 copy-start.3
  0.0 0.0 copy-start.4
  0.0 6.0 %shard_map.118 = bf16[16,72,128]{2,1,0:T(8,128)(2,1)} custom-call(bf16[12,90,128]{2,1,0:T(8,128)(2,1)} %saved_h.1, bf16[12,90,128]{2,1,0:T(8,128)(2,1)} %cotan_h.1, bf16[128,512]{1,0:T(8,128)(2,1)} %w_in_h.1, f32[1,512]{1,0:T(1,128)} %bitcast.16, bf16[512,512]{1,0:T(8,128)(2,1)} %w_mid_h.1, f32[1,512]{1,0:T(1,128)} %bitcast.17, bf16[512,128]{1,0:T(8,128)(2,1)} %w_out_h.1), custom_call_target="tpu_custom_call" | custom-call | flops 1700000000 | bytes 4000000 | tf_op jit(solution)/shard_map/pallas_call | solution.py:252
  6.0 0.0 copy-start.1
  6.0 14.4 %all-to-all-start = ((bf16[16,72,128]{2,1,0:T(8,128)(2,1)}), bf16[16,72,128]{2,1,0:T(8,128)(2,1)S(1)}, u32[]{:S(2)}, u32[]{:S(2)}) async-start(bf16[16,72,128]{2,1,0:T(8,128)(2,1)} %shard_map.118), calls=%async_computation | async-start | bytes 589824 | tf_op jit(solution)/shard_map/all_to_all | solution.py:282
  20.4 0.0 copy-done.3
  20.5 0.0 copy-done.4
  20.5 0.1 pad_maximum_fusion.bases
  20.7 11.2 %all-to-all-done.circles = bf16[16,72,128]{2,1,0:T(8,128)(2,1)S(1)} async-done(((bf16[16,72,128]{2,1,0:T(8,128)(2,1)}), bf16[16,72,128]{2,1,0:T(8,128)(2,1)S(1)}, u32[]{:S(2)}, u32[]{:S(2)}) %all-to-all-start) | async-done | bytes 294944 | tf_op jit(solution)/shard_map/all_to_all | solution.py:282
  31.8 0.0 copy-done.1
  31.8 1.8 %shard_map.119 = bf16[32,24,512]{2,1,0:T(8,128)(2,1)} custom-call(bf16[16,72,128]{2,1,0:T(8,128)(2,1)S(1)} %all-to-all-done.circles, bf16[736,1536]{1,0:T(8,128)(2,1)S(1)} %copy-done.1, bf16[23,24,384]{2,1,0:T(8,128)(2,1)S(1)} %pad_maximum_fusion.bases), custom_call_target="tpu_custom_call" | custom-call | flops 300000000 | tf_op jit(solution)/shard_map/pallas_call | solution.py:252
  33.6 0.0 copy-start.2
  33.6 12.9 %all-to-all-start.1 = ((bf16[32,24,512]{2,1,0:T(8,128)(2,1)}), bf16[32,24,512]{2,1,0:T(8,128)(2,1)S(1)}, u32[]{:S(2)}, u32[]{:S(2)}) async-start(bf16[32,24,512]{2,1,0:T(8,128)(2,1)} %shard_map.119), calls=%async_computation.1 | async-start | bytes 1572864 | tf_op jit(solution)/shard_map/all_to_all | solution.py:289
  46.5 0.1 pad_add_fusion.place
  46.6 20.1 %all-to-all-done.1.arrived = bf16[32,24,512]{2,1,0:T(8,128)(2,1)S(1)} async-done(((bf16[32,24,512]{2,1,0:T(8,128)(2,1)}), bf16[32,24,512]{2,1,0:T(8,128)(2,1)S(1)}, u32[]{:S(2)}, u32[]{:S(2)}) %all-to-all-start.1) | async-done | bytes 786464 | tf_op jit(solution)/shard_map/all_to_all | solution.py:289
  66.6 0.4 shard_map.120
  67.0 0.0 copy-start
  67.0 1.5 %shard_map.121.tables = bf16[2,384,384]{2,1,0:T(8,128)(2,1)S(1)} custom-call(s32[2]{0:T(128)S(1)} %pad_add_fusion.place, bf16[32,24,384]{2,1,0:T(8,128)(2,1)S(1)} %get-tuple-element.8.bases), custom_call_target="tpu_custom_call" | custom-call | flops 600000000 | bytes 3000000 | tf_op jit(solution)/shard_map/pallas_call | solution.py:252
  68.6 6.2 %collective-permute-start = (bf16[2,384,384]{2,1,0:T(8,128)(2,1)S(1)}, bf16[2,384,384]{2,1,0:T(8,128)(2,1)S(1)}, u32[]{:S(2)}, u32[]{:S(2)}) collective-permute-start(bf16[2,384,384]{2,1,0:T(8,128)(2,1)S(1)} %shard_map.121.tables), channel_id=1, source_target_pairs={{0,1},{1,0},{2,3},{3,2},{4,5},{5,4},{6,7},{7,6},{8,9},{9,8},{10,11... | collective-permute-start | bytes 1769480 | tf_op jit(solution)/shard_map/ppermute | solution.py:302
  74.8 13.0 %all_to_all.25.coeffs = bf16[8,96,128]{2,1,0:T(8,128)(2,1)S(1)} all-to-all(bf16[8,96,128]{2,1,0:T(8,128)(2,1)S(1)} %get-tuple-element.7), channel_id=1, replica_groups=mesh['lat'=32,'pair'=8,'core'=2] {'pair'}, dimensions={0} | all-to-all | bytes 393216 | tf_op jit(solution)/shard_map/all_to_all | solution.py:296
  87.8 0.0 collective-permute-done.others
  87.8 0.0 copy-done.2
  87.8 2.1 %shard_map.122 = bf16[1024,128]{1,0:T(8,128)(2,1)S(1)} custom-call(s32[2]{0:T(128)S(1)} %pad_add_fusion.place, bf16[8,96,128]{2,1,0:T(8,128)(2,1)S(1)} %all_to_all.25.coeffs, bf16[2,384,384]{2,1,0:T(8,128)(2,1)S(1)} %shard_map.121.tables, bf16[2,384,384]{2,1,0:T(8,128)(2,1)S(1)} %collective-permute-done.others, f32[384,128]{1,0:T(8,128)S(1)} %copy-done.2), custom_call_target="tpu_custom_call" | custom-call | flops 200000000 | tf_op jit(solution)/shard_map/pallas_call | solution.py:252
  89.9 23.2 %all_to_all.26 = bf16[256,4,128]{2,1,0:T(4,128)(2,1)S(1)} all-to-all(bf16[256,4,128]{2,1,0:T(4,128)(2,1)S(1)} %bitcast.13), channel_id=1, replica_groups=mesh['lat'=32,'pair'=8,'core'=2] {'lat','pair'}, dimensions={0} | all-to-all | bytes 524288 | tf_op jit(solution)/shard_map/all_to_all | solution.py:311
  113.1 0.0 copy-done
  113.1 1.6 %shard_map.123 = bf16[16,72,128]{2,1,0:T(8,128)(2,1)S(1)} custom-call(bf16[1024,128]{1,0:T(8,128)(2,1)S(1)} %bitcast.12, bf16[1536,736]{1,0:T(8,128)(2,1)S(1)} %copy-done), custom_call_target="tpu_custom_call" | custom-call | flops 300000000 | tf_op jit(solution)/shard_map/pallas_call | solution.py:252
  114.7 18.9 %all_to_all.27.pieces = bf16[16,72,128]{2,1,0:T(8,128)(2,1)S(1)} all-to-all(bf16[16,72,128]{2,1,0:T(8,128)(2,1)S(1)} %shard_map.123), channel_id=1, replica_groups=mesh['lat'=32,'pair'=8,'core'=2] {'pair','core'}, dimensions={0} | all-to-all | bytes 589824 | tf_op jit(solution)/shard_map/all_to_all | solution.py:315
  133.5 1.1 shard_map.124
  (2 shorter events, 0.1 us)
Async XLA Ops:
  0.0 20.4 %copy-start.3 = (bf16[384,23,12]{0,1,2:T(8,128)(2,1)S(1)}, bf16[384,23,12]{0,1,2:T(8,128)(2,1)}, u32[]{:S(2)}) copy-start(bf16[384,23,12]{0,1,2:T(8,128)(2,1)} %param.20) | copy-start | bytes 635908
  0.0 20.5 %copy-start.4 = (bf16[12,23,384]{2,1,0:T(8,128)(2,1)S(1)}, bf16[12,23,384]{2,1,0:T(8,128)(2,1)}, u32[]{:S(2)}) copy-start(bf16[12,23,384]{2,1,0:T(8,128)(2,1)} %param.21) | copy-start | bytes 635908
  6.0 25.8 %copy-start.1 = (bf16[736,1536]{1,0:T(8,128)(2,1)S(1)}, bf16[736,1536]{1,0:T(8,128)(2,1)}, u32[]{:S(2)}) copy-start(bf16[736,1536]{1,0:T(8,128)(2,1)} %constant.22.clone.table) | copy-start | bytes 6782980
  6.0 25.8 %all-to-all-start = ((bf16[16,72,128]{2,1,0:T(8,128)(2,1)}), bf16[16,72,128]{2,1,0:T(8,128)(2,1)S(1)}, u32[]{:S(2)}, u32[]{:S(2)}) async-start(bf16[16,72,128]{2,1,0:T(8,128)(2,1)} %shard_map.118), calls=%async_computation | async-start | bytes 589824 | tf_op jit(solution)/shard_map/all_to_all | solution.py:282
  33.6 54.2 %copy-start.2 = (f32[384,128]{1,0:T(8,128)S(1)}, f32[384,128]{1,0:T(8,128)}, u32[]{:S(2)}) copy-start(f32[384,128]{1,0:T(8,128)} %gain.1) | copy-start | bytes 589828
  33.6 33.0 %all-to-all-start.1 = ((bf16[32,24,512]{2,1,0:T(8,128)(2,1)}), bf16[32,24,512]{2,1,0:T(8,128)(2,1)S(1)}, u32[]{:S(2)}, u32[]{:S(2)}) async-start(bf16[32,24,512]{2,1,0:T(8,128)(2,1)} %shard_map.119), calls=%async_computation.1 | async-start | bytes 1572864 | tf_op jit(solution)/shard_map/all_to_all | solution.py:289
  67.0 46.1 %copy-start = (bf16[1536,736]{1,0:T(8,128)(2,1)S(1)}, bf16[1536,736]{1,0:T(8,128)(2,1)}, u32[]{:S(2)}) copy-start(bf16[1536,736]{1,0:T(8,128)(2,1)} %constant.23.clone.table) | copy-start | bytes 6782980
  68.6 19.3 %collective-permute-start = (bf16[2,384,384]{2,1,0:T(8,128)(2,1)S(1)}, bf16[2,384,384]{2,1,0:T(8,128)(2,1)S(1)}, u32[]{:S(2)}, u32[]{:S(2)}) collective-permute-start(bf16[2,384,384]{2,1,0:T(8,128)(2,1)S(1)} %shard_map.121.tables), channel_id=1, source_target_pairs={{0,1},{1,0},{2,3},{3,2},{4,5},{5,4},{6,7},{7,6},{8,9},{9,8},{10,11... | collective-permute-start | bytes 1769480 | tf_op jit(solution)/shard_map/ppermute | solution.py:302

commit v6 on v5

--- a/solution.py
+++ b/solution.py
@@ -112,7 +112,7 @@
             out[owner(xg, cg)] = jnp.concatenate(parts, axis=1).astype(bf16)
 
 
-def zonal_kernel(circles, table, bases, out):
+def zonal_kernel(circles, table, out):
     main, extra = [], []
     for j in range(LON_DEV):
         piece = circles[j].astype(f32)
@@ -120,31 +120,8 @@
         parts = [piece[Y_EXT * xx : Y_EXT * (xx + 1), 96:128] for xx in range(X_SUB)]
         extra.append(jnp.concatenate(parts + [jnp.zeros((Y_EXT, C_SUB), f32)], axis=1))
     g = jnp.concatenate(main + extra, axis=0).astype(bf16)
-    spectrum = dot(table[...], g)
-    for i in range(M_DEV):
-        first = 2 * LON_DEV * i
-        rest = spectrum[first + 24 : first + 32]
-        parts = [rest[:, C_SUB * xx : C_SUB * (xx + 1)] for xx in range(X_SUB)]
-        block = [spectrum[first : first + 24, 0:96], jnp.concatenate(parts, axis=0)]
-        out[i, :, 0:128] = jnp.concatenate(block, axis=1).astype(bf16)
-        out[i, :, 128:512] = bases[i]
-    out[M_DEV:] = jnp.zeros((LAT_DEV - M_DEV, 24, 512), bf16)
-
-
-def regroup_kernel(arrived, out, bases, rows):
-    for i in range(LAT_DEV):
-        block = arrived[i, :, 0:128].astype(f32)
-        parts = [block[8 * xx : 8 * (xx + 1), 96:128] for xx in range(X_SUB)]
-        rows[32 * i : 32 * i + 24, :] = block
-        rows[32 * i + 24 : 32 * (i + 1), :] = jnp.concatenate(
-            parts + [jnp.zeros((8, C_SUB), f32)], axis=1
-        )
-    for k in range(PAIRS):
-        quarter = [rows[pl.ds(4 * k + n, LAT_DEV, stride=32), :] for n in range(4)]
-        parts = [quarter[3][:, C_SUB * xx : C_SUB * (xx + 1)] for xx in range(X_SUB)]
-        main = jnp.concatenate(quarter[0:3], axis=0)[:, 0:96]
-        out[k] = jnp.concatenate([main, jnp.concatenate(parts, axis=0)], axis=1).astype(bf16)
-    bases[...] = arrived[:, :, 128:512]
+    out[0:ROWS, :] = dot(table[...], g).astype(bf16)
+    out[ROWS:, :] = jnp.zeros((2 * DEVS - ROWS, 128), bf16)
 
 
 def bases_kernel(place, bases, out):
@@ -179,12 +156,10 @@
     def swapped(pair):
         return jnp.where(core == 0, pair[0], pair[1]), jnp.where(core == 0, pair[1], pair[0])
 
-    blocks = []
-    for k in range(PAIRS):
-        block = coeffs[k].astype(f32)
-        parts = [block[32 * xx : 32 * (xx + 1), 96:128] for xx in range(X_SUB)]
-        last = jnp.concatenate(parts + [jnp.zeros((32, C_SUB), f32)], axis=1)
-        blocks.append([block[0:32], block[32:64], block[64:96], last])
+    rows[...] = coeffs[...].astype(f32)
+    blocks = [
+        [rows[pl.ds(4 * k + n, LAT_DEV, stride=32), :] for n in range(4)] for k in range(PAIRS)
+    ]
     modes = []
     for h in range(2):
         stack = []
@@ -266,6 +241,12 @@
     saved, cotangent, w_in, b_in, w_mid, b_mid, w_out, spectral_gain, basis_in, basis_out
 ):
     forward, back = zonal_tables()
+    bases = jnp.concatenate(
+        [jnp.transpose(basis_in, (1, 2, 0)), jnp.transpose(basis_out, (1, 0, 2))], axis=1
+    )
+    bases = jnp.pad(bases, ((0, LAT_DEV - M_DEV), (0, 0), (0, 0)))
+    bases, saved = lax.optimization_barrier((bases, saved))
+    bases = lax.all_to_all(bases, "lat", 0, 0, tiled=True)
     weights = (w_in, b_in.reshape(1, -1), w_mid, b_mid.reshape(1, -1), w_out)
     held = [pltpu.VMEM(a.shape, a.dtype) for a in (saved, cotangent) + weights]
     pad = pltpu.VMEM((X_DEV, Y_PAD, CHAN), bf16)
@@ -279,27 +260,18 @@
         moved=4_000_000,
         limit=NETWORK_VMEM,
     )(saved, cotangent, *weights)
+    bases, pieces = lax.optimization_barrier((bases, pieces))
     pieces = lax.all_to_all(pieces, LON, 0, 0, tiled=True)
-    bases = jnp.concatenate(
-        [jnp.transpose(basis_in, (1, 2, 0)), jnp.transpose(basis_out, (1, 0, 2))], axis=1
-    )
-    coeffs = call(zonal_kernel, (LAT_DEV, 24, 512), bf16, flops=300_000_000)(
-        pieces, jnp.asarray(forward), bases
-    )
-    coeffs = lax.all_to_all(coeffs, "lat", 0, 0, tiled=True)
-    coeffs, bases = call(
-        regroup_kernel,
-        [(PAIRS, 96, 128), (LAT_DEV, 24, NL)],
-        bf16,
-        (pltpu.VMEM((2 * DEVS, 128), f32),),
-    )(coeffs)
-    coeffs = lax.all_to_all(coeffs, "pair", 0, 0, tiled=True)
     mode = M_DEV * lax.axis_index(LON) + lax.axis_index("lat")
     place = jnp.stack([mode, lax.axis_index("core")]).astype(jnp.int32)
     tables = call(bases_kernel, (2, NL, NLAT), bf16, smem=1, flops=600_000_000, moved=3_000_000)(
         place, bases
     )
     others = lax.ppermute(tables, "core", [(0, 1), (1, 0)])
+    coeffs = call(zonal_kernel, (2 * DEVS, 128), bf16, flops=300_000_000)(
+        pieces, jnp.asarray(forward)
+    )
+    coeffs = lax.all_to_all(coeffs.reshape(DEVS // 2, 4, 128), ("lat", "pair"), 0, 0, tiled=True)
     coeffs = call(
         legendre_kernel,
         (2 * DEVS, 128),
@@ -307,7 +279,7 @@
         (pltpu.VMEM((2 * DEVS, 128), f32),),
         smem=1,
         flops=200_000_000,
-    )(place, coeffs, tables, others, spectral_gain)
+    )(place, coeffs.reshape(2 * DEVS, 128), tables, others, spectral_gain)
     coeffs = lax.all_to_all(coeffs.reshape(DEVS // 2, 4, 128), ("lat", "pair"), 0, 0, tiled=True)
     pieces = call(inverse_kernel, (LON_DEV, Y_MAIN, 128), bf16, flops=300_000_000)(
         coeffs.reshape(2 * DEVS, 128), jnp.asarray(back)

time: 136 us -> 134 us (0.985)
  blocking collectives: 55.1 us -> 41.8 us
  starting transfers between devices: 33.5 us -> 41.3 us
  local copies, waits for them, and re-layouts: 0.1 us -> 1.96 us
    all_to_all x1 -> x0, blocking collectives: 13 us -> none  [on_device(): coeffs = lax.all_to_all(coeffs, 'pair', 0, 0, tiled=True)]
    all_to_all x1 -> x2, starting transfers between devices: 12.9 us -> 25.2 us  [the longest x1 13.5 us: on_device(): bases = lax.all_to_all(bases, 'lat', 0, 0, tiled=True)]
    ppermute x1, starting transfers between devices: 6.21 us -> 2.14 us  [on_device(): others = lax.ppermute(tables, 'core', [(0, 1), (1, 0)])]
    all_to_all x1, waiting for transfers between devices: 11.2 us -> 7.64 us  [on_device(): pieces = lax.all_to_all(pieces, LON, 0, 0, tiled=True)]
    all_to_all x1 -> x2, waiting for transfers between devices: 20.1 us -> 23.4 us  [the longest x1 13.2 us: on_device(): lax.all_to_all(coeffs.reshape(DEVS // 2, 4, 128), ('lat', 'pair'), 0, 0,...]
    unnamed x12 -> x8, local copies, waits for them, and re-layouts: 0.1 us -> 1.96 us
    pallas_call x7 -> x6, Pallas kernels: 14.4 us -> 15.4 us  [run(): pl.pallas_call(kernel, out_shape=outs[0] if single else outs, in_specs=sp...]
  transfers between devices with their start and end apart: 3 -> 4, of which waited for: 2 -> 3; matrix products, arithmetic and copies ran while one was open for 0% -> 0% of each run, Pallas kernels for 0% -> 7%
where the time goes in v6:
time: 134 us; the launch traced here: 133 us
  blocking collectives  41.8 us (31%)
  starting transfers between devices  41.3 us (31%)
  waiting for transfers between devices  31 us (23%)
  Pallas kernels  15.4 us (11%)
  local copies, waits for them, and re-layouts  1.96 us (1%)
    all_to_all x1, blocking collectives, on_device(): lax.all_to_all(coeffs.reshape(DEVS // 2, 4, 128), ('lat', 'pair'), 0, 0,...  22.7 us
    all_to_all x1, blocking collectives, on_device(): pieces = lax.all_to_all(pieces, LON, 0, 0, tiled=True)  19 us
    pallas_call x6, Pallas kernels, run(): pl.pallas_call(kernel, out_shape=outs[0] if single else outs, in_specs=sp...  15.4 us
    all_to_all x1, starting transfers between devices, on_device(): pieces = lax.all_to_all(pieces, LON, 0, 0, tiled=True)  14 us
    all_to_all x1, starting transfers between devices, on_device(): bases = lax.all_to_all(bases, 'lat', 0, 0, tiled=True)  13.5 us
    all_to_all x1, waiting for transfers between devices, on_device(): lax.all_to_all(coeffs.reshape(DEVS // 2, 4, 128), ('lat', 'pair'), 0, 0,...  13.2 us
    all_to_all x1, starting transfers between devices, on_device(): lax.all_to_all(coeffs.reshape(DEVS // 2, 4, 128), ('lat', 'pair'), 0, 0,...  11.7 us
    all_to_all x1, waiting for transfers between devices, on_device(): bases = lax.all_to_all(bases, 'lat', 0, 0, tiled=True)  10.2 us
  transfers between devices with their start and end apart: 4, of which 3 were waited for; matrix products, arithmetic and copies ran while one was open for 0% of the time, Pallas kernels for 7%

profile of v6, /device:TPU:1, one launch (start us, length us, event | category | flops | bytes accessed | tf_op | source)
XLA Modules:
  0.0 132.6 jit_solution(16293948159305910627)
XLA Ops:
  0.0 1.0 copy.18
  1.0 1.0 copy.17
  2.0 0.9 fusion.2
  2.9 13.5 %all-to-all-start = ((bf16[32,24,384]{2,1,0:T(8,128)(2,1)}), bf16[32,24,384]{2,1,0:T(8,128)(2,1)S(1)}, u32[]{:S(2)}, u32[]{:S(2)}) async-start(bf16[32,24,384]{2,1,0:T(8,128)(2,1)} %fusion.2), calls=%async_computation | async-start | bytes 1179648 | tf_op jit(solution)/shard_map/all_to_all | solution.py:249
  16.4 5.9 %shard_map.118 = bf16[16,72,128]{2,1,0:T(8,128)(2,1)} custom-call(bf16[12,90,128]{2,1,0:T(8,128)(2,1)} %saved_h, bf16[12,90,128]{2,1,0:T(8,128)(2,1)} %cotan_h.1, bf16[128,512]{1,0:T(8,128)(2,1)} %w_in_h.1, f32[1,512]{1,0:T(1,128)} %bitcast.19, bf16[512,512]{1,0:T(8,128)(2,1)} %w_mid_h.1, f32[1,512]{1,0:T(1,128)} %bitcast.20, bf16[512,128]{1,0:T(8,128)(2,1)} %w_out_h.1), custom_call_target="tpu_custom_call" | custom-call | flops 1700000000 | bytes 4000000 | tf_op jit(solution)/shard_map/pallas_call | solution.py:227
  22.3 10.2 %all-to-all-done.bases = bf16[32,24,384]{2,1,0:T(8,128)(2,1)S(1)} async-done(((bf16[32,24,384]{2,1,0:T(8,128)(2,1)}), bf16[32,24,384]{2,1,0:T(8,128)(2,1)S(1)}, u32[]{:S(2)}, u32[]{:S(2)}) %all-to-all-start) | async-done | bytes 589856 | tf_op jit(solution)/shard_map/all_to_all | solution.py:249
  32.5 0.0 copy-start.1
  32.5 14.0 %all-to-all-start.1 = ((bf16[16,72,128]{2,1,0:T(8,128)(2,1)}), bf16[16,72,128]{2,1,0:T(8,128)(2,1)S(1)}, u32[]{:S(2)}, u32[]{:S(2)}) async-start(bf16[16,72,128]{2,1,0:T(8,128)(2,1)} %shard_map.118), calls=%async_computation.1 | async-start | bytes 589824 | tf_op jit(solution)/shard_map/all_to_all | solution.py:264
  46.6 0.1 pad_add_fusion.place
  46.6 2.4 %shard_map.120.tables = bf16[2,384,384]{2,1,0:T(8,128)(2,1)} custom-call(s32[2]{0:T(128)S(1)} %pad_add_fusion.place, bf16[32,24,384]{2,1,0:T(8,128)(2,1)S(1)} %all-to-all-done.bases), custom_call_target="tpu_custom_call" | custom-call | flops 600000000 | bytes 3000000 | tf_op jit(solution)/shard_map/pallas_call | solution.py:227
  49.0 0.0 copy-start.2
  49.0 2.1 %collective-permute-start = (bf16[2,384,384]{2,1,0:T(8,128)(2,1)}, bf16[2,384,384]{2,1,0:T(8,128)(2,1)S(1)}, u32[]{:S(2)}, u32[]{:S(2)}) collective-permute-start(bf16[2,384,384]{2,1,0:T(8,128)(2,1)} %shard_map.120.tables), channel_id=1, source_target_pairs={{0,1},{1,0},{2,3},{3,2},{4,5},{5,4},{6,7},{7,6},{8,9},{9,8},{10,11... | collective-permute-start | bytes 1769480 | tf_op jit(solution)/shard_map/ppermute | solution.py:270
  51.1 7.6 %all-to-all-done.1.circles = bf16[16,72,128]{2,1,0:T(8,128)(2,1)S(1)} async-done(((bf16[16,72,128]{2,1,0:T(8,128)(2,1)}), bf16[16,72,128]{2,1,0:T(8,128)(2,1)S(1)}, u32[]{:S(2)}, u32[]{:S(2)}) %all-to-all-start.1) | async-done | bytes 294944 | tf_op jit(solution)/shard_map/all_to_all | solution.py:264
  58.8 0.0 copy-done.1
  58.8 1.4 %shard_map.119 = bf16[1024,128]{1,0:T(8,128)(2,1)} custom-call(bf16[16,72,128]{2,1,0:T(8,128)(2,1)S(1)} %all-to-all-done.1.circles, bf16[736,1536]{1,0:T(8,128)(2,1)S(1)} %copy-done.1), custom_call_target="tpu_custom_call" | custom-call | flops 300000000 | tf_op jit(solution)/shard_map/pallas_call | solution.py:227
  60.2 11.7 %all-to-all-start.2 = ((bf16[256,4,128]{2,1,0:T(4,128)(2,1)}), bf16[256,4,128]{2,1,0:T(4,128)(2,1)S(1)}, u32[]{:S(2)}, u32[]{:S(2)}) async-start(bf16[256,4,128]{2,1,0:T(4,128)(2,1)} %bitcast.6), calls=%async_computation.2 | async-start | bytes 524288 | tf_op jit(solution)/shard_map/all_to_all | solution.py:274
  72.0 0.0 collective-permute-done.others
  72.0 13.2 %all-to-all-done.2 = bf16[256,4,128]{2,1,0:T(4,128)(2,1)S(1)} async-done(((bf16[256,4,128]{2,1,0:T(4,128)(2,1)}), bf16[256,4,128]{2,1,0:T(4,128)(2,1)S(1)}, u32[]{:S(2)}, u32[]{:S(2)}) %all-to-all-start.2) | async-done | bytes 262176 | tf_op jit(solution)/shard_map/all_to_all | solution.py:274
  85.1 0.0 copy-done.2
  85.1 0.0 copy-start
  85.1 3.0 %shard_map.121 = bf16[1024,128]{1,0:T(8,128)(2,1)S(1)} custom-call(s32[2]{0:T(128)S(1)} %pad_add_fusion.place, bf16[1024,128]{1,0:T(8,128)(2,1)S(1)} %bitcast.15, bf16[2,384,384]{2,1,0:T(8,128)(2,1)} %shard_map.120.tables, bf16[2,384,384]{2,1,0:T(8,128)(2,1)S(1)} %collective-permute-done.others, f32[384,128]{1,0:T(8,128)S(1)} %copy-done.2), custom_call_target="tpu_custom_call" | custom-call | flops 200000000 | tf_op jit(solution)/shard_map/pallas_call | solution.py:227
  88.1 22.7 %all_to_all.25 = bf16[256,4,128]{2,1,0:T(4,128)(2,1)S(1)} all-to-all(bf16[256,4,128]{2,1,0:T(4,128)(2,1)S(1)} %bitcast.16), channel_id=1, replica_groups=mesh['lat'=32,'pair'=8,'core'=2] {'lat','pair'}, dimensions={0} | all-to-all | bytes 524288 | tf_op jit(solution)/shard_map/all_to_all | solution.py:283
  110.8 0.0 copy-done
  110.8 1.6 %shard_map.122 = bf16[16,72,128]{2,1,0:T(8,128)(2,1)S(1)} custom-call(bf16[1024,128]{1,0:T(8,128)(2,1)S(1)} %bitcast.14, bf16[1536,736]{1,0:T(8,128)(2,1)S(1)} %copy-done), custom_call_target="tpu_custom_call" | custom-call | flops 300000000 | tf_op jit(solution)/shard_map/pallas_call | solution.py:227
  112.4 19.0 %all_to_all.26.pieces = bf16[16,72,128]{2,1,0:T(8,128)(2,1)S(1)} all-to-all(bf16[16,72,128]{2,1,0:T(8,128)(2,1)S(1)} %shard_map.122), channel_id=1, replica_groups=mesh['lat'=32,'pair'=8,'core'=2] {'pair','core'}, dimensions={0} | all-to-all | bytes 589824 | tf_op jit(solution)/shard_map/all_to_all | solution.py:287
  131.4 1.1 shard_map.123
Async XLA Ops:
  2.9 29.6 %all-to-all-start = ((bf16[32,24,384]{2,1,0:T(8,128)(2,1)}), bf16[32,24,384]{2,1,0:T(8,128)(2,1)S(1)}, u32[]{:S(2)}, u32[]{:S(2)}) async-start(bf16[32,24,384]{2,1,0:T(8,128)(2,1)} %fusion.2), calls=%async_computation | async-start | bytes 1179648 | tf_op jit(solution)/shard_map/all_to_all | solution.py:249
  32.5 26.3 %copy-start.1 = (bf16[736,1536]{1,0:T(8,128)(2,1)S(1)}, bf16[736,1536]{1,0:T(8,128)(2,1)}, u32[]{:S(2)}) copy-start(bf16[736,1536]{1,0:T(8,128)(2,1)} %constant.25.clone.table) | copy-start | bytes 6782980
  32.5 26.2 %all-to-all-start.1 = ((bf16[16,72,128]{2,1,0:T(8,128)(2,1)}), bf16[16,72,128]{2,1,0:T(8,128)(2,1)S(1)}, u32[]{:S(2)}, u32[]{:S(2)}) async-start(bf16[16,72,128]{2,1,0:T(8,128)(2,1)} %shard_map.118), calls=%async_computation.1 | async-start | bytes 589824 | tf_op jit(solution)/shard_map/all_to_all | solution.py:264
  49.0 36.1 %copy-start.2 = (f32[384,128]{1,0:T(8,128)S(1)}, f32[384,128]{1,0:T(8,128)}, u32[]{:S(2)}) copy-start(f32[384,128]{1,0:T(8,128)} %gain.1) | copy-start | bytes 589828
  49.0 23.0 %collective-permute-start = (bf16[2,384,384]{2,1,0:T(8,128)(2,1)}, bf16[2,384,384]{2,1,0:T(8,128)(2,1)S(1)}, u32[]{:S(2)}, u32[]{:S(2)}) collective-permute-start(bf16[2,384,384]{2,1,0:T(8,128)(2,1)} %shard_map.120.tables), channel_id=1, source_target_pairs={{0,1},{1,0},{2,3},{3,2},{4,5},{5,4},{6,7},{7,6},{8,9},{9,8},{10,11... | collective-permute-start | bytes 1769480 | tf_op jit(solution)/shard_map/ppermute | solution.py:270
  60.2 24.9 %all-to-all-start.2 = ((bf16[256,4,128]{2,1,0:T(4,128)(2,1)}), bf16[256,4,128]{2,1,0:T(4,128)(2,1)S(1)}, u32[]{:S(2)}, u32[]{:S(2)}) async-start(bf16[256,4,128]{2,1,0:T(4,128)(2,1)} %bitcast.6), calls=%async_computation.2 | async-start | bytes 524288 | tf_op jit(solution)/shard_map/all_to_all | solution.py:274
  85.1 25.7 %copy-start = (bf16[1536,736]{1,0:T(8,128)(2,1)S(1)}, bf16[1536,736]{1,0:T(8,128)(2,1)}, u32[]{:S(2)}) copy-start(bf16[1536,736]{1,0:T(8,128)(2,1)} %constant.26.clone.table) | copy-start | bytes 6782980

commit v7 on v6

--- a/solution.py
+++ b/solution.py
@@ -60,6 +60,25 @@
 
 def sigmoid(v):
     return 0.5 * jnp.tanh(0.5 * v) + 0.5
+
+
+def arrange_kernel(first_h, second_h, out, first, second, rows, sems):
+    copies = [
+        pltpu.make_async_copy(first_h, first, sems.at[0]),
+        pltpu.make_async_copy(second_h, second, sems.at[1]),
+    ]
+    for copy in copies:
+        copy.start()
+    out[M_DEV:] = jnp.zeros((LAT_DEV - M_DEV, 24, NL), bf16)
+    for half, source in enumerate((first, second)):
+        copies[half].wait()
+        for k in range(12):
+            block = source[k].astype(f32)
+            for t in range(3):
+                rows[t, pl.ds(12 * half + k, M_DEV, stride=24), :] = block[:, 128 * t : 128 * (t + 1)]
+    for m in range(M_DEV):
+        for t in range(3):
+            out[m, :, 128 * t : 128 * (t + 1)] = rows[t, 24 * m : 24 * (m + 1), :].astype(bf16)
 
 
 def network_kernel(
@@ -237,14 +256,24 @@
     return run
 
 
+def arrange(first, second):
+    shape = pltpu.VMEM((12, M_DEV, NL), bf16)
+    rows = pltpu.VMEM((3, M_DEV * 24, 128), f32)
+    return call(
+        arrange_kernel,
+        (LAT_DEV, 24, NL),
+        bf16,
+        (shape, shape, rows, pltpu.SemaphoreType.DMA((2,))),
+        space=pltpu.HBM,
+        limit=NETWORK_VMEM,
+    )(first, second)
+
+
 def on_device(
     saved, cotangent, w_in, b_in, w_mid, b_mid, w_out, spectral_gain, basis_in, basis_out
 ):
     forward, back = zonal_tables()
-    bases = jnp.concatenate(
-        [jnp.transpose(basis_in, (1, 2, 0)), jnp.transpose(basis_out, (1, 0, 2))], axis=1
-    )
-    bases = jnp.pad(bases, ((0, LAT_DEV - M_DEV), (0, 0), (0, 0)))
+    bases = arrange(jnp.transpose(basis_in, (2, 1, 0)), basis_out)
     bases, saved = lax.optimization_barrier((bases, saved))
     bases = lax.all_to_all(bases, "lat", 0, 0, tiled=True)
     weights = (w_in, b_in.reshape(1, -1), w_mid, b_mid.reshape(1, -1), w_out)
@@ -271,6 +300,7 @@
     coeffs = call(zonal_kernel, (2 * DEVS, 128), bf16, flops=300_000_000)(
         pieces, jnp.asarray(forward)
     )
+    others, coeffs = lax.optimization_barrier((others, coeffs))
     coeffs = lax.all_to_all(coeffs.reshape(DEVS // 2, 4, 128), ("lat", "pair"), 0, 0, tiled=True)
     coeffs = call(
         legendre_kernel,

time: 134 us -> 136 us (1.015)
  blocking collectives: 41.8 us -> 89 us
  starting transfers between devices: 41.3 us -> 19.4 us
  waiting for transfers between devices: 31 us -> 10.1 us
  local copies, waits for them, and re-layouts: 1.96 us -> 0.02 us
    all_to_all x2 -> x0, starting transfers between devices: 25.7 us -> none  [the longest x1 14 us: on_device(): pieces = lax.all_to_all(pieces, LON, 0, 0, tiled=True)]
    all_to_all x1 -> x2, blocking collectives: 22.7 us -> 47.9 us  [on_device(): lax.all_to_all(coeffs.reshape(DEVS // 2, 4, 128), ('lat', 'pair'), 0, 0,...]
    all_to_all x1 -> x2, blocking collectives: 19 us -> 41.1 us  [on_device(): pieces = lax.all_to_all(pieces, LON, 0, 0, tiled=True)]
    all_to_all x2 -> x0, waiting for transfers between devices: 20.8 us -> none  [the longest x1 13.2 us: on_device(): lax.all_to_all(coeffs.reshape(DEVS // 2, 4, 128), ('lat', 'pair'), 0, 0,...]
    ppermute x1, starting transfers between devices: 2.14 us -> 5.88 us  [on_device(): others = lax.ppermute(tables, 'core', [(0, 1), (1, 0)])]
    unnamed x8 -> x6, local copies, waits for them, and re-layouts: 1.96 us -> 0.02 us
    pallas_call x6 -> x7, Pallas kernels: 15.4 us -> 15.2 us  [run(): pl.pallas_call(kernel, out_shape=outs[0] if single else outs, in_specs=sp...]
  transfers between devices with their start and end apart: 4 -> 2, of which waited for: 3 -> 1; matrix products, arithmetic and copies ran while one was open for 0% -> 0% of each run, Pallas kernels for 7% -> 5%
where the time goes in v7:
time: 136 us; the launch traced here: 134 us
  blocking collectives  89 us (65%)
  starting transfers between devices  19.4 us (14%)
  Pallas kernels  15.2 us (11%)
  waiting for transfers between devices  10.1 us (7%)
    all_to_all x2, blocking collectives, on_device(): lax.all_to_all(coeffs.reshape(DEVS // 2, 4, 128), ('lat', 'pair'), 0, 0,...  47.9 us
    all_to_all x2, blocking collectives, on_device(): pieces = lax.all_to_all(pieces, LON, 0, 0, tiled=True)  41.1 us
    pallas_call x7, Pallas kernels, run(): pl.pallas_call(kernel, out_shape=outs[0] if single else outs, in_specs=sp...  15.2 us
    all_to_all x1, starting transfers between devices, on_device(): bases = lax.all_to_all(bases, 'lat', 0, 0, tiled=True)  13.5 us
    all_to_all x1, waiting for transfers between devices, on_device(): bases = lax.all_to_all(bases, 'lat', 0, 0, tiled=True)  10.1 us
    ppermute x1, starting transfers between devices, on_device(): others = lax.ppermute(tables, 'core', [(0, 1), (1, 0)])  5.88 us
  transfers between devices with their start and end apart: 2, of which 1 were waited for; matrix products, arithmetic and copies ran while one was open for 0% of the time, Pallas kernels for 5%

profile of v7, /device:TPU:1, one launch (start us, length us, event | category | flops | bytes accessed | tf_op | source)
XLA Modules:
  0.0 133.9 jit_solution(12668153911474841081)
XLA Ops:
  0.0 2.0 %shard_map.118 = bf16[32,24,384]{2,1,0:T(8,128)(2,1)} custom-call(bf16[12,23,384]{2,1,0:T(8,128)(2,1)} %bitcast.13, bf16[12,23,384]{2,1,0:T(8,128)(2,1)} %second_h.1), custom_call_target="tpu_custom_call" | custom-call | tf_op jit(solution)/shard_map/pallas_call | solution.py:246
  2.0 13.5 %all-to-all-start = ((bf16[32,24,384]{2,1,0:T(8,128)(2,1)}), bf16[32,24,384]{2,1,0:T(8,128)(2,1)S(1)}, u32[]{:S(2)}, u32[]{:S(2)}) async-start(bf16[32,24,384]{2,1,0:T(8,128)(2,1)} %shard_map.118), calls=%async_computation | async-start | bytes 1179648 | tf_op jit(solution)/shard_map/all_to_all | solution.py:278
  15.5 0.1 pad_add_fusion.place
  15.6 5.9 %shard_map.119 = bf16[16,72,128]{2,1,0:T(8,128)(2,1)} custom-call(bf16[12,90,128]{2,1,0:T(8,128)(2,1)} %saved_h, bf16[12,90,128]{2,1,0:T(8,128)(2,1)} %cotan_h.1, bf16[128,512]{1,0:T(8,128)(2,1)} %w_in_h.1, f32[1,512]{1,0:T(1,128)} %bitcast.14, bf16[512,512]{1,0:T(8,128)(2,1)} %w_mid_h.1, f32[1,512]{1,0:T(1,128)} %bitcast.15, bf16[512,128]{1,0:T(8,128)(2,1)} %w_out_h.1), custom_call_target="tpu_custom_call" | custom-call | flops 1700000000 | bytes 4000000 | tf_op jit(solution)/shard_map/pallas_call | solution.py:246
  21.6 0.0 copy-start.1
  21.6 10.1 %all-to-all-done.bases = bf16[32,24,384]{2,1,0:T(8,128)(2,1)S(1)} async-done(((bf16[32,24,384]{2,1,0:T(8,128)(2,1)}), bf16[32,24,384]{2,1,0:T(8,128)(2,1)S(1)}, u32[]{:S(2)}, u32[]{:S(2)}) %all-to-all-start) | async-done | bytes 589856 | tf_op jit(solution)/shard_map/all_to_all | solution.py:278
  31.7 1.5 %shard_map.120.tables = bf16[2,384,384]{2,1,0:T(8,128)(2,1)S(1)} custom-call(s32[2]{0:T(128)S(1)} %pad_add_fusion.place, bf16[32,24,384]{2,1,0:T(8,128)(2,1)S(1)} %all-to-all-done.bases), custom_call_target="tpu_custom_call" | custom-call | flops 600000000 | bytes 3000000 | tf_op jit(solution)/shard_map/pallas_call | solution.py:246
  33.2 0.0 copy-start.2
  33.2 5.9 %collective-permute-start = (bf16[2,384,384]{2,1,0:T(8,128)(2,1)S(1)}, bf16[2,384,384]{2,1,0:T(8,128)(2,1)S(1)}, u32[]{:S(2)}, u32[]{:S(2)}) collective-permute-start(bf16[2,384,384]{2,1,0:T(8,128)(2,1)S(1)} %shard_map.120.tables), channel_id=1, source_target_pairs={{0,1},{1,0},{2,3},{3,2},{4,5},{5,4},{6,7},{7,6},{8,9},{9,8},{10,11... | collective-permute-start | bytes 1769480 | tf_op jit(solution)/shard_map/ppermute | solution.py:299
  39.1 22.4 %all_to_all.25.circles = bf16[16,72,128]{2,1,0:T(8,128)(2,1)S(1)} all-to-all(bf16[16,72,128]{2,1,0:T(8,128)(2,1)} %shard_map.119), channel_id=1, replica_groups=mesh['lat'=32,'pair'=8,'core'=2] {'pair','core'}, dimensions={0} | all-to-all | bytes 589824 | tf_op jit(solution)/shard_map/all_to_all | solution.py:293
  61.5 0.0 copy-done.1
  61.5 0.0 copy-start
  61.5 0.8 shard_map.121
  62.3 0.0 collective-permute-done.others
  62.3 24.8 %all_to_all.26 = bf16[256,4,128]{2,1,0:T(4,128)(2,1)S(1)} all-to-all(bf16[256,4,128]{2,1,0:T(4,128)(2,1)S(1)} %bitcast.12), channel_id=1, replica_groups=mesh['lat'=32,'pair'=8,'core'=2] {'lat','pair'}, dimensions={0} | all-to-all | bytes 524288 | tf_op jit(solution)/shard_map/all_to_all | solution.py:304
  87.1 0.0 copy-done.2
  87.1 2.3 %shard_map.122 = bf16[1024,128]{1,0:T(8,128)(2,1)S(1)} custom-call(s32[2]{0:T(128)S(1)} %pad_add_fusion.place, bf16[1024,128]{1,0:T(8,128)(2,1)S(1)} %bitcast.10, bf16[2,384,384]{2,1,0:T(8,128)(2,1)S(1)} %shard_map.120.tables, bf16[2,384,384]{2,1,0:T(8,128)(2,1)S(1)} %collective-permute-done.others, f32[384,128]{1,0:T(8,128)S(1)} %copy-done.2), custom_call_target="tpu_custom_call" | custom-call | flops 200000000 | tf_op jit(solution)/shard_map/pallas_call | solution.py:246
  89.3 23.1 %all_to_all.27 = bf16[256,4,128]{2,1,0:T(4,128)(2,1)S(1)} all-to-all(bf16[256,4,128]{2,1,0:T(4,128)(2,1)S(1)} %bitcast.11), channel_id=1, replica_groups=mesh['lat'=32,'pair'=8,'core'=2] {'lat','pair'}, dimensions={0} | all-to-all | bytes 524288 | tf_op jit(solution)/shard_map/all_to_all | solution.py:313
  112.5 0.0 copy-done
  112.5 1.6 %shard_map.123 = bf16[16,72,128]{2,1,0:T(8,128)(2,1)S(1)} custom-call(bf16[1024,128]{1,0:T(8,128)(2,1)S(1)} %bitcast.9, bf16[1536,736]{1,0:T(8,128)(2,1)S(1)} %copy-done), custom_call_target="tpu_custom_call" | custom-call | flops 300000000 | tf_op jit(solution)/shard_map/pallas_call | solution.py:246
  114.0 18.8 %all_to_all.28.pieces = bf16[16,72,128]{2,1,0:T(8,128)(2,1)S(1)} all-to-all(bf16[16,72,128]{2,1,0:T(8,128)(2,1)S(1)} %shard_map.123), channel_id=1, replica_groups=mesh['lat'=32,'pair'=8,'core'=2] {'pair','core'}, dimensions={0} | all-to-all | bytes 589824 | tf_op jit(solution)/shard_map/all_to_all | solution.py:317
  132.8 1.1 shard_map.124
Async XLA Ops:
  2.0 29.7 %all-to-all-start = ((bf16[32,24,384]{2,1,0:T(8,128)(2,1)}), bf16[32,24,384]{2,1,0:T(8,128)(2,1)S(1)}, u32[]{:S(2)}, u32[]{:S(2)}) async-start(bf16[32,24,384]{2,1,0:T(8,128)(2,1)} %shard_map.118), calls=%async_computation | async-start | bytes 1179648 | tf_op jit(solution)/shard_map/all_to_all | solution.py:278
  21.6 40.0 %copy-start.1 = (bf16[736,1536]{1,0:T(8,128)(2,1)S(1)}, bf16[736,1536]{1,0:T(8,128)(2,1)}, u32[]{:S(2)}) copy-start(bf16[736,1536]{1,0:T(8,128)(2,1)} %constant.22.clone.table) | copy-start | bytes 6782980
  33.2 53.8 %copy-start.2 = (f32[384,128]{1,0:T(8,128)S(1)}, f32[384,128]{1,0:T(8,128)}, u32[]{:S(2)}) copy-start(f32[384,128]{1,0:T(8,128)} %gain.1) | copy-start | bytes 589828
  33.2 29.1 %collective-permute-start = (bf16[2,384,384]{2,1,0:T(8,128)(2,1)S(1)}, bf16[2,384,384]{2,1,0:T(8,128)(2,1)S(1)}, u32[]{:S(2)}, u32[]{:S(2)}) collective-permute-start(bf16[2,384,384]{2,1,0:T(8,128)(2,1)S(1)} %shard_map.120.tables), channel_id=1, source_target_pairs={{0,1},{1,0},{2,3},{3,2},{4,5},{5,4},{6,7},{7,6},{8,9},{9,8},{10,11... | collective-permute-start | bytes 1769480 | tf_op jit(solution)/shard_map/ppermute | solution.py:299
  61.5 50.9 %copy-start = (bf16[1536,736]{1,0:T(8,128)(2,1)S(1)}, bf16[1536,736]{1,0:T(8,128)(2,1)}, u32[]{:S(2)}) copy-start(bf16[1536,736]{1,0:T(8,128)(2,1)} %constant.23.clone.table) | copy-start | bytes 6782980

commit v8 on v7

--- a/solution.py
+++ b/solution.py
@@ -21,7 +21,7 @@
 XG = X_DEV // X_SUB
 DEVS = LAT_DEV * LON_DEV
 ROWS = 2 * NM
-LON = ("pair", "core")
+LON = ("x", "z_hi", "core")
 VMEM = 16 * 1024 * 1024
 NETWORK_VMEM = 59 * 1024 * 1024
 
@@ -82,7 +82,7 @@
 
 
 def network_kernel(
-    saved_h, cotan_h, w_in_h, b_in_h, w_mid_h, b_mid_h, w_out_h, out,
+    z_hi, saved_h, cotan_h, w_in_h, b_in_h, w_mid_h, b_mid_h, w_out_h, kept, sent,
     saved, cotan, w_in, b_in, w_mid, b_mid, w_out, rows_s, rows_c, sems,
 ):
     pairs = (
@@ -123,18 +123,24 @@
         back_one = (dot_t(back_two, w_mid[...]) * slope_one).astype(bf16)
         grad = c.astype(f32) + dot_t(back_one, w_in[...])
         grad = grad.reshape(X_SUB, Y_PAD, CHAN)
-        for cg in range(CG):
-            parts = [grad[xx][:, C_SUB * cg : C_SUB * (cg + 1)] for xx in range(X_SUB)]
-            parts = [p[0:Y_MAIN] for p in parts] + [
-                jnp.concatenate([p[Y_MAIN:] for p in parts], axis=0)
-            ]
-            out[owner(xg, cg)] = jnp.concatenate(parts, axis=1).astype(bf16)
-
-
-def zonal_kernel(circles, table, out):
+        for h in range(2):
+            blocks = []
+            for cg in (2 * h, 2 * h + 1):
+                parts = [grad[xx][:, C_SUB * cg : C_SUB * (cg + 1)] for xx in range(X_SUB)]
+                parts = [p[0:Y_MAIN] for p in parts] + [
+                    jnp.concatenate([p[Y_MAIN:] for p in parts], axis=0)
+                ]
+                blocks.append(jnp.concatenate(parts, axis=1))
+            low = z_hi[0] == 0
+            kept[2 * xg + h] = jnp.where(low, blocks[0], blocks[1]).astype(bf16)
+            sent[2 * xg + h] = jnp.where(low, blocks[1], blocks[0]).astype(bf16)
+
+
+def zonal_kernel(z_hi, circles, table, out):
     main, extra = [], []
     for j in range(LON_DEV):
-        piece = circles[j].astype(f32)
+        x, z, core = j // 4, j // 2 % 2, j % 2
+        piece = circles[2 * x + core, z_hi[0] ^ z].astype(f32)
         main.append(piece)
         parts = [piece[Y_EXT * xx : Y_EXT * (xx + 1), 96:128] for xx in range(X_SUB)]
         extra.append(jnp.concatenate(parts + [jnp.zeros((Y_EXT, C_SUB), f32)], axis=1))
@@ -276,32 +282,35 @@
     bases = arrange(jnp.transpose(basis_in, (2, 1, 0)), basis_out)
     bases, saved = lax.optimization_barrier((bases, saved))
     bases = lax.all_to_all(bases, "lat", 0, 0, tiled=True)
+    z_hi = lax.axis_index("z_hi").astype(jnp.int32).reshape(1)
     weights = (w_in, b_in.reshape(1, -1), w_mid, b_mid.reshape(1, -1), w_out)
     held = [pltpu.VMEM(a.shape, a.dtype) for a in (saved, cotangent) + weights]
     pad = pltpu.VMEM((X_DEV, Y_PAD, CHAN), bf16)
-    pieces = call(
+    kept, sent = call(
         network_kernel,
-        (LON_DEV, Y_MAIN, 128),
+        [(PAIRS, Y_MAIN, 128), (PAIRS, Y_MAIN, 128)],
         bf16,
         held + [pad, pad, pltpu.SemaphoreType.DMA((7,))],
+        smem=1,
         space=pltpu.HBM,
         flops=1_700_000_000,
         moved=4_000_000,
         limit=NETWORK_VMEM,
-    )(saved, cotangent, *weights)
+    )(z_hi, saved, cotangent, *weights)
+    sent = lax.ppermute(sent, "z_hi", [(0, 1), (1, 0)])
+    pieces = jnp.stack([kept, sent], axis=1)
     bases, pieces = lax.optimization_barrier((bases, pieces))
-    pieces = lax.all_to_all(pieces, LON, 0, 0, tiled=True)
+    pieces = lax.all_to_all(pieces, ("x", "core"), 0, 0, tiled=True)
     mode = M_DEV * lax.axis_index(LON) + lax.axis_index("lat")
     place = jnp.stack([mode, lax.axis_index("core")]).astype(jnp.int32)
     tables = call(bases_kernel, (2, NL, NLAT), bf16, smem=1, flops=600_000_000, moved=3_000_000)(
         place, bases
     )
     others = lax.ppermute(tables, "core", [(0, 1), (1, 0)])
-    coeffs = call(zonal_kernel, (2 * DEVS, 128), bf16, flops=300_000_000)(
-        pieces, jnp.asarray(forward)
-    )
-    others, coeffs = lax.optimization_barrier((others, coeffs))
-    coeffs = lax.all_to_all(coeffs.reshape(DEVS // 2, 4, 128), ("lat", "pair"), 0, 0, tiled=True)
+    coeffs = call(zonal_kernel, (2 * DEVS, 128), bf16, smem=1, flops=300_000_000)(
+        z_hi, pieces, jnp.asarray(forward)
+    )
+    coeffs = lax.all_to_all(coeffs.reshape(DEVS // 2, 4, 128), ("lat", "x", "z_hi"), 0, 0, tiled=True)
     coeffs = call(
         legendre_kernel,
         (2 * DEVS, 128),
@@ -310,7 +319,7 @@
         smem=1,
         flops=200_000_000,
     )(place, coeffs.reshape(2 * DEVS, 128), tables, others, spectral_gain)
-    coeffs = lax.all_to_all(coeffs.reshape(DEVS // 2, 4, 128), ("lat", "pair"), 0, 0, tiled=True)
+    coeffs = lax.all_to_all(coeffs.reshape(DEVS // 2, 4, 128), ("lat", "x", "z_hi"), 0, 0, tiled=True)
     pieces = call(inverse_kernel, (LON_DEV, Y_MAIN, 128), bf16, flops=300_000_000)(
         coeffs.reshape(2 * DEVS, 128), jnp.asarray(back)
     )
@@ -321,5 +330,5 @@
 def solution(mesh):
     grid = P("lat", LON, None)
     placed = (grid, grid, P(), P(), P(), P(), P(), P(), P(None, LON, "lat"), grid)
-    fine = Mesh(mesh.devices.reshape(LAT_DEV, PAIRS, 2), ("lat",) + LON)
+    fine = Mesh(mesh.devices.reshape(LAT_DEV, XG, 2, 2), ("lat",) + LON)
     return jax.shard_map(on_device, mesh=fine, in_specs=placed, out_specs=grid, check_vma=False)

time: 136 us -> 134 us (0.985)
  blocking collectives: 89 us -> 42.5 us
  starting transfers between devices: 19.4 us -> 41.7 us
  waiting for transfers between devices: 10.1 us -> 28 us
  other arithmetic: 0.08 us -> 1.73 us
  local copies, waits for them, and re-layouts: 0.02 us -> 1.65 us
    all_to_all x2 -> x1, blocking collectives: 47.9 us -> 23.5 us  [on_device(): lax.all_to_all(coeffs.reshape(DEVS // 2, 4, 128), ('lat', 'x', 'z_hi'), 0...]
    all_to_all x2 -> x1, blocking collectives: 41.1 us -> 19 us  [on_device(): pieces = lax.all_to_all(pieces, LON, 0, 0, tiled=True)]
    all_to_all x0 -> x2, starting transfers between devices: none -> 18.3 us  [the longest x1 12 us: on_device(): lax.all_to_all(coeffs.reshape(DEVS // 2, 4, 128), ('lat', 'x', 'z_hi'), 0...]
    all_to_all x0 -> x2, waiting for transfers between devices: none -> 15.5 us  [the longest x1 12.4 us: on_device(): lax.all_to_all(coeffs.reshape(DEVS // 2, 4, 128), ('lat', 'x', 'z_hi'), 0...]
    ppermute x0 -> x1, waiting for transfers between devices: none -> 12.5 us  [on_device(): sent = lax.ppermute(sent, 'z_hi', [(0, 1), (1, 0)])]
    all_to_all x1, waiting for transfers between devices: 10.1 us -> 0.01 us  [on_device(): bases = lax.all_to_all(bases, 'lat', 0, 0, tiled=True)]
    ppermute x0 -> x1, starting transfers between devices: none -> 7.94 us  [on_device(): sent = lax.ppermute(sent, 'z_hi', [(0, 1), (1, 0)])]
    ppermute x1, starting transfers between devices: 5.88 us -> 2.05 us  [on_device(): others = lax.ppermute(tables, 'core', [(0, 1), (1, 0)])]
  transfers between devices with their start and end apart: 2 -> 5, of which waited for: 1 -> 3; matrix products, arithmetic and copies ran while one was open for 0% -> 1% of each run, Pallas kernels for 5% -> 7%
where the time goes in v8:
time: 134 us; the launch traced here: 132 us
  blocking collectives  42.5 us (32%)
  starting transfers between devices  41.7 us (31%)
  waiting for transfers between devices  28 us (21%)
  Pallas kernels  16.5 us (12%)
  other arithmetic  1.73 us (1%)
  local copies, waits for them, and re-layouts  1.65 us (1%)
    all_to_all x1, blocking collectives, on_device(): lax.all_to_all(coeffs.reshape(DEVS // 2, 4, 128), ('lat', 'x', 'z_hi'), 0...  23.5 us
    all_to_all x1, blocking collectives, on_device(): pieces = lax.all_to_all(pieces, LON, 0, 0, tiled=True)  19 us
    pallas_call x7, Pallas kernels, run(): pl.pallas_call(kernel, out_shape=outs[0] if single else outs, in_specs=sp...  16.5 us
    all_to_all x1, starting transfers between devices, on_device(): bases = lax.all_to_all(bases, 'lat', 0, 0, tiled=True)  13.5 us
    ppermute x1, waiting for transfers between devices, on_device(): sent = lax.ppermute(sent, 'z_hi', [(0, 1), (1, 0)])  12.5 us
    all_to_all x1, waiting for transfers between devices, on_device(): lax.all_to_all(coeffs.reshape(DEVS // 2, 4, 128), ('lat', 'x', 'z_hi'), 0...  12.4 us
    all_to_all x1, starting transfers between devices, on_device(): lax.all_to_all(coeffs.reshape(DEVS // 2, 4, 128), ('lat', 'x', 'z_hi'), 0...  12 us
    ppermute x1, starting transfers between devices, on_device(): sent = lax.ppermute(sent, 'z_hi', [(0, 1), (1, 0)])  7.94 us
  transfers between devices with their start and end apart: 5, of which 3 were waited for; matrix products, arithmetic and copies ran while one was open for 1% of the time, Pallas kernels for 7%

profile of v8, /device:TPU:1, one launch (start us, length us, event | category | flops | bytes accessed | tf_op | source)
XLA Modules:
  0.0 132.2 jit_solution(17511980962286888936)
XLA Ops:
  0.0 2.0 %shard_map.118 = bf16[32,24,384]{2,1,0:T(8,128)(2,1)} custom-call(bf16[12,23,384]{2,1,0:T(8,128)(2,1)} %bitcast.15, bf16[12,23,384]{2,1,0:T(8,128)(2,1)} %second_h.1), custom_call_target="tpu_custom_call" | custom-call | tf_op jit(solution)/shard_map/pallas_call | solution.py:252
  2.0 13.5 %all-to-all-start = ((bf16[32,24,384]{2,1,0:T(8,128)(2,1)}), bf16[32,24,384]{2,1,0:T(8,128)(2,1)S(1)}, u32[]{:S(2)}, u32[]{:S(2)}) async-start(bf16[32,24,384]{2,1,0:T(8,128)(2,1)} %shard_map.118), calls=%async_computation | async-start | bytes 1179648 | tf_op jit(solution)/shard_map/all_to_all | solution.py:284
  15.5 6.0 %shard_map.119 = (bf16[8,72,128]{2,1,0:T(8,128)(2,1)}, bf16[8,72,128]{2,1,0:T(8,128)(2,1)}) custom-call(s32[1]{0:T(128)} %bitcast.2.z_hi, bf16[12,90,128]{2,1,0:T(8,128)(2,1)} %saved_h, bf16[12,90,128]{2,1,0:T(8,128)(2,1)} %cotan_h.1, bf16[128,512]{1,0:T(8,128)(2,1)} %w_in_h.1, f32[1,512]{1,0:T(1,128)} %bitcast.18, bf16[512,512]{1,0:T(8,128)(2,1)} %w_mid_h.1, ...), custom_call_target="tpu_custom_call" | custom-call | flops 1700000000 | bytes 4000000 | tf_op jit(solution)/shard_map/pallas_call | solution.py:252
  21.5 7.9 %collective-permute-start = (bf16[8,72,128]{2,1,0:T(8,128)(2,1)}, bf16[8,72,128]{2,1,0:T(8,128)(2,1)S(1)}, u32[]{:S(2)}, u32[]{:S(2)}) collective-permute-start(bf16[8,72,128]{2,1,0:T(8,128)(2,1)} %get-tuple-element.14), channel_id=1, source_target_pairs={{0,2},{2,0},{1,3},{3,1},{4,6},{6,4},{5,7},{7,5},{8,10},{10,8},{9,1... | collective-permute-start | bytes 442376 | tf_op jit(solution)/shard_map/ppermute | solution.py:300
  29.4 12.5 %collective-permute-done = bf16[8,72,128]{2,1,0:T(8,128)(2,1)S(1)} collective-permute-done((bf16[8,72,128]{2,1,0:T(8,128)(2,1)}, bf16[8,72,128]{2,1,0:T(8,128)(2,1)S(1)}, u32[]{:S(2)}, u32[]{:S(2)}) %collective-permute-start) | collective-permute-done | bytes 147488 | tf_op jit(solution)/shard_map/ppermute | solution.py:300
  42.0 1.7 %pad_maximum_fusion = bf16[8,2,72,128]{3,2,1,0:T(8,128)(2,1)} fusion(bf16[8,1,72,128]{3,2,1,0:T(8,128)(2,1)S(1)} %bitcast.17, bf16[8,1,72,128]{3,2,1,0:T(8,128)(2,1)} %bitcast.16), kind=kLoop, calls=%fused_computation | loop fusion | flops 147456 | bytes 589824 | tf_op jit(solution)/shard_map/stack | solution.py:301
  43.6 0.0 all-to-all-done.bases
  43.6 6.3 %all-to-all-start.1 = ((bf16[8,2,72,128]{3,2,1,0:T(8,128)(2,1)}), bf16[8,2,72,128]{3,2,1,0:T(8,128)(2,1)S(1)}, u32[]{:S(2)}, u32[]{:S(2)}) async-start(bf16[8,2,72,128]{3,2,1,0:T(8,128)(2,1)} %pad_maximum_fusion), calls=%async_computation.1 | async-start | bytes 589824 | tf_op jit(solution)/shard_map/all_to_all | solution.py:303
  49.9 0.1 pad_add_fusion.place
  50.0 0.0 copy-start.2
  50.0 1.5 %shard_map.121.tables = bf16[2,384,384]{2,1,0:T(8,128)(2,1)S(1)} custom-call(s32[2]{0:T(128)S(1)} %pad_add_fusion.place, bf16[32,24,384]{2,1,0:T(8,128)(2,1)S(1)} %all-to-all-done.bases), custom_call_target="tpu_custom_call" | custom-call | flops 600000000 | bytes 3000000 | tf_op jit(solution)/shard_map/pallas_call | solution.py:252
  51.5 0.0 copy-start
  51.5 2.1 %collective-permute-start.1 = (bf16[2,384,384]{2,1,0:T(8,128)(2,1)S(1)}, bf16[2,384,384]{2,1,0:T(8,128)(2,1)}, u32[]{:S(2)}, u32[]{:S(2)}) collective-permute-start(bf16[2,384,384]{2,1,0:T(8,128)(2,1)S(1)} %shard_map.121.tables), channel_id=1, source_target_pairs={{0,1},{1,0},{2,3},{3,2},{4,5},{5,4},{6,7},{7,6},{8,9},{9,8},{10,11... | collective-permute-start | bytes 1769480 | tf_op jit(solution)/shard_map/ppermute | solution.py:309
  53.6 3.1 %all-to-all-done.1.circles = bf16[8,2,72,128]{3,2,1,0:T(8,128)(2,1)S(1)} async-done(((bf16[8,2,72,128]{3,2,1,0:T(8,128)(2,1)}), bf16[8,2,72,128]{3,2,1,0:T(8,128)(2,1)S(1)}, u32[]{:S(2)}, u32[]{:S(2)}) %all-to-all-start.1) | async-done | bytes 294944 | tf_op jit(solution)/shard_map/all_to_all | solution.py:303
  56.7 0.0 copy-start.1
  56.7 1.6 %copy-done.1 = bf16[736,1536]{1,0:T(8,128)(2,1)S(1)} copy-done((bf16[736,1536]{1,0:T(8,128)(2,1)S(1)}, bf16[736,1536]{1,0:T(8,128)(2,1)}, u32[]{:S(2)}) %copy-start.1) | copy-done | bytes 2261016
  58.3 1.5 %shard_map.120 = bf16[1024,128]{1,0:T(8,128)(2,1)} custom-call(s32[1]{0:T(128)} %bitcast.2.z_hi, bf16[8,2,72,128]{3,2,1,0:T(8,128)(2,1)S(1)} %all-to-all-done.1.circles, bf16[736,1536]{1,0:T(8,128)(2,1)S(1)} %copy-done.1), custom_call_target="tpu_custom_call" | custom-call | flops 300000000 | tf_op jit(solution)/shard_map/pallas_call | solution.py:252
  59.8 12.0 %all-to-all-start.2 = ((bf16[256,4,128]{2,1,0:T(4,128)(2,1)}), bf16[256,4,128]{2,1,0:T(4,128)(2,1)S(1)}, u32[]{:S(2)}, u32[]{:S(2)}) async-start(bf16[256,4,128]{2,1,0:T(4,128)(2,1)} %bitcast.8), calls=%async_computation.2 | async-start | bytes 524288 | tf_op jit(solution)/shard_map/all_to_all | solution.py:313
  71.8 0.0 collective-permute-done.1.others
  71.8 12.4 %all-to-all-done.2 = bf16[256,4,128]{2,1,0:T(4,128)(2,1)S(1)} async-done(((bf16[256,4,128]{2,1,0:T(4,128)(2,1)}), bf16[256,4,128]{2,1,0:T(4,128)(2,1)S(1)}, u32[]{:S(2)}, u32[]{:S(2)}) %all-to-all-start.2) | async-done | bytes 262176 | tf_op jit(solution)/shard_map/all_to_all | solution.py:313
  84.2 0.0 copy-done.2
  84.2 2.8 %shard_map.122 = bf16[1024,128]{1,0:T(8,128)(2,1)S(1)} custom-call(s32[2]{0:T(128)S(1)} %pad_add_fusion.place, bf16[1024,128]{1,0:T(8,128)(2,1)S(1)} %bitcast.13, bf16[2,384,384]{2,1,0:T(8,128)(2,1)S(1)} %shard_map.121.tables, bf16[2,384,384]{2,1,0:T(8,128)(2,1)} %collective-permute-done.1.others, f32[384,128]{1,0:T(8,128)S(1)} %copy-done.2), custom_call_target="tpu_custom_call" | custom-call | flops 200000000 | tf_op jit(solution)/shard_map/pallas_call | solution.py:252
  87.0 23.5 %all_to_all.25 = bf16[256,4,128]{2,1,0:T(4,128)(2,1)S(1)} all-to-all(bf16[256,4,128]{2,1,0:T(4,128)(2,1)S(1)} %bitcast.14), channel_id=1, replica_groups=mesh['lat'=32,'x'=4,'z_hi'=2,'core'=2] {'lat','x','z_hi'}, dimensions={0} | all-to-all | bytes 524288 | tf_op jit(solution)/shard_map/all_to_all | solution.py:322
  110.5 0.0 copy-done
  110.5 1.6 %shard_map.123 = bf16[16,72,128]{2,1,0:T(8,128)(2,1)S(1)} custom-call(bf16[1024,128]{1,0:T(8,128)(2,1)S(1)} %bitcast.12, bf16[1536,736]{1,0:T(8,128)(2,1)S(1)} %copy-done), custom_call_target="tpu_custom_call" | custom-call | flops 300000000 | tf_op jit(solution)/shard_map/pallas_call | solution.py:252
  112.1 19.0 %all_to_all.26.pieces = bf16[16,72,128]{2,1,0:T(8,128)(2,1)S(1)} all-to-all(bf16[16,72,128]{2,1,0:T(8,128)(2,1)S(1)} %shard_map.123), channel_id=1, replica_groups=mesh['lat'=32,'x'=4,'z_hi'=2,'core'=2] {'x','z_hi','core'}, dimensions={0} | all-to-all | bytes 589824 | tf_op jit(solution)/shard_map/all_to_all | solution.py:326
  131.1 1.1 shard_map.124
Async XLA Ops:
  2.0 41.6 %all-to-all-start = ((bf16[32,24,384]{2,1,0:T(8,128)(2,1)}), bf16[32,24,384]{2,1,0:T(8,128)(2,1)S(1)}, u32[]{:S(2)}, u32[]{:S(2)}) async-start(bf16[32,24,384]{2,1,0:T(8,128)(2,1)} %shard_map.118), calls=%async_computation | async-start | bytes 1179648 | tf_op jit(solution)/shard_map/all_to_all | solution.py:284
  21.5 20.5 %collective-permute-start = (bf16[8,72,128]{2,1,0:T(8,128)(2,1)}, bf16[8,72,128]{2,1,0:T(8,128)(2,1)S(1)}, u32[]{:S(2)}, u32[]{:S(2)}) collective-permute-start(bf16[8,72,128]{2,1,0:T(8,128)(2,1)} %get-tuple-element.14), channel_id=1, source_target_pairs={{0,2},{2,0},{1,3},{3,1},{4,6},{6,4},{5,7},{7,5},{8,10},{10,8},{9,1... | collective-permute-start | bytes 442376 | tf_op jit(solution)/shard_map/ppermute | solution.py:300
  43.6 13.1 %all-to-all-start.1 = ((bf16[8,2,72,128]{3,2,1,0:T(8,128)(2,1)}), bf16[8,2,72,128]{3,2,1,0:T(8,128)(2,1)S(1)}, u32[]{:S(2)}, u32[]{:S(2)}) async-start(bf16[8,2,72,128]{3,2,1,0:T(8,128)(2,1)} %pad_maximum_fusion), calls=%async_computation.1 | async-start | bytes 589824 | tf_op jit(solution)/shard_map/all_to_all | solution.py:303
  50.0 34.2 %copy-start.2 = (f32[384,128]{1,0:T(8,128)S(1)}, f32[384,128]{1,0:T(8,128)}, u32[]{:S(2)}) copy-start(f32[384,128]{1,0:T(8,128)} %gain.1) | copy-start | bytes 589828
  51.5 59.0 %copy-start = (bf16[1536,736]{1,0:T(8,128)(2,1)S(1)}, bf16[1536,736]{1,0:T(8,128)(2,1)}, u32[]{:S(2)}) copy-start(bf16[1536,736]{1,0:T(8,128)(2,1)} %constant.28.clone.table) | copy-start | bytes 6782980
  51.5 20.3 %collective-permute-start.1 = (bf16[2,384,384]{2,1,0:T(8,128)(2,1)S(1)}, bf16[2,384,384]{2,1,0:T(8,128)(2,1)}, u32[]{:S(2)}, u32[]{:S(2)}) collective-permute-start(bf16[2,384,384]{2,1,0:T(8,128)(2,1)S(1)} %shard_map.121.tables), channel_id=1, source_target_pairs={{0,1},{1,0},{2,3},{3,2},{4,5},{5,4},{6,7},{7,6},{8,9},{9,8},{10,11... | collective-permute-start | bytes 1769480 | tf_op jit(solution)/shard_map/ppermute | solution.py:309
  56.7 1.6 %copy-start.1 = (bf16[736,1536]{1,0:T(8,128)(2,1)S(1)}, bf16[736,1536]{1,0:T(8,128)(2,1)}, u32[]{:S(2)}) copy-start(bf16[736,1536]{1,0:T(8,128)(2,1)} %constant.27.clone.table) | copy-start | bytes 6782980
  59.8 24.4 %all-to-all-start.2 = ((bf16[256,4,128]{2,1,0:T(4,128)(2,1)}), bf16[256,4,128]{2,1,0:T(4,128)(2,1)S(1)}, u32[]{:S(2)}, u32[]{:S(2)}) async-start(bf16[256,4,128]{2,1,0:T(4,128)(2,1)} %bitcast.8), calls=%async_computation.2 | async-start | bytes 524288 | tf_op jit(solution)/shard_map/all_to_all | solution.py:313

commit v9 on v8

--- a/solution.py
+++ b/solution.py
@@ -136,6 +136,12 @@
             sent[2 * xg + h] = jnp.where(low, blocks[1], blocks[0]).astype(bf16)
 
 
+def join_kernel(kept, sent, out):
+    for k in range(PAIRS):
+        out[k, 0] = kept[k]
+        out[k, 1] = sent[k]
+
+
 def zonal_kernel(z_hi, circles, table, out):
     main, extra = [], []
     for j in range(LON_DEV):
@@ -175,7 +181,15 @@
     out[1] = jnp.where(index((NLAT, NL), 1) >= m, table, 0.0).astype(bf16)
 
 
-def legendre_kernel(place, coeffs, tables, others, gain, out, rows):
+def legendre_kernel(place, coeffs, tables_h, others_h, gain, out, rows, tables, others, sems):
+    copies = [
+        pltpu.make_async_copy(tables_h.at[0], tables.at[0], sems.at[0]),
+        pltpu.make_async_copy(others_h.at[0], others.at[0], sems.at[1]),
+        pltpu.make_async_copy(tables_h.at[1], tables.at[1], sems.at[2]),
+        pltpu.make_async_copy(others_h.at[1], others.at[1], sems.at[3]),
+    ]
+    for copy in copies:
+        copy.start()
     core = place[1]
 
     def swapped(pair):
@@ -199,10 +213,13 @@
         modes.append(jnp.concatenate(stack, axis=0))
     half = jnp.where(core == 0, gain[:, 0:64], gain[:, 64:128])
     gains = jnp.concatenate([half, half], axis=1)
-    results = []
-    for fourier, table in zip(swapped(modes), (tables, others)):
-        filtered = (dot(table[0], fourier.astype(bf16)) * gains).astype(bf16)
-        results.append(dot(table[1], filtered))
+    fourier = [f.astype(bf16) for f in swapped(modes)]
+    for copy in copies[0:2]:
+        copy.wait()
+    filtered = [(dot(t[0], f) * gains).astype(bf16) for t, f in zip((tables, others), fourier)]
+    for copy in copies[2:4]:
+        copy.wait()
+    results = [dot(t[1], f) for t, f in zip((tables, others), filtered)]
     results = swapped(results)
     for k in range(PAIRS):
         xg, cq = k // 2, k % 2
@@ -239,7 +256,7 @@
 
 
 def call(
-    kernel, shape, dtype, scratch=(), smem=0, space=pltpu.VMEM, flops=0, moved=0, limit=VMEM
+    kernel, shape, dtype, scratch=(), smem=0, space=pltpu.VMEM, far=(), flops=0, moved=0, limit=VMEM
 ):
     outs = [jax.ShapeDtypeStruct(s, dtype) for s in (shape if isinstance(shape, list) else [shape])]
     places = [pl.BlockSpec(memory_space=pltpu.VMEM) for _ in outs]
@@ -247,7 +264,8 @@
 
     def run(*args):
         specs = [
-            pl.BlockSpec(memory_space=pltpu.SMEM if k < smem else space) for k in range(len(args))
+            pl.BlockSpec(memory_space=pltpu.SMEM if k < smem else pltpu.HBM if k in far else space)
+            for k in range(len(args))
         ]
         return pl.pallas_call(
             kernel,
@@ -298,9 +316,10 @@
         limit=NETWORK_VMEM,
     )(z_hi, saved, cotangent, *weights)
     sent = lax.ppermute(sent, "z_hi", [(0, 1), (1, 0)])
-    pieces = jnp.stack([kept, sent], axis=1)
+    pieces = call(join_kernel, (PAIRS, 2, Y_MAIN, 128), bf16)(kept, sent)
     bases, pieces = lax.optimization_barrier((bases, pieces))
     pieces = lax.all_to_all(pieces, ("x", "core"), 0, 0, tiled=True)
+    pieces, bases = lax.optimization_barrier((pieces, bases))
     mode = M_DEV * lax.axis_index(LON) + lax.axis_index("lat")
     place = jnp.stack([mode, lax.axis_index("core")]).astype(jnp.int32)
     tables = call(bases_kernel, (2, NL, NLAT), bf16, smem=1, flops=600_000_000, moved=3_000_000)(
@@ -315,8 +334,14 @@
         legendre_kernel,
         (2 * DEVS, 128),
         bf16,
-        (pltpu.VMEM((2 * DEVS, 128), f32),),
+        (
+            pltpu.VMEM((2 * DEVS, 128), f32),
+            pltpu.VMEM((2, NL, NLAT), bf16),
+            pltpu.VMEM((2, NL, NLAT), bf16),
+            pltpu.SemaphoreType.DMA((4,)),
+        ),
         smem=1,
+        far=(2, 3),
         flops=200_000_000,
     )(place, coeffs.reshape(2 * DEVS, 128), tables, others, spectral_gain)
     coeffs = lax.all_to_all(coeffs.reshape(DEVS // 2, 4, 128), ("lat", "x", "z_hi"), 0, 0, tiled=True)

time: 134 us -> 136 us (1.015)
  blocking collectives: 42.5 us -> 66.8 us
  starting transfers between devices: 41.7 us -> 30 us
  waiting for transfers between devices: 28 us -> 20 us
  other arithmetic: 1.73 us -> 0.07 us
    all_to_all x1 -> x2, blocking collectives: 23.5 us -> 47.8 us  [on_device(): lax.all_to_all(coeffs.reshape(DEVS // 2, 4, 128), ('lat', 'x', 'z_hi'), 0...]
    all_to_all x1 -> x0, waiting for transfers between devices: 12.4 us -> none  [on_device(): lax.all_to_all(coeffs.reshape(DEVS // 2, 4, 128), ('lat', 'x', 'z_hi'), 0...]
    all_to_all x1 -> x0, starting transfers between devices: 12 us -> none  [on_device(): lax.all_to_all(coeffs.reshape(DEVS // 2, 4, 128), ('lat', 'x', 'z_hi'), 0...]
    all_to_all x1, waiting for transfers between devices: 3.12 us -> 6.73 us  [on_device(): pieces = lax.all_to_all(pieces, ('x', 'core'), 0, 0, tiled=True)]
    another operation x1 -> x0, other arithmetic: 1.65 us -> none  [on_device(): pieces = jnp.stack([kept, sent], axis=1)]
    pallas_call x7 -> x8, Pallas kernels: 16.5 us -> 16.3 us  [run(): pl.pallas_call(kernel, out_shape=outs[0] if single else outs, in_specs=sp...]
  transfers between devices with their start and end apart: 5 -> 4, of which waited for: 3 -> 2; matrix products, arithmetic and copies ran while one was open for 1% -> 0% of each run, Pallas kernels for 7% -> 6%
where the time goes in v9:
time: 136 us; the launch traced here: 134 us
  blocking collectives  66.8 us (49%)
  starting transfers between devices  30 us (22%)
  waiting for transfers between devices  20 us (15%)
  Pallas kernels  16.3 us (12%)
    all_to_all x2, blocking collectives, on_device(): lax.all_to_all(coeffs.reshape(DEVS // 2, 4, 128), ('lat', 'x', 'z_hi'), 0...  47.8 us
    all_to_all x1, blocking collectives, on_device(): pieces = lax.all_to_all(pieces, LON, 0, 0, tiled=True)  19 us
    pallas_call x8, Pallas kernels, run(): pl.pallas_call(kernel, out_shape=outs[0] if single else outs, in_specs=sp...  16.3 us
    all_to_all x1, starting transfers between devices, on_device(): bases = lax.all_to_all(bases, 'lat', 0, 0, tiled=True)  13.5 us
    ppermute x1, waiting for transfers between devices, on_device(): sent = lax.ppermute(sent, 'z_hi', [(0, 1), (1, 0)])  13.3 us
    ppermute x1, starting transfers between devices, on_device(): sent = lax.ppermute(sent, 'z_hi', [(0, 1), (1, 0)])  8.07 us
    all_to_all x1, waiting for transfers between devices, on_device(): pieces = lax.all_to_all(pieces, ('x', 'core'), 0, 0, tiled=True)  6.73 us
    all_to_all x1, starting transfers between devices, on_device(): pieces = lax.all_to_all(pieces, ('x', 'core'), 0, 0, tiled=True)  5.36 us
  transfers between devices with their start and end apart: 4, of which 2 were waited for; matrix products, arithmetic and copies ran while one was open for 0% of the time, Pallas kernels for 6%

profile of v9, /device:TPU:1, one launch (start us, length us, event | category | flops | bytes accessed | tf_op | source)
XLA Modules:
  0.0 134.3 jit_solution(6658779430318705595)
XLA Ops:
  0.0 2.0 %shard_map.118 = bf16[32,24,384]{2,1,0:T(8,128)(2,1)} custom-call(bf16[12,23,384]{2,1,0:T(8,128)(2,1)} %bitcast.14, bf16[12,23,384]{2,1,0:T(8,128)(2,1)} %second_h.1), custom_call_target="tpu_custom_call" | custom-call | tf_op jit(solution)/shard_map/pallas_call | solution.py:270
  2.0 13.5 %all-to-all-start = ((bf16[32,24,384]{2,1,0:T(8,128)(2,1)}), bf16[32,24,384]{2,1,0:T(8,128)(2,1)S(1)}, u32[]{:S(2)}, u32[]{:S(2)}) async-start(bf16[32,24,384]{2,1,0:T(8,128)(2,1)} %shard_map.118), calls=%async_computation | async-start | bytes 1179648 | tf_op jit(solution)/shard_map/all_to_all | solution.py:302
  15.5 6.0 %shard_map.119 = (bf16[8,72,128]{2,1,0:T(8,128)(2,1)}, bf16[8,72,128]{2,1,0:T(8,128)(2,1)}) custom-call(s32[1]{0:T(128)} %bitcast.2.z_hi, bf16[12,90,128]{2,1,0:T(8,128)(2,1)} %saved_h, bf16[12,90,128]{2,1,0:T(8,128)(2,1)} %cotan_h.1, bf16[128,512]{1,0:T(8,128)(2,1)} %w_in_h.1, f32[1,512]{1,0:T(1,128)} %bitcast.15, bf16[512,512]{1,0:T(8,128)(2,1)} %w_mid_h.1, ...), custom_call_target="tpu_custom_call" | custom-call | flops 1700000000 | bytes 4000000 | tf_op jit(solution)/shard_map/pallas_call | solution.py:270
  21.5 0.0 copy-start.1
  21.5 8.1 %collective-permute-start = (bf16[8,72,128]{2,1,0:T(8,128)(2,1)}, bf16[8,72,128]{2,1,0:T(8,128)(2,1)S(1)}, u32[]{:S(2)}, u32[]{:S(2)}) collective-permute-start(bf16[8,72,128]{2,1,0:T(8,128)(2,1)} %get-tuple-element.16), channel_id=1, source_target_pairs={{0,2},{2,0},{1,3},{3,1},{4,6},{6,4},{5,7},{7,5},{8,10},{10,8},{9,1... | collective-permute-start | bytes 442376 | tf_op jit(solution)/shard_map/ppermute | solution.py:318
  29.6 13.3 %collective-permute-done.sent = bf16[8,72,128]{2,1,0:T(8,128)(2,1)S(1)} collective-permute-done((bf16[8,72,128]{2,1,0:T(8,128)(2,1)}, bf16[8,72,128]{2,1,0:T(8,128)(2,1)S(1)}, u32[]{:S(2)}, u32[]{:S(2)}) %collective-permute-start) | collective-permute-done | bytes 147488 | tf_op jit(solution)/shard_map/ppermute | solution.py:318
  42.9 0.0 copy-start.3
  42.9 0.9 copy-done.3
  43.8 0.7 shard_map.120
  44.5 0.0 all-to-all-done.bases
  44.5 5.4 %all-to-all-start.1 = ((bf16[8,2,72,128]{3,2,1,0:T(8,128)(2,1)}), bf16[8,2,72,128]{3,2,1,0:T(8,128)(2,1)S(1)}, u32[]{:S(2)}, u32[]{:S(2)}) async-start(bf16[8,2,72,128]{3,2,1,0:T(8,128)(2,1)} %shard_map.120), calls=%async_computation.1 | async-start | bytes 589824 | tf_op jit(solution)/shard_map/all_to_all | solution.py:321
  49.9 0.1 pad_add_fusion.place
  50.0 0.0 copy-start.2
  50.0 6.7 %all-to-all-done.1.circles = bf16[8,2,72,128]{3,2,1,0:T(8,128)(2,1)S(1)} async-done(((bf16[8,2,72,128]{3,2,1,0:T(8,128)(2,1)}), bf16[8,2,72,128]{3,2,1,0:T(8,128)(2,1)S(1)}, u32[]{:S(2)}, u32[]{:S(2)}) %all-to-all-start.1) | async-done | bytes 294944 | tf_op jit(solution)/shard_map/all_to_all | solution.py:321
  56.7 1.5 %shard_map.122.tables_h = bf16[2,384,384]{2,1,0:T(8,128)(2,1)S(1)} custom-call(s32[2]{0:T(128)S(1)} %pad_add_fusion.place, bf16[32,24,384]{2,1,0:T(8,128)(2,1)S(1)} %all-to-all-done.bases), custom_call_target="tpu_custom_call" | custom-call | flops 600000000 | bytes 3000000 | tf_op jit(solution)/shard_map/pallas_call | solution.py:270
  58.2 0.0 copy-start
  58.3 3.1 %collective-permute-start.1 = (bf16[2,384,384]{2,1,0:T(8,128)(2,1)S(1)}, bf16[2,384,384]{2,1,0:T(8,128)(2,1)S(1)}, u32[]{:S(2)}, u32[]{:S(2)}) collective-permute-start(bf16[2,384,384]{2,1,0:T(8,128)(2,1)S(1)} %shard_map.122.tables_h), channel_id=1, source_target_pairs={{0,1},{1,0},{2,3},{3,2},{4,5},{5,4},{6,7},{7,6},{8,9},{9,8},{10,11... | collective-permute-start | bytes 1769480 | tf_op jit(solution)/shard_map/ppermute | solution.py:328
  61.4 0.0 copy-done.1
  61.4 0.8 shard_map.121
  62.2 25.8 %all_to_all.25 = bf16[256,4,128]{2,1,0:T(4,128)(2,1)S(1)} all-to-all(bf16[256,4,128]{2,1,0:T(4,128)(2,1)S(1)} %bitcast.10), channel_id=1, replica_groups=mesh['lat'=32,'x'=4,'z_hi'=2,'core'=2] {'lat','x','z_hi'}, dimensions={0} | all-to-all | bytes 524288 | tf_op jit(solution)/shard_map/all_to_all | solution.py:332
  88.0 0.0 collective-permute-done.1.others_h
  88.0 0.0 copy-done.2
  88.0 2.6 %shard_map.123 = bf16[1024,128]{1,0:T(8,128)(2,1)S(1)} custom-call(s32[2]{0:T(128)S(1)} %pad_add_fusion.place, bf16[1024,128]{1,0:T(8,128)(2,1)S(1)} %bitcast.12, bf16[2,384,384]{2,1,0:T(8,128)(2,1)S(1)} %shard_map.122.tables_h, bf16[2,384,384]{2,1,0:T(8,128)(2,1)S(1)} %collective-permute-done.1.others_h, f32[384,128]{1,0:T(8,128)S(1)} %copy-done.2), custom_call_target="tpu_custom_call" | custom-call | flops 200000000 | tf_op jit(solution)/shard_map/pallas_call | solution.py:270
  90.6 22.0 %all_to_all.26 = bf16[256,4,128]{2,1,0:T(4,128)(2,1)S(1)} all-to-all(bf16[256,4,128]{2,1,0:T(4,128)(2,1)S(1)} %bitcast.13), channel_id=1, replica_groups=mesh['lat'=32,'x'=4,'z_hi'=2,'core'=2] {'lat','x','z_hi'}, dimensions={0} | all-to-all | bytes 524288 | tf_op jit(solution)/shard_map/all_to_all | solution.py:347
  112.6 0.0 copy-done
  112.6 1.6 %shard_map.124 = bf16[16,72,128]{2,1,0:T(8,128)(2,1)S(1)} custom-call(bf16[1024,128]{1,0:T(8,128)(2,1)S(1)} %bitcast.11, bf16[1536,736]{1,0:T(8,128)(2,1)S(1)} %copy-done), custom_call_target="tpu_custom_call" | custom-call | flops 300000000 | tf_op jit(solution)/shard_map/pallas_call | solution.py:270
  114.2 19.0 %all_to_all.27.pieces = bf16[16,72,128]{2,1,0:T(8,128)(2,1)S(1)} all-to-all(bf16[16,72,128]{2,1,0:T(8,128)(2,1)S(1)} %shard_map.124), channel_id=1, replica_groups=mesh['lat'=32,'x'=4,'z_hi'=2,'core'=2] {'x','z_hi','core'}, dimensions={0} | all-to-all | bytes 589824 | tf_op jit(solution)/shard_map/all_to_all | solution.py:351
  133.1 1.1 shard_map.125
Async XLA Ops:
  2.0 42.5 %all-to-all-start = ((bf16[32,24,384]{2,1,0:T(8,128)(2,1)}), bf16[32,24,384]{2,1,0:T(8,128)(2,1)S(1)}, u32[]{:S(2)}, u32[]{:S(2)}) async-start(bf16[32,24,384]{2,1,0:T(8,128)(2,1)} %shard_map.118), calls=%async_computation | async-start | bytes 1179648 | tf_op jit(solution)/shard_map/all_to_all | solution.py:302
  21.5 39.9 %copy-start.1 = (bf16[736,1536]{1,0:T(8,128)(2,1)S(1)}, bf16[736,1536]{1,0:T(8,128)(2,1)}, u32[]{:S(2)}) copy-start(bf16[736,1536]{1,0:T(8,128)(2,1)} %constant.27.clone.table) | copy-start | bytes 6782980
  21.5 21.4 %collective-permute-start = (bf16[8,72,128]{2,1,0:T(8,128)(2,1)}, bf16[8,72,128]{2,1,0:T(8,128)(2,1)S(1)}, u32[]{:S(2)}, u32[]{:S(2)}) collective-permute-start(bf16[8,72,128]{2,1,0:T(8,128)(2,1)} %get-tuple-element.16), channel_id=1, source_target_pairs={{0,2},{2,0},{1,3},{3,1},{4,6},{6,4},{5,7},{7,5},{8,10},{10,8},{9,1... | collective-permute-start | bytes 442376 | tf_op jit(solution)/shard_map/ppermute | solution.py:318
  42.9 0.9 copy-start.3
  44.5 12.2 %all-to-all-start.1 = ((bf16[8,2,72,128]{3,2,1,0:T(8,128)(2,1)}), bf16[8,2,72,128]{3,2,1,0:T(8,128)(2,1)S(1)}, u32[]{:S(2)}, u32[]{:S(2)}) async-start(bf16[8,2,72,128]{3,2,1,0:T(8,128)(2,1)} %shard_map.120), calls=%async_computation.1 | async-start | bytes 589824 | tf_op jit(solution)/shard_map/all_to_all | solution.py:321
  50.0 38.0 %copy-start.2 = (f32[384,128]{1,0:T(8,128)S(1)}, f32[384,128]{1,0:T(8,128)}, u32[]{:S(2)}) copy-start(f32[384,128]{1,0:T(8,128)} %gain.1) | copy-start | bytes 589828
  58.2 54.4 %copy-start = (bf16[1536,736]{1,0:T(8,128)(2,1)S(1)}, bf16[1536,736]{1,0:T(8,128)(2,1)}, u32[]{:S(2)}) copy-start(bf16[1536,736]{1,0:T(8,128)(2,1)} %constant.28.clone.table) | copy-start | bytes 6782980
  58.3 29.7 %collective-permute-start.1 = (bf16[2,384,384]{2,1,0:T(8,128)(2,1)S(1)}, bf16[2,384,384]{2,1,0:T(8,128)(2,1)S(1)}, u32[]{:S(2)}, u32[]{:S(2)}) collective-permute-start(bf16[2,384,384]{2,1,0:T(8,128)(2,1)S(1)} %shard_map.122.tables_h), channel_id=1, source_target_pairs={{0,1},{1,0},{2,3},{3,2},{4,5},{5,4},{6,7},{7,6},{8,9},{9,8},{10,11... | collective-permute-start | bytes 1769480 | tf_op jit(solution)/shard_map/ppermute | solution.py:328

commit v10 on v7

--- a/solution.py
+++ b/solution.py
@@ -169,7 +169,15 @@
     out[1] = jnp.where(index((NLAT, NL), 1) >= m, table, 0.0).astype(bf16)
 
 
-def legendre_kernel(place, coeffs, tables, others, gain, out, rows):
+def legendre_kernel(place, coeffs, tables_h, others_h, gain, out, rows, tables, others, sems):
+    copies = [
+        pltpu.make_async_copy(tables_h.at[0], tables.at[0], sems.at[0]),
+        pltpu.make_async_copy(others_h.at[0], others.at[0], sems.at[1]),
+        pltpu.make_async_copy(tables_h.at[1], tables.at[1], sems.at[2]),
+        pltpu.make_async_copy(others_h.at[1], others.at[1], sems.at[3]),
+    ]
+    for copy in copies:
+        copy.start()
     core = place[1]
 
     def swapped(pair):
@@ -193,10 +201,13 @@
         modes.append(jnp.concatenate(stack, axis=0))
     half = jnp.where(core == 0, gain[:, 0:64], gain[:, 64:128])
     gains = jnp.concatenate([half, half], axis=1)
-    results = []
-    for fourier, table in zip(swapped(modes), (tables, others)):
-        filtered = (dot(table[0], fourier.astype(bf16)) * gains).astype(bf16)
-        results.append(dot(table[1], filtered))
+    fourier = [f.astype(bf16) for f in swapped(modes)]
+    for copy in copies[0:2]:
+        copy.wait()
+    filtered = [(dot(t[0], f) * gains).astype(bf16) for t, f in zip((tables, others), fourier)]
+    for copy in copies[2:4]:
+        copy.wait()
+    results = [dot(t[1], f) for t, f in zip((tables, others), filtered)]
     results = swapped(results)
     for k in range(PAIRS):
         xg, cq = k // 2, k % 2
@@ -233,7 +244,7 @@
 
 
 def call(
-    kernel, shape, dtype, scratch=(), smem=0, space=pltpu.VMEM, flops=0, moved=0, limit=VMEM
+    kernel, shape, dtype, scratch=(), smem=0, space=pltpu.VMEM, far=(), flops=0, moved=0, limit=VMEM
 ):
     outs = [jax.ShapeDtypeStruct(s, dtype) for s in (shape if isinstance(shape, list) else [shape])]
     places = [pl.BlockSpec(memory_space=pltpu.VMEM) for _ in outs]
@@ -241,7 +252,8 @@
 
     def run(*args):
         specs = [
-            pl.BlockSpec(memory_space=pltpu.SMEM if k < smem else space) for k in range(len(args))
+            pl.BlockSpec(memory_space=pltpu.SMEM if k < smem else pltpu.HBM if k in far else space)
+            for k in range(len(args))
         ]
         return pl.pallas_call(
             kernel,
@@ -300,14 +312,19 @@
     coeffs = call(zonal_kernel, (2 * DEVS, 128), bf16, flops=300_000_000)(
         pieces, jnp.asarray(forward)
     )
-    others, coeffs = lax.optimization_barrier((others, coeffs))
     coeffs = lax.all_to_all(coeffs.reshape(DEVS // 2, 4, 128), ("lat", "pair"), 0, 0, tiled=True)
     coeffs = call(
         legendre_kernel,
         (2 * DEVS, 128),
         bf16,
-        (pltpu.VMEM((2 * DEVS, 128), f32),),
+        (
+            pltpu.VMEM((2 * DEVS, 128), f32),
+            pltpu.VMEM((2, NL, NLAT), bf16),
+            pltpu.VMEM((2, NL, NLAT), bf16),
+            pltpu.SemaphoreType.DMA((4,)),
+        ),
         smem=1,
+        far=(2, 3),
         flops=200_000_000,
     )(place, coeffs.reshape(2 * DEVS, 128), tables, others, spectral_gain)
     coeffs = lax.all_to_all(coeffs.reshape(DEVS // 2, 4, 128), ("lat", "pair"), 0, 0, tiled=True)

time: 136 us -> 135 us (level)
  blocking collectives: 89 us -> 41.8 us
  starting transfers between devices: 19.4 us -> 41.2 us
  waiting for transfers between devices: 10.1 us -> 31.8 us
  local copies, waits for them, and re-layouts: 0.02 us -> 1.65 us
  Pallas kernels: 15.2 us -> 16.7 us
    all_to_all x0 -> x2, starting transfers between devices: none -> 25.6 us  [the longest x1 13.9 us: on_device(): pieces = lax.all_to_all(pieces, LON, 0, 0, tiled=True)]
    all_to_all x2 -> x1, blocking collectives: 47.9 us -> 22.8 us  [on_device(): lax.all_to_all(coeffs.reshape(DEVS // 2, 4, 128), ('lat', 'pair'), 0, 0,...]
    all_to_all x2 -> x1, blocking collectives: 41.1 us -> 19 us  [on_device(): pieces = lax.all_to_all(pieces, LON, 0, 0, tiled=True)]
    all_to_all x0 -> x2, waiting for transfers between devices: none -> 21.6 us  [the longest x1 13.2 us: on_device(): lax.all_to_all(coeffs.reshape(DEVS // 2, 4, 128), ('lat', 'pair'), 0, 0,...]
    ppermute x1, starting transfers between devices: 5.88 us -> 2.15 us  [on_device(): others = lax.ppermute(tables, 'core', [(0, 1), (1, 0)])]
    unnamed x6, local copies, waits for them, and re-layouts: 0.02 us -> 1.65 us
    pallas_call x7, Pallas kernels: 15.2 us -> 16.7 us  [run(): pl.pallas_call(kernel, out_shape=outs[0] if single else outs, in_specs=sp...]
  transfers between devices with their start and end apart: 2 -> 4, of which waited for: 1 -> 3; matrix products, arithmetic and copies ran while one was open for 0% -> 0% of each run, Pallas kernels for 5% -> 7%
where the time goes in v10:
time: 135 us; the launch traced here: 133 us
  blocking collectives  41.8 us (31%)
  starting transfers between devices  41.2 us (31%)
  waiting for transfers between devices  31.8 us (24%)
  Pallas kernels  16.7 us (12%)
  local copies, waits for them, and re-layouts  1.65 us (1%)
    all_to_all x1, blocking collectives, on_device(): lax.all_to_all(coeffs.reshape(DEVS // 2, 4, 128), ('lat', 'pair'), 0, 0,...  22.8 us
    all_to_all x1, blocking collectives, on_device(): pieces = lax.all_to_all(pieces, LON, 0, 0, tiled=True)  19 us
    pallas_call x7, Pallas kernels, run(): pl.pallas_call(kernel, out_shape=outs[0] if single else outs, in_specs=sp...  16.7 us
    all_to_all x1, starting transfers between devices, on_device(): pieces = lax.all_to_all(pieces, LON, 0, 0, tiled=True)  13.9 us
    all_to_all x1, starting transfers between devices, on_device(): bases = lax.all_to_all(bases, 'lat', 0, 0, tiled=True)  13.5 us
    all_to_all x1, waiting for transfers between devices, on_device(): lax.all_to_all(coeffs.reshape(DEVS // 2, 4, 128), ('lat', 'pair'), 0, 0,...  13.2 us
    all_to_all x1, starting transfers between devices, on_device(): lax.all_to_all(coeffs.reshape(DEVS // 2, 4, 128), ('lat', 'pair'), 0, 0,...  11.7 us
    all_to_all x1, waiting for transfers between devices, on_device(): bases = lax.all_to_all(bases, 'lat', 0, 0, tiled=True)  10.2 us
  transfers between devices with their start and end apart: 4, of which 3 were waited for; matrix products, arithmetic and copies ran while one was open for 0% of the time, Pallas kernels for 7%

profile of v10, /device:TPU:1, one launch (start us, length us, event | category | flops | bytes accessed | tf_op | source)
XLA Modules:
  0.0 133.3 jit_solution(491287631300355788)
XLA Ops:
  0.0 2.0 %shard_map.118 = bf16[32,24,384]{2,1,0:T(8,128)(2,1)} custom-call(bf16[12,23,384]{2,1,0:T(8,128)(2,1)} %bitcast.12, bf16[12,23,384]{2,1,0:T(8,128)(2,1)} %second_h.1), custom_call_target="tpu_custom_call" | custom-call | tf_op jit(solution)/shard_map/pallas_call | solution.py:258
  2.0 13.5 %all-to-all-start = ((bf16[32,24,384]{2,1,0:T(8,128)(2,1)}), bf16[32,24,384]{2,1,0:T(8,128)(2,1)S(1)}, u32[]{:S(2)}, u32[]{:S(2)}) async-start(bf16[32,24,384]{2,1,0:T(8,128)(2,1)} %shard_map.118), calls=%async_computation | async-start | bytes 1179648 | tf_op jit(solution)/shard_map/all_to_all | solution.py:290
  15.5 6.0 %shard_map.119 = bf16[16,72,128]{2,1,0:T(8,128)(2,1)} custom-call(bf16[12,90,128]{2,1,0:T(8,128)(2,1)} %saved_h, bf16[12,90,128]{2,1,0:T(8,128)(2,1)} %cotan_h.1, bf16[128,512]{1,0:T(8,128)(2,1)} %w_in_h.1, f32[1,512]{1,0:T(1,128)} %bitcast.13, bf16[512,512]{1,0:T(8,128)(2,1)} %w_mid_h.1, f32[1,512]{1,0:T(1,128)} %bitcast.14, bf16[512,128]{1,0:T(8,128)(2,1)} %w_out_h.1), custom_call_target="tpu_custom_call" | custom-call | flops 1700000000 | bytes 4000000 | tf_op jit(solution)/shard_map/pallas_call | solution.py:258
  21.5 10.2 %all-to-all-done.bases = bf16[32,24,384]{2,1,0:T(8,128)(2,1)S(1)} async-done(((bf16[32,24,384]{2,1,0:T(8,128)(2,1)}), bf16[32,24,384]{2,1,0:T(8,128)(2,1)S(1)}, u32[]{:S(2)}, u32[]{:S(2)}) %all-to-all-start) | async-done | bytes 589856 | tf_op jit(solution)/shard_map/all_to_all | solution.py:290
  31.7 13.9 %all-to-all-start.1 = ((bf16[16,72,128]{2,1,0:T(8,128)(2,1)}), bf16[16,72,128]{2,1,0:T(8,128)(2,1)S(1)}, u32[]{:S(2)}, u32[]{:S(2)}) async-start(bf16[16,72,128]{2,1,0:T(8,128)(2,1)} %shard_map.119), calls=%async_computation.1 | async-start | bytes 589824 | tf_op jit(solution)/shard_map/all_to_all | solution.py:305
  45.6 0.1 pad_add_fusion.place
  45.7 0.0 copy-start.2
  45.7 1.5 %shard_map.121.tables_h = bf16[2,384,384]{2,1,0:T(8,128)(2,1)S(1)} custom-call(s32[2]{0:T(128)S(1)} %pad_add_fusion.place, bf16[32,24,384]{2,1,0:T(8,128)(2,1)S(1)} %all-to-all-done.bases), custom_call_target="tpu_custom_call" | custom-call | flops 600000000 | bytes 3000000 | tf_op jit(solution)/shard_map/pallas_call | solution.py:258
  47.2 0.0 copy-start
  47.2 2.2 %collective-permute-start = (bf16[2,384,384]{2,1,0:T(8,128)(2,1)S(1)}, bf16[2,384,384]{2,1,0:T(8,128)(2,1)}, u32[]{:S(2)}, u32[]{:S(2)}) collective-permute-start(bf16[2,384,384]{2,1,0:T(8,128)(2,1)S(1)} %shard_map.121.tables_h), channel_id=1, source_target_pairs={{0,1},{1,0},{2,3},{3,2},{4,5},{5,4},{6,7},{7,6},{8,9},{9,8},{10,11... | collective-permute-start | bytes 1769480 | tf_op jit(solution)/shard_map/ppermute | solution.py:311
  49.4 8.4 %all-to-all-done.1.circles = bf16[16,72,128]{2,1,0:T(8,128)(2,1)S(1)} async-done(((bf16[16,72,128]{2,1,0:T(8,128)(2,1)}), bf16[16,72,128]{2,1,0:T(8,128)(2,1)S(1)}, u32[]{:S(2)}, u32[]{:S(2)}) %all-to-all-start.1) | async-done | bytes 294944 | tf_op jit(solution)/shard_map/all_to_all | solution.py:305
  57.8 0.0 copy-start.1
  57.8 1.6 %copy-done.1 = bf16[736,1536]{1,0:T(8,128)(2,1)S(1)} copy-done((bf16[736,1536]{1,0:T(8,128)(2,1)S(1)}, bf16[736,1536]{1,0:T(8,128)(2,1)}, u32[]{:S(2)}) %copy-start.1) | copy-done | bytes 2261016
  59.4 1.5 %shard_map.120 = bf16[1024,128]{1,0:T(8,128)(2,1)} custom-call(bf16[16,72,128]{2,1,0:T(8,128)(2,1)S(1)} %all-to-all-done.1.circles, bf16[736,1536]{1,0:T(8,128)(2,1)S(1)} %copy-done.1), custom_call_target="tpu_custom_call" | custom-call | flops 300000000 | tf_op jit(solution)/shard_map/pallas_call | solution.py:258
  60.9 11.7 %all-to-all-start.2 = ((bf16[256,4,128]{2,1,0:T(4,128)(2,1)}), bf16[256,4,128]{2,1,0:T(4,128)(2,1)S(1)}, u32[]{:S(2)}, u32[]{:S(2)}) async-start(bf16[256,4,128]{2,1,0:T(4,128)(2,1)} %bitcast.5), calls=%async_computation.2 | async-start | bytes 524288 | tf_op jit(solution)/shard_map/all_to_all | solution.py:315
  72.6 0.0 collective-permute-done.others_h
  72.6 13.2 %all-to-all-done.2 = bf16[256,4,128]{2,1,0:T(4,128)(2,1)S(1)} async-done(((bf16[256,4,128]{2,1,0:T(4,128)(2,1)}), bf16[256,4,128]{2,1,0:T(4,128)(2,1)S(1)}, u32[]{:S(2)}, u32[]{:S(2)}) %all-to-all-start.2) | async-done | bytes 262176 | tf_op jit(solution)/shard_map/all_to_all | solution.py:315
  85.8 0.0 copy-done.2
  85.8 3.1 %shard_map.122 = bf16[1024,128]{1,0:T(8,128)(2,1)S(1)} custom-call(s32[2]{0:T(128)S(1)} %pad_add_fusion.place, bf16[1024,128]{1,0:T(8,128)(2,1)S(1)} %bitcast.10, bf16[2,384,384]{2,1,0:T(8,128)(2,1)S(1)} %shard_map.121.tables_h, bf16[2,384,384]{2,1,0:T(8,128)(2,1)} %collective-permute-done.others_h, f32[384,128]{1,0:T(8,128)S(1)} %copy-done.2), custom_call_target="tpu_custom_call" | custom-call | flops 200000000 | tf_op jit(solution)/shard_map/pallas_call | solution.py:258
  88.9 22.8 %all_to_all.25 = bf16[256,4,128]{2,1,0:T(4,128)(2,1)S(1)} all-to-all(bf16[256,4,128]{2,1,0:T(4,128)(2,1)S(1)} %bitcast.11), channel_id=1, replica_groups=mesh['lat'=32,'pair'=8,'core'=2] {'lat','pair'}, dimensions={0} | all-to-all | bytes 524288 | tf_op jit(solution)/shard_map/all_to_all | solution.py:330
  111.7 0.0 copy-done
  111.7 1.6 %shard_map.123 = bf16[16,72,128]{2,1,0:T(8,128)(2,1)S(1)} custom-call(bf16[1024,128]{1,0:T(8,128)(2,1)S(1)} %bitcast.9, bf16[1536,736]{1,0:T(8,128)(2,1)S(1)} %copy-done), custom_call_target="tpu_custom_call" | custom-call | flops 300000000 | tf_op jit(solution)/shard_map/pallas_call | solution.py:258
  113.2 19.0 %all_to_all.26.pieces = bf16[16,72,128]{2,1,0:T(8,128)(2,1)S(1)} all-to-all(bf16[16,72,128]{2,1,0:T(8,128)(2,1)S(1)} %shard_map.123), channel_id=1, replica_groups=mesh['lat'=32,'pair'=8,'core'=2] {'pair','core'}, dimensions={0} | all-to-all | bytes 589824 | tf_op jit(solution)/shard_map/all_to_all | solution.py:334
  132.2 1.1 shard_map.124
Async XLA Ops:
  2.0 29.7 %all-to-all-start = ((bf16[32,24,384]{2,1,0:T(8,128)(2,1)}), bf16[32,24,384]{2,1,0:T(8,128)(2,1)S(1)}, u32[]{:S(2)}, u32[]{:S(2)}) async-start(bf16[32,24,384]{2,1,0:T(8,128)(2,1)} %shard_map.118), calls=%async_computation | async-start | bytes 1179648 | tf_op jit(solution)/shard_map/all_to_all | solution.py:290
  31.7 26.1 %all-to-all-start.1 = ((bf16[16,72,128]{2,1,0:T(8,128)(2,1)}), bf16[16,72,128]{2,1,0:T(8,128)(2,1)S(1)}, u32[]{:S(2)}, u32[]{:S(2)}) async-start(bf16[16,72,128]{2,1,0:T(8,128)(2,1)} %shard_map.119), calls=%async_computation.1 | async-start | bytes 589824 | tf_op jit(solution)/shard_map/all_to_all | solution.py:305
  45.7 40.1 %copy-start.2 = (f32[384,128]{1,0:T(8,128)S(1)}, f32[384,128]{1,0:T(8,128)}, u32[]{:S(2)}) copy-start(f32[384,128]{1,0:T(8,128)} %gain.1) | copy-start | bytes 589828
  47.2 64.5 %copy-start = (bf16[1536,736]{1,0:T(8,128)(2,1)S(1)}, bf16[1536,736]{1,0:T(8,128)(2,1)}, u32[]{:S(2)}) copy-start(bf16[1536,736]{1,0:T(8,128)(2,1)} %constant.23.clone.table) | copy-start | bytes 6782980
  47.2 25.4 %collective-permute-start = (bf16[2,384,384]{2,1,0:T(8,128)(2,1)S(1)}, bf16[2,384,384]{2,1,0:T(8,128)(2,1)}, u32[]{:S(2)}, u32[]{:S(2)}) collective-permute-start(bf16[2,384,384]{2,1,0:T(8,128)(2,1)S(1)} %shard_map.121.tables_h), channel_id=1, source_target_pairs={{0,1},{1,0},{2,3},{3,2},{4,5},{5,4},{6,7},{7,6},{8,9},{9,8},{10,11... | collective-permute-start | bytes 1769480 | tf_op jit(solution)/shard_map/ppermute | solution.py:311
  57.8 1.6 %copy-start.1 = (bf16[736,1536]{1,0:T(8,128)(2,1)S(1)}, bf16[736,1536]{1,0:T(8,128)(2,1)}, u32[]{:S(2)}) copy-start(bf16[736,1536]{1,0:T(8,128)(2,1)} %constant.22.clone.table) | copy-start | bytes 6782980
  60.9 24.9 %all-to-all-start.2 = ((bf16[256,4,128]{2,1,0:T(4,128)(2,1)}), bf16[256,4,128]{2,1,0:T(4,128)(2,1)S(1)}, u32[]{:S(2)}, u32[]{:S(2)}) async-start(bf16[256,4,128]{2,1,0:T(4,128)(2,1)} %bitcast.5), calls=%async_computation.2 | async-start | bytes 524288 | tf_op jit(solution)/shard_map/all_to_all | solution.py:315

commit v11 on v10

--- a/solution.py
+++ b/solution.py
@@ -10,7 +10,7 @@
 f32 = jnp.float32
 
 LAT_DEV, LON_DEV = 32, 16
-PAIRS = LON_DEV // 2
+QUADS = 4
 X_DEV, Y_DEV = 12, 90
 Y_PAD = 96
 Y_MAIN, Y_EXT = 72, 24
@@ -21,13 +21,16 @@
 XG = X_DEV // X_SUB
 DEVS = LAT_DEV * LON_DEV
 ROWS = 2 * NM
-LON = ("pair", "core")
+LON = ("x_hi", "x_lo", "z_hi", "core")
+LONG = ("x_lo", "z_hi", "lat")
+KEPT = 192
 VMEM = 16 * 1024 * 1024
 NETWORK_VMEM = 59 * 1024 * 1024
 
 
 def zonal_tables():
-    order = (M_DEV * np.arange(LON_DEV)[None, :] + np.arange(M_DEV)[:, None]).reshape(-1)
+    q, i, e = np.meshgrid(np.arange(4), np.arange(M_DEV), np.arange(4), indexing="ij")
+    order = (M_DEV * (8 * (e // 2) + 2 * q + e % 2) + i).reshape(-1)
     turns = (order[:, None] * np.arange(NLON)[None, :]) % NLON
     angles = turns.astype(np.float64) * (2.0 * np.pi / NLON)
     table = np.stack([np.cos(angles), -np.sin(angles)], 1).reshape(ROWS, NLON)
@@ -35,9 +38,11 @@
     back = table * np.repeat(weight, 2)[:, None]
 
     def split_y(t):
-        t = np.pad(t.reshape(ROWS, LON_DEV, Y_DEV), ((0, 0), (0, 0), (0, Y_PAD - Y_DEV)))
-        main = t[:, :, :Y_MAIN].reshape(ROWS, LON_DEV * Y_MAIN)
-        extra = t[:, :, Y_MAIN:].reshape(ROWS, LON_DEV * Y_EXT)
+        t = np.pad(t.reshape(QUADS, ROWS // QUADS, NLON), ((0, 0), (0, KEPT - ROWS // QUADS), (0, 0)))
+        t = t.reshape(QUADS * KEPT, LON_DEV, Y_DEV)
+        t = np.pad(t, ((0, 0), (0, 0), (0, Y_PAD - Y_DEV)))
+        main = t[:, :, :Y_MAIN].reshape(QUADS * KEPT, LON_DEV * Y_MAIN)
+        extra = t[:, :, Y_MAIN:].reshape(QUADS * KEPT, LON_DEV * Y_EXT)
         return np.concatenate([main, extra], 1)
 
     return (
@@ -47,7 +52,7 @@
 
 
 def owner(xg, cg):
-    return CG * xg + 2 * (cg % 2) + cg // 2
+    return 8 * (cg % 2) + 2 * xg + cg // 2
 
 
 def dot(a, b):
@@ -139,8 +144,10 @@
         parts = [piece[Y_EXT * xx : Y_EXT * (xx + 1), 96:128] for xx in range(X_SUB)]
         extra.append(jnp.concatenate(parts + [jnp.zeros((Y_EXT, C_SUB), f32)], axis=1))
     g = jnp.concatenate(main + extra, axis=0).astype(bf16)
-    out[0:ROWS, :] = dot(table[...], g).astype(bf16)
-    out[ROWS:, :] = jnp.zeros((2 * DEVS - ROWS, 128), bf16)
+    spectrum = dot(table[...], g).astype(bf16)
+    for q in range(QUADS):
+        out[256 * q : 256 * q + KEPT, :] = spectrum[KEPT * q : KEPT * (q + 1)]
+        out[256 * q + KEPT : 256 * (q + 1), :] = jnp.zeros((256 - KEPT, 128), bf16)
 
 
 def bases_kernel(place, bases, out):
@@ -169,62 +176,51 @@
     out[1] = jnp.where(index((NLAT, NL), 1) >= m, table, 0.0).astype(bf16)
 
 
-def legendre_kernel(place, coeffs, tables_h, others_h, gain, out, rows, tables, others, sems):
+def legendre_kernel(place, coeffs, own, core_s, far_s, both_s, gain, out, rows, tables, sems):
+    mine = place[1]
     copies = [
-        pltpu.make_async_copy(tables_h.at[0], tables.at[0], sems.at[0]),
-        pltpu.make_async_copy(others_h.at[0], others.at[0], sems.at[1]),
-        pltpu.make_async_copy(tables_h.at[1], tables.at[1], sems.at[2]),
-        pltpu.make_async_copy(others_h.at[1], others.at[1], sems.at[3]),
+        pltpu.make_async_copy(source, tables.at[mine ^ d], sems.at[d])
+        for d, source in enumerate((own, core_s, far_s, both_s))
     ]
     for copy in copies:
         copy.start()
-    core = place[1]
-
-    def swapped(pair):
-        return jnp.where(core == 0, pair[0], pair[1]), jnp.where(core == 0, pair[1], pair[0])
-
     rows[...] = coeffs[...].astype(f32)
-    blocks = [
-        [rows[pl.ds(4 * k + n, LAT_DEV, stride=32), :] for n in range(4)] for k in range(PAIRS)
-    ]
-    modes = []
-    for h in range(2):
+    fourier = []
+    for e in range(4):
+        blocks = [
+            [rows[pl.ds(256 * xg + 2 * e + r, LAT_DEV, stride=8), :] for r in range(2)]
+            for xg in range(XG)
+        ]
         stack = []
         for xx in range(X_SUB):
             for xg in range(XG):
+                parts = [blocks[xg][r][:, C_SUB * xx : C_SUB * (xx + 1)] for r in range(2)]
+                stack.append(jnp.concatenate(parts, axis=1))
+        fourier.append(jnp.concatenate(stack, axis=0).astype(bf16))
+    quarter = [gain[:, C_SUB * cg : C_SUB * (cg + 1)] for cg in range(CG)]
+    low = jnp.where(mine // 2 == 0, quarter[0], quarter[1])
+    high = jnp.where(mine // 2 == 0, quarter[2], quarter[3])
+    quarter = jnp.where(mine % 2 == 0, low, high)
+    gains = jnp.concatenate([quarter, quarter], axis=1)
+    for copy in copies:
+        copy.wait()
+    filtered = [(dot(tables[e, 0], fourier[e]) * gains).astype(bf16) for e in range(4)]
+    results = [dot(tables[e, 1], filtered[e]) for e in range(4)]
+    for xg in range(XG):
+        for e in range(4):
+            for r in range(2):
                 parts = [
-                    blocks[2 * xg + cq][2 * h + r][:, C_SUB * xx : C_SUB * (xx + 1)]
-                    for r in range(2)
-                    for cq in range(2)
-                ]
-                stack.append(jnp.concatenate(parts, axis=1))
-        modes.append(jnp.concatenate(stack, axis=0))
-    half = jnp.where(core == 0, gain[:, 0:64], gain[:, 64:128])
-    gains = jnp.concatenate([half, half], axis=1)
-    fourier = [f.astype(bf16) for f in swapped(modes)]
-    for copy in copies[0:2]:
-        copy.wait()
-    filtered = [(dot(t[0], f) * gains).astype(bf16) for t, f in zip((tables, others), fourier)]
-    for copy in copies[2:4]:
-        copy.wait()
-    results = [dot(t[1], f) for t, f in zip((tables, others), filtered)]
-    results = swapped(results)
-    for k in range(PAIRS):
-        xg, cq = k // 2, k % 2
-        for h in range(2):
-            for r in range(2):
-                first = 64 * r + C_SUB * cq
-                parts = [
-                    results[h][32 * (XG * xx + xg) : 32 * (XG * xx + xg + 1), first : first + C_SUB]
+                    results[e][32 * (XG * xx + xg) : 32 * (XG * xx + xg + 1), C_SUB * r : C_SUB * (r + 1)]
                     for xx in range(X_SUB)
                 ]
                 parts.append(jnp.zeros((LAT_DEV, C_SUB), f32))
-                rows[pl.ds(4 * k + 2 * h + r, LAT_DEV, stride=32), :] = jnp.concatenate(parts, axis=1)
+                rows[pl.ds(256 * xg + 2 * e + r, LAT_DEV, stride=8), :] = jnp.concatenate(parts, axis=1)
     out[...] = rows[...].astype(bf16)
 
 
 def inverse_kernel(coeffs, table, out):
-    g = dot(table[...], coeffs[0:ROWS, :])
+    z = jnp.concatenate([coeffs[256 * q : 256 * q + KEPT, :] for q in range(QUADS)], axis=0)
+    g = dot(table[...], z)
     for j in range(LON_DEV):
         main = g[Y_MAIN * j : Y_MAIN * (j + 1), 0:96]
         first = LON_DEV * Y_MAIN + Y_EXT * j
@@ -304,32 +300,39 @@
     bases, pieces = lax.optimization_barrier((bases, pieces))
     pieces = lax.all_to_all(pieces, LON, 0, 0, tiled=True)
     mode = M_DEV * lax.axis_index(LON) + lax.axis_index("lat")
-    place = jnp.stack([mode, lax.axis_index("core")]).astype(jnp.int32)
+    mine = 2 * lax.axis_index("x_hi") + lax.axis_index("core")
+    place = jnp.stack([mode, mine]).astype(jnp.int32)
     tables = call(bases_kernel, (2, NL, NLAT), bf16, smem=1, flops=600_000_000, moved=3_000_000)(
         place, bases
     )
-    others = lax.ppermute(tables, "core", [(0, 1), (1, 0)])
+    swap = [(0, 1), (1, 0)]
+    shared = (
+        tables,
+        lax.ppermute(tables, "core", swap),
+        lax.ppermute(tables, "x_hi", swap),
+        lax.ppermute(tables, ("x_hi", "core"), [(0, 3), (1, 2), (2, 1), (3, 0)]),
+    )
     coeffs = call(zonal_kernel, (2 * DEVS, 128), bf16, flops=300_000_000)(
         pieces, jnp.asarray(forward)
     )
-    coeffs = lax.all_to_all(coeffs.reshape(DEVS // 2, 4, 128), ("lat", "pair"), 0, 0, tiled=True)
+    coeffs = lax.all_to_all(coeffs.reshape(DEVS // 4, 8, 128), LONG, 0, 0, tiled=True)
     coeffs = call(
         legendre_kernel,
         (2 * DEVS, 128),
         bf16,
         (
             pltpu.VMEM((2 * DEVS, 128), f32),
-            pltpu.VMEM((2, NL, NLAT), bf16),
-            pltpu.VMEM((2, NL, NLAT), bf16),
+            pltpu.VMEM((4, 2, NL, NLAT), bf16),
             pltpu.SemaphoreType.DMA((4,)),
         ),
         smem=1,
-        far=(2, 3),
+        far=(2, 3, 4, 5),
         flops=200_000_000,
-    )(place, coeffs.reshape(2 * DEVS, 128), tables, others, spectral_gain)
-    coeffs = lax.all_to_all(coeffs.reshape(DEVS // 2, 4, 128), ("lat", "pair"), 0, 0, tiled=True)
+    )(place, coeffs.reshape(2 * DEVS, 128), *shared, spectral_gain)
+    coeffs, back = lax.optimization_barrier((coeffs, jnp.asarray(back)))
+    coeffs = lax.all_to_all(coeffs.reshape(DEVS // 4, 8, 128), LONG, 0, 0, tiled=True)
     pieces = call(inverse_kernel, (LON_DEV, Y_MAIN, 128), bf16, flops=300_000_000)(
-        coeffs.reshape(2 * DEVS, 128), jnp.asarray(back)
+        coeffs.reshape(2 * DEVS, 128), back
     )
     pieces = lax.all_to_all(pieces, LON, 0, 0, tiled=True)
     return call(grid_kernel, (X_DEV, Y_DEV, CHAN), f32)(pieces)
@@ -338,5 +341,5 @@
 def solution(mesh):
     grid = P("lat", LON, None)
     placed = (grid, grid, P(), P(), P(), P(), P(), P(), P(None, LON, "lat"), grid)
-    fine = Mesh(mesh.devices.reshape(LAT_DEV, PAIRS, 2), ("lat",) + LON)
+    fine = Mesh(mesh.devices.reshape(LAT_DEV, 2, 2, 2, 2), ("lat",) + LON)
     return jax.shard_map(on_device, mesh=fine, in_specs=placed, out_specs=grid, check_vma=False)

time: 135 us -> 134 us (level)
  starting transfers between devices: 41.2 us -> 47.9 us
  waiting for transfers between devices: 31.8 us -> 25.2 us
  blocking collectives: 41.8 us -> 40 us
    ppermute x1 -> x3, waiting for transfers between devices: 0.01 us -> 12.9 us  [the longest x1 12.9 us: on_device(): lax.ppermute(tables, 'x_hi', swap)]
    all_to_all x1, waiting for transfers between devices: 13.2 us -> 1.97 us  [on_device(): lax.all_to_all(coeffs.reshape(DEVS // 4, 8, 128), LONG, 0, 0, tiled=True)]
    all_to_all x1, waiting for transfers between devices: 8.43 us -> 0.13 us  [on_device(): pieces = lax.all_to_all(pieces, LON, 0, 0, tiled=True)]
    ppermute x1 -> x3, starting transfers between devices: 2.15 us -> 9.41 us  [the longest x1 5.05 us: on_device(): lax.ppermute(tables, ('x_hi', 'core'), [(0, 3), (1, 2), (2, 1), (3, 0)])]
  transfers between devices with their start and end apart: 4 -> 6, of which waited for: 3 -> 4; matrix products, arithmetic and copies ran while one was open for 0% -> 0% of each run, Pallas kernels for 7% -> 7%
where the time goes in v11:
time: 134 us; the launch traced here: 132 us
  starting transfers between devices  47.9 us (36%)
  blocking collectives  40 us (30%)
  waiting for transfers between devices  25.2 us (19%)
  Pallas kernels  16.7 us (12%)
  local copies, waits for them, and re-layouts  1.89 us (1%)
    all_to_all x1, blocking collectives, on_device(): lax.all_to_all(coeffs.reshape(DEVS // 4, 8, 128), LONG, 0, 0, tiled=True)  22.2 us
    all_to_all x1, blocking collectives, on_device(): pieces = lax.all_to_all(pieces, LON, 0, 0, tiled=True)  17.8 us
    pallas_call x7, Pallas kernels, run(): pl.pallas_call(kernel, out_shape=outs[0] if single else outs, in_specs=sp...  16.7 us
    all_to_all x1, starting transfers between devices, on_device(): pieces = lax.all_to_all(pieces, LON, 0, 0, tiled=True)  13.9 us
    all_to_all x1, starting transfers between devices, on_device(): bases = lax.all_to_all(bases, 'lat', 0, 0, tiled=True)  13.5 us
    ppermute x1, waiting for transfers between devices, on_device(): lax.ppermute(tables, 'x_hi', swap)  12.9 us
    all_to_all x1, starting transfers between devices, on_device(): lax.all_to_all(coeffs.reshape(DEVS // 4, 8, 128), LONG, 0, 0, tiled=True)  11.1 us
    all_to_all x1, waiting for transfers between devices, on_device(): bases = lax.all_to_all(bases, 'lat', 0, 0, tiled=True)  10.2 us
  transfers between devices with their start and end apart: 6, of which 4 were waited for; matrix products, arithmetic and copies ran while one was open for 0% of the time, Pallas kernels for 7%

profile of v11, /device:TPU:1, one launch (start us, length us, event | category | flops | bytes accessed | tf_op | source)
XLA Modules:
  0.0 132.0 jit_solution(12686673505701313775)
XLA Ops:
  0.0 2.0 %shard_map.118 = bf16[32,24,384]{2,1,0:T(8,128)(2,1)} custom-call(bf16[12,23,384]{2,1,0:T(8,128)(2,1)} %bitcast.12, bf16[12,23,384]{2,1,0:T(8,128)(2,1)} %second_h.1), custom_call_target="tpu_custom_call" | custom-call | tf_op jit(solution)/shard_map/pallas_call | solution.py:254
  2.0 13.5 %all-to-all-start = ((bf16[32,24,384]{2,1,0:T(8,128)(2,1)}), bf16[32,24,384]{2,1,0:T(8,128)(2,1)S(1)}, u32[]{:S(2)}, u32[]{:S(2)}) async-start(bf16[32,24,384]{2,1,0:T(8,128)(2,1)} %shard_map.118), calls=%async_computation | async-start | bytes 1179648 | tf_op jit(solution)/shard_map/all_to_all | solution.py:286
  15.5 6.0 %shard_map.119 = bf16[16,72,128]{2,1,0:T(8,128)(2,1)} custom-call(bf16[12,90,128]{2,1,0:T(8,128)(2,1)} %saved_h, bf16[12,90,128]{2,1,0:T(8,128)(2,1)} %cotan_h.1, bf16[128,512]{1,0:T(8,128)(2,1)} %w_in_h.1, f32[1,512]{1,0:T(1,128)} %bitcast.13, bf16[512,512]{1,0:T(8,128)(2,1)} %w_mid_h.1, f32[1,512]{1,0:T(1,128)} %bitcast.14, bf16[512,128]{1,0:T(8,128)(2,1)} %w_out_h.1), custom_call_target="tpu_custom_call" | custom-call | flops 1700000000 | bytes 4000000 | tf_op jit(solution)/shard_map/pallas_call | solution.py:254
  21.5 0.0 copy-start.1
  21.5 10.2 %all-to-all-done.bases = bf16[32,24,384]{2,1,0:T(8,128)(2,1)S(1)} async-done(((bf16[32,24,384]{2,1,0:T(8,128)(2,1)}), bf16[32,24,384]{2,1,0:T(8,128)(2,1)S(1)}, u32[]{:S(2)}, u32[]{:S(2)}) %all-to-all-start) | async-done | bytes 589856 | tf_op jit(solution)/shard_map/all_to_all | solution.py:286
  31.7 0.0 copy-start.2
  31.7 0.8 copy-done.2
  32.5 13.9 %all-to-all-start.1 = ((bf16[16,72,128]{2,1,0:T(8,128)(2,1)}), bf16[16,72,128]{2,1,0:T(8,128)(2,1)S(1)}, u32[]{:S(2)}, u32[]{:S(2)}) async-start(bf16[16,72,128]{2,1,0:T(8,128)(2,1)} %shard_map.119), calls=%async_computation.1 | async-start | bytes 589824 | tf_op jit(solution)/shard_map/all_to_all | solution.py:301
  46.4 0.1 pad_add_fusion.place
  46.5 0.0 copy-start.3
  46.5 1.1 copy-done.3
  47.5 0.0 copy-start.4
  47.5 1.5 %shard_map.121.own = bf16[2,384,384]{2,1,0:T(8,128)(2,1)S(1)} custom-call(s32[2]{0:T(128)S(1)} %pad_add_fusion.place, bf16[32,24,384]{2,1,0:T(8,128)(2,1)S(1)} %copy-done.3), custom_call_target="tpu_custom_call" | custom-call | flops 600000000 | bytes 3000000 | tf_op jit(solution)/shard_map/pallas_call | solution.py:254
  49.1 5.0 %collective-permute-start.2 = (bf16[2,384,384]{2,1,0:T(8,128)(2,1)S(1)}, bf16[2,384,384]{2,1,0:T(8,128)(2,1)}, u32[]{:S(2)}, u32[]{:S(2)}) collective-permute-start(bf16[2,384,384]{2,1,0:T(8,128)(2,1)S(1)} %shard_map.121.own), channel_id=1, source_target_pairs={{0,9},{1,8},{8,1},{9,0},{2,11},{3,10},{10,3},{11,2},{4,13},{5,12},... | collective-permute-start | bytes 1769480 | tf_op jit(solution)/shard_map/ppermute | solution.py:313
  54.1 1.9 %collective-permute-start.1 = (bf16[2,384,384]{2,1,0:T(8,128)(2,1)S(1)}, bf16[2,384,384]{2,1,0:T(8,128)(2,1)}, u32[]{:S(2)}, u32[]{:S(2)}) collective-permute-start(bf16[2,384,384]{2,1,0:T(8,128)(2,1)S(1)} %shard_map.121.own), channel_id=1, source_target_pairs={{0,8},{8,0},{1,9},{9,1},{2,10},{10,2},{3,11},{11,3},{4,12},{12,4},... | collective-permute-start | bytes 1769480 | tf_op jit(solution)/shard_map/ppermute | solution.py:312
  56.1 2.4 %collective-permute-start = (bf16[2,384,384]{2,1,0:T(8,128)(2,1)S(1)}, bf16[2,384,384]{2,1,0:T(8,128)(2,1)}, u32[]{:S(2)}, u32[]{:S(2)}) collective-permute-start(bf16[2,384,384]{2,1,0:T(8,128)(2,1)S(1)} %shard_map.121.own), channel_id=1, source_target_pairs={{0,1},{1,0},{2,3},{3,2},{4,5},{5,4},{6,7},{7,6},{8,9},{9,8},{10,11... | collective-permute-start | bytes 1769480 | tf_op jit(solution)/shard_map/ppermute | solution.py:311
  58.5 0.1 all-to-all-done.1.circles
  58.6 0.0 copy-done.1
  58.7 1.5 %shard_map.120 = bf16[1024,128]{1,0:T(8,128)(2,1)} custom-call(bf16[16,72,128]{2,1,0:T(8,128)(2,1)S(1)} %all-to-all-done.1.circles, bf16[768,1536]{1,0:T(8,128)(2,1)S(1)} %copy-done.1), custom_call_target="tpu_custom_call" | custom-call | flops 300000000 | tf_op jit(solution)/shard_map/pallas_call | solution.py:254
  60.1 0.0 copy-start
  60.1 11.1 %all-to-all-start.2 = ((bf16[128,8,128]{2,1,0:T(8,128)(2,1)}), bf16[128,8,128]{2,1,0:T(8,128)(2,1)S(1)}, u32[]{:S(2)}, u32[]{:S(2)}) async-start(bf16[128,8,128]{2,1,0:T(8,128)(2,1)} %bitcast.5), calls=%async_computation.2 | async-start | bytes 524288 | tf_op jit(solution)/shard_map/all_to_all | solution.py:318
  71.3 0.0 collective-permute-done.2.both_s
  71.3 12.9 %collective-permute-done.1.far_s = bf16[2,384,384]{2,1,0:T(8,128)(2,1)} collective-permute-done((bf16[2,384,384]{2,1,0:T(8,128)(2,1)S(1)}, bf16[2,384,384]{2,1,0:T(8,128)(2,1)}, u32[]{:S(2)}, u32[]{:S(2)}) %collective-permute-start.1) | collective-permute-done | bytes 589856 | tf_op jit(solution)/shard_map/ppermute | solution.py:312
  84.2 0.0 collective-permute-done.core_s
  84.2 2.0 %all-to-all-done.2 = bf16[128,8,128]{2,1,0:T(8,128)(2,1)S(1)} async-done(((bf16[128,8,128]{2,1,0:T(8,128)(2,1)}), bf16[128,8,128]{2,1,0:T(8,128)(2,1)S(1)}, u32[]{:S(2)}, u32[]{:S(2)}) %all-to-all-start.2) | async-done | bytes 262176 | tf_op jit(solution)/shard_map/all_to_all | solution.py:318
  86.2 0.0 copy-done.4
  86.2 3.0 %shard_map.122 = bf16[1024,128]{1,0:T(8,128)(2,1)S(1)} custom-call(s32[2]{0:T(128)S(1)} %pad_add_fusion.place, bf16[1024,128]{1,0:T(8,128)(2,1)S(1)} %bitcast.9, bf16[2,384,384]{2,1,0:T(8,128)(2,1)S(1)} %shard_map.121.own, bf16[2,384,384]{2,1,0:T(8,128)(2,1)} %collective-permute-done.core_s, bf16[2,384,384]{2,1,0:T(8,128)(2,1)} %collective-permute-done.1.far_s, ...), custom_call_target="tpu_custom_call" | custom-call | flops 200000000 | tf_op jit(solution)/shard_map/pallas_call | solution.py:254
  89.3 22.2 %all_to_all.25 = bf16[128,8,128]{2,1,0:T(8,128)(2,1)S(1)} all-to-all(bf16[128,8,128]{2,1,0:T(8,128)(2,1)S(1)} %bitcast.10), channel_id=1, replica_groups=mesh['lat'=32,'x_hi'=2,'x_lo'=2,'z_hi'=2,'core'=2] {'x_lo','z_hi','lat'}, dimensions={0} | all-to-all | bytes 524288 | tf_op jit(solution)/shard_map/all_to_all | solution.py:333
  111.5 0.0 copy-done
  111.5 1.6 %shard_map.123 = bf16[16,72,128]{2,1,0:T(8,128)(2,1)S(1)} custom-call(bf16[1024,128]{1,0:T(8,128)(2,1)S(1)} %bitcast.11, bf16[1536,768]{1,0:T(8,128)(2,1)S(1)} %copy-done), custom_call_target="tpu_custom_call" | custom-call | flops 300000000 | tf_op jit(solution)/shard_map/pallas_call | solution.py:254
  113.0 17.8 %all_to_all.26.pieces = bf16[16,72,128]{2,1,0:T(8,128)(2,1)S(1)} all-to-all(bf16[16,72,128]{2,1,0:T(8,128)(2,1)S(1)} %shard_map.123), channel_id=1, replica_groups=mesh['lat'=32,'x_hi'=2,'x_lo'=2,'z_hi'=2,'core'=2] {'x_hi','x_lo','z_hi'..., dimensions={0} | all-to-all | bytes 589824 | tf_op jit(solution)/shard_map/all_to_all | solution.py:337
  130.9 1.1 shard_map.124
Async XLA Ops:
  2.0 29.7 %all-to-all-start = ((bf16[32,24,384]{2,1,0:T(8,128)(2,1)}), bf16[32,24,384]{2,1,0:T(8,128)(2,1)S(1)}, u32[]{:S(2)}, u32[]{:S(2)}) async-start(bf16[32,24,384]{2,1,0:T(8,128)(2,1)} %shard_map.118), calls=%async_computation | async-start | bytes 1179648 | tf_op jit(solution)/shard_map/all_to_all | solution.py:286
  21.5 37.2 %copy-start.1 = (bf16[768,1536]{1,0:T(8,128)(2,1)S(1)}, bf16[768,1536]{1,0:T(8,128)(2,1)}, u32[]{:S(2)}) copy-start(bf16[768,1536]{1,0:T(8,128)(2,1)} %constant.32.clone.table) | copy-start | bytes 7077892
  31.7 0.8 copy-start.2
  32.5 26.1 %all-to-all-start.1 = ((bf16[16,72,128]{2,1,0:T(8,128)(2,1)}), bf16[16,72,128]{2,1,0:T(8,128)(2,1)S(1)}, u32[]{:S(2)}, u32[]{:S(2)}) async-start(bf16[16,72,128]{2,1,0:T(8,128)(2,1)} %shard_map.119), calls=%async_computation.1 | async-start | bytes 589824 | tf_op jit(solution)/shard_map/all_to_all | solution.py:301
  46.5 1.1 copy-start.3
  47.5 38.7 %copy-start.4 = (f32[384,128]{1,0:T(8,128)S(1)}, f32[384,128]{1,0:T(8,128)}, u32[]{:S(2)}) copy-start(f32[384,128]{1,0:T(8,128)} %gain.1) | copy-start | bytes 589828
  49.1 22.2 %collective-permute-start.2 = (bf16[2,384,384]{2,1,0:T(8,128)(2,1)S(1)}, bf16[2,384,384]{2,1,0:T(8,128)(2,1)}, u32[]{:S(2)}, u32[]{:S(2)}) collective-permute-start(bf16[2,384,384]{2,1,0:T(8,128)(2,1)S(1)} %shard_map.121.own), channel_id=1, source_target_pairs={{0,9},{1,8},{8,1},{9,0},{2,11},{3,10},{10,3},{11,2},{4,13},{5,12},... | collective-permute-start | bytes 1769480 | tf_op jit(solution)/shard_map/ppermute | solution.py:313
  54.1 30.1 %collective-permute-start.1 = (bf16[2,384,384]{2,1,0:T(8,128)(2,1)S(1)}, bf16[2,384,384]{2,1,0:T(8,128)(2,1)}, u32[]{:S(2)}, u32[]{:S(2)}) collective-permute-start(bf16[2,384,384]{2,1,0:T(8,128)(2,1)S(1)} %shard_map.121.own), channel_id=1, source_target_pairs={{0,8},{8,0},{1,9},{9,1},{2,10},{10,2},{3,11},{11,3},{4,12},{12,4},... | collective-permute-start | bytes 1769480 | tf_op jit(solution)/shard_map/ppermute | solution.py:312
  56.1 28.2 %collective-permute-start = (bf16[2,384,384]{2,1,0:T(8,128)(2,1)S(1)}, bf16[2,384,384]{2,1,0:T(8,128)(2,1)}, u32[]{:S(2)}, u32[]{:S(2)}) collective-permute-start(bf16[2,384,384]{2,1,0:T(8,128)(2,1)S(1)} %shard_map.121.own), channel_id=1, source_target_pairs={{0,1},{1,0},{2,3},{3,2},{4,5},{5,4},{6,7},{7,6},{8,9},{9,8},{10,11... | collective-permute-start | bytes 1769480 | tf_op jit(solution)/shard_map/ppermute | solution.py:311
  60.1 51.3 %copy-start = (bf16[1536,768]{1,0:T(8,128)(2,1)S(1)}, bf16[1536,768]{1,0:T(8,128)(2,1)}, u32[]{:S(2)}) copy-start(bf16[1536,768]{1,0:T(8,128)(2,1)} %constant.33.clone.table) | copy-start | bytes 7077892
  60.1 26.1 %all-to-all-start.2 = ((bf16[128,8,128]{2,1,0:T(8,128)(2,1)}), bf16[128,8,128]{2,1,0:T(8,128)(2,1)S(1)}, u32[]{:S(2)}, u32[]{:S(2)}) async-start(bf16[128,8,128]{2,1,0:T(8,128)(2,1)} %bitcast.5), calls=%async_computation.2 | async-start | bytes 524288 | tf_op jit(solution)/shard_map/all_to_all | solution.py:318

commit v12 on v11

--- a/solution.py
+++ b/solution.py
@@ -306,11 +306,12 @@
         place, bases
     )
     swap = [(0, 1), (1, 0)]
+    far = lax.ppermute(tables, "x_hi", swap)
     shared = (
         tables,
         lax.ppermute(tables, "core", swap),
-        lax.ppermute(tables, "x_hi", swap),
-        lax.ppermute(tables, ("x_hi", "core"), [(0, 3), (1, 2), (2, 1), (3, 0)]),
+        far,
+        lax.ppermute(far, "core", swap),
     )
     coeffs = call(zonal_kernel, (2 * DEVS, 128), bf16, flops=300_000_000)(
         pieces, jnp.asarray(forward)

time: 134 us -> 135 us (level)
  waiting for transfers between devices: 25.2 us -> 31.7 us
  starting transfers between devices: 47.9 us -> 43.5 us
    ppermute x2, waiting for transfers between devices: 12.9 us -> 0.01 us  [the longest x1 0.01 us: on_device(): far = lax.ppermute(tables, 'x_hi', swap)]
    all_to_all x1, waiting for transfers between devices: 1.97 us -> 13.7 us  [on_device(): lax.all_to_all(coeffs.reshape(DEVS // 4, 8, 128), LONG, 0, 0, tiled=True)]
    all_to_all x1, waiting for transfers between devices: 0.13 us -> 7.88 us  [on_device(): pieces = lax.all_to_all(pieces, LON, 0, 0, tiled=True)]
    all_to_all x1, starting transfers between devices: 11.1 us -> 8.58 us  [on_device(): lax.all_to_all(coeffs.reshape(DEVS // 4, 8, 128), LONG, 0, 0, tiled=True)]
    all_to_all x1, blocking collectives: 22.2 us -> 19.9 us  [on_device(): lax.all_to_all(coeffs.reshape(DEVS // 4, 8, 128), LONG, 0, 0, tiled=True)]
    all_to_all x1, starting transfers between devices: 13.9 us -> 12.3 us  [on_device(): pieces = lax.all_to_all(pieces, LON, 0, 0, tiled=True)]
  transfers between devices with their start and end apart: 6 -> 6, of which waited for: 4 -> 3; matrix products, arithmetic and copies ran while one was open for 0% -> 0% of each run, Pallas kernels for 7% -> 6%
where the time goes in v12:
time: 135 us; the launch traced here: 133 us
  starting transfers between devices  43.5 us (32%)
  blocking collectives  38.8 us (29%)
  waiting for transfers between devices  31.7 us (23%)
  Pallas kernels  16.7 us (12%)
  local copies, waits for them, and re-layouts  1.89 us (1%)
    all_to_all x1, blocking collectives, on_device(): lax.all_to_all(coeffs.reshape(DEVS // 4, 8, 128), LONG, 0, 0, tiled=True)  19.9 us
    all_to_all x1, blocking collectives, on_device(): pieces = lax.all_to_all(pieces, LON, 0, 0, tiled=True)  18.9 us
    pallas_call x7, Pallas kernels, run(): pl.pallas_call(kernel, out_shape=outs[0] if single else outs, in_specs=sp...  16.7 us
    all_to_all x1, waiting for transfers between devices, on_device(): lax.all_to_all(coeffs.reshape(DEVS // 4, 8, 128), LONG, 0, 0, tiled=True)  13.7 us
    all_to_all x1, starting transfers between devices, on_device(): bases = lax.all_to_all(bases, 'lat', 0, 0, tiled=True)  13.5 us
    all_to_all x1, starting transfers between devices, on_device(): pieces = lax.all_to_all(pieces, LON, 0, 0, tiled=True)  12.3 us
    all_to_all x1, waiting for transfers between devices, on_device(): bases = lax.all_to_all(bases, 'lat', 0, 0, tiled=True)  10.1 us
    all_to_all x1, starting transfers between devices, on_device(): lax.all_to_all(coeffs.reshape(DEVS // 4, 8, 128), LONG, 0, 0, tiled=True)  8.58 us
  transfers between devices with their start and end apart: 6, of which 3 were waited for; matrix products, arithmetic and copies ran while one was open for 0% of the time, Pallas kernels for 6%

profile of v12, /device:TPU:1, one launch (start us, length us, event | category | flops | bytes accessed | tf_op | source)
XLA Modules:
  0.0 132.8 jit_solution(6284655369139369722)
XLA Ops:
  0.0 2.0 %shard_map.118 = bf16[32,24,384]{2,1,0:T(8,128)(2,1)} custom-call(bf16[12,23,384]{2,1,0:T(8,128)(2,1)} %bitcast.12, bf16[12,23,384]{2,1,0:T(8,128)(2,1)} %second_h.1), custom_call_target="tpu_custom_call" | custom-call | tf_op jit(solution)/shard_map/pallas_call | solution.py:254
  2.0 13.5 %all-to-all-start = ((bf16[32,24,384]{2,1,0:T(8,128)(2,1)}), bf16[32,24,384]{2,1,0:T(8,128)(2,1)S(1)}, u32[]{:S(2)}, u32[]{:S(2)}) async-start(bf16[32,24,384]{2,1,0:T(8,128)(2,1)} %shard_map.118), calls=%async_computation | async-start | bytes 1179648 | tf_op jit(solution)/shard_map/all_to_all | solution.py:286
  15.5 0.1 pad_add_fusion.place
  15.6 6.0 %shard_map.119 = bf16[16,72,128]{2,1,0:T(8,128)(2,1)} custom-call(bf16[12,90,128]{2,1,0:T(8,128)(2,1)} %saved_h, bf16[12,90,128]{2,1,0:T(8,128)(2,1)} %cotan_h.1, bf16[128,512]{1,0:T(8,128)(2,1)} %w_in_h.1, f32[1,512]{1,0:T(1,128)} %bitcast.13, bf16[512,512]{1,0:T(8,128)(2,1)} %w_mid_h.1, f32[1,512]{1,0:T(1,128)} %bitcast.14, bf16[512,128]{1,0:T(8,128)(2,1)} %w_out_h.1), custom_call_target="tpu_custom_call" | custom-call | flops 1700000000 | bytes 4000000 | tf_op jit(solution)/shard_map/pallas_call | solution.py:254
  21.6 0.0 copy-start.1
  21.6 10.1 %all-to-all-done.bases = bf16[32,24,384]{2,1,0:T(8,128)(2,1)S(1)} async-done(((bf16[32,24,384]{2,1,0:T(8,128)(2,1)}), bf16[32,24,384]{2,1,0:T(8,128)(2,1)S(1)}, u32[]{:S(2)}, u32[]{:S(2)}) %all-to-all-start) | async-done | bytes 589856 | tf_op jit(solution)/shard_map/all_to_all | solution.py:286
  31.7 0.0 copy-start.2
  31.7 0.8 copy-done.2
  32.5 0.0 copy-start.3
  32.5 1.1 copy-done.3
  33.6 1.5 %shard_map.121.own = bf16[2,384,384]{2,1,0:T(8,128)(2,1)S(1)} custom-call(s32[2]{0:T(128)S(1)} %pad_add_fusion.place, bf16[32,24,384]{2,1,0:T(8,128)(2,1)S(1)} %copy-done.3), custom_call_target="tpu_custom_call" | custom-call | flops 600000000 | bytes 3000000 | tf_op jit(solution)/shard_map/pallas_call | solution.py:254
  35.1 0.0 copy-start.4
  35.1 4.8 %collective-permute-start.1 = (bf16[2,384,384]{2,1,0:T(8,128)(2,1)S(1)}, bf16[2,384,384]{2,1,0:T(8,128)(2,1)}, u32[]{:S(2)}, u32[]{:S(2)}) collective-permute-start(bf16[2,384,384]{2,1,0:T(8,128)(2,1)S(1)} %shard_map.121.own), channel_id=1, source_target_pairs={{0,8},{8,0},{1,9},{9,1},{2,10},{10,2},{3,11},{11,3},{4,12},{12,4},... | collective-permute-start | bytes 1769480 | tf_op jit(solution)/shard_map/ppermute | solution.py:309
  39.9 12.3 %all-to-all-start.1 = ((bf16[16,72,128]{2,1,0:T(8,128)(2,1)}), bf16[16,72,128]{2,1,0:T(8,128)(2,1)S(1)}, u32[]{:S(2)}, u32[]{:S(2)}) async-start(bf16[16,72,128]{2,1,0:T(8,128)(2,1)} %shard_map.119), calls=%async_computation.1 | async-start | bytes 589824 | tf_op jit(solution)/shard_map/all_to_all | solution.py:301
  52.2 2.0 %collective-permute-start = (bf16[2,384,384]{2,1,0:T(8,128)(2,1)S(1)}, bf16[2,384,384]{2,1,0:T(8,128)(2,1)}, u32[]{:S(2)}, u32[]{:S(2)}) collective-permute-start(bf16[2,384,384]{2,1,0:T(8,128)(2,1)S(1)} %shard_map.121.own), channel_id=1, source_target_pairs={{0,1},{1,0},{2,3},{3,2},{4,5},{5,4},{6,7},{7,6},{8,9},{9,8},{10,11... | collective-permute-start | bytes 1769480 | tf_op jit(solution)/shard_map/ppermute | solution.py:312
  54.2 0.0 collective-permute-done.1.far_s
  54.2 2.3 %collective-permute-start.2 = (bf16[2,384,384]{2,1,0:T(8,128)(2,1)}, bf16[2,384,384]{2,1,0:T(8,128)(2,1)}, u32[]{:S(2)}, u32[]{:S(2)}) collective-permute-start(bf16[2,384,384]{2,1,0:T(8,128)(2,1)} %collective-permute-done.1.far_s), channel_id=1, source_target_pairs={{0,1},{1,0},{2,3},{3,2},{4,5},{5,4},{6,7},{7,6},{8,9},{9,8},{10,11... | collective-permute-start | bytes 1769480 | tf_op jit(solution)/shard_map/ppermute | solution.py:314
  56.6 7.9 %all-to-all-done.1.circles = bf16[16,72,128]{2,1,0:T(8,128)(2,1)S(1)} async-done(((bf16[16,72,128]{2,1,0:T(8,128)(2,1)}), bf16[16,72,128]{2,1,0:T(8,128)(2,1)S(1)}, u32[]{:S(2)}, u32[]{:S(2)}) %all-to-all-start.1) | async-done | bytes 294944 | tf_op jit(solution)/shard_map/all_to_all | solution.py:301
  64.4 0.0 copy-done.1
  64.4 1.5 %shard_map.120 = bf16[1024,128]{1,0:T(8,128)(2,1)} custom-call(bf16[16,72,128]{2,1,0:T(8,128)(2,1)S(1)} %all-to-all-done.1.circles, bf16[768,1536]{1,0:T(8,128)(2,1)S(1)} %copy-done.1), custom_call_target="tpu_custom_call" | custom-call | flops 300000000 | tf_op jit(solution)/shard_map/pallas_call | solution.py:254
  65.9 0.0 copy-start
  65.9 8.6 %all-to-all-start.2 = ((bf16[128,8,128]{2,1,0:T(8,128)(2,1)}), bf16[128,8,128]{2,1,0:T(8,128)(2,1)S(1)}, u32[]{:S(2)}, u32[]{:S(2)}) async-start(bf16[128,8,128]{2,1,0:T(8,128)(2,1)} %bitcast.5), calls=%async_computation.2 | async-start | bytes 524288 | tf_op jit(solution)/shard_map/all_to_all | solution.py:319
  74.5 0.0 collective-permute-done.core_s
  74.5 13.7 %all-to-all-done.2 = bf16[128,8,128]{2,1,0:T(8,128)(2,1)S(1)} async-done(((bf16[128,8,128]{2,1,0:T(8,128)(2,1)}), bf16[128,8,128]{2,1,0:T(8,128)(2,1)S(1)}, u32[]{:S(2)}, u32[]{:S(2)}) %all-to-all-start.2) | async-done | bytes 262176 | tf_op jit(solution)/shard_map/all_to_all | solution.py:319
  88.3 0.0 collective-permute-done.2.both_s
  88.3 0.0 copy-done.4
  88.3 3.0 %shard_map.122 = bf16[1024,128]{1,0:T(8,128)(2,1)S(1)} custom-call(s32[2]{0:T(128)S(1)} %pad_add_fusion.place, bf16[1024,128]{1,0:T(8,128)(2,1)S(1)} %bitcast.9, bf16[2,384,384]{2,1,0:T(8,128)(2,1)S(1)} %shard_map.121.own, bf16[2,384,384]{2,1,0:T(8,128)(2,1)} %collective-permute-done.core_s, bf16[2,384,384]{2,1,0:T(8,128)(2,1)} %collective-permute-done.1.far_s, ...), custom_call_target="tpu_custom_call" | custom-call | flops 200000000 | tf_op jit(solution)/shard_map/pallas_call | solution.py:254
  91.3 19.9 %all_to_all.25 = bf16[128,8,128]{2,1,0:T(8,128)(2,1)S(1)} all-to-all(bf16[128,8,128]{2,1,0:T(8,128)(2,1)S(1)} %bitcast.10), channel_id=1, replica_groups=mesh['lat'=32,'x_hi'=2,'x_lo'=2,'z_hi'=2,'core'=2] {'x_lo','z_hi','lat'}, dimensions={0} | all-to-all | bytes 524288 | tf_op jit(solution)/shard_map/all_to_all | solution.py:334
  111.2 0.0 copy-done
  111.2 1.6 %shard_map.123 = bf16[16,72,128]{2,1,0:T(8,128)(2,1)S(1)} custom-call(bf16[1024,128]{1,0:T(8,128)(2,1)S(1)} %bitcast.11, bf16[1536,768]{1,0:T(8,128)(2,1)S(1)} %copy-done), custom_call_target="tpu_custom_call" | custom-call | flops 300000000 | tf_op jit(solution)/shard_map/pallas_call | solution.py:254
  112.8 18.9 %all_to_all.26.pieces = bf16[16,72,128]{2,1,0:T(8,128)(2,1)S(1)} all-to-all(bf16[16,72,128]{2,1,0:T(8,128)(2,1)S(1)} %shard_map.123), channel_id=1, replica_groups=mesh['lat'=32,'x_hi'=2,'x_lo'=2,'z_hi'=2,'core'=2] {'x_hi','x_lo','z_hi'..., dimensions={0} | all-to-all | bytes 589824 | tf_op jit(solution)/shard_map/all_to_all | solution.py:338
  131.7 1.1 shard_map.124
Async XLA Ops:
  2.0 29.7 %all-to-all-start = ((bf16[32,24,384]{2,1,0:T(8,128)(2,1)}), bf16[32,24,384]{2,1,0:T(8,128)(2,1)S(1)}, u32[]{:S(2)}, u32[]{:S(2)}) async-start(bf16[32,24,384]{2,1,0:T(8,128)(2,1)} %shard_map.118), calls=%async_computation | async-start | bytes 1179648 | tf_op jit(solution)/shard_map/all_to_all | solution.py:286
  21.6 42.9 %copy-start.1 = (bf16[768,1536]{1,0:T(8,128)(2,1)S(1)}, bf16[768,1536]{1,0:T(8,128)(2,1)}, u32[]{:S(2)}) copy-start(bf16[768,1536]{1,0:T(8,128)(2,1)} %constant.32.clone.table) | copy-start | bytes 7077892
  31.7 0.8 copy-start.2
  32.5 1.1 copy-start.3
  35.1 53.2 %copy-start.4 = (f32[384,128]{1,0:T(8,128)S(1)}, f32[384,128]{1,0:T(8,128)}, u32[]{:S(2)}) copy-start(f32[384,128]{1,0:T(8,128)} %gain.1) | copy-start | bytes 589828
  35.1 19.1 %collective-permute-start.1 = (bf16[2,384,384]{2,1,0:T(8,128)(2,1)S(1)}, bf16[2,384,384]{2,1,0:T(8,128)(2,1)}, u32[]{:S(2)}, u32[]{:S(2)}) collective-permute-start(bf16[2,384,384]{2,1,0:T(8,128)(2,1)S(1)} %shard_map.121.own), channel_id=1, source_target_pairs={{0,8},{8,0},{1,9},{9,1},{2,10},{10,2},{3,11},{11,3},{4,12},{12,4},... | collective-permute-start | bytes 1769480 | tf_op jit(solution)/shard_map/ppermute | solution.py:309
  39.9 24.5 %all-to-all-start.1 = ((bf16[16,72,128]{2,1,0:T(8,128)(2,1)}), bf16[16,72,128]{2,1,0:T(8,128)(2,1)S(1)}, u32[]{:S(2)}, u32[]{:S(2)}) async-start(bf16[16,72,128]{2,1,0:T(8,128)(2,1)} %shard_map.119), calls=%async_computation.1 | async-start | bytes 589824 | tf_op jit(solution)/shard_map/all_to_all | solution.py:301
  52.2 22.3 %collective-permute-start = (bf16[2,384,384]{2,1,0:T(8,128)(2,1)S(1)}, bf16[2,384,384]{2,1,0:T(8,128)(2,1)}, u32[]{:S(2)}, u32[]{:S(2)}) collective-permute-start(bf16[2,384,384]{2,1,0:T(8,128)(2,1)S(1)} %shard_map.121.own), channel_id=1, source_target_pairs={{0,1},{1,0},{2,3},{3,2},{4,5},{5,4},{6,7},{7,6},{8,9},{9,8},{10,11... | collective-permute-start | bytes 1769480 | tf_op jit(solution)/shard_map/ppermute | solution.py:312
  54.2 34.0 %collective-permute-start.2 = (bf16[2,384,384]{2,1,0:T(8,128)(2,1)}, bf16[2,384,384]{2,1,0:T(8,128)(2,1)}, u32[]{:S(2)}, u32[]{:S(2)}) collective-permute-start(bf16[2,384,384]{2,1,0:T(8,128)(2,1)} %collective-permute-done.1.far_s), channel_id=1, source_target_pairs={{0,1},{1,0},{2,3},{3,2},{4,5},{5,4},{6,7},{7,6},{8,9},{9,8},{10,11... | collective-permute-start | bytes 1769480 | tf_op jit(solution)/shard_map/ppermute | solution.py:314
  65.9 45.3 %copy-start = (bf16[1536,768]{1,0:T(8,128)(2,1)S(1)}, bf16[1536,768]{1,0:T(8,128)(2,1)}, u32[]{:S(2)}) copy-start(bf16[1536,768]{1,0:T(8,128)(2,1)} %constant.33.clone.table) | copy-start | bytes 7077892
  65.9 22.3 %all-to-all-start.2 = ((bf16[128,8,128]{2,1,0:T(8,128)(2,1)}), bf16[128,8,128]{2,1,0:T(8,128)(2,1)S(1)}, u32[]{:S(2)}, u32[]{:S(2)}) async-start(bf16[128,8,128]{2,1,0:T(8,128)(2,1)} %bitcast.5), calls=%async_computation.2 | async-start | bytes 524288 | tf_op jit(solution)/shard_map/all_to_all | solution.py:319

commit v13 on v12

--- a/solution.py
+++ b/solution.py
@@ -150,7 +150,9 @@
         out[256 * q + KEPT : 256 * (q + 1), :] = jnp.zeros((256 - KEPT, 128), bf16)
 
 
-def bases_kernel(place, bases, out):
+def bases_kernel(place, bases_h, out, bases, sem):
+    copy = pltpu.make_async_copy(bases_h, bases, sem)
+    copy.start()
     m = place[0]
 
     def index(shape, axis):
@@ -159,6 +161,7 @@
     def pick(mask):
         return jnp.where(mask, 1.0, 0.0).astype(bf16)
 
+    copy.wait()
     rows = bases[...].astype(f32).reshape(LAT_DEV * 24, NL).astype(bf16)
     wave = index((NL, 1), 0)
     tile = lax.shift_right_logical(wave * 5462, 16)
@@ -302,20 +305,24 @@
     mode = M_DEV * lax.axis_index(LON) + lax.axis_index("lat")
     mine = 2 * lax.axis_index("x_hi") + lax.axis_index("core")
     place = jnp.stack([mode, mine]).astype(jnp.int32)
-    tables = call(bases_kernel, (2, NL, NLAT), bf16, smem=1, flops=600_000_000, moved=3_000_000)(
-        place, bases
-    )
+    tables = call(
+        bases_kernel,
+        (2, NL, NLAT),
+        bf16,
+        (pltpu.VMEM((LAT_DEV, 24, NL), bf16), pltpu.SemaphoreType.DMA),
+        smem=1,
+        far=(1,),
+        flops=600_000_000,
+        moved=3_000_000,
+    )(place, bases)
     swap = [(0, 1), (1, 0)]
     far = lax.ppermute(tables, "x_hi", swap)
-    shared = (
-        tables,
-        lax.ppermute(tables, "core", swap),
-        far,
-        lax.ppermute(far, "core", swap),
-    )
+    near = lax.ppermute(tables, "core", swap)
     coeffs = call(zonal_kernel, (2 * DEVS, 128), bf16, flops=300_000_000)(
         pieces, jnp.asarray(forward)
     )
+    late, _ = lax.optimization_barrier((far, coeffs))
+    shared = (tables, near, far, lax.ppermute(late, "core", swap))
     coeffs = lax.all_to_all(coeffs.reshape(DEVS // 4, 8, 128), LONG, 0, 0, tiled=True)
     coeffs = call(
         legendre_kernel,

time: 135 us -> 137 us (1.015)
  waiting for transfers between devices: 31.7 us -> 35.4 us
  blocking collectives: 38.8 us -> 36.6 us
    all_to_all x1, waiting for transfers between devices: 7.88 us -> 10.2 us  [on_device(): pieces = lax.all_to_all(pieces, LON, 0, 0, tiled=True)]
  transfers between devices with their start and end apart: 6 -> 6, of which waited for: 3 -> 3; matrix products, arithmetic and copies ran while one was open for 0% -> 0% of each run, Pallas kernels for 6% -> 5%
where the time goes in v13:
time: 137 us; the launch traced here: 135 us
  starting transfers between devices  44.1 us (32%)
  blocking collectives  36.6 us (27%)
  waiting for transfers between devices  35.4 us (26%)
  Pallas kernels  16.8 us (12%)
  local copies, waits for them, and re-layouts  1.89 us (1%)
    all_to_all x1, blocking collectives, on_device(): lax.all_to_all(coeffs.reshape(DEVS // 4, 8, 128), LONG, 0, 0, tiled=True)  18.9 us
    all_to_all x1, blocking collectives, on_device(): pieces = lax.all_to_all(pieces, LON, 0, 0, tiled=True)  17.7 us
    pallas_call x7, Pallas kernels, run(): pl.pallas_call(kernel, out_shape=outs[0] if single else outs, in_specs=sp...  16.8 us
    all_to_all x1, waiting for transfers between devices, on_device(): lax.all_to_all(coeffs.reshape(DEVS // 4, 8, 128), LONG, 0, 0, tiled=True)  15 us
    all_to_all x1, starting transfers between devices, on_device(): bases = lax.all_to_all(bases, 'lat', 0, 0, tiled=True)  13.5 us
    all_to_all x1, starting transfers between devices, on_device(): pieces = lax.all_to_all(pieces, LON, 0, 0, tiled=True)  12.3 us
    all_to_all x1, waiting for transfers between devices, on_device(): pieces = lax.all_to_all(pieces, LON, 0, 0, tiled=True)  10.2 us
    all_to_all x1, waiting for transfers between devices, on_device(): bases = lax.all_to_all(bases, 'lat', 0, 0, tiled=True)  10.1 us
  transfers between devices with their start and end apart: 6, of which 3 were waited for; matrix products, arithmetic and copies ran while one was open for 0% of the time, Pallas kernels for 5%

profile of v13, /device:TPU:1, one launch (start us, length us, event | category | flops | bytes accessed | tf_op | source)
XLA Modules:
  0.0 135.0 jit_solution(14333291542911070401)
XLA Ops:
  0.0 2.0 %shard_map.118 = bf16[32,24,384]{2,1,0:T(8,128)(2,1)} custom-call(bf16[12,23,384]{2,1,0:T(8,128)(2,1)} %bitcast.12, bf16[12,23,384]{2,1,0:T(8,128)(2,1)} %second_h.1), custom_call_target="tpu_custom_call" | custom-call | tf_op jit(solution)/shard_map/pallas_call | solution.py:257
  2.0 13.5 %all-to-all-start = ((bf16[32,24,384]{2,1,0:T(8,128)(2,1)}), bf16[32,24,384]{2,1,0:T(8,128)(2,1)S(1)}, u32[]{:S(2)}, u32[]{:S(2)}) async-start(bf16[32,24,384]{2,1,0:T(8,128)(2,1)} %shard_map.118), calls=%async_computation | async-start | bytes 1179648 | tf_op jit(solution)/shard_map/all_to_all | solution.py:289
  15.5 0.1 pad_add_fusion.place
  15.6 5.9 %shard_map.119 = bf16[16,72,128]{2,1,0:T(8,128)(2,1)} custom-call(bf16[12,90,128]{2,1,0:T(8,128)(2,1)} %saved_h, bf16[12,90,128]{2,1,0:T(8,128)(2,1)} %cotan_h.1, bf16[128,512]{1,0:T(8,128)(2,1)} %w_in_h.1, f32[1,512]{1,0:T(1,128)} %bitcast.13, bf16[512,512]{1,0:T(8,128)(2,1)} %w_mid_h.1, f32[1,512]{1,0:T(1,128)} %bitcast.14, bf16[512,128]{1,0:T(8,128)(2,1)} %w_out_h.1), custom_call_target="tpu_custom_call" | custom-call | flops 1700000000 | bytes 4000000 | tf_op jit(solution)/shard_map/pallas_call | solution.py:257
  21.6 0.0 copy-start.1
  21.6 10.1 %all-to-all-done.bases_h = bf16[32,24,384]{2,1,0:T(8,128)(2,1)S(1)} async-done(((bf16[32,24,384]{2,1,0:T(8,128)(2,1)}), bf16[32,24,384]{2,1,0:T(8,128)(2,1)S(1)}, u32[]{:S(2)}, u32[]{:S(2)}) %all-to-all-start) | async-done | bytes 589856 | tf_op jit(solution)/shard_map/all_to_all | solution.py:289
  31.7 0.0 copy-start.2
  31.7 0.8 copy-done.2
  32.5 0.0 copy-start.3
  32.5 1.1 copy-done.3
  33.6 1.7 %shard_map.121.own = bf16[2,384,384]{2,1,0:T(8,128)(2,1)S(1)} custom-call(s32[2]{0:T(128)S(1)} %pad_add_fusion.place, bf16[32,24,384]{2,1,0:T(8,128)(2,1)S(1)} %copy-done.3), custom_call_target="tpu_custom_call" | custom-call | flops 600000000 | bytes 3000000 | tf_op jit(solution)/shard_map/pallas_call | solution.py:257
  35.2 0.0 copy-start.4
  35.3 4.8 %collective-permute-start.1 = (bf16[2,384,384]{2,1,0:T(8,128)(2,1)S(1)}, bf16[2,384,384]{2,1,0:T(8,128)(2,1)}, u32[]{:S(2)}, u32[]{:S(2)}) collective-permute-start(bf16[2,384,384]{2,1,0:T(8,128)(2,1)S(1)} %shard_map.121.own), channel_id=1, source_target_pairs={{0,8},{8,0},{1,9},{9,1},{2,10},{10,2},{3,11},{11,3},{4,12},{12,4},... | collective-permute-start | bytes 1769480 | tf_op jit(solution)/shard_map/ppermute | solution.py:319
  40.0 12.3 %all-to-all-start.1 = ((bf16[16,72,128]{2,1,0:T(8,128)(2,1)}), bf16[16,72,128]{2,1,0:T(8,128)(2,1)S(1)}, u32[]{:S(2)}, u32[]{:S(2)}) async-start(bf16[16,72,128]{2,1,0:T(8,128)(2,1)} %shard_map.119), calls=%async_computation.1 | async-start | bytes 589824 | tf_op jit(solution)/shard_map/all_to_all | solution.py:304
  52.4 2.0 %collective-permute-start = (bf16[2,384,384]{2,1,0:T(8,128)(2,1)S(1)}, bf16[2,384,384]{2,1,0:T(8,128)(2,1)}, u32[]{:S(2)}, u32[]{:S(2)}) collective-permute-start(bf16[2,384,384]{2,1,0:T(8,128)(2,1)S(1)} %shard_map.121.own), channel_id=1, source_target_pairs={{0,1},{1,0},{2,3},{3,2},{4,5},{5,4},{6,7},{7,6},{8,9},{9,8},{10,11... | collective-permute-start | bytes 1769480 | tf_op jit(solution)/shard_map/ppermute | solution.py:320
  54.4 10.2 %all-to-all-done.1.circles = bf16[16,72,128]{2,1,0:T(8,128)(2,1)S(1)} async-done(((bf16[16,72,128]{2,1,0:T(8,128)(2,1)}), bf16[16,72,128]{2,1,0:T(8,128)(2,1)S(1)}, u32[]{:S(2)}, u32[]{:S(2)}) %all-to-all-start.1) | async-done | bytes 294944 | tf_op jit(solution)/shard_map/all_to_all | solution.py:304
  64.6 0.0 copy-done.1
  64.6 1.5 %shard_map.120 = bf16[1024,128]{1,0:T(8,128)(2,1)} custom-call(bf16[16,72,128]{2,1,0:T(8,128)(2,1)S(1)} %all-to-all-done.1.circles, bf16[768,1536]{1,0:T(8,128)(2,1)S(1)} %copy-done.1), custom_call_target="tpu_custom_call" | custom-call | flops 300000000 | tf_op jit(solution)/shard_map/pallas_call | solution.py:257
  66.1 0.0 copy-start
  66.1 0.0 collective-permute-done.1.far_s
  66.1 3.1 %collective-permute-start.2 = (bf16[2,384,384]{2,1,0:T(8,128)(2,1)}, bf16[2,384,384]{2,1,0:T(8,128)(2,1)}, u32[]{:S(2)}, u32[]{:S(2)}) collective-permute-start(bf16[2,384,384]{2,1,0:T(8,128)(2,1)} %collective-permute-done.1.far_s), channel_id=1, source_target_pairs={{0,1},{1,0},{2,3},{3,2},{4,5},{5,4},{6,7},{7,6},{8,9},{9,8},{10,11... | collective-permute-start | bytes 1769480 | tf_op jit(solution)/shard_map/ppermute | solution.py:325
  69.2 8.4 %all-to-all-start.2 = ((bf16[128,8,128]{2,1,0:T(8,128)(2,1)}), bf16[128,8,128]{2,1,0:T(8,128)(2,1)S(1)}, u32[]{:S(2)}, u32[]{:S(2)}) async-start(bf16[128,8,128]{2,1,0:T(8,128)(2,1)} %bitcast.5), calls=%async_computation.2 | async-start | bytes 524288 | tf_op jit(solution)/shard_map/all_to_all | solution.py:326
  77.6 0.0 collective-permute-done.core_s
  77.6 15.0 %all-to-all-done.2 = bf16[128,8,128]{2,1,0:T(8,128)(2,1)S(1)} async-done(((bf16[128,8,128]{2,1,0:T(8,128)(2,1)}), bf16[128,8,128]{2,1,0:T(8,128)(2,1)S(1)}, u32[]{:S(2)}, u32[]{:S(2)}) %all-to-all-start.2) | async-done | bytes 262176 | tf_op jit(solution)/shard_map/all_to_all | solution.py:326
  92.6 0.0 collective-permute-done.2.both_s
  92.6 0.0 copy-done.4
  92.6 3.0 %shard_map.122 = bf16[1024,128]{1,0:T(8,128)(2,1)S(1)} custom-call(s32[2]{0:T(128)S(1)} %pad_add_fusion.place, bf16[1024,128]{1,0:T(8,128)(2,1)S(1)} %bitcast.9, bf16[2,384,384]{2,1,0:T(8,128)(2,1)S(1)} %shard_map.121.own, bf16[2,384,384]{2,1,0:T(8,128)(2,1)} %collective-permute-done.core_s, bf16[2,384,384]{2,1,0:T(8,128)(2,1)} %collective-permute-done.1.far_s, ...), custom_call_target="tpu_custom_call" | custom-call | flops 200000000 | tf_op jit(solution)/shard_map/pallas_call | solution.py:257
  95.6 18.9 %all_to_all.25 = bf16[128,8,128]{2,1,0:T(8,128)(2,1)S(1)} all-to-all(bf16[128,8,128]{2,1,0:T(8,128)(2,1)S(1)} %bitcast.10), channel_id=1, replica_groups=mesh['lat'=32,'x_hi'=2,'x_lo'=2,'z_hi'=2,'core'=2] {'x_lo','z_hi','lat'}, dimensions={0} | all-to-all | bytes 524288 | tf_op jit(solution)/shard_map/all_to_all | solution.py:341
  114.5 0.0 copy-done
  114.5 1.6 %shard_map.123 = bf16[16,72,128]{2,1,0:T(8,128)(2,1)S(1)} custom-call(bf16[1024,128]{1,0:T(8,128)(2,1)S(1)} %bitcast.11, bf16[1536,768]{1,0:T(8,128)(2,1)S(1)} %copy-done), custom_call_target="tpu_custom_call" | custom-call | flops 300000000 | tf_op jit(solution)/shard_map/pallas_call | solution.py:257
  116.1 17.7 %all_to_all.26.pieces = bf16[16,72,128]{2,1,0:T(8,128)(2,1)S(1)} all-to-all(bf16[16,72,128]{2,1,0:T(8,128)(2,1)S(1)} %shard_map.123), channel_id=1, replica_groups=mesh['lat'=32,'x_hi'=2,'x_lo'=2,'z_hi'=2,'core'=2] {'x_hi','x_lo','z_hi'..., dimensions={0} | all-to-all | bytes 589824 | tf_op jit(solution)/shard_map/all_to_all | solution.py:345
  133.9 1.1 shard_map.124
Async XLA Ops:
  2.0 29.7 %all-to-all-start = ((bf16[32,24,384]{2,1,0:T(8,128)(2,1)}), bf16[32,24,384]{2,1,0:T(8,128)(2,1)S(1)}, u32[]{:S(2)}, u32[]{:S(2)}) async-start(bf16[32,24,384]{2,1,0:T(8,128)(2,1)} %shard_map.118), calls=%async_computation | async-start | bytes 1179648 | tf_op jit(solution)/shard_map/all_to_all | solution.py:289
  21.6 43.0 %copy-start.1 = (bf16[768,1536]{1,0:T(8,128)(2,1)S(1)}, bf16[768,1536]{1,0:T(8,128)(2,1)}, u32[]{:S(2)}) copy-start(bf16[768,1536]{1,0:T(8,128)(2,1)} %constant.32.clone.table) | copy-start | bytes 7077892
  31.7 0.8 copy-start.2
  32.5 1.1 copy-start.3
  35.2 57.4 %copy-start.4 = (f32[384,128]{1,0:T(8,128)S(1)}, f32[384,128]{1,0:T(8,128)}, u32[]{:S(2)}) copy-start(f32[384,128]{1,0:T(8,128)} %gain.1) | copy-start | bytes 589828
  35.3 30.8 %collective-permute-start.1 = (bf16[2,384,384]{2,1,0:T(8,128)(2,1)S(1)}, bf16[2,384,384]{2,1,0:T(8,128)(2,1)}, u32[]{:S(2)}, u32[]{:S(2)}) collective-permute-start(bf16[2,384,384]{2,1,0:T(8,128)(2,1)S(1)} %shard_map.121.own), channel_id=1, source_target_pairs={{0,8},{8,0},{1,9},{9,1},{2,10},{10,2},{3,11},{11,3},{4,12},{12,4},... | collective-permute-start | bytes 1769480 | tf_op jit(solution)/shard_map/ppermute | solution.py:319
  40.0 24.5 %all-to-all-start.1 = ((bf16[16,72,128]{2,1,0:T(8,128)(2,1)}), bf16[16,72,128]{2,1,0:T(8,128)(2,1)S(1)}, u32[]{:S(2)}, u32[]{:S(2)}) async-start(bf16[16,72,128]{2,1,0:T(8,128)(2,1)} %shard_map.119), calls=%async_computation.1 | async-start | bytes 589824 | tf_op jit(solution)/shard_map/all_to_all | solution.py:304
  52.4 25.2 %collective-permute-start = (bf16[2,384,384]{2,1,0:T(8,128)(2,1)S(1)}, bf16[2,384,384]{2,1,0:T(8,128)(2,1)}, u32[]{:S(2)}, u32[]{:S(2)}) collective-permute-start(bf16[2,384,384]{2,1,0:T(8,128)(2,1)S(1)} %shard_map.121.own), channel_id=1, source_target_pairs={{0,1},{1,0},{2,3},{3,2},{4,5},{5,4},{6,7},{7,6},{8,9},{9,8},{10,11... | collective-permute-start | bytes 1769480 | tf_op jit(solution)/shard_map/ppermute | solution.py:320
  66.1 48.5 %copy-start = (bf16[1536,768]{1,0:T(8,128)(2,1)S(1)}, bf16[1536,768]{1,0:T(8,128)(2,1)}, u32[]{:S(2)}) copy-start(bf16[1536,768]{1,0:T(8,128)(2,1)} %constant.33.clone.table) | copy-start | bytes 7077892
  66.1 26.5 %collective-permute-start.2 = (bf16[2,384,384]{2,1,0:T(8,128)(2,1)}, bf16[2,384,384]{2,1,0:T(8,128)(2,1)}, u32[]{:S(2)}, u32[]{:S(2)}) collective-permute-start(bf16[2,384,384]{2,1,0:T(8,128)(2,1)} %collective-permute-done.1.far_s), channel_id=1, source_target_pairs={{0,1},{1,0},{2,3},{3,2},{4,5},{5,4},{6,7},{7,6},{8,9},{9,8},{10,11... | collective-permute-start | bytes 1769480 | tf_op jit(solution)/shard_map/ppermute | solution.py:325
  69.2 23.4 %all-to-all-start.2 = ((bf16[128,8,128]{2,1,0:T(8,128)(2,1)}), bf16[128,8,128]{2,1,0:T(8,128)(2,1)S(1)}, u32[]{:S(2)}, u32[]{:S(2)}) async-start(bf16[128,8,128]{2,1,0:T(8,128)(2,1)} %bitcast.5), calls=%async_computation.2 | async-start | bytes 524288 | tf_op jit(solution)/shard_map/all_to_all | solution.py:326

commit v14 on v7

--- a/solution.py
+++ b/solution.py
@@ -22,12 +22,15 @@
 DEVS = LAT_DEV * LON_DEV
 ROWS = 2 * NM
 LON = ("pair", "core")
+LONG = ("pair", "lat")
+KEPT = 96
 VMEM = 16 * 1024 * 1024
 NETWORK_VMEM = 59 * 1024 * 1024
 
 
 def zonal_tables():
-    order = (M_DEV * np.arange(LON_DEV)[None, :] + np.arange(M_DEV)[:, None]).reshape(-1)
+    k, i, h = np.meshgrid(np.arange(PAIRS), np.arange(M_DEV), np.arange(2), indexing="ij")
+    order = (M_DEV * (2 * k + h) + i).reshape(-1)
     turns = (order[:, None] * np.arange(NLON)[None, :]) % NLON
     angles = turns.astype(np.float64) * (2.0 * np.pi / NLON)
     table = np.stack([np.cos(angles), -np.sin(angles)], 1).reshape(ROWS, NLON)
@@ -35,9 +38,11 @@
     back = table * np.repeat(weight, 2)[:, None]
 
     def split_y(t):
-        t = np.pad(t.reshape(ROWS, LON_DEV, Y_DEV), ((0, 0), (0, 0), (0, Y_PAD - Y_DEV)))
-        main = t[:, :, :Y_MAIN].reshape(ROWS, LON_DEV * Y_MAIN)
-        extra = t[:, :, Y_MAIN:].reshape(ROWS, LON_DEV * Y_EXT)
+        t = np.pad(t.reshape(PAIRS, ROWS // PAIRS, NLON), ((0, 0), (0, KEPT - ROWS // PAIRS), (0, 0)))
+        t = t.reshape(PAIRS * KEPT, LON_DEV, Y_DEV)
+        t = np.pad(t, ((0, 0), (0, 0), (0, Y_PAD - Y_DEV)))
+        main = t[:, :, :Y_MAIN].reshape(PAIRS * KEPT, LON_DEV * Y_MAIN)
+        extra = t[:, :, Y_MAIN:].reshape(PAIRS * KEPT, LON_DEV * Y_EXT)
         return np.concatenate([main, extra], 1)
 
     return (
@@ -139,8 +144,10 @@
         parts = [piece[Y_EXT * xx : Y_EXT * (xx + 1), 96:128] for xx in range(X_SUB)]
         extra.append(jnp.concatenate(parts + [jnp.zeros((Y_EXT, C_SUB), f32)], axis=1))
     g = jnp.concatenate(main + extra, axis=0).astype(bf16)
-    out[0:ROWS, :] = dot(table[...], g).astype(bf16)
-    out[ROWS:, :] = jnp.zeros((2 * DEVS - ROWS, 128), bf16)
+    spectrum = dot(table[...], g).astype(bf16)
+    for k in range(PAIRS):
+        out[128 * k : 128 * k + KEPT, :] = spectrum[KEPT * k : KEPT * (k + 1)]
+        out[128 * k + KEPT : 128 * (k + 1), :] = jnp.zeros((128 - KEPT, 128), bf16)
 
 
 def bases_kernel(place, bases, out):
@@ -177,7 +184,7 @@
 
     rows[...] = coeffs[...].astype(f32)
     blocks = [
-        [rows[pl.ds(4 * k + n, LAT_DEV, stride=32), :] for n in range(4)] for k in range(PAIRS)
+        [rows[pl.ds(128 * k + n, LAT_DEV, stride=4), :] for n in range(4)] for k in range(PAIRS)
     ]
     modes = []
     for h in range(2):
@@ -208,12 +215,13 @@
                     for xx in range(X_SUB)
                 ]
                 parts.append(jnp.zeros((LAT_DEV, C_SUB), f32))
-                rows[pl.ds(4 * k + 2 * h + r, LAT_DEV, stride=32), :] = jnp.concatenate(parts, axis=1)
+                rows[pl.ds(128 * k + 2 * h + r, LAT_DEV, stride=4), :] = jnp.concatenate(parts, axis=1)
     out[...] = rows[...].astype(bf16)
 
 
 def inverse_kernel(coeffs, table, out):
-    g = dot(table[...], coeffs[0:ROWS, :])
+    z = jnp.concatenate([coeffs[128 * k : 128 * k + KEPT, :] for k in range(PAIRS)], axis=0)
+    g = dot(table[...], z)
     for j in range(LON_DEV):
         main = g[Y_MAIN * j : Y_MAIN * (j + 1), 0:96]
         first = LON_DEV * Y_MAIN + Y_EXT * j
@@ -300,8 +308,7 @@
     coeffs = call(zonal_kernel, (2 * DEVS, 128), bf16, flops=300_000_000)(
         pieces, jnp.asarray(forward)
     )
-    others, coeffs = lax.optimization_barrier((others, coeffs))
-    coeffs = lax.all_to_all(coeffs.reshape(DEVS // 2, 4, 128), ("lat", "pair"), 0, 0, tiled=True)
+    coeffs = lax.all_to_all(coeffs.reshape(DEVS // 2, 4, 128), LONG, 0, 0, tiled=True)
     coeffs = call(
         legendre_kernel,
         (2 * DEVS, 128),
@@ -310,9 +317,10 @@
         smem=1,
         flops=200_000_000,
     )(place, coeffs.reshape(2 * DEVS, 128), tables, others, spectral_gain)
-    coeffs = lax.all_to_all(coeffs.reshape(DEVS // 2, 4, 128), ("lat", "pair"), 0, 0, tiled=True)
+    coeffs, back = lax.optimization_barrier((coeffs, jnp.asarray(back)))
+    coeffs = lax.all_to_all(coeffs.reshape(DEVS // 2, 4, 128), LONG, 0, 0, tiled=True)
     pieces = call(inverse_kernel, (LON_DEV, Y_MAIN, 128), bf16, flops=300_000_000)(
-        coeffs.reshape(2 * DEVS, 128), jnp.asarray(back)
+        coeffs.reshape(2 * DEVS, 128), back
     )
     pieces = lax.all_to_all(pieces, LON, 0, 0, tiled=True)
     return call(grid_kernel, (X_DEV, Y_DEV, CHAN), f32)(pieces)

time: 136 us -> 134 us (0.985)
  blocking collectives: 89 us -> 41.3 us
  waiting for transfers between devices: 10.1 us -> 32.1 us
  starting transfers between devices: 19.4 us -> 41.2 us
  local copies, waits for them, and re-layouts: 0.02 us -> 1.68 us
    all_to_all x0 -> x2, starting transfers between devices: none -> 25.6 us  [the longest x1 13.9 us: on_device(): pieces = lax.all_to_all(pieces, LON, 0, 0, tiled=True)]
    all_to_all x2 -> x1, blocking collectives: 47.9 us -> 23.4 us  [on_device(): lax.all_to_all(coeffs.reshape(DEVS // 2, 4, 128), LONG, 0, 0, tiled=True)]
    all_to_all x2 -> x1, blocking collectives: 41.1 us -> 17.8 us  [on_device(): pieces = lax.all_to_all(pieces, LON, 0, 0, tiled=True)]
    all_to_all x0 -> x2, waiting for transfers between devices: none -> 21.9 us  [the longest x1 13.4 us: on_device(): lax.all_to_all(coeffs.reshape(DEVS // 2, 4, 128), LONG, 0, 0, tiled=True)]
    ppermute x1, starting transfers between devices: 5.88 us -> 2.15 us  [on_device(): others = lax.ppermute(tables, 'core', [(0, 1), (1, 0)])]
    unnamed x6, local copies, waits for them, and re-layouts: 0.02 us -> 1.68 us
  transfers between devices with their start and end apart: 2 -> 4, of which waited for: 1 -> 3; matrix products, arithmetic and copies ran while one was open for 0% -> 0% of each run, Pallas kernels for 5% -> 7%
where the time goes in v14:
time: 134 us; the launch traced here: 132 us
  blocking collectives  41.3 us (31%)
  starting transfers between devices  41.2 us (31%)
  waiting for transfers between devices  32.1 us (24%)
  Pallas kernels  16 us (12%)
  local copies, waits for them, and re-layouts  1.68 us (1%)
    all_to_all x1, blocking collectives, on_device(): lax.all_to_all(coeffs.reshape(DEVS // 2, 4, 128), LONG, 0, 0, tiled=True)  23.4 us
    all_to_all x1, blocking collectives, on_device(): pieces = lax.all_to_all(pieces, LON, 0, 0, tiled=True)  17.8 us
    pallas_call x7, Pallas kernels, run(): pl.pallas_call(kernel, out_shape=outs[0] if single else outs, in_specs=sp...  16 us
    all_to_all x1, starting transfers between devices, on_device(): pieces = lax.all_to_all(pieces, LON, 0, 0, tiled=True)  13.9 us
    all_to_all x1, starting transfers between devices, on_device(): bases = lax.all_to_all(bases, 'lat', 0, 0, tiled=True)  13.5 us
    all_to_all x1, waiting for transfers between devices, on_device(): lax.all_to_all(coeffs.reshape(DEVS // 2, 4, 128), LONG, 0, 0, tiled=True)  13.4 us
    all_to_all x1, starting transfers between devices, on_device(): lax.all_to_all(coeffs.reshape(DEVS // 2, 4, 128), LONG, 0, 0, tiled=True)  11.7 us
    all_to_all x1, waiting for transfers between devices, on_device(): bases = lax.all_to_all(bases, 'lat', 0, 0, tiled=True)  10.2 us
  transfers between devices with their start and end apart: 4, of which 3 were waited for; matrix products, arithmetic and copies ran while one was open for 0% of the time, Pallas kernels for 7%

profile of v14, /device:TPU:1, one launch (start us, length us, event | category | flops | bytes accessed | tf_op | source)
XLA Modules:
  0.0 132.4 jit_solution(10644079751156734191)
XLA Ops:
  0.0 2.0 %shard_map.118 = bf16[32,24,384]{2,1,0:T(8,128)(2,1)} custom-call(bf16[12,23,384]{2,1,0:T(8,128)(2,1)} %bitcast.12, bf16[12,23,384]{2,1,0:T(8,128)(2,1)} %second_h.1), custom_call_target="tpu_custom_call" | custom-call | tf_op jit(solution)/shard_map/pallas_call | solution.py:254
  2.0 13.5 %all-to-all-start = ((bf16[32,24,384]{2,1,0:T(8,128)(2,1)}), bf16[32,24,384]{2,1,0:T(8,128)(2,1)S(1)}, u32[]{:S(2)}, u32[]{:S(2)}) async-start(bf16[32,24,384]{2,1,0:T(8,128)(2,1)} %shard_map.118), calls=%async_computation | async-start | bytes 1179648 | tf_op jit(solution)/shard_map/all_to_all | solution.py:286
  15.5 6.0 %shard_map.119 = bf16[16,72,128]{2,1,0:T(8,128)(2,1)} custom-call(bf16[12,90,128]{2,1,0:T(8,128)(2,1)} %saved_h, bf16[12,90,128]{2,1,0:T(8,128)(2,1)} %cotan_h.1, bf16[128,512]{1,0:T(8,128)(2,1)} %w_in_h.1, f32[1,512]{1,0:T(1,128)} %bitcast.13, bf16[512,512]{1,0:T(8,128)(2,1)} %w_mid_h.1, f32[1,512]{1,0:T(1,128)} %bitcast.14, bf16[512,128]{1,0:T(8,128)(2,1)} %w_out_h.1), custom_call_target="tpu_custom_call" | custom-call | flops 1700000000 | bytes 4000000 | tf_op jit(solution)/shard_map/pallas_call | solution.py:254
  21.5 10.2 %all-to-all-done.bases = bf16[32,24,384]{2,1,0:T(8,128)(2,1)S(1)} async-done(((bf16[32,24,384]{2,1,0:T(8,128)(2,1)}), bf16[32,24,384]{2,1,0:T(8,128)(2,1)S(1)}, u32[]{:S(2)}, u32[]{:S(2)}) %all-to-all-start) | async-done | bytes 589856 | tf_op jit(solution)/shard_map/all_to_all | solution.py:286
  31.7 13.9 %all-to-all-start.1 = ((bf16[16,72,128]{2,1,0:T(8,128)(2,1)}), bf16[16,72,128]{2,1,0:T(8,128)(2,1)S(1)}, u32[]{:S(2)}, u32[]{:S(2)}) async-start(bf16[16,72,128]{2,1,0:T(8,128)(2,1)} %shard_map.119), calls=%async_computation.1 | async-start | bytes 589824 | tf_op jit(solution)/shard_map/all_to_all | solution.py:301
  45.6 0.1 pad_add_fusion.place
  45.7 0.0 copy-start.2
  45.7 1.5 %shard_map.121.tables = bf16[2,384,384]{2,1,0:T(8,128)(2,1)S(1)} custom-call(s32[2]{0:T(128)S(1)} %pad_add_fusion.place, bf16[32,24,384]{2,1,0:T(8,128)(2,1)S(1)} %all-to-all-done.bases), custom_call_target="tpu_custom_call" | custom-call | flops 600000000 | bytes 3000000 | tf_op jit(solution)/shard_map/pallas_call | solution.py:254
  47.2 0.0 copy-start
  47.2 2.2 %collective-permute-start = (bf16[2,384,384]{2,1,0:T(8,128)(2,1)S(1)}, bf16[2,384,384]{2,1,0:T(8,128)(2,1)}, u32[]{:S(2)}, u32[]{:S(2)}) collective-permute-start(bf16[2,384,384]{2,1,0:T(8,128)(2,1)S(1)} %shard_map.121.tables), channel_id=1, source_target_pairs={{0,1},{1,0},{2,3},{3,2},{4,5},{5,4},{6,7},{7,6},{8,9},{9,8},{10,11... | collective-permute-start | bytes 1769480 | tf_op jit(solution)/shard_map/ppermute | solution.py:307
  49.4 8.4 %all-to-all-done.1.circles = bf16[16,72,128]{2,1,0:T(8,128)(2,1)S(1)} async-done(((bf16[16,72,128]{2,1,0:T(8,128)(2,1)}), bf16[16,72,128]{2,1,0:T(8,128)(2,1)S(1)}, u32[]{:S(2)}, u32[]{:S(2)}) %all-to-all-start.1) | async-done | bytes 294944 | tf_op jit(solution)/shard_map/all_to_all | solution.py:301
  57.8 0.0 copy-start.1
  57.8 1.7 %copy-done.1 = bf16[768,1536]{1,0:T(8,128)(2,1)S(1)} copy-done((bf16[768,1536]{1,0:T(8,128)(2,1)S(1)}, bf16[768,1536]{1,0:T(8,128)(2,1)}, u32[]{:S(2)}) %copy-start.1) | copy-done | bytes 2359320
  59.5 1.5 %shard_map.120 = bf16[1024,128]{1,0:T(8,128)(2,1)} custom-call(bf16[16,72,128]{2,1,0:T(8,128)(2,1)S(1)} %all-to-all-done.1.circles, bf16[768,1536]{1,0:T(8,128)(2,1)S(1)} %copy-done.1), custom_call_target="tpu_custom_call" | custom-call | flops 300000000 | tf_op jit(solution)/shard_map/pallas_call | solution.py:254
  61.0 11.7 %all-to-all-start.2 = ((bf16[256,4,128]{2,1,0:T(4,128)(2,1)}), bf16[256,4,128]{2,1,0:T(4,128)(2,1)S(1)}, u32[]{:S(2)}, u32[]{:S(2)}) async-start(bf16[256,4,128]{2,1,0:T(4,128)(2,1)} %bitcast.5), calls=%async_computation.2 | async-start | bytes 524288 | tf_op jit(solution)/shard_map/all_to_all | solution.py:311
  72.7 0.0 collective-permute-done.others
  72.7 13.4 %all-to-all-done.2 = bf16[256,4,128]{2,1,0:T(4,128)(2,1)S(1)} async-done(((bf16[256,4,128]{2,1,0:T(4,128)(2,1)}), bf16[256,4,128]{2,1,0:T(4,128)(2,1)S(1)}, u32[]{:S(2)}, u32[]{:S(2)}) %all-to-all-start.2) | async-done | bytes 262176 | tf_op jit(solution)/shard_map/all_to_all | solution.py:311
  86.1 0.0 copy-done.2
  86.1 2.3 %shard_map.122 = bf16[1024,128]{1,0:T(8,128)(2,1)S(1)} custom-call(s32[2]{0:T(128)S(1)} %pad_add_fusion.place, bf16[1024,128]{1,0:T(8,128)(2,1)S(1)} %bitcast.10, bf16[2,384,384]{2,1,0:T(8,128)(2,1)S(1)} %shard_map.121.tables, bf16[2,384,384]{2,1,0:T(8,128)(2,1)} %collective-permute-done.others, f32[384,128]{1,0:T(8,128)S(1)} %copy-done.2), custom_call_target="tpu_custom_call" | custom-call | flops 200000000 | tf_op jit(solution)/shard_map/pallas_call | solution.py:254
  88.4 23.4 %all_to_all.25 = bf16[256,4,128]{2,1,0:T(4,128)(2,1)S(1)} all-to-all(bf16[256,4,128]{2,1,0:T(4,128)(2,1)S(1)} %bitcast.11), channel_id=1, replica_groups=mesh['lat'=32,'pair'=8,'core'=2] {'pair','lat'}, dimensions={0} | all-to-all | bytes 524288 | tf_op jit(solution)/shard_map/all_to_all | solution.py:321
  111.9 0.0 copy-done
  111.9 1.6 %shard_map.123 = bf16[16,72,128]{2,1,0:T(8,128)(2,1)S(1)} custom-call(bf16[1024,128]{1,0:T(8,128)(2,1)S(1)} %bitcast.9, bf16[1536,768]{1,0:T(8,128)(2,1)S(1)} %copy-done), custom_call_target="tpu_custom_call" | custom-call | flops 300000000 | tf_op jit(solution)/shard_map/pallas_call | solution.py:254
  113.5 17.8 %all_to_all.26.pieces = bf16[16,72,128]{2,1,0:T(8,128)(2,1)S(1)} all-to-all(bf16[16,72,128]{2,1,0:T(8,128)(2,1)S(1)} %shard_map.123), channel_id=1, replica_groups=mesh['lat'=32,'pair'=8,'core'=2] {'pair','core'}, dimensions={0} | all-to-all | bytes 589824 | tf_op jit(solution)/shard_map/all_to_all | solution.py:325
  131.3 1.1 shard_map.124
Async XLA Ops:
  2.0 29.7 %all-to-all-start = ((bf16[32,24,384]{2,1,0:T(8,128)(2,1)}), bf16[32,24,384]{2,1,0:T(8,128)(2,1)S(1)}, u32[]{:S(2)}, u32[]{:S(2)}) async-start(bf16[32,24,384]{2,1,0:T(8,128)(2,1)} %shard_map.118), calls=%async_computation | async-start | bytes 1179648 | tf_op jit(solution)/shard_map/all_to_all | solution.py:286
  31.7 26.1 %all-to-all-start.1 = ((bf16[16,72,128]{2,1,0:T(8,128)(2,1)}), bf16[16,72,128]{2,1,0:T(8,128)(2,1)S(1)}, u32[]{:S(2)}, u32[]{:S(2)}) async-start(bf16[16,72,128]{2,1,0:T(8,128)(2,1)} %shard_map.119), calls=%async_computation.1 | async-start | bytes 589824 | tf_op jit(solution)/shard_map/all_to_all | solution.py:301
  45.7 40.4 %copy-start.2 = (f32[384,128]{1,0:T(8,128)S(1)}, f32[384,128]{1,0:T(8,128)}, u32[]{:S(2)}) copy-start(f32[384,128]{1,0:T(8,128)} %gain.1) | copy-start | bytes 589828
  47.2 64.7 %copy-start = (bf16[1536,768]{1,0:T(8,128)(2,1)S(1)}, bf16[1536,768]{1,0:T(8,128)(2,1)}, u32[]{:S(2)}) copy-start(bf16[1536,768]{1,0:T(8,128)(2,1)} %constant.23.clone.table) | copy-start | bytes 7077892
  47.2 25.5 %collective-permute-start = (bf16[2,384,384]{2,1,0:T(8,128)(2,1)S(1)}, bf16[2,384,384]{2,1,0:T(8,128)(2,1)}, u32[]{:S(2)}, u32[]{:S(2)}) collective-permute-start(bf16[2,384,384]{2,1,0:T(8,128)(2,1)S(1)} %shard_map.121.tables), channel_id=1, source_target_pairs={{0,1},{1,0},{2,3},{3,2},{4,5},{5,4},{6,7},{7,6},{8,9},{9,8},{10,11... | collective-permute-start | bytes 1769480 | tf_op jit(solution)/shard_map/ppermute | solution.py:307
  57.8 1.7 %copy-start.1 = (bf16[768,1536]{1,0:T(8,128)(2,1)S(1)}, bf16[768,1536]{1,0:T(8,128)(2,1)}, u32[]{:S(2)}) copy-start(bf16[768,1536]{1,0:T(8,128)(2,1)} %constant.22.clone.table) | copy-start | bytes 7077892
  61.0 25.2 %all-to-all-start.2 = ((bf16[256,4,128]{2,1,0:T(4,128)(2,1)}), bf16[256,4,128]{2,1,0:T(4,128)(2,1)S(1)}, u32[]{:S(2)}, u32[]{:S(2)}) async-start(bf16[256,4,128]{2,1,0:T(4,128)(2,1)} %bitcast.5), calls=%async_computation.2 | async-start | bytes 524288 | tf_op jit(solution)/shard_map/all_to_all | solution.py:311

commit v15 on v11

--- a/solution.py
+++ b/solution.py
@@ -150,7 +150,7 @@
         out[256 * q + KEPT : 256 * (q + 1), :] = jnp.zeros((256 - KEPT, 128), bf16)
 
 
-def bases_kernel(place, bases, out):
+def bases_kernel(place, bases, first, second):
     m = place[0]
 
     def index(shape, axis):
@@ -168,19 +168,20 @@
     spot = index((1, NLAT), 1)
     x = 12 * (spot & 31) + X_SUB * ((spot >> 5) & 3) + (spot >> 7)
     columns = pick(index((NLAT, NLAT), 0) == x)
-    out[0] = dot(table, columns).astype(bf16)
+    first[...] = dot(table, columns).astype(bf16)
     spot = index((NLAT, 1), 0)
     row = 24 * (spot & 31) + 12 + X_SUB * ((spot >> 5) & 3) + (spot >> 7)
     chosen = pick(index((NLAT, LAT_DEV * 24), 1) == row)
     table = dot(chosen, rows)
-    out[1] = jnp.where(index((NLAT, NL), 1) >= m, table, 0.0).astype(bf16)
-
-
-def legendre_kernel(place, coeffs, own, core_s, far_s, both_s, gain, out, rows, tables, sems):
+    second[...] = jnp.where(index((NLAT, NL), 1) >= m, table, 0.0).astype(bf16)
+
+
+def legendre_kernel(place, coeffs, *rest):
+    sources, (gain, out, rows, tables, sems) = rest[:8], rest[8:]
     mine = place[1]
     copies = [
-        pltpu.make_async_copy(source, tables.at[mine ^ d], sems.at[d])
-        for d, source in enumerate((own, core_s, far_s, both_s))
+        pltpu.make_async_copy(source, tables.at[mine ^ (n // 2), n % 2], sems.at[n])
+        for n, source in enumerate(sources)
     ]
     for copy in copies:
         copy.start()
@@ -302,16 +303,14 @@
     mode = M_DEV * lax.axis_index(LON) + lax.axis_index("lat")
     mine = 2 * lax.axis_index("x_hi") + lax.axis_index("core")
     place = jnp.stack([mode, mine]).astype(jnp.int32)
-    tables = call(bases_kernel, (2, NL, NLAT), bf16, smem=1, flops=600_000_000, moved=3_000_000)(
-        place, bases
-    )
+    tables = call(
+        bases_kernel, [(NL, NLAT), (NLAT, NL)], bf16, smem=1, flops=600_000_000, moved=3_000_000
+    )(place, bases)
     swap = [(0, 1), (1, 0)]
-    shared = (
-        tables,
-        lax.ppermute(tables, "core", swap),
-        lax.ppermute(tables, "x_hi", swap),
-        lax.ppermute(tables, ("x_hi", "core"), [(0, 3), (1, 2), (2, 1), (3, 0)]),
-    )
+    near = [lax.ppermute(t, "core", swap) for t in tables]
+    far = [lax.ppermute(t, "x_hi", swap) for t in tables]
+    both = [lax.ppermute(t, "core", swap) for t in far]
+    shared = (*tables, *near, *far, *both)
     coeffs = call(zonal_kernel, (2 * DEVS, 128), bf16, flops=300_000_000)(
         pieces, jnp.asarray(forward)
     )
@@ -323,10 +322,11 @@
         (
             pltpu.VMEM((2 * DEVS, 128), f32),
             pltpu.VMEM((4, 2, NL, NLAT), bf16),
-            pltpu.SemaphoreType.DMA((4,)),
+            pltpu.SemaphoreType.DMA((8,)),
         ),
         smem=1,
-        far=(2, 3, 4, 5),
+        far=tuple(range(2, 10)),
+        limit=57 * 1024 * 1024,
         flops=200_000_000,
     )(place, coeffs.reshape(2 * DEVS, 128), *shared, spectral_gain)
     coeffs, back = lax.optimization_barrier((coeffs, jnp.asarray(back)))

time: 134 us -> 135 us (level)
  waiting for transfers between devices: 25.2 us -> 15.9 us
  starting transfers between devices: 47.9 us -> 52.3 us
  blocking collectives: 40 us -> 43.7 us
  Pallas kernels: 16.7 us -> 18.6 us
    ppermute x3 -> x6, waiting for transfers between devices: 12.9 us -> 0.39 us  [the longest x2 0.38 us: on_device(): both = [lax.ppermute(t, 'core', swap) for t in far]]
    ppermute x3 -> x6, starting transfers between devices: 9.41 us -> 16.3 us  [the longest x2 6.78 us: on_device(): far = [lax.ppermute(t, 'x_hi', swap) for t in tables]]
    all_to_all x1, blocking collectives: 22.2 us -> 27.2 us  [on_device(): lax.all_to_all(coeffs.reshape(DEVS // 4, 8, 128), LONG, 0, 0, tiled=True)]
    all_to_all x1, waiting for transfers between devices: 0.13 us -> 3.12 us  [on_device(): pieces = lax.all_to_all(pieces, LON, 0, 0, tiled=True)]
    all_to_all x1, starting transfers between devices: 11.1 us -> 8.65 us  [on_device(): lax.all_to_all(coeffs.reshape(DEVS // 4, 8, 128), LONG, 0, 0, tiled=True)]
    pallas_call x7, Pallas kernels: 16.7 us -> 18.6 us  [run(): pl.pallas_call(kernel, out_shape=outs[0] if single else outs, in_specs=sp...]
  transfers between devices with their start and end apart: 6 -> 9, of which waited for: 4 -> 4; matrix products, arithmetic and copies ran while one was open for 0% -> 0% of each run, Pallas kernels for 7% -> 7%
where the time goes in v15:
time: 135 us; the launch traced here: 133 us
  starting transfers between devices  52.3 us (39%)
  blocking collectives  43.7 us (32%)
  Pallas kernels  18.6 us (14%)
  waiting for transfers between devices  15.9 us (12%)
  local copies, waits for them, and re-layouts  2.18 us (2%)
    all_to_all x1, blocking collectives, on_device(): lax.all_to_all(coeffs.reshape(DEVS // 4, 8, 128), LONG, 0, 0, tiled=True)  27.2 us
    pallas_call x7, Pallas kernels, run(): pl.pallas_call(kernel, out_shape=outs[0] if single else outs, in_specs=sp...  18.6 us
    all_to_all x1, blocking collectives, on_device(): pieces = lax.all_to_all(pieces, LON, 0, 0, tiled=True)  16.5 us
    all_to_all x1, starting transfers between devices, on_device(): pieces = lax.all_to_all(pieces, LON, 0, 0, tiled=True)  13.9 us
    all_to_all x1, starting transfers between devices, on_device(): bases = lax.all_to_all(bases, 'lat', 0, 0, tiled=True)  13.5 us
    all_to_all x1, waiting for transfers between devices, on_device(): bases = lax.all_to_all(bases, 'lat', 0, 0, tiled=True)  10.2 us
    all_to_all x1, starting transfers between devices, on_device(): lax.all_to_all(coeffs.reshape(DEVS // 4, 8, 128), LONG, 0, 0, tiled=True)  8.65 us
    ppermute x2, starting transfers between devices, on_device(): far = [lax.ppermute(t, 'x_hi', swap) for t in tables]  6.78 us
  transfers between devices with their start and end apart: 9, of which 4 were waited for; matrix products, arithmetic and copies ran while one was open for 0% of the time, Pallas kernels for 7%

profile of v15, /device:TPU:1, one launch (start us, length us, event | category | flops | bytes accessed | tf_op | source)
XLA Modules:
  0.0 133.0 jit_solution(7347449912780329582)
XLA Ops:
  0.0 2.0 %shard_map.118 = bf16[32,24,384]{2,1,0:T(8,128)(2,1)} custom-call(bf16[12,23,384]{2,1,0:T(8,128)(2,1)} %bitcast.12, bf16[12,23,384]{2,1,0:T(8,128)(2,1)} %second_h.1), custom_call_target="tpu_custom_call" | custom-call | tf_op jit(solution)/shard_map/pallas_call | solution.py:255
  2.0 13.5 %all-to-all-start = ((bf16[32,24,384]{2,1,0:T(8,128)(2,1)}), bf16[32,24,384]{2,1,0:T(8,128)(2,1)S(1)}, u32[]{:S(2)}, u32[]{:S(2)}) async-start(bf16[32,24,384]{2,1,0:T(8,128)(2,1)} %shard_map.118), calls=%async_computation | async-start | bytes 1179648 | tf_op jit(solution)/shard_map/all_to_all | solution.py:287
  15.5 6.0 %shard_map.119 = bf16[16,72,128]{2,1,0:T(8,128)(2,1)} custom-call(bf16[12,90,128]{2,1,0:T(8,128)(2,1)} %saved_h, bf16[12,90,128]{2,1,0:T(8,128)(2,1)} %cotan_h.1, bf16[128,512]{1,0:T(8,128)(2,1)} %w_in_h.1, f32[1,512]{1,0:T(1,128)} %bitcast.13, bf16[512,512]{1,0:T(8,128)(2,1)} %w_mid_h.1, f32[1,512]{1,0:T(1,128)} %bitcast.14, bf16[512,128]{1,0:T(8,128)(2,1)} %w_out_h.1), custom_call_target="tpu_custom_call" | custom-call | flops 1700000000 | bytes 4000000 | tf_op jit(solution)/shard_map/pallas_call | solution.py:255
  21.5 0.0 copy-start.1
  21.5 10.2 %all-to-all-done.bases = bf16[32,24,384]{2,1,0:T(8,128)(2,1)S(1)} async-done(((bf16[32,24,384]{2,1,0:T(8,128)(2,1)}), bf16[32,24,384]{2,1,0:T(8,128)(2,1)S(1)}, u32[]{:S(2)}, u32[]{:S(2)}) %all-to-all-start) | async-done | bytes 589856 | tf_op jit(solution)/shard_map/all_to_all | solution.py:287
  31.7 13.9 %all-to-all-start.1 = ((bf16[16,72,128]{2,1,0:T(8,128)(2,1)}), bf16[16,72,128]{2,1,0:T(8,128)(2,1)S(1)}, u32[]{:S(2)}, u32[]{:S(2)}) async-start(bf16[16,72,128]{2,1,0:T(8,128)(2,1)} %shard_map.119), calls=%async_computation.1 | async-start | bytes 589824 | tf_op jit(solution)/shard_map/all_to_all | solution.py:302
  45.6 0.1 pad_add_fusion.place
  45.7 0.0 copy-start.3
  45.7 2.2 %shard_map.121 = (bf16[384,384]{1,0:T(8,128)(2,1)S(1)}, bf16[384,384]{1,0:T(8,128)(2,1)}) custom-call(s32[2]{0:T(128)S(1)} %pad_add_fusion.place, bf16[32,24,384]{2,1,0:T(8,128)(2,1)S(1)} %all-to-all-done.bases), custom_call_target="tpu_custom_call" | custom-call | flops 600000000 | bytes 3000000 | tf_op jit(solution)/shard_map/pallas_call | solution.py:255
  47.9 0.0 copy-start.2
  47.9 4.8 %collective-permute-start.2 = (bf16[384,384]{1,0:T(8,128)(2,1)S(1)}, bf16[384,384]{1,0:T(8,128)(2,1)S(1)}, u32[]{:S(2)}, u32[]{:S(2)}) collective-permute-start(bf16[384,384]{1,0:T(8,128)(2,1)S(1)} %get-tuple-element.17.rest_0_), channel_id=1, source_target_pairs={{0,8},{8,0},{1,9},{9,1},{2,10},{10,2},{3,11},{11,3},{4,12},{12,4},... | collective-permute-start | bytes 884744 | tf_op jit(solution)/shard_map/ppermute | solution.py:311
  52.7 2.0 %collective-permute-start.3 = (bf16[384,384]{1,0:T(8,128)(2,1)}, bf16[384,384]{1,0:T(8,128)(2,1)}, u32[]{:S(2)}, u32[]{:S(2)}) collective-permute-start(bf16[384,384]{1,0:T(8,128)(2,1)} %get-tuple-element.18.rest_1_), channel_id=1, source_target_pairs={{0,8},{8,0},{1,9},{9,1},{2,10},{10,2},{3,11},{11,3},{4,12},{12,4},... | collective-permute-start | bytes 884744 | tf_op jit(solution)/shard_map/ppermute | solution.py:311
  54.7 3.1 %all-to-all-done.1.circles = bf16[16,72,128]{2,1,0:T(8,128)(2,1)S(1)} async-done(((bf16[16,72,128]{2,1,0:T(8,128)(2,1)}), bf16[16,72,128]{2,1,0:T(8,128)(2,1)S(1)}, u32[]{:S(2)}, u32[]{:S(2)}) %all-to-all-start.1) | async-done | bytes 294944 | tf_op jit(solution)/shard_map/all_to_all | solution.py:302
  57.8 0.0 copy-done.1
  57.8 1.5 %shard_map.120 = bf16[1024,128]{1,0:T(8,128)(2,1)} custom-call(bf16[16,72,128]{2,1,0:T(8,128)(2,1)S(1)} %all-to-all-done.1.circles, bf16[768,1536]{1,0:T(8,128)(2,1)S(1)} %copy-done.1), custom_call_target="tpu_custom_call" | custom-call | flops 300000000 | tf_op jit(solution)/shard_map/pallas_call | solution.py:255
  59.3 0.0 copy-done.3
  59.3 0.0 copy-start
  59.3 8.7 %all-to-all-start.2 = ((bf16[128,8,128]{2,1,0:T(8,128)(2,1)}), bf16[128,8,128]{2,1,0:T(8,128)(2,1)S(1)}, u32[]{:S(2)}, u32[]{:S(2)}) async-start(bf16[128,8,128]{2,1,0:T(8,128)(2,1)} %bitcast.5), calls=%async_computation.2 | async-start | bytes 524288 | tf_op jit(solution)/shard_map/all_to_all | solution.py:317
  68.0 3.3 %collective-permute-start = (bf16[384,384]{1,0:T(8,128)(2,1)S(1)}, bf16[384,384]{1,0:T(8,128)(2,1)S(1)}, u32[]{:S(2)}, u32[]{:S(2)}) collective-permute-start(bf16[384,384]{1,0:T(8,128)(2,1)S(1)} %get-tuple-element.17.rest_0_), channel_id=1, source_target_pairs={{0,1},{1,0},{2,3},{3,2},{4,5},{5,4},{6,7},{7,6},{8,9},{9,8},{10,11... | collective-permute-start | bytes 884744 | tf_op jit(solution)/shard_map/ppermute | solution.py:310
  71.3 1.9 %collective-permute-start.1 = (bf16[384,384]{1,0:T(8,128)(2,1)}, bf16[384,384]{1,0:T(8,128)(2,1)S(1)}, u32[]{:S(2)}, u32[]{:S(2)}) collective-permute-start(bf16[384,384]{1,0:T(8,128)(2,1)} %get-tuple-element.18.rest_1_), channel_id=1, source_target_pairs={{0,1},{1,0},{2,3},{3,2},{4,5},{5,4},{6,7},{7,6},{8,9},{9,8},{10,11... | collective-permute-start | bytes 884744 | tf_op jit(solution)/shard_map/ppermute | solution.py:310
  73.2 0.0 collective-permute-done.2.rest_4_
  73.2 0.0 copy-start.5
  73.2 2.4 %collective-permute-start.4 = (bf16[384,384]{1,0:T(8,128)(2,1)S(1)}, bf16[384,384]{1,0:T(8,128)(2,1)S(1)}, u32[]{:S(2)}, u32[]{:S(2)}) collective-permute-start(bf16[384,384]{1,0:T(8,128)(2,1)S(1)} %collective-permute-done.2.rest_4_), channel_id=1, source_target_pairs={{0,1},{1,0},{2,3},{3,2},{4,5},{5,4},{6,7},{7,6},{8,9},{9,8},{10,11... | collective-permute-start | bytes 884744 | tf_op jit(solution)/shard_map/ppermute | solution.py:312
  75.6 0.0 collective-permute-done.3.rest_5_
  75.6 1.9 %collective-permute-start.5 = (bf16[384,384]{1,0:T(8,128)(2,1)}, bf16[384,384]{1,0:T(8,128)(2,1)}, u32[]{:S(2)}, u32[]{:S(2)}) collective-permute-start(bf16[384,384]{1,0:T(8,128)(2,1)} %collective-permute-done.3.rest_5_), channel_id=1, source_target_pairs={{0,1},{1,0},{2,3},{3,2},{4,5},{5,4},{6,7},{7,6},{8,9},{9,8},{10,11... | collective-permute-start | bytes 884744 | tf_op jit(solution)/shard_map/ppermute | solution.py:312
  77.6 0.0 collective-permute-done.rest_2_
  77.6 0.0 copy-start.6
  77.6 0.0 collective-permute-done.1.rest_3_
  77.6 0.0 copy-start.7
  77.6 0.0 collective-permute-done.4.rest_6_
  77.6 0.8 copy-done.7
  78.4 0.0 copy-start.8
  78.4 0.7 copy-done.8
  79.1 0.4 collective-permute-done.5.rest_7_
  79.4 2.2 %all-to-all-done.2 = bf16[128,8,128]{2,1,0:T(8,128)(2,1)S(1)} async-done(((bf16[128,8,128]{2,1,0:T(8,128)(2,1)}), bf16[128,8,128]{2,1,0:T(8,128)(2,1)S(1)}, u32[]{:S(2)}, u32[]{:S(2)}) %all-to-all-start.2) | async-done | bytes 262176 | tf_op jit(solution)/shard_map/all_to_all | solution.py:317
  81.7 0.0 copy-start.4
  81.7 0.0 copy-done.2
  81.7 0.0 copy-done.5
  81.7 0.0 copy-done.6
  81.7 0.7 copy-done.4
  82.4 4.2 %shard_map.122 = bf16[1024,128]{1,0:T(8,128)(2,1)} custom-call(s32[2]{0:T(128)} %copy-done.3, bf16[1024,128]{1,0:T(8,128)(2,1)} %bitcast.10, bf16[384,384]{1,0:T(8,128)(2,1)} %copy-done.2, bf16[384,384]{1,0:T(8,128)(2,1)} %get-tuple-element.18.rest_1_, bf16[384,384]{1,0:T(8,128)(2,1)} %copy-done.6, bf16[384,384]{1,0:T(8,128)(2,1)} %copy-done.7, ...), custom_call_target="tpu_custom_call" | custom-call | flops 200000000 | tf_op jit(solution)/shard_map/pallas_call | solution.py:255
  86.6 27.2 %all_to_all.25 = bf16[128,8,128]{2,1,0:T(8,128)(2,1)S(1)} all-to-all(bf16[128,8,128]{2,1,0:T(8,128)(2,1)} %bitcast.11), channel_id=1, replica_groups=mesh['lat'=32,'x_hi'=2,'x_lo'=2,'z_hi'=2,'core'=2] {'x_lo','z_hi','lat'}, dimensions={0} | all-to-all | bytes 524288 | tf_op jit(solution)/shard_map/all_to_all | solution.py:333
  113.8 0.0 copy-done
  113.9 1.6 %shard_map.123 = bf16[16,72,128]{2,1,0:T(8,128)(2,1)S(1)} custom-call(bf16[1024,128]{1,0:T(8,128)(2,1)S(1)} %bitcast.9, bf16[1536,768]{1,0:T(8,128)(2,1)S(1)} %copy-done), custom_call_target="tpu_custom_call" | custom-call | flops 300000000 | tf_op jit(solution)/shard_map/pallas_call | solution.py:255
  115.4 16.5 %all_to_all.26.pieces = bf16[16,72,128]{2,1,0:T(8,128)(2,1)S(1)} all-to-all(bf16[16,72,128]{2,1,0:T(8,128)(2,1)S(1)} %shard_map.123), channel_id=1, replica_groups=mesh['lat'=32,'x_hi'=2,'x_lo'=2,'z_hi'=2,'core'=2] {'x_hi','x_lo','z_hi'..., dimensions={0} | all-to-all | bytes 589824 | tf_op jit(solution)/shard_map/all_to_all | solution.py:337
  131.9 1.1 shard_map.124
Async XLA Ops:
  2.0 29.7 %all-to-all-start = ((bf16[32,24,384]{2,1,0:T(8,128)(2,1)}), bf16[32,24,384]{2,1,0:T(8,128)(2,1)S(1)}, u32[]{:S(2)}, u32[]{:S(2)}) async-start(bf16[32,24,384]{2,1,0:T(8,128)(2,1)} %shard_map.118), calls=%async_computation | async-start | bytes 1179648 | tf_op jit(solution)/shard_map/all_to_all | solution.py:287
  21.5 36.4 %copy-start.1 = (bf16[768,1536]{1,0:T(8,128)(2,1)S(1)}, bf16[768,1536]{1,0:T(8,128)(2,1)}, u32[]{:S(2)}) copy-start(bf16[768,1536]{1,0:T(8,128)(2,1)} %constant.32.clone.table) | copy-start | bytes 7077892
  31.7 26.1 %all-to-all-start.1 = ((bf16[16,72,128]{2,1,0:T(8,128)(2,1)}), bf16[16,72,128]{2,1,0:T(8,128)(2,1)S(1)}, u32[]{:S(2)}, u32[]{:S(2)}) async-start(bf16[16,72,128]{2,1,0:T(8,128)(2,1)} %shard_map.119), calls=%async_computation.1 | async-start | bytes 589824 | tf_op jit(solution)/shard_map/all_to_all | solution.py:302
  45.7 13.6 %copy-start.3 = (s32[2]{0:T(128)}, s32[2]{0:T(128)S(1)}, u32[]{:S(2)}) copy-start(s32[2]{0:T(128)S(1)} %pad_add_fusion.place) | copy-start | bytes 28
  47.9 33.7 %copy-start.2 = (bf16[384,384]{1,0:T(8,128)(2,1)}, bf16[384,384]{1,0:T(8,128)(2,1)S(1)}, u32[]{:S(2)}) copy-start(bf16[384,384]{1,0:T(8,128)(2,1)S(1)} %get-tuple-element.17.rest_0_) | copy-start | bytes 884740
  47.9 25.3 %collective-permute-start.2 = (bf16[384,384]{1,0:T(8,128)(2,1)S(1)}, bf16[384,384]{1,0:T(8,128)(2,1)S(1)}, u32[]{:S(2)}, u32[]{:S(2)}) collective-permute-start(bf16[384,384]{1,0:T(8,128)(2,1)S(1)} %get-tuple-element.17.rest_0_), channel_id=1, source_target_pairs={{0,8},{8,0},{1,9},{9,1},{2,10},{10,2},{3,11},{11,3},{4,12},{12,4},... | collective-permute-start | bytes 884744 | tf_op jit(solution)/shard_map/ppermute | solution.py:311
  52.7 22.9 %collective-permute-start.3 = (bf16[384,384]{1,0:T(8,128)(2,1)}, bf16[384,384]{1,0:T(8,128)(2,1)}, u32[]{:S(2)}, u32[]{:S(2)}) collective-permute-start(bf16[384,384]{1,0:T(8,128)(2,1)} %get-tuple-element.18.rest_1_), channel_id=1, source_target_pairs={{0,8},{8,0},{1,9},{9,1},{2,10},{10,2},{3,11},{11,3},{4,12},{12,4},... | collective-permute-start | bytes 884744 | tf_op jit(solution)/shard_map/ppermute | solution.py:311
  59.3 54.5 %copy-start = (bf16[1536,768]{1,0:T(8,128)(2,1)S(1)}, bf16[1536,768]{1,0:T(8,128)(2,1)}, u32[]{:S(2)}) copy-start(bf16[1536,768]{1,0:T(8,128)(2,1)} %constant.33.clone.table) | copy-start | bytes 7077892
  59.3 22.3 %all-to-all-start.2 = ((bf16[128,8,128]{2,1,0:T(8,128)(2,1)}), bf16[128,8,128]{2,1,0:T(8,128)(2,1)S(1)}, u32[]{:S(2)}, u32[]{:S(2)}) async-start(bf16[128,8,128]{2,1,0:T(8,128)(2,1)} %bitcast.5), calls=%async_computation.2 | async-start | bytes 524288 | tf_op jit(solution)/shard_map/all_to_all | solution.py:317
  68.0 9.6 %collective-permute-start = (bf16[384,384]{1,0:T(8,128)(2,1)S(1)}, bf16[384,384]{1,0:T(8,128)(2,1)S(1)}, u32[]{:S(2)}, u32[]{:S(2)}) collective-permute-start(bf16[384,384]{1,0:T(8,128)(2,1)S(1)} %get-tuple-element.17.rest_0_), channel_id=1, source_target_pairs={{0,1},{1,0},{2,3},{3,2},{4,5},{5,4},{6,7},{7,6},{8,9},{9,8},{10,11... | collective-permute-start | bytes 884744 | tf_op jit(solution)/shard_map/ppermute | solution.py:310
  71.3 6.3 %collective-permute-start.1 = (bf16[384,384]{1,0:T(8,128)(2,1)}, bf16[384,384]{1,0:T(8,128)(2,1)S(1)}, u32[]{:S(2)}, u32[]{:S(2)}) collective-permute-start(bf16[384,384]{1,0:T(8,128)(2,1)} %get-tuple-element.18.rest_1_), channel_id=1, source_target_pairs={{0,1},{1,0},{2,3},{3,2},{4,5},{5,4},{6,7},{7,6},{8,9},{9,8},{10,11... | collective-permute-start | bytes 884744 | tf_op jit(solution)/shard_map/ppermute | solution.py:310
  73.2 8.5 %copy-start.5 = (bf16[384,384]{1,0:T(8,128)(2,1)}, bf16[384,384]{1,0:T(8,128)(2,1)S(1)}, u32[]{:S(2)}) copy-start(bf16[384,384]{1,0:T(8,128)(2,1)S(1)} %collective-permute-done.2.rest_4_) | copy-start | bytes 884740
  73.2 4.4 %collective-permute-start.4 = (bf16[384,384]{1,0:T(8,128)(2,1)S(1)}, bf16[384,384]{1,0:T(8,128)(2,1)S(1)}, u32[]{:S(2)}, u32[]{:S(2)}) collective-permute-start(bf16[384,384]{1,0:T(8,128)(2,1)S(1)} %collective-permute-done.2.rest_4_), channel_id=1, source_target_pairs={{0,1},{1,0},{2,3},{3,2},{4,5},{5,4},{6,7},{7,6},{8,9},{9,8},{10,11... | collective-permute-start | bytes 884744 | tf_op jit(solution)/shard_map/ppermute | solution.py:312
  75.6 3.8 %collective-permute-start.5 = (bf16[384,384]{1,0:T(8,128)(2,1)}, bf16[384,384]{1,0:T(8,128)(2,1)}, u32[]{:S(2)}, u32[]{:S(2)}) collective-permute-start(bf16[384,384]{1,0:T(8,128)(2,1)} %collective-permute-done.3.rest_5_), channel_id=1, source_target_pairs={{0,1},{1,0},{2,3},{3,2},{4,5},{5,4},{6,7},{7,6},{8,9},{9,8},{10,11... | collective-permute-start | bytes 884744 | tf_op jit(solution)/shard_map/ppermute | solution.py:312
  77.6 4.1 %copy-start.6 = (bf16[384,384]{1,0:T(8,128)(2,1)}, bf16[384,384]{1,0:T(8,128)(2,1)S(1)}, u32[]{:S(2)}) copy-start(bf16[384,384]{1,0:T(8,128)(2,1)S(1)} %collective-permute-done.rest_2_) | copy-start | bytes 884740
  77.6 0.8 copy-start.7
  78.4 0.7 copy-start.8
  81.7 0.7 copy-start.4

commit v16 on v15

--- a/solution.py
+++ b/solution.py
@@ -150,7 +150,7 @@
         out[256 * q + KEPT : 256 * (q + 1), :] = jnp.zeros((256 - KEPT, 128), bf16)
 
 
-def bases_kernel(place, bases, first, second):
+def bases_kernel(place, bases, pair, first, second):
     m = place[0]
 
     def index(shape, axis):
@@ -169,19 +169,23 @@
     x = 12 * (spot & 31) + X_SUB * ((spot >> 5) & 3) + (spot >> 7)
     columns = pick(index((NLAT, NLAT), 0) == x)
     first[...] = dot(table, columns).astype(bf16)
+    pair[0] = first[...]
     spot = index((NLAT, 1), 0)
     row = 24 * (spot & 31) + 12 + X_SUB * ((spot >> 5) & 3) + (spot >> 7)
     chosen = pick(index((NLAT, LAT_DEV * 24), 1) == row)
     table = dot(chosen, rows)
     second[...] = jnp.where(index((NLAT, NL), 1) >= m, table, 0.0).astype(bf16)
+    pair[1] = second[...]
 
 
 def legendre_kernel(place, coeffs, *rest):
-    sources, (gain, out, rows, tables, sems) = rest[:8], rest[8:]
+    sources, (gain, out, rows, tables, sems) = rest[:6], rest[6:]
     mine = place[1]
+    slots = [tables.at[mine], tables.at[mine ^ 1]]
+    slots += [tables.at[mine ^ d, n] for d in (2, 3) for n in range(2)]
     copies = [
-        pltpu.make_async_copy(source, tables.at[mine ^ (n // 2), n % 2], sems.at[n])
-        for n, source in enumerate(sources)
+        pltpu.make_async_copy(source, slot, sems.at[n])
+        for n, (source, slot) in enumerate(zip(sources, slots))
     ]
     for copy in copies:
         copy.start()
@@ -303,14 +307,14 @@
     mode = M_DEV * lax.axis_index(LON) + lax.axis_index("lat")
     mine = 2 * lax.axis_index("x_hi") + lax.axis_index("core")
     place = jnp.stack([mode, mine]).astype(jnp.int32)
-    tables = call(
-        bases_kernel, [(NL, NLAT), (NLAT, NL)], bf16, smem=1, flops=600_000_000, moved=3_000_000
+    pair, *tables = call(
+        bases_kernel, [(2, NL, NLAT), (NL, NLAT), (NLAT, NL)], bf16, smem=1, flops=600_000_000, moved=3_000_000
     )(place, bases)
     swap = [(0, 1), (1, 0)]
-    near = [lax.ppermute(t, "core", swap) for t in tables]
+    near = lax.ppermute(pair, "core", swap)
     far = [lax.ppermute(t, "x_hi", swap) for t in tables]
     both = [lax.ppermute(t, "core", swap) for t in far]
-    shared = (*tables, *near, *far, *both)
+    shared = (pair, near, *far, *both)
     coeffs = call(zonal_kernel, (2 * DEVS, 128), bf16, flops=300_000_000)(
         pieces, jnp.asarray(forward)
     )
@@ -322,11 +326,10 @@
         (
             pltpu.VMEM((2 * DEVS, 128), f32),
             pltpu.VMEM((4, 2, NL, NLAT), bf16),
-            pltpu.SemaphoreType.DMA((8,)),
+            pltpu.SemaphoreType.DMA((6,)),
         ),
         smem=1,
-        far=tuple(range(2, 10)),
-        limit=57 * 1024 * 1024,
+        far=tuple(range(2, 8)),
         flops=200_000_000,
     )(place, coeffs.reshape(2 * DEVS, 128), *shared, spectral_gain)
     coeffs, back = lax.optimization_barrier((coeffs, jnp.asarray(back)))

time: 135 us -> 136 us (level)
  blocking collectives: 43.7 us -> 38 us
  local copies, waits for them, and re-layouts: 2.18 us -> 6.16 us
  waiting for transfers between devices: 15.9 us -> 19.4 us
  Pallas kernels: 18.6 us -> 17.2 us
    all_to_all x1, blocking collectives: 27.2 us -> 19.5 us  [on_device(): lax.all_to_all(coeffs.reshape(DEVS // 4, 8, 128), LONG, 0, 0, tiled=True)]
    all_to_all x1, waiting for transfers between devices: 2.21 us -> 8.41 us  [on_device(): lax.all_to_all(coeffs.reshape(DEVS // 4, 8, 128), LONG, 0, 0, tiled=True)]
    unnamed x18, local copies, waits for them, and re-layouts: 2.18 us -> 6.16 us
    all_to_all x1, waiting for transfers between devices: 3.12 us -> 0.01 us  [on_device(): pieces = lax.all_to_all(pieces, LON, 0, 0, tiled=True)]
    all_to_all x1, starting transfers between devices: 8.65 us -> 11.5 us  [on_device(): lax.all_to_all(coeffs.reshape(DEVS // 4, 8, 128), LONG, 0, 0, tiled=True)]
    ppermute x2 -> x1, starting transfers between devices: 5.19 us -> 2.62 us  [on_device(): near = lax.ppermute(pair, 'core', swap)]
    all_to_all x1, blocking collectives: 16.5 us -> 18.4 us  [on_device(): pieces = lax.all_to_all(pieces, LON, 0, 0, tiled=True)]
    pallas_call x7, Pallas kernels: 18.6 us -> 17.2 us  [run(): pl.pallas_call(kernel, out_shape=outs[0] if single else outs, in_specs=sp...]
  transfers between devices with their start and end apart: 9 -> 8, of which waited for: 4 -> 3; matrix products, arithmetic and copies ran while one was open for 0% -> 0% of each run, Pallas kernels for 7% -> 7%
where the time goes in v16:
time: 136 us; the launch traced here: 134 us
  starting transfers between devices  52.6 us (39%)
  blocking collectives  38 us (28%)
  waiting for transfers between devices  19.4 us (14%)
  Pallas kernels  17.2 us (13%)
  local copies, waits for them, and re-layouts  6.16 us (5%)
    all_to_all x1, blocking collectives, on_device(): lax.all_to_all(coeffs.reshape(DEVS // 4, 8, 128), LONG, 0, 0, tiled=True)  19.5 us
    all_to_all x1, blocking collectives, on_device(): pieces = lax.all_to_all(pieces, LON, 0, 0, tiled=True)  18.4 us
    pallas_call x7, Pallas kernels, run(): pl.pallas_call(kernel, out_shape=outs[0] if single else outs, in_specs=sp...  17.2 us
    all_to_all x1, starting transfers between devices, on_device(): pieces = lax.all_to_all(pieces, LON, 0, 0, tiled=True)  13.9 us
    all_to_all x1, starting transfers between devices, on_device(): bases = lax.all_to_all(bases, 'lat', 0, 0, tiled=True)  13.5 us
    all_to_all x1, starting transfers between devices, on_device(): lax.all_to_all(coeffs.reshape(DEVS // 4, 8, 128), LONG, 0, 0, tiled=True)  11.5 us
    all_to_all x1, waiting for transfers between devices, on_device(): bases = lax.all_to_all(bases, 'lat', 0, 0, tiled=True)  10.2 us
    all_to_all x1, waiting for transfers between devices, on_device(): lax.all_to_all(coeffs.reshape(DEVS // 4, 8, 128), LONG, 0, 0, tiled=True)  8.41 us
  transfers between devices with their start and end apart: 8, of which 3 were waited for; matrix products, arithmetic and copies ran while one was open for 0% of the time, Pallas kernels for 7%

profile of v16, /device:TPU:1, one launch (start us, length us, event | category | flops | bytes accessed | tf_op | source)
XLA Modules:
  0.0 133.6 jit_solution(17374750631767900479)
XLA Ops:
  0.0 2.0 %shard_map.118 = bf16[32,24,384]{2,1,0:T(8,128)(2,1)} custom-call(bf16[12,23,384]{2,1,0:T(8,128)(2,1)} %bitcast.12, bf16[12,23,384]{2,1,0:T(8,128)(2,1)} %second_h.1), custom_call_target="tpu_custom_call" | custom-call | tf_op jit(solution)/shard_map/pallas_call | solution.py:259
  2.0 13.5 %all-to-all-start = ((bf16[32,24,384]{2,1,0:T(8,128)(2,1)}), bf16[32,24,384]{2,1,0:T(8,128)(2,1)S(1)}, u32[]{:S(2)}, u32[]{:S(2)}) async-start(bf16[32,24,384]{2,1,0:T(8,128)(2,1)} %shard_map.118), calls=%async_computation | async-start | bytes 1179648 | tf_op jit(solution)/shard_map/all_to_all | solution.py:291
  15.5 5.9 %shard_map.119 = bf16[16,72,128]{2,1,0:T(8,128)(2,1)} custom-call(bf16[12,90,128]{2,1,0:T(8,128)(2,1)} %saved_h, bf16[12,90,128]{2,1,0:T(8,128)(2,1)} %cotan_h.1, bf16[128,512]{1,0:T(8,128)(2,1)} %w_in_h.1, f32[1,512]{1,0:T(1,128)} %bitcast.13, bf16[512,512]{1,0:T(8,128)(2,1)} %w_mid_h.1, f32[1,512]{1,0:T(1,128)} %bitcast.14, bf16[512,128]{1,0:T(8,128)(2,1)} %w_out_h.1), custom_call_target="tpu_custom_call" | custom-call | flops 1700000000 | bytes 4000000 | tf_op jit(solution)/shard_map/pallas_call | solution.py:259
  21.5 0.0 copy-start.1
  21.5 10.2 %all-to-all-done.bases = bf16[32,24,384]{2,1,0:T(8,128)(2,1)S(1)} async-done(((bf16[32,24,384]{2,1,0:T(8,128)(2,1)}), bf16[32,24,384]{2,1,0:T(8,128)(2,1)S(1)}, u32[]{:S(2)}, u32[]{:S(2)}) %all-to-all-start) | async-done | bytes 589856 | tf_op jit(solution)/shard_map/all_to_all | solution.py:291
  31.7 0.0 copy-start.2
  31.7 0.8 copy-done.2
  32.5 13.9 %all-to-all-start.1 = ((bf16[16,72,128]{2,1,0:T(8,128)(2,1)}), bf16[16,72,128]{2,1,0:T(8,128)(2,1)S(1)}, u32[]{:S(2)}, u32[]{:S(2)}) async-start(bf16[16,72,128]{2,1,0:T(8,128)(2,1)} %shard_map.119), calls=%async_computation.1 | async-start | bytes 589824 | tf_op jit(solution)/shard_map/all_to_all | solution.py:306
  46.4 0.1 pad_add_fusion.place
  46.5 0.0 copy-start.3
  46.5 1.1 copy-done.3
  47.5 2.3 %shard_map.121 = (bf16[2,384,384]{2,1,0:T(8,128)(2,1)S(1)}, bf16[384,384]{1,0:T(8,128)(2,1)}, bf16[384,384]{1,0:T(8,128)(2,1)}) custom-call(s32[2]{0:T(128)S(1)} %pad_add_fusion.place, bf16[32,24,384]{2,1,0:T(8,128)(2,1)S(1)} %copy-done.3), custom_call_target="tpu_custom_call" | custom-call | flops 600000000 | bytes 3000000 | tf_op jit(solution)/shard_map/pallas_call | solution.py:259
  49.9 4.8 %collective-permute-start.1 = (bf16[384,384]{1,0:T(8,128)(2,1)}, bf16[384,384]{1,0:T(8,128)(2,1)S(1)}, u32[]{:S(2)}, u32[]{:S(2)}) collective-permute-start(bf16[384,384]{1,0:T(8,128)(2,1)} %get-tuple-element.19), channel_id=1, source_target_pairs={{0,8},{8,0},{1,9},{9,1},{2,10},{10,2},{3,11},{11,3},{4,12},{12,4},... | collective-permute-start | bytes 884744 | tf_op jit(solution)/shard_map/ppermute | solution.py:315
  54.7 2.0 %collective-permute-start.2 = (bf16[384,384]{1,0:T(8,128)(2,1)}, bf16[384,384]{1,0:T(8,128)(2,1)}, u32[]{:S(2)}, u32[]{:S(2)}) collective-permute-start(bf16[384,384]{1,0:T(8,128)(2,1)} %get-tuple-element.20), channel_id=1, source_target_pairs={{0,8},{8,0},{1,9},{9,1},{2,10},{10,2},{3,11},{11,3},{4,12},{12,4},... | collective-permute-start | bytes 884744 | tf_op jit(solution)/shard_map/ppermute | solution.py:315
  56.6 2.6 %collective-permute-start = (bf16[2,384,384]{2,1,0:T(8,128)(2,1)S(1)}, bf16[2,384,384]{2,1,0:T(8,128)(2,1)}, u32[]{:S(2)}, u32[]{:S(2)}) collective-permute-start(bf16[2,384,384]{2,1,0:T(8,128)(2,1)S(1)} %get-tuple-element.18.rest_0_), channel_id=1, source_target_pairs={{0,1},{1,0},{2,3},{3,2},{4,5},{5,4},{6,7},{7,6},{8,9},{9,8},{10,11... | collective-permute-start | bytes 1769480 | tf_op jit(solution)/shard_map/ppermute | solution.py:314
  59.3 0.0 all-to-all-done.1.circles
  59.3 0.0 copy-done.1
  59.3 1.5 %shard_map.120 = bf16[1024,128]{1,0:T(8,128)(2,1)} custom-call(bf16[16,72,128]{2,1,0:T(8,128)(2,1)S(1)} %all-to-all-done.1.circles, bf16[768,1536]{1,0:T(8,128)(2,1)S(1)} %copy-done.1), custom_call_target="tpu_custom_call" | custom-call | flops 300000000 | tf_op jit(solution)/shard_map/pallas_call | solution.py:259
  60.8 0.0 copy-start
  60.8 11.5 %all-to-all-start.2 = ((bf16[128,8,128]{2,1,0:T(8,128)(2,1)}), bf16[128,8,128]{2,1,0:T(8,128)(2,1)S(1)}, u32[]{:S(2)}, u32[]{:S(2)}) async-start(bf16[128,8,128]{2,1,0:T(8,128)(2,1)} %bitcast.5), calls=%async_computation.2 | async-start | bytes 524288 | tf_op jit(solution)/shard_map/all_to_all | solution.py:321
  72.3 0.0 collective-permute-done.1.rest_2_
  72.3 2.2 %collective-permute-start.3 = (bf16[384,384]{1,0:T(8,128)(2,1)S(1)}, bf16[384,384]{1,0:T(8,128)(2,1)S(1)}, u32[]{:S(2)}, u32[]{:S(2)}) collective-permute-start(bf16[384,384]{1,0:T(8,128)(2,1)S(1)} %collective-permute-done.1.rest_2_), channel_id=1, source_target_pairs={{0,1},{1,0},{2,3},{3,2},{4,5},{5,4},{6,7},{7,6},{8,9},{9,8},{10,11... | collective-permute-start | bytes 884744 | tf_op jit(solution)/shard_map/ppermute | solution.py:316
  74.5 0.0 collective-permute-done.2.rest_3_
  74.5 2.1 %collective-permute-start.4 = (bf16[384,384]{1,0:T(8,128)(2,1)}, bf16[384,384]{1,0:T(8,128)(2,1)S(1)}, u32[]{:S(2)}, u32[]{:S(2)}) collective-permute-start(bf16[384,384]{1,0:T(8,128)(2,1)} %collective-permute-done.2.rest_3_), channel_id=1, source_target_pairs={{0,1},{1,0},{2,3},{3,2},{4,5},{5,4},{6,7},{7,6},{8,9},{9,8},{10,11... | collective-permute-start | bytes 884744 | tf_op jit(solution)/shard_map/ppermute | solution.py:316
  76.6 0.0 collective-permute-done.3.rest_4_
  76.6 0.0 copy-start.4
  76.7 0.7 copy-done.4
  77.4 0.8 collective-permute-done.4.rest_5_
  78.2 0.0 copy-start.6
  78.2 0.7 copy-done.6
  78.9 0.0 collective-permute-done.rest_1_
  78.9 8.4 %all-to-all-done.2 = bf16[128,8,128]{2,1,0:T(8,128)(2,1)S(1)} async-done(((bf16[128,8,128]{2,1,0:T(8,128)(2,1)}), bf16[128,8,128]{2,1,0:T(8,128)(2,1)S(1)}, u32[]{:S(2)}, u32[]{:S(2)}) %all-to-all-start.2) | async-done | bytes 262176 | tf_op jit(solution)/shard_map/all_to_all | solution.py:321
  87.3 0.0 copy-start.5
  87.3 1.0 copy-done.5
  88.3 0.0 copy-start.7
  88.3 1.0 copy-done.7
  89.2 0.0 copy-start.8
  89.2 0.9 copy-done.8
  90.2 2.7 %shard_map.122 = bf16[1024,128]{1,0:T(8,128)(2,1)S(1)} custom-call(s32[2]{0:T(128)S(1)} %pad_add_fusion.place, bf16[1024,128]{1,0:T(8,128)(2,1)S(1)} %bitcast.9, bf16[2,384,384]{2,1,0:T(8,128)(2,1)S(1)} %get-tuple-element.18.rest_0_, bf16[2,384,384]{2,1,0:T(8,128)(2,1)} %collective-permute-done.rest_1_, bf16[384,384]{1,0:T(8,128)(2,1)S(1)} %collective-permute-done.1.rest_2_, ...), custom_call_target="tpu_custom_call" | custom-call | flops 200000000 | tf_op jit(solution)/shard_map/pallas_call | solution.py:259
  92.9 19.5 %all_to_all.25 = bf16[128,8,128]{2,1,0:T(8,128)(2,1)S(1)} all-to-all(bf16[128,8,128]{2,1,0:T(8,128)(2,1)S(1)} %bitcast.10), channel_id=1, replica_groups=mesh['lat'=32,'x_hi'=2,'x_lo'=2,'z_hi'=2,'core'=2] {'x_lo','z_hi','lat'}, dimensions={0} | all-to-all | bytes 524288 | tf_op jit(solution)/shard_map/all_to_all | solution.py:336
  112.4 0.0 copy-done
  112.4 1.6 %shard_map.123 = bf16[16,72,128]{2,1,0:T(8,128)(2,1)S(1)} custom-call(bf16[1024,128]{1,0:T(8,128)(2,1)S(1)} %bitcast.11, bf16[1536,768]{1,0:T(8,128)(2,1)S(1)} %copy-done), custom_call_target="tpu_custom_call" | custom-call | flops 300000000 | tf_op jit(solution)/shard_map/pallas_call | solution.py:259
  114.0 18.4 %all_to_all.26.pieces = bf16[16,72,128]{2,1,0:T(8,128)(2,1)S(1)} all-to-all(bf16[16,72,128]{2,1,0:T(8,128)(2,1)S(1)} %shard_map.123), channel_id=1, replica_groups=mesh['lat'=32,'x_hi'=2,'x_lo'=2,'z_hi'=2,'core'=2] {'x_hi','x_lo','z_hi'..., dimensions={0} | all-to-all | bytes 589824 | tf_op jit(solution)/shard_map/all_to_all | solution.py:340
  132.5 1.1 shard_map.124
Async XLA Ops:
  2.0 29.7 %all-to-all-start = ((bf16[32,24,384]{2,1,0:T(8,128)(2,1)}), bf16[32,24,384]{2,1,0:T(8,128)(2,1)S(1)}, u32[]{:S(2)}, u32[]{:S(2)}) async-start(bf16[32,24,384]{2,1,0:T(8,128)(2,1)} %shard_map.118), calls=%async_computation | async-start | bytes 1179648 | tf_op jit(solution)/shard_map/all_to_all | solution.py:291
  21.5 37.8 %copy-start.1 = (bf16[768,1536]{1,0:T(8,128)(2,1)S(1)}, bf16[768,1536]{1,0:T(8,128)(2,1)}, u32[]{:S(2)}) copy-start(bf16[768,1536]{1,0:T(8,128)(2,1)} %constant.32.clone.table) | copy-start | bytes 7077892
  31.7 0.8 copy-start.2
  32.5 26.8 %all-to-all-start.1 = ((bf16[16,72,128]{2,1,0:T(8,128)(2,1)}), bf16[16,72,128]{2,1,0:T(8,128)(2,1)S(1)}, u32[]{:S(2)}, u32[]{:S(2)}) async-start(bf16[16,72,128]{2,1,0:T(8,128)(2,1)} %shard_map.119), calls=%async_computation.1 | async-start | bytes 589824 | tf_op jit(solution)/shard_map/all_to_all | solution.py:306
  46.5 1.1 copy-start.3
  49.9 22.4 %collective-permute-start.1 = (bf16[384,384]{1,0:T(8,128)(2,1)}, bf16[384,384]{1,0:T(8,128)(2,1)S(1)}, u32[]{:S(2)}, u32[]{:S(2)}) collective-permute-start(bf16[384,384]{1,0:T(8,128)(2,1)} %get-tuple-element.19), channel_id=1, source_target_pairs={{0,8},{8,0},{1,9},{9,1},{2,10},{10,2},{3,11},{11,3},{4,12},{12,4},... | collective-permute-start | bytes 884744 | tf_op jit(solution)/shard_map/ppermute | solution.py:315
  54.7 19.8 %collective-permute-start.2 = (bf16[384,384]{1,0:T(8,128)(2,1)}, bf16[384,384]{1,0:T(8,128)(2,1)}, u32[]{:S(2)}, u32[]{:S(2)}) collective-permute-start(bf16[384,384]{1,0:T(8,128)(2,1)} %get-tuple-element.20), channel_id=1, source_target_pairs={{0,8},{8,0},{1,9},{9,1},{2,10},{10,2},{3,11},{11,3},{4,12},{12,4},... | collective-permute-start | bytes 884744 | tf_op jit(solution)/shard_map/ppermute | solution.py:315
  56.6 22.3 %collective-permute-start = (bf16[2,384,384]{2,1,0:T(8,128)(2,1)S(1)}, bf16[2,384,384]{2,1,0:T(8,128)(2,1)}, u32[]{:S(2)}, u32[]{:S(2)}) collective-permute-start(bf16[2,384,384]{2,1,0:T(8,128)(2,1)S(1)} %get-tuple-element.18.rest_0_), channel_id=1, source_target_pairs={{0,1},{1,0},{2,3},{3,2},{4,5},{5,4},{6,7},{7,6},{8,9},{9,8},{10,11... | collective-permute-start | bytes 1769480 | tf_op jit(solution)/shard_map/ppermute | solution.py:314
  60.8 51.7 %copy-start = (bf16[1536,768]{1,0:T(8,128)(2,1)S(1)}, bf16[1536,768]{1,0:T(8,128)(2,1)}, u32[]{:S(2)}) copy-start(bf16[1536,768]{1,0:T(8,128)(2,1)} %constant.33.clone.table) | copy-start | bytes 7077892
  60.8 26.5 %all-to-all-start.2 = ((bf16[128,8,128]{2,1,0:T(8,128)(2,1)}), bf16[128,8,128]{2,1,0:T(8,128)(2,1)S(1)}, u32[]{:S(2)}, u32[]{:S(2)}) async-start(bf16[128,8,128]{2,1,0:T(8,128)(2,1)} %bitcast.5), calls=%async_computation.2 | async-start | bytes 524288 | tf_op jit(solution)/shard_map/all_to_all | solution.py:321
  72.3 4.4 %collective-permute-start.3 = (bf16[384,384]{1,0:T(8,128)(2,1)S(1)}, bf16[384,384]{1,0:T(8,128)(2,1)S(1)}, u32[]{:S(2)}, u32[]{:S(2)}) collective-permute-start(bf16[384,384]{1,0:T(8,128)(2,1)S(1)} %collective-permute-done.1.rest_2_), channel_id=1, source_target_pairs={{0,1},{1,0},{2,3},{3,2},{4,5},{5,4},{6,7},{7,6},{8,9},{9,8},{10,11... | collective-permute-start | bytes 884744 | tf_op jit(solution)/shard_map/ppermute | solution.py:316
  74.5 3.7 %collective-permute-start.4 = (bf16[384,384]{1,0:T(8,128)(2,1)}, bf16[384,384]{1,0:T(8,128)(2,1)S(1)}, u32[]{:S(2)}, u32[]{:S(2)}) collective-permute-start(bf16[384,384]{1,0:T(8,128)(2,1)} %collective-permute-done.2.rest_3_), channel_id=1, source_target_pairs={{0,1},{1,0},{2,3},{3,2},{4,5},{5,4},{6,7},{7,6},{8,9},{9,8},{10,11... | collective-permute-start | bytes 884744 | tf_op jit(solution)/shard_map/ppermute | solution.py:316
  76.6 0.7 copy-start.4
  78.2 0.7 copy-start.6
  87.3 1.0 copy-start.5
  88.3 1.0 copy-start.7
  89.2 0.9 copy-start.8

commit v17 on v14

--- a/solution.py
+++ b/solution.py
@@ -150,7 +150,7 @@
         out[128 * k + KEPT : 128 * (k + 1), :] = jnp.zeros((128 - KEPT, 128), bf16)
 
 
-def bases_kernel(place, bases, out):
+def bases_kernel(place, bases, first, second):
     m = place[0]
 
     def index(shape, axis):
@@ -168,15 +168,16 @@
     spot = index((1, NLAT), 1)
     x = 12 * (spot & 31) + X_SUB * ((spot >> 5) & 3) + (spot >> 7)
     columns = pick(index((NLAT, NLAT), 0) == x)
-    out[0] = dot(table, columns).astype(bf16)
+    first[...] = dot(table, columns).astype(bf16)
     spot = index((NLAT, 1), 0)
     row = 24 * (spot & 31) + 12 + X_SUB * ((spot >> 5) & 3) + (spot >> 7)
     chosen = pick(index((NLAT, LAT_DEV * 24), 1) == row)
     table = dot(chosen, rows)
-    out[1] = jnp.where(index((NLAT, NL), 1) >= m, table, 0.0).astype(bf16)
-
-
-def legendre_kernel(place, coeffs, tables, others, gain, out, rows):
+    second[...] = jnp.where(index((NLAT, NL), 1) >= m, table, 0.0).astype(bf16)
+
+
+def legendre_kernel(place, coeffs, *rest):
+    tables, others, (gain, out, rows) = rest[0:2], rest[2:4], rest[4:]
     core = place[1]
 
     def swapped(pair):
@@ -202,8 +203,8 @@
     gains = jnp.concatenate([half, half], axis=1)
     results = []
     for fourier, table in zip(swapped(modes), (tables, others)):
-        filtered = (dot(table[0], fourier.astype(bf16)) * gains).astype(bf16)
-        results.append(dot(table[1], filtered))
+        filtered = (dot(table[0][...], fourier.astype(bf16)) * gains).astype(bf16)
+        results.append(dot(table[1][...], filtered))
     results = swapped(results)
     for k in range(PAIRS):
         xg, cq = k // 2, k % 2
@@ -301,10 +302,10 @@
     pieces = lax.all_to_all(pieces, LON, 0, 0, tiled=True)
     mode = M_DEV * lax.axis_index(LON) + lax.axis_index("lat")
     place = jnp.stack([mode, lax.axis_index("core")]).astype(jnp.int32)
-    tables = call(bases_kernel, (2, NL, NLAT), bf16, smem=1, flops=600_000_000, moved=3_000_000)(
-        place, bases
-    )
-    others = lax.ppermute(tables, "core", [(0, 1), (1, 0)])
+    tables = call(
+        bases_kernel, [(NL, NLAT), (NLAT, NL)], bf16, smem=1, flops=600_000_000, moved=3_000_000
+    )(place, bases)
+    others = [lax.ppermute(t, "core", [(0, 1), (1, 0)]) for t in tables]
     coeffs = call(zonal_kernel, (2 * DEVS, 128), bf16, flops=300_000_000)(
         pieces, jnp.asarray(forward)
     )
@@ -316,7 +317,7 @@
         (pltpu.VMEM((2 * DEVS, 128), f32),),
         smem=1,
         flops=200_000_000,
-    )(place, coeffs.reshape(2 * DEVS, 128), tables, others, spectral_gain)
+    )(place, coeffs.reshape(2 * DEVS, 128), *tables, *others, spectral_gain)
     coeffs, back = lax.optimization_barrier((coeffs, jnp.asarray(back)))
     coeffs = lax.all_to_all(coeffs.reshape(DEVS // 2, 4, 128), LONG, 0, 0, tiled=True)
     pieces = call(inverse_kernel, (LON_DEV, Y_MAIN, 128), bf16, flops=300_000_000)(

time: 134 us -> 136 us (1.015)
  blocking collectives: 41.3 us -> 69.4 us
  waiting for transfers between devices: 32.1 us -> 16.6 us
  starting transfers between devices: 41.2 us -> 29.7 us
    all_to_all x1 -> x2, blocking collectives: 17.8 us -> 43.1 us  [on_device(): pieces = lax.all_to_all(pieces, LON, 0, 0, tiled=True)]
    all_to_all x1 -> x0, starting transfers between devices: 13.9 us -> none  [on_device(): pieces = lax.all_to_all(pieces, LON, 0, 0, tiled=True)]
    all_to_all x1 -> x0, waiting for transfers between devices: 8.43 us -> none  [on_device(): pieces = lax.all_to_all(pieces, LON, 0, 0, tiled=True)]
    all_to_all x1, waiting for transfers between devices: 13.4 us -> 5.72 us  [on_device(): lax.all_to_all(coeffs.reshape(DEVS // 2, 4, 128), LONG, 0, 0, tiled=True)]
    all_to_all x1, blocking collectives: 23.4 us -> 26.4 us  [on_device(): lax.all_to_all(coeffs.reshape(DEVS // 2, 4, 128), LONG, 0, 0, tiled=True)]
    ppermute x1 -> x2, starting transfers between devices: 2.15 us -> 4.51 us  [on_device(): others = [lax.ppermute(t, 'core', [(0, 1), (1, 0)]) for t in tables]]
  transfers between devices with their start and end apart: 4 -> 4, of which waited for: 3 -> 3; matrix products, arithmetic and copies ran while one was open for 0% -> 0% of each run, Pallas kernels for 7% -> 6%
where the time goes in v17:
time: 136 us; the launch traced here: 134 us
  blocking collectives  69.4 us (51%)
  starting transfers between devices  29.7 us (22%)
  waiting for transfers between devices  16.6 us (12%)
  Pallas kernels  15.6 us (11%)
  local copies, waits for them, and re-layouts  2.61 us (2%)
    all_to_all x2, blocking collectives, on_device(): pieces = lax.all_to_all(pieces, LON, 0, 0, tiled=True)  43.1 us
    all_to_all x1, blocking collectives, on_device(): lax.all_to_all(coeffs.reshape(DEVS // 2, 4, 128), LONG, 0, 0, tiled=True)  26.4 us
    pallas_call x7, Pallas kernels, run(): pl.pallas_call(kernel, out_shape=outs[0] if single else outs, in_specs=sp...  15.6 us
    all_to_all x1, starting transfers between devices, on_device(): bases = lax.all_to_all(bases, 'lat', 0, 0, tiled=True)  13.5 us
    all_to_all x1, starting transfers between devices, on_device(): lax.all_to_all(coeffs.reshape(DEVS // 2, 4, 128), LONG, 0, 0, tiled=True)  11.7 us
    all_to_all x1, waiting for transfers between devices, on_device(): bases = lax.all_to_all(bases, 'lat', 0, 0, tiled=True)  10.1 us
    all_to_all x1, waiting for transfers between devices, on_device(): lax.all_to_all(coeffs.reshape(DEVS // 2, 4, 128), LONG, 0, 0, tiled=True)  5.72 us
    ppermute x2, starting transfers between devices, on_device(): others = [lax.ppermute(t, 'core', [(0, 1), (1, 0)]) for t in tables]  4.51 us
  transfers between devices with their start and end apart: 4, of which 3 were waited for; matrix products, arithmetic and copies ran while one was open for 0% of the time, Pallas kernels for 6%

profile of v17, /device:TPU:1, one launch (start us, length us, event | category | flops | bytes accessed | tf_op | source)
XLA Modules:
  0.0 134.1 jit_solution(1712829390943870033)
XLA Ops:
  0.0 2.0 %shard_map.118 = bf16[32,24,384]{2,1,0:T(8,128)(2,1)} custom-call(bf16[12,23,384]{2,1,0:T(8,128)(2,1)} %bitcast.12, bf16[12,23,384]{2,1,0:T(8,128)(2,1)} %second_h.1), custom_call_target="tpu_custom_call" | custom-call | tf_op jit(solution)/shard_map/pallas_call | solution.py:255
  2.0 13.5 %all-to-all-start = ((bf16[32,24,384]{2,1,0:T(8,128)(2,1)}), bf16[32,24,384]{2,1,0:T(8,128)(2,1)S(1)}, u32[]{:S(2)}, u32[]{:S(2)}) async-start(bf16[32,24,384]{2,1,0:T(8,128)(2,1)} %shard_map.118), calls=%async_computation | async-start | bytes 1179648 | tf_op jit(solution)/shard_map/all_to_all | solution.py:287
  15.5 0.0 copy-start.1
  15.5 6.1 %shard_map.119 = bf16[16,72,128]{2,1,0:T(8,128)(2,1)} custom-call(bf16[12,90,128]{2,1,0:T(8,128)(2,1)} %saved_h, bf16[12,90,128]{2,1,0:T(8,128)(2,1)} %cotan_h.1, bf16[128,512]{1,0:T(8,128)(2,1)} %w_in_h.1, f32[1,512]{1,0:T(1,128)} %bitcast.13, bf16[512,512]{1,0:T(8,128)(2,1)} %w_mid_h.1, f32[1,512]{1,0:T(1,128)} %bitcast.14, bf16[512,128]{1,0:T(8,128)(2,1)} %w_out_h.1), custom_call_target="tpu_custom_call" | custom-call | flops 1700000000 | bytes 4000000 | tf_op jit(solution)/shard_map/pallas_call | solution.py:255
  21.6 10.1 %all-to-all-done.bases = bf16[32,24,384]{2,1,0:T(8,128)(2,1)S(1)} async-done(((bf16[32,24,384]{2,1,0:T(8,128)(2,1)}), bf16[32,24,384]{2,1,0:T(8,128)(2,1)S(1)}, u32[]{:S(2)}, u32[]{:S(2)}) %all-to-all-start) | async-done | bytes 589856 | tf_op jit(solution)/shard_map/all_to_all | solution.py:287
  31.7 26.1 %all_to_all.25.circles = bf16[16,72,128]{2,1,0:T(8,128)(2,1)S(1)} all-to-all(bf16[16,72,128]{2,1,0:T(8,128)(2,1)} %shard_map.119), channel_id=1, replica_groups=mesh['lat'=32,'pair'=8,'core'=2] {'pair','core'}, dimensions={0} | all-to-all | bytes 589824 | tf_op jit(solution)/shard_map/all_to_all | solution.py:302
  57.8 0.0 copy-done.1
  57.8 1.5 %shard_map.120 = bf16[1024,128]{1,0:T(8,128)(2,1)} custom-call(bf16[16,72,128]{2,1,0:T(8,128)(2,1)S(1)} %all_to_all.25.circles, bf16[768,1536]{1,0:T(8,128)(2,1)S(1)} %copy-done.1), custom_call_target="tpu_custom_call" | custom-call | flops 300000000 | tf_op jit(solution)/shard_map/pallas_call | solution.py:255
  59.3 11.7 %all-to-all-start.2 = ((bf16[256,4,128]{2,1,0:T(4,128)(2,1)}), bf16[256,4,128]{2,1,0:T(4,128)(2,1)S(1)}, u32[]{:S(2)}, u32[]{:S(2)}) async-start(bf16[256,4,128]{2,1,0:T(4,128)(2,1)} %bitcast.5), calls=%async_computation.2 | async-start | bytes 524288 | tf_op jit(solution)/shard_map/all_to_all | solution.py:312
  71.0 0.0 copy-start
  71.0 0.1 pad_add_fusion.place
  71.1 1.5 %shard_map.121 = (bf16[384,384]{1,0:T(8,128)(2,1)S(1)}, bf16[384,384]{1,0:T(8,128)(2,1)S(1)}) custom-call(s32[2]{0:T(128)S(1)} %pad_add_fusion.place, bf16[32,24,384]{2,1,0:T(8,128)(2,1)S(1)} %all-to-all-done.bases), custom_call_target="tpu_custom_call" | custom-call | flops 600000000 | bytes 3000000 | tf_op jit(solution)/shard_map/pallas_call | solution.py:255
  72.6 2.6 %collective-permute-start = (bf16[384,384]{1,0:T(8,128)(2,1)S(1)}, bf16[384,384]{1,0:T(8,128)(2,1)S(1)}, u32[]{:S(2)}, u32[]{:S(2)}) collective-permute-start(bf16[384,384]{1,0:T(8,128)(2,1)S(1)} %get-tuple-element.17.rest_0_), channel_id=1, source_target_pairs={{0,1},{1,0},{2,3},{3,2},{4,5},{5,4},{6,7},{7,6},{8,9},{9,8},{10,11... | collective-permute-start | bytes 884744 | tf_op jit(solution)/shard_map/ppermute | solution.py:308
  75.2 1.9 %collective-permute-start.1 = (bf16[384,384]{1,0:T(8,128)(2,1)S(1)}, bf16[384,384]{1,0:T(8,128)(2,1)S(1)}, u32[]{:S(2)}, u32[]{:S(2)}) collective-permute-start(bf16[384,384]{1,0:T(8,128)(2,1)S(1)} %get-tuple-element.18.rest_1_), channel_id=1, source_target_pairs={{0,1},{1,0},{2,3},{3,2},{4,5},{5,4},{6,7},{7,6},{8,9},{9,8},{10,11... | collective-permute-start | bytes 884744 | tf_op jit(solution)/shard_map/ppermute | solution.py:308
  77.2 0.0 copy-start.2
  77.2 0.7 copy-done.2
  77.9 0.0 collective-permute-done.rest_2_
  77.9 0.8 collective-permute-done.1.rest_3_
  78.7 5.7 %all-to-all-done.2 = bf16[256,4,128]{2,1,0:T(4,128)(2,1)S(1)} async-done(((bf16[256,4,128]{2,1,0:T(4,128)(2,1)}), bf16[256,4,128]{2,1,0:T(4,128)(2,1)S(1)}, u32[]{:S(2)}, u32[]{:S(2)}) %all-to-all-start.2) | async-done | bytes 262176 | tf_op jit(solution)/shard_map/all_to_all | solution.py:312
  84.4 0.0 copy-start.3
  84.4 1.0 copy-done.3
  85.4 0.0 copy-start.4
  85.4 0.9 copy-done.4
  86.3 1.8 %shard_map.122 = bf16[1024,128]{1,0:T(8,128)(2,1)S(1)} custom-call(s32[2]{0:T(128)S(1)} %pad_add_fusion.place, bf16[1024,128]{1,0:T(8,128)(2,1)S(1)} %bitcast.10, bf16[384,384]{1,0:T(8,128)(2,1)S(1)} %get-tuple-element.17.rest_0_, bf16[384,384]{1,0:T(8,128)(2,1)S(1)} %copy-done.3, bf16[384,384]{1,0:T(8,128)(2,1)S(1)} %collective-permute-done.rest_2_, ...), custom_call_target="tpu_custom_call" | custom-call | flops 200000000 | tf_op jit(solution)/shard_map/pallas_call | solution.py:255
  88.1 26.4 %all_to_all.26 = bf16[256,4,128]{2,1,0:T(4,128)(2,1)S(1)} all-to-all(bf16[256,4,128]{2,1,0:T(4,128)(2,1)S(1)} %bitcast.11), channel_id=1, replica_groups=mesh['lat'=32,'pair'=8,'core'=2] {'pair','lat'}, dimensions={0} | all-to-all | bytes 524288 | tf_op jit(solution)/shard_map/all_to_all | solution.py:322
  114.5 0.0 copy-done
  114.5 1.6 %shard_map.123 = bf16[16,72,128]{2,1,0:T(8,128)(2,1)S(1)} custom-call(bf16[1024,128]{1,0:T(8,128)(2,1)S(1)} %bitcast.9, bf16[1536,768]{1,0:T(8,128)(2,1)S(1)} %copy-done), custom_call_target="tpu_custom_call" | custom-call | flops 300000000 | tf_op jit(solution)/shard_map/pallas_call | solution.py:255
  116.1 17.0 %all_to_all.27.pieces = bf16[16,72,128]{2,1,0:T(8,128)(2,1)S(1)} all-to-all(bf16[16,72,128]{2,1,0:T(8,128)(2,1)S(1)} %shard_map.123), channel_id=1, replica_groups=mesh['lat'=32,'pair'=8,'core'=2] {'pair','core'}, dimensions={0} | all-to-all | bytes 589824 | tf_op jit(solution)/shard_map/all_to_all | solution.py:326
  133.0 1.1 shard_map.124
Async XLA Ops:
  2.0 29.7 %all-to-all-start = ((bf16[32,24,384]{2,1,0:T(8,128)(2,1)}), bf16[32,24,384]{2,1,0:T(8,128)(2,1)S(1)}, u32[]{:S(2)}, u32[]{:S(2)}) async-start(bf16[32,24,384]{2,1,0:T(8,128)(2,1)} %shard_map.118), calls=%async_computation | async-start | bytes 1179648 | tf_op jit(solution)/shard_map/all_to_all | solution.py:287
  15.5 42.3 %copy-start.1 = (bf16[768,1536]{1,0:T(8,128)(2,1)S(1)}, bf16[768,1536]{1,0:T(8,128)(2,1)}, u32[]{:S(2)}) copy-start(bf16[768,1536]{1,0:T(8,128)(2,1)} %constant.22.clone.table) | copy-start | bytes 7077892
  59.3 25.2 %all-to-all-start.2 = ((bf16[256,4,128]{2,1,0:T(4,128)(2,1)}), bf16[256,4,128]{2,1,0:T(4,128)(2,1)S(1)}, u32[]{:S(2)}, u32[]{:S(2)}) async-start(bf16[256,4,128]{2,1,0:T(4,128)(2,1)} %bitcast.5), calls=%async_computation.2 | async-start | bytes 524288 | tf_op jit(solution)/shard_map/all_to_all | solution.py:312
  71.0 43.5 %copy-start = (bf16[1536,768]{1,0:T(8,128)(2,1)S(1)}, bf16[1536,768]{1,0:T(8,128)(2,1)}, u32[]{:S(2)}) copy-start(bf16[1536,768]{1,0:T(8,128)(2,1)} %constant.23.clone.table) | copy-start | bytes 7077892
  72.6 5.2 %collective-permute-start = (bf16[384,384]{1,0:T(8,128)(2,1)S(1)}, bf16[384,384]{1,0:T(8,128)(2,1)S(1)}, u32[]{:S(2)}, u32[]{:S(2)}) collective-permute-start(bf16[384,384]{1,0:T(8,128)(2,1)S(1)} %get-tuple-element.17.rest_0_), channel_id=1, source_target_pairs={{0,1},{1,0},{2,3},{3,2},{4,5},{5,4},{6,7},{7,6},{8,9},{9,8},{10,11... | collective-permute-start | bytes 884744 | tf_op jit(solution)/shard_map/ppermute | solution.py:308
  75.2 3.5 %collective-permute-start.1 = (bf16[384,384]{1,0:T(8,128)(2,1)S(1)}, bf16[384,384]{1,0:T(8,128)(2,1)S(1)}, u32[]{:S(2)}, u32[]{:S(2)}) collective-permute-start(bf16[384,384]{1,0:T(8,128)(2,1)S(1)} %get-tuple-element.18.rest_1_), channel_id=1, source_target_pairs={{0,1},{1,0},{2,3},{3,2},{4,5},{5,4},{6,7},{7,6},{8,9},{9,8},{10,11... | collective-permute-start | bytes 884744 | tf_op jit(solution)/shard_map/ppermute | solution.py:308
  77.2 0.7 copy-start.2
  84.4 1.0 copy-start.3
  85.4 0.9 copy-start.4

commit v18 on v14

--- a/solution.py
+++ b/solution.py
@@ -65,25 +65,6 @@
 
 def sigmoid(v):
     return 0.5 * jnp.tanh(0.5 * v) + 0.5
-
-
-def arrange_kernel(first_h, second_h, out, first, second, rows, sems):
-    copies = [
-        pltpu.make_async_copy(first_h, first, sems.at[0]),
-        pltpu.make_async_copy(second_h, second, sems.at[1]),
-    ]
-    for copy in copies:
-        copy.start()
-    out[M_DEV:] = jnp.zeros((LAT_DEV - M_DEV, 24, NL), bf16)
-    for half, source in enumerate((first, second)):
-        copies[half].wait()
-        for k in range(12):
-            block = source[k].astype(f32)
-            for t in range(3):
-                rows[t, pl.ds(12 * half + k, M_DEV, stride=24), :] = block[:, 128 * t : 128 * (t + 1)]
-    for m in range(M_DEV):
-        for t in range(3):
-            out[m, :, 128 * t : 128 * (t + 1)] = rows[t, 24 * m : 24 * (m + 1), :].astype(bf16)
 
 
 def network_kernel(
@@ -264,24 +245,14 @@
     return run
 
 
-def arrange(first, second):
-    shape = pltpu.VMEM((12, M_DEV, NL), bf16)
-    rows = pltpu.VMEM((3, M_DEV * 24, 128), f32)
-    return call(
-        arrange_kernel,
-        (LAT_DEV, 24, NL),
-        bf16,
-        (shape, shape, rows, pltpu.SemaphoreType.DMA((2,))),
-        space=pltpu.HBM,
-        limit=NETWORK_VMEM,
-    )(first, second)
-
-
 def on_device(
     saved, cotangent, w_in, b_in, w_mid, b_mid, w_out, spectral_gain, basis_in, basis_out
 ):
     forward, back = zonal_tables()
-    bases = arrange(jnp.transpose(basis_in, (2, 1, 0)), basis_out)
+    bases = jnp.concatenate(
+        [jnp.transpose(basis_in, (1, 2, 0)), jnp.transpose(basis_out, (1, 0, 2))], axis=1
+    )
+    bases = jnp.pad(bases, ((0, LAT_DEV - M_DEV), (0, 0), (0, 0)))
     bases, saved = lax.optimization_barrier((bases, saved))
     bases = lax.all_to_all(bases, "lat", 0, 0, tiled=True)
     weights = (w_in, b_in.reshape(1, -1), w_mid, b_mid.reshape(1, -1), w_out)

time: 134 us -> 134 us (level)
    pallas_call x7 -> x6, Pallas kernels: 16 us -> 14.9 us  [run(): pl.pallas_call(kernel, out_shape=outs[0] if single else outs, in_specs=sp...]
where the time goes in v18:
time: 134 us; the launch traced here: 132 us
  starting transfers between devices  41.3 us (31%)
  blocking collectives  41.3 us (31%)
  waiting for transfers between devices  31.3 us (23%)
  Pallas kernels  14.9 us (11%)
  local copies, waits for them, and re-layouts  1.96 us (1%)
    all_to_all x1, blocking collectives, on_device(): lax.all_to_all(coeffs.reshape(DEVS // 2, 4, 128), LONG, 0, 0, tiled=True)  23.4 us
    all_to_all x1, blocking collectives, on_device(): pieces = lax.all_to_all(pieces, LON, 0, 0, tiled=True)  17.8 us
    pallas_call x6, Pallas kernels, run(): pl.pallas_call(kernel, out_shape=outs[0] if single else outs, in_specs=sp...  14.9 us
    all_to_all x1, starting transfers between devices, on_device(): pieces = lax.all_to_all(pieces, LON, 0, 0, tiled=True)  14 us
    all_to_all x1, starting transfers between devices, on_device(): bases = lax.all_to_all(bases, 'lat', 0, 0, tiled=True)  13.5 us
    all_to_all x1, waiting for transfers between devices, on_device(): lax.all_to_all(coeffs.reshape(DEVS // 2, 4, 128), LONG, 0, 0, tiled=True)  13.4 us
    all_to_all x1, starting transfers between devices, on_device(): lax.all_to_all(coeffs.reshape(DEVS // 2, 4, 128), LONG, 0, 0, tiled=True)  11.7 us
    all_to_all x1, waiting for transfers between devices, on_device(): bases = lax.all_to_all(bases, 'lat', 0, 0, tiled=True)  10.2 us
  transfers between devices with their start and end apart: 4, of which 3 were waited for; matrix products, arithmetic and copies ran while one was open for 0% of the time, Pallas kernels for 7%

profile of v18, /device:TPU:1, one launch (start us, length us, event | category | flops | bytes accessed | tf_op | source)
XLA Modules:
  0.0 131.9 jit_solution(802348743338859326)
XLA Ops:
  0.0 1.0 copy.18
  1.0 1.0 copy.17
  2.0 0.9 fusion.2
  2.9 13.5 %all-to-all-start = ((bf16[32,24,384]{2,1,0:T(8,128)(2,1)}), bf16[32,24,384]{2,1,0:T(8,128)(2,1)S(1)}, u32[]{:S(2)}, u32[]{:S(2)}) async-start(bf16[32,24,384]{2,1,0:T(8,128)(2,1)} %fusion.2), calls=%async_computation | async-start | bytes 1179648 | tf_op jit(solution)/shard_map/all_to_all | solution.py:257
  16.4 5.9 %shard_map.118 = bf16[16,72,128]{2,1,0:T(8,128)(2,1)} custom-call(bf16[12,90,128]{2,1,0:T(8,128)(2,1)} %saved_h, bf16[12,90,128]{2,1,0:T(8,128)(2,1)} %cotan_h.1, bf16[128,512]{1,0:T(8,128)(2,1)} %w_in_h.1, f32[1,512]{1,0:T(1,128)} %bitcast.19, bf16[512,512]{1,0:T(8,128)(2,1)} %w_mid_h.1, f32[1,512]{1,0:T(1,128)} %bitcast.20, bf16[512,128]{1,0:T(8,128)(2,1)} %w_out_h.1), custom_call_target="tpu_custom_call" | custom-call | flops 1700000000 | bytes 4000000 | tf_op jit(solution)/shard_map/pallas_call | solution.py:235
  22.3 10.2 %all-to-all-done.bases = bf16[32,24,384]{2,1,0:T(8,128)(2,1)S(1)} async-done(((bf16[32,24,384]{2,1,0:T(8,128)(2,1)}), bf16[32,24,384]{2,1,0:T(8,128)(2,1)S(1)}, u32[]{:S(2)}, u32[]{:S(2)}) %all-to-all-start) | async-done | bytes 589856 | tf_op jit(solution)/shard_map/all_to_all | solution.py:257
  32.5 0.0 copy-start.1
  32.5 14.0 %all-to-all-start.1 = ((bf16[16,72,128]{2,1,0:T(8,128)(2,1)}), bf16[16,72,128]{2,1,0:T(8,128)(2,1)S(1)}, u32[]{:S(2)}, u32[]{:S(2)}) async-start(bf16[16,72,128]{2,1,0:T(8,128)(2,1)} %shard_map.118), calls=%async_computation.1 | async-start | bytes 589824 | tf_op jit(solution)/shard_map/all_to_all | solution.py:272
  46.6 0.1 pad_add_fusion.place
  46.6 2.4 %shard_map.120.tables = bf16[2,384,384]{2,1,0:T(8,128)(2,1)} custom-call(s32[2]{0:T(128)S(1)} %pad_add_fusion.place, bf16[32,24,384]{2,1,0:T(8,128)(2,1)S(1)} %all-to-all-done.bases), custom_call_target="tpu_custom_call" | custom-call | flops 600000000 | bytes 3000000 | tf_op jit(solution)/shard_map/pallas_call | solution.py:235
  49.0 0.0 copy-start.2
  49.0 2.1 %collective-permute-start = (bf16[2,384,384]{2,1,0:T(8,128)(2,1)}, bf16[2,384,384]{2,1,0:T(8,128)(2,1)S(1)}, u32[]{:S(2)}, u32[]{:S(2)}) collective-permute-start(bf16[2,384,384]{2,1,0:T(8,128)(2,1)} %shard_map.120.tables), channel_id=1, source_target_pairs={{0,1},{1,0},{2,3},{3,2},{4,5},{5,4},{6,7},{7,6},{8,9},{9,8},{10,11... | collective-permute-start | bytes 1769480 | tf_op jit(solution)/shard_map/ppermute | solution.py:278
  51.1 7.6 %all-to-all-done.1.circles = bf16[16,72,128]{2,1,0:T(8,128)(2,1)S(1)} async-done(((bf16[16,72,128]{2,1,0:T(8,128)(2,1)}), bf16[16,72,128]{2,1,0:T(8,128)(2,1)S(1)}, u32[]{:S(2)}, u32[]{:S(2)}) %all-to-all-start.1) | async-done | bytes 294944 | tf_op jit(solution)/shard_map/all_to_all | solution.py:272
  58.8 0.0 copy-done.1
  58.8 1.5 %shard_map.119 = bf16[1024,128]{1,0:T(8,128)(2,1)} custom-call(bf16[16,72,128]{2,1,0:T(8,128)(2,1)S(1)} %all-to-all-done.1.circles, bf16[768,1536]{1,0:T(8,128)(2,1)S(1)} %copy-done.1), custom_call_target="tpu_custom_call" | custom-call | flops 300000000 | tf_op jit(solution)/shard_map/pallas_call | solution.py:235
  60.3 11.7 %all-to-all-start.2 = ((bf16[256,4,128]{2,1,0:T(4,128)(2,1)}), bf16[256,4,128]{2,1,0:T(4,128)(2,1)S(1)}, u32[]{:S(2)}, u32[]{:S(2)}) async-start(bf16[256,4,128]{2,1,0:T(4,128)(2,1)} %bitcast.6), calls=%async_computation.2 | async-start | bytes 524288 | tf_op jit(solution)/shard_map/all_to_all | solution.py:282
  72.0 0.0 collective-permute-done.others
  72.0 13.4 %all-to-all-done.2 = bf16[256,4,128]{2,1,0:T(4,128)(2,1)S(1)} async-done(((bf16[256,4,128]{2,1,0:T(4,128)(2,1)}), bf16[256,4,128]{2,1,0:T(4,128)(2,1)S(1)}, u32[]{:S(2)}, u32[]{:S(2)}) %all-to-all-start.2) | async-done | bytes 262176 | tf_op jit(solution)/shard_map/all_to_all | solution.py:282
  85.4 0.0 copy-done.2
  85.4 0.0 copy-start
  85.4 2.5 %shard_map.121 = bf16[1024,128]{1,0:T(8,128)(2,1)S(1)} custom-call(s32[2]{0:T(128)S(1)} %pad_add_fusion.place, bf16[1024,128]{1,0:T(8,128)(2,1)S(1)} %bitcast.15, bf16[2,384,384]{2,1,0:T(8,128)(2,1)} %shard_map.120.tables, bf16[2,384,384]{2,1,0:T(8,128)(2,1)S(1)} %collective-permute-done.others, f32[384,128]{1,0:T(8,128)S(1)} %copy-done.2), custom_call_target="tpu_custom_call" | custom-call | flops 200000000 | tf_op jit(solution)/shard_map/pallas_call | solution.py:235
  87.9 23.4 %all_to_all.25 = bf16[256,4,128]{2,1,0:T(4,128)(2,1)S(1)} all-to-all(bf16[256,4,128]{2,1,0:T(4,128)(2,1)S(1)} %bitcast.16), channel_id=1, replica_groups=mesh['lat'=32,'pair'=8,'core'=2] {'pair','lat'}, dimensions={0} | all-to-all | bytes 524288 | tf_op jit(solution)/shard_map/all_to_all | solution.py:292
  111.3 0.0 copy-done
  111.3 1.6 %shard_map.122 = bf16[16,72,128]{2,1,0:T(8,128)(2,1)S(1)} custom-call(bf16[1024,128]{1,0:T(8,128)(2,1)S(1)} %bitcast.14, bf16[1536,768]{1,0:T(8,128)(2,1)S(1)} %copy-done), custom_call_target="tpu_custom_call" | custom-call | flops 300000000 | tf_op jit(solution)/shard_map/pallas_call | solution.py:235
  112.9 17.8 %all_to_all.26.pieces = bf16[16,72,128]{2,1,0:T(8,128)(2,1)S(1)} all-to-all(bf16[16,72,128]{2,1,0:T(8,128)(2,1)S(1)} %shard_map.122), channel_id=1, replica_groups=mesh['lat'=32,'pair'=8,'core'=2] {'pair','core'}, dimensions={0} | all-to-all | bytes 589824 | tf_op jit(solution)/shard_map/all_to_all | solution.py:296
  130.7 1.1 shard_map.123
Async XLA Ops:
  2.9 29.6 %all-to-all-start = ((bf16[32,24,384]{2,1,0:T(8,128)(2,1)}), bf16[32,24,384]{2,1,0:T(8,128)(2,1)S(1)}, u32[]{:S(2)}, u32[]{:S(2)}) async-start(bf16[32,24,384]{2,1,0:T(8,128)(2,1)} %fusion.2), calls=%async_computation | async-start | bytes 1179648 | tf_op jit(solution)/shard_map/all_to_all | solution.py:257
  32.5 26.3 %copy-start.1 = (bf16[768,1536]{1,0:T(8,128)(2,1)S(1)}, bf16[768,1536]{1,0:T(8,128)(2,1)}, u32[]{:S(2)}) copy-start(bf16[768,1536]{1,0:T(8,128)(2,1)} %constant.25.clone.table) | copy-start | bytes 7077892
  32.5 26.2 %all-to-all-start.1 = ((bf16[16,72,128]{2,1,0:T(8,128)(2,1)}), bf16[16,72,128]{2,1,0:T(8,128)(2,1)S(1)}, u32[]{:S(2)}, u32[]{:S(2)}) async-start(bf16[16,72,128]{2,1,0:T(8,128)(2,1)} %shard_map.118), calls=%async_computation.1 | async-start | bytes 589824 | tf_op jit(solution)/shard_map/all_to_all | solution.py:272
  49.0 36.4 %copy-start.2 = (f32[384,128]{1,0:T(8,128)S(1)}, f32[384,128]{1,0:T(8,128)}, u32[]{:S(2)}) copy-start(f32[384,128]{1,0:T(8,128)} %gain.1) | copy-start | bytes 589828
  49.0 23.0 %collective-permute-start = (bf16[2,384,384]{2,1,0:T(8,128)(2,1)}, bf16[2,384,384]{2,1,0:T(8,128)(2,1)S(1)}, u32[]{:S(2)}, u32[]{:S(2)}) collective-permute-start(bf16[2,384,384]{2,1,0:T(8,128)(2,1)} %shard_map.120.tables), channel_id=1, source_target_pairs={{0,1},{1,0},{2,3},{3,2},{4,5},{5,4},{6,7},{7,6},{8,9},{9,8},{10,11... | collective-permute-start | bytes 1769480 | tf_op jit(solution)/shard_map/ppermute | solution.py:278
  60.3 25.2 %all-to-all-start.2 = ((bf16[256,4,128]{2,1,0:T(4,128)(2,1)}), bf16[256,4,128]{2,1,0:T(4,128)(2,1)S(1)}, u32[]{:S(2)}, u32[]{:S(2)}) async-start(bf16[256,4,128]{2,1,0:T(4,128)(2,1)} %bitcast.6), calls=%async_computation.2 | async-start | bytes 524288 | tf_op jit(solution)/shard_map/all_to_all | solution.py:282
  85.4 25.9 %copy-start = (bf16[1536,768]{1,0:T(8,128)(2,1)S(1)}, bf16[1536,768]{1,0:T(8,128)(2,1)}, u32[]{:S(2)}) copy-start(bf16[1536,768]{1,0:T(8,128)(2,1)} %constant.26.clone.table) | copy-start | bytes 7077892

commit v19 on v18

--- a/solution.py
+++ b/solution.py
@@ -211,7 +211,8 @@
         out[j] = jnp.concatenate([main, jnp.concatenate(parts, axis=0)], axis=1).astype(bf16)
 
 
-def grid_kernel(pieces, out):
+def grid_kernel(pieces, out_h, out, sems):
+    copies = []
     for xg in range(XG):
         blocks = [pieces[owner(xg, cg)].astype(f32) for cg in range(CG)]
         for xx in range(X_SUB):
@@ -219,13 +220,18 @@
             extra = [b[Y_EXT * xx : Y_EXT * (xx + 1), 96:128] for b in blocks]
             out[X_SUB * xg + xx, 0:Y_MAIN, :] = jnp.concatenate(main, axis=1)
             out[X_SUB * xg + xx, Y_MAIN:, :] = jnp.concatenate(extra, axis=1)[0 : Y_DEV - Y_MAIN]
+        rows = pl.ds(X_SUB * xg, X_SUB)
+        copies.append(pltpu.make_async_copy(out.at[rows], out_h.at[rows], sems.at[xg]))
+        copies[-1].start()
+    for copy in copies:
+        copy.wait()
 
 
 def call(
-    kernel, shape, dtype, scratch=(), smem=0, space=pltpu.VMEM, flops=0, moved=0, limit=VMEM
+    kernel, shape, dtype, scratch=(), smem=0, space=pltpu.VMEM, flops=0, moved=0, limit=VMEM, out_space=pltpu.VMEM
 ):
     outs = [jax.ShapeDtypeStruct(s, dtype) for s in (shape if isinstance(shape, list) else [shape])]
-    places = [pl.BlockSpec(memory_space=pltpu.VMEM) for _ in outs]
+    places = [pl.BlockSpec(memory_space=out_space) for _ in outs]
     single = not isinstance(shape, list)
 
     def run(*args):
@@ -294,7 +300,8 @@
         coeffs.reshape(2 * DEVS, 128), back
     )
     pieces = lax.all_to_all(pieces, LON, 0, 0, tiled=True)
-    return call(grid_kernel, (X_DEV, Y_DEV, CHAN), f32)(pieces)
+    held = (pltpu.VMEM((X_DEV, Y_DEV, CHAN), f32), pltpu.SemaphoreType.DMA((XG,)))
+    return call(grid_kernel, (X_DEV, Y_DEV, CHAN), f32, held, out_space=pltpu.HBM)(pieces)
 
 
 def solution(mesh):

time: 134 us -> 134 us (level)
  no operation moved by 1% of the time
where the time goes in v19:
time: 134 us; the launch traced here: 132 us
  starting transfers between devices  41.3 us (31%)
  blocking collectives  41.3 us (31%)
  waiting for transfers between devices  31.3 us (23%)
  Pallas kernels  14.8 us (11%)
  local copies, waits for them, and re-layouts  1.96 us (1%)
    all_to_all x1, blocking collectives, on_device(): lax.all_to_all(coeffs.reshape(DEVS // 2, 4, 128), LONG, 0, 0, tiled=True)  23.4 us
    all_to_all x1, blocking collectives, on_device(): pieces = lax.all_to_all(pieces, LON, 0, 0, tiled=True)  17.8 us
    pallas_call x6, Pallas kernels, run(): pl.pallas_call(kernel, out_shape=outs[0] if single else outs, in_specs=sp...  14.8 us
    all_to_all x1, starting transfers between devices, on_device(): pieces = lax.all_to_all(pieces, LON, 0, 0, tiled=True)  14 us
    all_to_all x1, starting transfers between devices, on_device(): bases = lax.all_to_all(bases, 'lat', 0, 0, tiled=True)  13.5 us
    all_to_all x1, waiting for transfers between devices, on_device(): lax.all_to_all(coeffs.reshape(DEVS // 2, 4, 128), LONG, 0, 0, tiled=True)  13.4 us
    all_to_all x1, starting transfers between devices, on_device(): lax.all_to_all(coeffs.reshape(DEVS // 2, 4, 128), LONG, 0, 0, tiled=True)  11.7 us
    all_to_all x1, waiting for transfers between devices, on_device(): bases = lax.all_to_all(bases, 'lat', 0, 0, tiled=True)  10.2 us
  transfers between devices with their start and end apart: 4, of which 3 were waited for; matrix products, arithmetic and copies ran while one was open for 0% of the time, Pallas kernels for 7%

profile of v19, /device:TPU:1, one launch (start us, length us, event | category | flops | bytes accessed | tf_op | source)
XLA Modules:
  0.0 131.9 jit_solution(15793663190597508500)
XLA Ops:
  0.0 1.0 copy.18
  1.0 1.0 copy.17
  2.0 0.9 fusion.2
  2.9 13.5 %all-to-all-start = ((bf16[32,24,384]{2,1,0:T(8,128)(2,1)}), bf16[32,24,384]{2,1,0:T(8,128)(2,1)S(1)}, u32[]{:S(2)}, u32[]{:S(2)}) async-start(bf16[32,24,384]{2,1,0:T(8,128)(2,1)} %fusion.2), calls=%async_computation | async-start | bytes 1179648 | tf_op jit(solution)/shard_map/all_to_all | solution.py:263
  16.4 5.9 %shard_map.118 = bf16[16,72,128]{2,1,0:T(8,128)(2,1)} custom-call(bf16[12,90,128]{2,1,0:T(8,128)(2,1)} %saved_h, bf16[12,90,128]{2,1,0:T(8,128)(2,1)} %cotan_h.1, bf16[128,512]{1,0:T(8,128)(2,1)} %w_in_h.1, f32[1,512]{1,0:T(1,128)} %bitcast.19, bf16[512,512]{1,0:T(8,128)(2,1)} %w_mid_h.1, f32[1,512]{1,0:T(1,128)} %bitcast.20, bf16[512,128]{1,0:T(8,128)(2,1)} %w_out_h.1), custom_call_target="tpu_custom_call" | custom-call | flops 1700000000 | bytes 4000000 | tf_op jit(solution)/shard_map/pallas_call | solution.py:241
  22.3 10.2 %all-to-all-done.bases = bf16[32,24,384]{2,1,0:T(8,128)(2,1)S(1)} async-done(((bf16[32,24,384]{2,1,0:T(8,128)(2,1)}), bf16[32,24,384]{2,1,0:T(8,128)(2,1)S(1)}, u32[]{:S(2)}, u32[]{:S(2)}) %all-to-all-start) | async-done | bytes 589856 | tf_op jit(solution)/shard_map/all_to_all | solution.py:263
  32.5 0.0 copy-start.1
  32.5 14.0 %all-to-all-start.1 = ((bf16[16,72,128]{2,1,0:T(8,128)(2,1)}), bf16[16,72,128]{2,1,0:T(8,128)(2,1)S(1)}, u32[]{:S(2)}, u32[]{:S(2)}) async-start(bf16[16,72,128]{2,1,0:T(8,128)(2,1)} %shard_map.118), calls=%async_computation.1 | async-start | bytes 589824 | tf_op jit(solution)/shard_map/all_to_all | solution.py:278
  46.6 0.1 pad_add_fusion.place
  46.6 2.4 %shard_map.120.tables = bf16[2,384,384]{2,1,0:T(8,128)(2,1)} custom-call(s32[2]{0:T(128)S(1)} %pad_add_fusion.place, bf16[32,24,384]{2,1,0:T(8,128)(2,1)S(1)} %all-to-all-done.bases), custom_call_target="tpu_custom_call" | custom-call | flops 600000000 | bytes 3000000 | tf_op jit(solution)/shard_map/pallas_call | solution.py:241
  49.0 0.0 copy-start.2
  49.0 2.1 %collective-permute-start = (bf16[2,384,384]{2,1,0:T(8,128)(2,1)}, bf16[2,384,384]{2,1,0:T(8,128)(2,1)S(1)}, u32[]{:S(2)}, u32[]{:S(2)}) collective-permute-start(bf16[2,384,384]{2,1,0:T(8,128)(2,1)} %shard_map.120.tables), channel_id=1, source_target_pairs={{0,1},{1,0},{2,3},{3,2},{4,5},{5,4},{6,7},{7,6},{8,9},{9,8},{10,11... | collective-permute-start | bytes 1769480 | tf_op jit(solution)/shard_map/ppermute | solution.py:284
  51.1 7.6 %all-to-all-done.1.circles = bf16[16,72,128]{2,1,0:T(8,128)(2,1)S(1)} async-done(((bf16[16,72,128]{2,1,0:T(8,128)(2,1)}), bf16[16,72,128]{2,1,0:T(8,128)(2,1)S(1)}, u32[]{:S(2)}, u32[]{:S(2)}) %all-to-all-start.1) | async-done | bytes 294944 | tf_op jit(solution)/shard_map/all_to_all | solution.py:278
  58.8 0.0 copy-done.1
  58.8 1.5 %shard_map.119 = bf16[1024,128]{1,0:T(8,128)(2,1)} custom-call(bf16[16,72,128]{2,1,0:T(8,128)(2,1)S(1)} %all-to-all-done.1.circles, bf16[768,1536]{1,0:T(8,128)(2,1)S(1)} %copy-done.1), custom_call_target="tpu_custom_call" | custom-call | flops 300000000 | tf_op jit(solution)/shard_map/pallas_call | solution.py:241
  60.3 11.7 %all-to-all-start.2 = ((bf16[256,4,128]{2,1,0:T(4,128)(2,1)}), bf16[256,4,128]{2,1,0:T(4,128)(2,1)S(1)}, u32[]{:S(2)}, u32[]{:S(2)}) async-start(bf16[256,4,128]{2,1,0:T(4,128)(2,1)} %bitcast.6), calls=%async_computation.2 | async-start | bytes 524288 | tf_op jit(solution)/shard_map/all_to_all | solution.py:288
  72.0 0.0 collective-permute-done.others
  72.0 13.4 %all-to-all-done.2 = bf16[256,4,128]{2,1,0:T(4,128)(2,1)S(1)} async-done(((bf16[256,4,128]{2,1,0:T(4,128)(2,1)}), bf16[256,4,128]{2,1,0:T(4,128)(2,1)S(1)}, u32[]{:S(2)}, u32[]{:S(2)}) %all-to-all-start.2) | async-done | bytes 262176 | tf_op jit(solution)/shard_map/all_to_all | solution.py:288
  85.4 0.0 copy-done.2
  85.4 0.0 copy-start
  85.4 2.5 %shard_map.121 = bf16[1024,128]{1,0:T(8,128)(2,1)S(1)} custom-call(s32[2]{0:T(128)S(1)} %pad_add_fusion.place, bf16[1024,128]{1,0:T(8,128)(2,1)S(1)} %bitcast.15, bf16[2,384,384]{2,1,0:T(8,128)(2,1)} %shard_map.120.tables, bf16[2,384,384]{2,1,0:T(8,128)(2,1)S(1)} %collective-permute-done.others, f32[384,128]{1,0:T(8,128)S(1)} %copy-done.2), custom_call_target="tpu_custom_call" | custom-call | flops 200000000 | tf_op jit(solution)/shard_map/pallas_call | solution.py:241
  87.9 23.4 %all_to_all.25 = bf16[256,4,128]{2,1,0:T(4,128)(2,1)S(1)} all-to-all(bf16[256,4,128]{2,1,0:T(4,128)(2,1)S(1)} %bitcast.16), channel_id=1, replica_groups=mesh['lat'=32,'pair'=8,'core'=2] {'pair','lat'}, dimensions={0} | all-to-all | bytes 524288 | tf_op jit(solution)/shard_map/all_to_all | solution.py:298
  111.3 0.0 copy-done
  111.3 1.6 %shard_map.122 = bf16[16,72,128]{2,1,0:T(8,128)(2,1)S(1)} custom-call(bf16[1024,128]{1,0:T(8,128)(2,1)S(1)} %bitcast.14, bf16[1536,768]{1,0:T(8,128)(2,1)S(1)} %copy-done), custom_call_target="tpu_custom_call" | custom-call | flops 300000000 | tf_op jit(solution)/shard_map/pallas_call | solution.py:241
  112.9 17.8 %all_to_all.26.pieces = bf16[16,72,128]{2,1,0:T(8,128)(2,1)S(1)} all-to-all(bf16[16,72,128]{2,1,0:T(8,128)(2,1)S(1)} %shard_map.122), channel_id=1, replica_groups=mesh['lat'=32,'pair'=8,'core'=2] {'pair','core'}, dimensions={0} | all-to-all | bytes 589824 | tf_op jit(solution)/shard_map/all_to_all | solution.py:302
  130.7 1.0 shard_map.123
Async XLA Ops:
  2.9 29.6 %all-to-all-start = ((bf16[32,24,384]{2,1,0:T(8,128)(2,1)}), bf16[32,24,384]{2,1,0:T(8,128)(2,1)S(1)}, u32[]{:S(2)}, u32[]{:S(2)}) async-start(bf16[32,24,384]{2,1,0:T(8,128)(2,1)} %fusion.2), calls=%async_computation | async-start | bytes 1179648 | tf_op jit(solution)/shard_map/all_to_all | solution.py:263
  32.5 26.3 %copy-start.1 = (bf16[768,1536]{1,0:T(8,128)(2,1)S(1)}, bf16[768,1536]{1,0:T(8,128)(2,1)}, u32[]{:S(2)}) copy-start(bf16[768,1536]{1,0:T(8,128)(2,1)} %constant.25.clone.table) | copy-start | bytes 7077892
  32.5 26.2 %all-to-all-start.1 = ((bf16[16,72,128]{2,1,0:T(8,128)(2,1)}), bf16[16,72,128]{2,1,0:T(8,128)(2,1)S(1)}, u32[]{:S(2)}, u32[]{:S(2)}) async-start(bf16[16,72,128]{2,1,0:T(8,128)(2,1)} %shard_map.118), calls=%async_computation.1 | async-start | bytes 589824 | tf_op jit(solution)/shard_map/all_to_all | solution.py:278
  49.0 36.4 %copy-start.2 = (f32[384,128]{1,0:T(8,128)S(1)}, f32[384,128]{1,0:T(8,128)}, u32[]{:S(2)}) copy-start(f32[384,128]{1,0:T(8,128)} %gain.1) | copy-start | bytes 589828
  49.0 23.0 %collective-permute-start = (bf16[2,384,384]{2,1,0:T(8,128)(2,1)}, bf16[2,384,384]{2,1,0:T(8,128)(2,1)S(1)}, u32[]{:S(2)}, u32[]{:S(2)}) collective-permute-start(bf16[2,384,384]{2,1,0:T(8,128)(2,1)} %shard_map.120.tables), channel_id=1, source_target_pairs={{0,1},{1,0},{2,3},{3,2},{4,5},{5,4},{6,7},{7,6},{8,9},{9,8},{10,11... | collective-permute-start | bytes 1769480 | tf_op jit(solution)/shard_map/ppermute | solution.py:284
  60.3 25.2 %all-to-all-start.2 = ((bf16[256,4,128]{2,1,0:T(4,128)(2,1)}), bf16[256,4,128]{2,1,0:T(4,128)(2,1)S(1)}, u32[]{:S(2)}, u32[]{:S(2)}) async-start(bf16[256,4,128]{2,1,0:T(4,128)(2,1)} %bitcast.6), calls=%async_computation.2 | async-start | bytes 524288 | tf_op jit(solution)/shard_map/all_to_all | solution.py:288
  85.4 25.9 %copy-start = (bf16[1536,768]{1,0:T(8,128)(2,1)S(1)}, bf16[1536,768]{1,0:T(8,128)(2,1)}, u32[]{:S(2)}) copy-start(bf16[1536,768]{1,0:T(8,128)(2,1)} %constant.26.clone.table) | copy-start | bytes 7077892
